TPU v7x, 32 devices: a whole 2x2x4 slice. The times are simulated.
32 devices in a mesh: seq: 8 (over z, core), tp: 4 (over y, x).
Axes of the slice: x: 2, y: 2, z: 4, core: 2. Of those that a mesh axis runs over, the one named last changes fastest.
Arguments:
- tokens: bfloat16 [96, 6, 32, 1024], P('seq'), may hold values from -6 to 6
- context: bfloat16 [4096, 6, 768], replicated, may hold values from -6 to 6
- group_ids: int32 [6], replicated, may hold values from 0 to 15
- source_table: float32 [16, 9216], replicated, may hold values from -3 to 3
- w_query: bfloat16 [1024, 1024], P(None, 'tp'), may hold values from -0.1875 to 0.1875
- w_key: bfloat16 [768, 1024], P(None, 'tp'), may hold values from -0.21875 to 0.21875
- w_value: bfloat16 [768, 1024], P(None, 'tp'), may hold values from -0.21875 to 0.21875
- w_out: bfloat16 [1024, 1024], P('tp'), may hold values from -4 to 4
- w_self_query: bfloat16 [1024, 1024], P(None, 'tp'), may hold values from -0.1875 to 0.1875
- w_self_key: bfloat16 [1024, 1024], P(None, 'tp'), may hold values from -0.1875 to 0.1875
- w_self_value: bfloat16 [1024, 1024], P(None, 'tp'), may hold values from -0.1875 to 0.1875
- w_self_out: bfloat16 [1024, 1024], P('tp'), may hold values from -4 to 4
- w_up: bfloat16 [1024, 4096], P(None, 'tp'), may hold values from -0.1875 to 0.1875
- w_down: bfloat16 [4096, 1024], P('tp'), may hold values from -0.4375 to 0.4375
- w_deconv: bfloat16 [1024, 1280], replicated, may hold values from -0.1875 to 0.1875
- deconv_bias: float32 [80], replicated, may hold values from -4 to 4
- out_cotangent: bfloat16 [96, 6, 32, 1024], P('seq', None, 'tp'), may hold values from -6 to 6
- plane_cotangent: bfloat16 [192, 6, 5120], P('seq', None, 'tp'), may hold values from -6 to 6
Outputs:
- out_tokens: bfloat16 [96, 6, 32, 1024], P('seq', None, 'tp')
- planes: float32 [192, 6, 5120], P('seq', None, 'tp')
- grad_tokens: float32 [96, 6, 32, 1024], P('seq')
- grad_query: float32 [1024, 1024], P('seq', 'tp')
- grad_key: float32 [768, 1024], P('seq', 'tp')
- grad_value: float32 [768, 1024], P('seq', 'tp')
- grad_out: float32 [1024, 1024], P('tp', 'seq')
- grad_self_query: float32 [1024, 1024], P('seq', 'tp')
- grad_self_key: float32 [1024, 1024], P('seq', 'tp')
- grad_self_value: float32 [1024, 1024], P('seq', 'tp')
- grad_self_out: float32 [1024, 1024], P('tp', 'seq')
- grad_up: float32 [1024, 4096], P('seq', 'tp')
- grad_down: float32 [4096, 1024], P('tp', 'seq')
- grad_deconv: float32 [1024, 1280], replicated
- grad_bias: float32 [80], replicated
- grad_table: float32 [16, 9216], replicated
Inputs may be any that keep to these rules, and one draw needn't show every extreme that they name: `group_ids`: each item's row of source_table.
All inputs are finite; a program needn't handle non-finite values.
Results may differ from a plain program's by a relative error of at most 0.025.
The roundings to bfloat16 on the way count: a program that leaves them out, or rounds other values in their place, can miss the bound.
Values may be sent and summed in bfloat16 or wider, within the bound.
No kernel may reach another device: no remote copies, remote signals or barrier semaphores. Data moves between devices by JAX's collectives and lax.ppermute only.
A program may use at most 896 MiB of HBM per device.

v0:
```python
import math

import jax
import jax.numpy as jnp
from jax import lax
from jax.sharding import PartitionSpec as P

HEAD = 64
COUT = 80
PLANE = 32
IMG = 4096
GROUPS = 16


highest = lax.Precision.HIGHEST
epsilon = 1e-06


def with_halo(x, sides, width):
    for axis, dim in sides:
        peers, length = (lax.axis_size(axis), x.shape[dim])
        up = [(i, (i + 1) % peers) for i in range(peers - 1)]
        down = [(j, i) for i, j in up]
        last = lax.slice_in_dim(x, length - width, length, axis=dim)
        initial = lax.slice_in_dim(x, 0, width, axis=dim)
        before = lax.ppermute(last, axis, up)
        after = lax.ppermute(initial, axis, down)
        x = jnp.concatenate([before, x, after], axis=dim)
    return x


def spread_taps(padded, upper, lower):
    even_rows = padded[1:-1, :, :, 1] + upper * padded[:-2, :, :, 3]
    odd_rows = lower * padded[2:, :, :, 0] + padded[1:-1, :, :, 2]
    rows_both = jnp.stack([even_rows, odd_rows], axis=1)
    even_cols = rows_both[:, :, :, 1:-1, 1] + rows_both[:, :, :, :-2, 3]
    odd_cols = rows_both[:, :, :, 2:, 0] + rows_both[:, :, :, 1:-1, 2]
    joined = jnp.stack([even_cols, odd_cols], axis=4)
    shape = joined.shape
    return joined.reshape(shape[0] * 2, shape[2], shape[3] * 2 * shape[5])


def norm_parts(value):
    centred = value - jnp.mean(value, axis=-1, keepdims=True)
    inverse = lax.rsqrt(jnp.mean(centred * centred, axis=-1, keepdims=True) + epsilon)
    return (centred * inverse, inverse)


def norm_back(normed, inverse, incoming):
    return inverse * (
        incoming
        - jnp.mean(incoming, axis=-1, keepdims=True)
        - normed * jnp.mean(incoming * normed, axis=-1, keepdims=True)
    )


def attend(query_heads, key_heads, value_heads):
    head_scale = 1.0 / math.sqrt(query_heads.shape[-1])
    scores = (
        jnp.einsum("iqhe,iphe->ihqp", query_heads, key_heads, preferred_element_type=jnp.float32)
        * head_scale
    )
    top_score = jnp.max(scores, axis=-1, keepdims=True)
    expon = jnp.exp(scores - top_score)
    totals = jnp.sum(expon, axis=-1, keepdims=True)
    probs = expon / totals
    log_total = top_score + jnp.log(totals)
    mixed = jnp.einsum(
        "ihqp,iphe->iqhe",
        probs.astype(jnp.bfloat16),
        value_heads,
        preferred_element_type=jnp.float32,
    ).astype(jnp.bfloat16)
    return (mixed, log_total)


def attend_back(query_heads, key_heads, value_heads, log_total, grad_mixed):
    head_scale = 1.0 / math.sqrt(query_heads.shape[-1])
    scores_again = (
        jnp.einsum("iqhe,iphe->ihqp", query_heads, key_heads, preferred_element_type=jnp.float32)
        * head_scale
    )
    probs_again = jnp.exp(scores_again - log_total)
    grad_probs = jnp.einsum(
        "iqhe,iphe->ihqp", grad_mixed, value_heads, preferred_element_type=jnp.float32
    )
    grad_values = jnp.einsum(
        "ihqp,iqhe->iphe",
        probs_again.astype(jnp.bfloat16),
        grad_mixed,
        preferred_element_type=jnp.float32,
    )
    grad_scores = (
        probs_again * (grad_probs - jnp.sum(probs_again * grad_probs, axis=-1, keepdims=True))
    ).astype(jnp.bfloat16)
    grad_queries = (
        jnp.einsum("ihqp,iphe->iqhe", grad_scores, key_heads, preferred_element_type=jnp.float32)
        * head_scale
    ).astype(jnp.bfloat16)
    grad_keys = (
        jnp.einsum("ihqp,iqhe->iphe", grad_scores, query_heads, preferred_element_type=jnp.float32)
        * head_scale
    )
    return (grad_queries, grad_keys, grad_values)


def share_keys(self_keys, self_values):
    return (
        lax.all_gather(self_keys, "seq", axis=1, tiled=True),
        lax.all_gather(self_values, "seq", axis=1, tiled=True),
    )


def body(
    tokens,
    context,
    group_ids,
    source_table,
    w_query,
    w_key,
    w_value,
    w_out,
    w_self_query,
    w_self_key,
    w_self_value,
    w_self_out,
    w_up,
    w_down,
    w_deconv,
    deconv_bias,
    out_cotangent,
    plane_cotangent,
):
    rows_here, item_count, plane_cols, model_width = tokens.shape
    cols_here = out_cotangent.shape[2]
    col_start = lax.axis_index("tp") * cols_here
    heads_here = w_query.shape[1] // HEAD
    local_width = w_query.shape[1]
    picker = (group_ids[:, None] == jnp.arange(GROUPS, dtype=jnp.int32)[None, :]).astype(
        jnp.float32
    )
    modulate = jnp.dot(picker, source_table, precision=highest).reshape(item_count, 9, model_width)

    def piece(index):
        return modulate[None, :, index][:, :, None, :]

    residual = tokens.astype(jnp.float32)
    first_hat, first_inv = norm_parts(residual)
    first_in = (first_hat * (1.0 + piece(1)) + piece(0)).astype(jnp.bfloat16)
    queries = jnp.einsum(
        "ricd,de->irce", first_in, w_query, preferred_element_type=jnp.float32
    ).astype(jnp.bfloat16)
    query_heads = queries.reshape(item_count, rows_here * plane_cols, heads_here, HEAD)
    key_rows = jnp.einsum("pid,de->ipe", context, w_key, preferred_element_type=jnp.float32).astype(
        jnp.bfloat16
    )
    value_rows = jnp.einsum(
        "pid,de->ipe", context, w_value, preferred_element_type=jnp.float32
    ).astype(jnp.bfloat16)
    key_heads = key_rows.reshape(item_count, IMG, heads_here, HEAD)
    value_heads = value_rows.reshape(item_count, IMG, heads_here, HEAD)
    mixed, cross_log = attend(query_heads, key_heads, value_heads)
    mixed_rows = mixed.reshape(item_count, rows_here, plane_cols, local_width)
    cross_part = jnp.einsum("irce,ef->ricf", mixed_rows, w_out, preferred_element_type=jnp.float32)
    branch_a = lax.psum(cross_part, "tp")
    middle = residual + piece(2) * branch_a
    self_hat, self_inv = norm_parts(middle)
    self_in = (self_hat * (1.0 + piece(4)) + piece(3)).astype(jnp.bfloat16)
    self_queries = jnp.einsum(
        "ricd,de->irce", self_in, w_self_query, preferred_element_type=jnp.float32
    ).astype(jnp.bfloat16)
    self_keys = jnp.einsum(
        "ricd,de->irce", self_in, w_self_key, preferred_element_type=jnp.float32
    ).astype(jnp.bfloat16)
    self_values = jnp.einsum(
        "ricd,de->irce", self_in, w_self_value, preferred_element_type=jnp.float32
    ).astype(jnp.bfloat16)
    all_keys, all_values = share_keys(self_keys, self_values)
    self_query_heads = self_queries.reshape(item_count, rows_here * plane_cols, heads_here, HEAD)
    self_mixed, self_log = attend(
        self_query_heads,
        all_keys.reshape(item_count, -1, heads_here, HEAD),
        all_values.reshape(item_count, -1, heads_here, HEAD),
    )
    self_rows = self_mixed.reshape(item_count, rows_here, plane_cols, local_width)
    self_part = jnp.einsum(
        "irce,ef->ricf", self_rows, w_self_out, preferred_element_type=jnp.float32
    )
    branch_s = lax.psum(self_part, "tp")
    middle_two = middle + piece(5) * branch_s
    second_hat, second_inv = norm_parts(middle_two)
    second_in = (second_hat * (1.0 + piece(7)) + piece(6)).astype(jnp.bfloat16)
    hidden = jnp.einsum("ricd,df->ricf", second_in, w_up, preferred_element_type=jnp.float32)
    active_f, gelu_back = jax.vjp(lambda value: jax.nn.gelu(value, approximate=False), hidden)
    active = active_f.astype(jnp.bfloat16)
    mlp_part = jnp.einsum("ricf,fd->ricd", active, w_down, preferred_element_type=jnp.float32)
    branch_b = lax.psum(mlp_part, "tp")
    result = middle_two + piece(8) * branch_b
    rounded = result.astype(jnp.bfloat16)
    out_tile = lax.dynamic_slice_in_dim(rounded, col_start, cols_here, 2)
    side = jnp.pad(rounded, ((0, 0), (0, 0), (1, 1), (0, 0)))
    wide_tile = lax.dynamic_slice_in_dim(side, col_start, cols_here + 2, 2)
    plane_row = (lax.axis_index("seq") * rows_here + jnp.arange(rows_here, dtype=jnp.int32)) % PLANE
    upper_keep = (plane_row != 0).astype(jnp.float32)
    lower_keep = (plane_row != PLANE - 1).astype(jnp.float32)
    widened = with_halo(wide_tile, (("seq", 0),), 1)
    taps = jnp.einsum("ricd,dt->rict", widened, w_deconv, preferred_element_type=jnp.float32)
    taps = taps.reshape(rows_here + 2, item_count, cols_here + 2, 4, 4, COUT)
    planes = spread_taps(
        taps, upper_keep[:, None, None, None, None], lower_keep[:, None, None, None, None]
    )
    planes = planes + jnp.tile(deconv_bias, 2 * cols_here)
    incoming = plane_cotangent.reshape(2 * rows_here, item_count, 2 * cols_here, COUT)
    grad_edges = with_halo(incoming, (("seq", 0), ("tp", 2)), 1)
    upper_mask = upper_keep.astype(jnp.bfloat16)[:, None, None, None]
    lower_mask = lower_keep.astype(jnp.bfloat16)[:, None, None, None]
    first_pair = grad_edges[:-2].reshape(rows_here, 2, item_count, 2 * cols_here + 2, COUT)
    last_pair = grad_edges[2:].reshape(rows_here, 2, item_count, 2 * cols_here + 2, COUT)
    row_taps = jnp.stack(
        [
            first_pair[:, 0] * upper_mask,
            first_pair[:, 1],
            last_pair[:, 0],
            last_pair[:, 1] * lower_mask,
        ],
        axis=3,
    )
    left_pair = row_taps[:, :, :-2].reshape(rows_here, item_count, cols_here, 2, 4, COUT)
    right_pair = row_taps[:, :, 2:].reshape(rows_here, item_count, cols_here, 2, 4, COUT)
    tap_grads = jnp.stack(
        [
            left_pair[:, :, :, 0],
            left_pair[:, :, :, 1],
            right_pair[:, :, :, 0],
            right_pair[:, :, :, 1],
        ],
        axis=4,
    )
    tap_grads = tap_grads.reshape(rows_here, item_count, cols_here, 16 * COUT)
    tile_grad = out_cotangent.astype(jnp.float32) + jnp.einsum(
        "rict,dt->ricd", tap_grads, w_deconv, preferred_element_type=jnp.float32
    )
    grad_deconv = jnp.einsum(
        "ricd,rict->dt", out_tile, tap_grads, preferred_element_type=jnp.float32
    )
    grad_bias = jnp.sum(incoming.astype(jnp.float32), axis=(0, 1, 2))
    grad_result = lax.all_gather(tile_grad, "tp", axis=2, tiled=True)
    grad_mlp = (piece(8) * grad_result).astype(jnp.bfloat16)
    grad_gate_b = jnp.sum(grad_result * branch_b, axis=(0, 2))
    grad_active = jnp.einsum("ricd,fd->ricf", grad_mlp, w_down, preferred_element_type=jnp.float32)
    grad_hidden = gelu_back(grad_active)[0].astype(jnp.bfloat16)
    grad_down = jnp.einsum("ricf,ricd->fd", active, grad_mlp, preferred_element_type=jnp.float32)
    grad_up = jnp.einsum(
        "ricd,ricf->df", second_in, grad_hidden, preferred_element_type=jnp.float32
    )
    second_part = jnp.einsum("ricf,df->ricd", grad_hidden, w_up, preferred_element_type=jnp.float32)
    grad_second = lax.psum(second_part, "tp")
    grad_shift_b = jnp.sum(grad_second, axis=(0, 2))
    grad_scale_b = jnp.sum(grad_second * second_hat, axis=(0, 2))
    grad_mid_two = grad_result + norm_back(second_hat, second_inv, grad_second * (1.0 + piece(7)))
    grad_self = (piece(5) * grad_mid_two).astype(jnp.bfloat16)
    grad_gate_s = jnp.sum(grad_mid_two * branch_s, axis=(0, 2))
    grad_self_mixed = jnp.einsum(
        "ricf,ef->irce", grad_self, w_self_out, preferred_element_type=jnp.float32
    ).astype(jnp.bfloat16)
    grad_self_out = jnp.einsum(
        "irce,ricf->ef", self_rows, grad_self, preferred_element_type=jnp.float32
    )
    back_keys, back_values = (all_keys, all_values)
    self_grad_q, self_grad_k, self_grad_v = attend_back(
        self_query_heads,
        back_keys.reshape(item_count, -1, heads_here, HEAD),
        back_values.reshape(item_count, -1, heads_here, HEAD),
        self_log,
        grad_self_mixed.reshape(item_count, rows_here * plane_cols, heads_here, HEAD),
    )
    full_shape = (item_count, back_keys.shape[1], plane_cols, local_width)
    local_k, local_v = (
        lax.psum_scatter(self_grad_k.reshape(full_shape), "seq", scatter_dimension=1, tiled=True),
        lax.psum_scatter(self_grad_v.reshape(full_shape), "seq", scatter_dimension=1, tiled=True),
    )
    local_k = local_k.astype(jnp.bfloat16)
    local_v = local_v.astype(jnp.bfloat16)
    self_grad_rows = self_grad_q.reshape(item_count, rows_here, plane_cols, local_width)
    grad_self_query = jnp.einsum(
        "ricd,irce->de", self_in, self_grad_rows, preferred_element_type=jnp.float32
    )
    grad_self_key = jnp.einsum(
        "ricd,irce->de", self_in, local_k, preferred_element_type=jnp.float32
    )
    grad_self_value = jnp.einsum(
        "ricd,irce->de", self_in, local_v, preferred_element_type=jnp.float32
    )
    self_back = jnp.einsum(
        "irce,de->ricd", self_grad_rows, w_self_query, preferred_element_type=jnp.float32
    )
    self_back = self_back + jnp.einsum(
        "irce,de->ricd", local_k, w_self_key, preferred_element_type=jnp.float32
    )
    self_back = self_back + jnp.einsum(
        "irce,de->ricd", local_v, w_self_value, preferred_element_type=jnp.float32
    )
    grad_third = lax.psum(self_back, "tp")
    grad_shift_s = jnp.sum(grad_third, axis=(0, 2))
    grad_scale_s = jnp.sum(grad_third * self_hat, axis=(0, 2))
    grad_middle = grad_mid_two + norm_back(self_hat, self_inv, grad_third * (1.0 + piece(4)))
    grad_attn = (piece(2) * grad_middle).astype(jnp.bfloat16)
    grad_gate_a = jnp.sum(grad_middle * branch_a, axis=(0, 2))
    grad_mixed = jnp.einsum(
        "ricf,ef->irce", grad_attn, w_out, preferred_element_type=jnp.float32
    ).astype(jnp.bfloat16)
    grad_out = jnp.einsum(
        "irce,ricf->ef", mixed_rows, grad_attn, preferred_element_type=jnp.float32
    )
    grad_queries, grad_keys, grad_values = attend_back(
        query_heads,
        key_heads,
        value_heads,
        cross_log,
        grad_mixed.reshape(item_count, rows_here * plane_cols, heads_here, HEAD),
    )
    grad_query_rows = grad_queries.reshape(item_count, rows_here, plane_cols, local_width)
    grad_query = jnp.einsum(
        "ricd,irce->de", first_in, grad_query_rows, preferred_element_type=jnp.float32
    )
    grad_key = jnp.einsum(
        "pid,ipe->de",
        context,
        grad_keys.astype(jnp.bfloat16).reshape(item_count, IMG, local_width),
        preferred_element_type=jnp.float32,
    )
    grad_value = jnp.einsum(
        "pid,ipe->de",
        context,
        grad_values.astype(jnp.bfloat16).reshape(item_count, IMG, local_width),
        preferred_element_type=jnp.float32,
    )
    first_part = jnp.einsum(
        "irce,de->ricd", grad_query_rows, w_query, preferred_element_type=jnp.float32
    )
    grad_first = lax.psum(first_part, "tp")
    grad_shift_a = jnp.sum(grad_first, axis=(0, 2))
    grad_scale_a = jnp.sum(grad_first * first_hat, axis=(0, 2))
    grad_tokens = grad_middle + norm_back(first_hat, first_inv, grad_first * (1.0 + piece(1)))
    grad_mods = jnp.stack(
        [
            grad_shift_a,
            grad_scale_a,
            grad_gate_a,
            grad_shift_s,
            grad_scale_s,
            grad_gate_s,
            grad_shift_b,
            grad_scale_b,
            grad_gate_b,
        ],
        axis=1,
    )
    grad_table = jnp.dot(
        picker.T, grad_mods.reshape(item_count, 9 * model_width), precision=highest
    )
    grad_table = grad_table * (lax.axis_index("tp") == 0).astype(jnp.float32)
    grad_deconv, grad_bias, grad_table = lax.psum(
        (grad_deconv, grad_bias, grad_table), ("seq", "tp")
    )
    (
        grad_query,
        grad_key,
        grad_value,
        grad_out,
        grad_self_query,
        grad_self_key,
        grad_self_value,
        grad_self_out,
        grad_up,
        grad_down,
    ) = (
        lax.psum_scatter(grad_query, "seq", scatter_dimension=0, tiled=True),
        lax.psum_scatter(grad_key, "seq", scatter_dimension=0, tiled=True),
        lax.psum_scatter(grad_value, "seq", scatter_dimension=0, tiled=True),
        lax.psum_scatter(grad_out, "seq", scatter_dimension=1, tiled=True),
        lax.psum_scatter(grad_self_query, "seq", scatter_dimension=0, tiled=True),
        lax.psum_scatter(grad_self_key, "seq", scatter_dimension=0, tiled=True),
        lax.psum_scatter(grad_self_value, "seq", scatter_dimension=0, tiled=True),
        lax.psum_scatter(grad_self_out, "seq", scatter_dimension=1, tiled=True),
        lax.psum_scatter(grad_up, "seq", scatter_dimension=0, tiled=True),
        lax.psum_scatter(grad_down, "seq", scatter_dimension=1, tiled=True),
    )
    return (
        out_tile,
        planes,
        grad_tokens,
        grad_query,
        grad_key,
        grad_value,
        grad_out,
        grad_self_query,
        grad_self_key,
        grad_self_value,
        grad_self_out,
        grad_up,
        grad_down,
        grad_deconv,
        grad_bias,
        grad_table,
    )


def solution(mesh):
    in_specs = (
        P("seq", None, None, None),
        P(),
        P(),
        P(),
        P(None, "tp"),
        P(None, "tp"),
        P(None, "tp"),
        P("tp", None),
        P(None, "tp"),
        P(None, "tp"),
        P(None, "tp"),
        P("tp", None),
        P(None, "tp"),
        P("tp", None),
        P(),
        P(),
        P("seq", None, "tp", None),
        P("seq", None, "tp"),
    )
    out_specs = (
        P("seq", None, "tp", None),
        P("seq", None, "tp"),
        P("seq", None, None, None),
        P("seq", "tp"),
        P("seq", "tp"),
        P("seq", "tp"),
        P("tp", "seq"),
        P("seq", "tp"),
        P("seq", "tp"),
        P("seq", "tp"),
        P("tp", "seq"),
        P("seq", "tp"),
        P("tp", "seq"),
        P(),
        P(),
        P(),
    )
    return jax.shard_map(body, mesh=mesh, in_specs=in_specs, out_specs=out_specs, check_vma=False)
```

profile of v0, /device:TPU:0, one launch (start us, length us, event | category | flops | bytes accessed | tf_op | source)
XLA Modules:
  0.0 3909.8 jit_solution(8087720281142453039)
XLA Ops:
  66.6 54.7 %multiply_reduce_fusion.1 = (f32[6,4,384]{2,1,0:T(4,128)S(1)}, f32[6,4,384,4096]{3,2,1,0:T(8,128)}) fusion(bf16[6,384,4,64]{1,3,2,0:T(8,128)(2,1)} %copy.391, bf16[6,4096,4,64]{1,3,2,0:T(8,128)(2,1)} %bitcast.341), kind=kOutput, calls=%fused_computation.6 | convolution fusion | flops 4907326464 | bytes 164794368 | tf_op jit(solution)/shard_map/iqhe,iphe->ihqp/dot_general | solution.py:60
  121.4 46.0 %fusion = f32[6,4,384]{2,1,0:T(4,128)S(1)} fusion(f32[6,4,384,4096]{3,2,1,0:T(8,128)} %get-tuple-element.190, f32[6,4,384]{2,1,0:T(4,128)S(1)} %get-tuple-element.189), kind=kLoop, calls=%fused_computation.5 | loop fusion | flops 113236992 | bytes 151068672 | tf_op jit(solution)/shard_map/reduce_sum | solution.py:65
  167.5 53.8 %fusion.124 = bf16[6,384,4,64]{1,3,2,0:T(8,128)(2,1)} fusion(bf16[6,4096,4,64]{1,3,2,0:T(8,128)(2,1)} %bitcast.347, f32[6,4,384,4096]{3,2,1,0:T(8,128)} %get-tuple-element.190, f32[6,4,384]{2,1,0:T(4,128)S(1)} %fusion, f32[6,4,384]{2,1,0:T(4,128)S(1)} %get-tuple-element.189), kind=kOutput, calls=%fused_computation.162 | convolution fusion | flops 4983422976 | bytes 164831232 | tf_op jit(solution)/shard_map/ihqp,iphe->iqhe/dot_general | solution.py:68
  237.4 191.5 %all-reduce.14.cloned.1.call-done = f32[12,6,32,1024]{3,2,0,1:T(8,128)} async-done(((f32[12,6,32,1024]{3,2,0,1:T(8,128)}), f32[12,6,32,1024]{3,2,0,1:T(8,128)}) %all-reduce.14.cloned.1.call-update) | async-done | bytes 9437200 | tf_op jit(solution)/shard_map/psum | solution.py:165
  473.4 70.8 %all-gather.4.cloned.1.call-done = bf16[6,96,32,256]{3,2,0,1:T(8,128)(2,1)} async-done(((bf16[6,12,32,256]{3,2,0,1:T(8,128)(2,1)}), bf16[6,96,32,256]{3,2,0,1:T(8,128)(2,1)}) %all-gather.4.cloned.1.call-update) | async-done | bytes 9437200 | tf_op jit(solution)/shard_map/all_gather | solution.py:110
  698.7 41.5 %multiply_reduce_fusion.3 = (f32[6,4,384]{2,1,0:T(4,128)S(1)}, f32[6,4,384,3072]{3,2,1,0:T(8,128)}) fusion(bf16[6,384,4,64]{1,3,2,0:T(8,128)(2,1)} %copy.399, bf16[6,3072,4,64]{1,3,2,0:T(8,128)(2,1)} %copy.400), kind=kOutput, calls=%fused_computation.14 | convolution fusion | flops 3680492544 | bytes 123899904 | tf_op jit(solution)/shard_map/iqhe,iphe->ihqp/dot_general | solution.py:60
  740.1 34.9 fusion.1
  775.1 41.4 %fusion.125 = bf16[6,384,4,64]{1,3,2,0:T(8,128)(2,1)} fusion(bf16[6,3072,4,64]{1,3,2,0:T(8,128)(2,1)} %copy.401, f32[6,4,384,3072]{3,2,1,0:T(8,128)} %get-tuple-element.192, f32[6,4,384]{2,1,0:T(4,128)S(1)} %fusion.1, f32[6,4,384]{2,1,0:T(4,128)S(1)} %get-tuple-element.191), kind=kOutput, calls=%fused_computation.163 | convolution fusion | flops 3737714688 | bytes 123936768 | tf_op jit(solution)/shard_map/ihqp,iphe->iqhe/dot_general | solution.py:68
  877.7 144.0 %all-reduce.16.cloned.1.call-done = f32[12,6,32,1024]{3,2,0,1:T(8,128)} async-done(((f32[12,6,32,1024]{3,2,0,1:T(8,128)}), f32[12,6,32,1024]{3,2,0,1:T(8,128)}) %all-reduce.16.cloned.1.call-update) | async-done | bytes 9437200 | tf_op jit(solution)/shard_map/psum | solution.py:189
  1069.7 50.1 %all-gather.8.cloned.1.call-done = f32[12,6,32,1024]{3,2,0,1:T(8,128)} async-done(((f32[12,6,8,1024]{3,2,0,1:T(8,128)}), f32[12,6,32,1024]{3,2,0,1:T(8,128)}) %all-gather.8.cloned.1.call-update) | async-done | bytes 9437200 | tf_op jit(solution)/shard_map/all_gather | solution.py:247
  1146.8 186.9 %all-reduce.18.cloned.1.call-done = f32[12,6,32,1024]{3,2,0,1:T(8,128)} async-done(((f32[12,6,32,1024]{3,2,0,1:T(8,128)}), f32[12,6,32,1024]{3,2,0,1:T(8,128)}) %all-reduce.18.cloned.1.call-update) | async-done | bytes 9437200 | tf_op jit(solution)/shard_map/psum | solution.py:257
  1371.0 75.7 %multiply_reduce_fusion.2 = (f32[6,4,384]{2,1,0:T(4,128)S(1)}, f32[6,4,384,3072]{3,2,1,0:T(8,128)}) fusion(f32[6,4,384,3072]{3,2,1,0:T(8,128)} %get-tuple-element.192, f32[6,4,384]{2,1,0:T(4,128)S(1)} %bitcast.362, bf16[6,384,4,64]{1,3,2,0:T(8,128)(2,1)} %copy.427, bf16[6,3072,4,64]{1,3,2,0:T(8,128)(2,1)} %copy.401), kind=kOutput, calls=%fused_computation.8 | convolution fusion | flops 3737115648 | bytes 237182976 | tf_op jit(solution)/shard_map/iqhe,iphe->ihqp/dot_general | solution.py:84
  1446.8 88.1 %multiply_convert_fusion.1 = bf16[6,4,384,3072]{3,2,1,0:T(8,128)(2,1)} fusion(f32[6,4,384,3072]{3,2,1,0:T(8,128)} %get-tuple-element.195, f32[6,4,384,3072]{3,2,1,0:T(8,128)} %get-tuple-element.192, f32[6,4,384]{2,1,0:T(4,128)S(1)} %get-tuple-element.194, f32[6,4,384]{2,1,0:T(4,128)S(1)} %bitcast.363), kind=kLoop, calls=%fused_computation.7 | loop fusion | flops 141557760 | bytes 283189248 | tf_op jit(solution)/shard_map/convert_element_type | solution.py:95
  1590.5 44.8 %fusion.37 = f32[6,3072,4,64]{1,3,2,0:T(8,128)} fusion(bf16[6,384,4,64]{1,3,2,0:T(8,128)(2,1)} %copy.427, f32[6,4,384,3072]{3,2,1,0:T(8,128)} %get-tuple-element.192, f32[6,4,384]{2,1,0:T(4,128)S(1)} %bitcast.364), kind=kOutput, calls=%fused_computation.88 | convolution fusion | flops 3708813312 | bytes 133337088 | tf_op jit(solution)/shard_map/ihqp,iqhe->iphe/dot_general | solution.py:87
  1651.3 33.4 copy.432
  1684.7 34.2 reshape.356
  1718.9 33.4 copy.434
  1752.3 34.2 reshape.357
  1786.6 731.6 %all-reduce.25 = (bf16[6,96,32,256]{3,2,1,0:T(8,128)(2,1)}, bf16[6,96,32,256]{3,2,1,0:T(8,128)(2,1)}) all-reduce(f32[6,96,32,256]{3,2,1,0:T(8,128)} %reshape.356, f32[6,96,32,256]{3,2,1,0:T(8,128)} %reshape.357), channel_id=2, replica_groups=mesh['seq'=8,'tp'=4] {'seq'}, use_global_device_ids=true, to_apply=%region_17.18.clone | all-reduce | flops 9437184 | bytes 56623104
  2542.0 175.5 %all-reduce.20.cloned.1.call-done = f32[12,6,32,1024]{3,2,0,1:T(8,128)} async-done(((f32[12,6,32,1024]{3,2,0,1:T(8,128)}), f32[12,6,32,1024]{3,2,0,1:T(8,128)}) %all-reduce.20.cloned.1.call-update) | async-done | bytes 9437200 | tf_op jit(solution)/shard_map/psum | solution.py:303
  2754.4 101.3 %multiply_reduce_fusion = (f32[6,4,384]{2,1,0:T(4,128)S(1)}, f32[6,4,384,4096]{3,2,1,0:T(8,128)}) fusion(f32[6,4,384,4096]{3,2,1,0:T(8,128)} %get-tuple-element.190, f32[6,4,384]{2,1,0:T(4,128)S(1)} %bitcast.355, bf16[6,384,4,64]{1,3,2,0:T(8,128)(2,1)} %copy.437, bf16[6,4096,4,64]{1,3,2,0:T(8,128)(2,1)} %bitcast.348), kind=kOutput, calls=%fused_computation.1 | convolution fusion | flops 4982823936 | bytes 315826176 | tf_op jit(solution)/shard_map/iqhe,iphe->ihqp/dot_general | solution.py:84
  2855.7 115.6 %multiply_convert_fusion = bf16[6,4,384,4096]{3,2,1,0:T(8,128)(2,1)} fusion(f32[6,4,384,4096]{3,2,1,0:T(8,128)} %get-tuple-element.197, f32[6,4,384,4096]{3,2,1,0:T(8,128)} %get-tuple-element.190, f32[6,4,384]{2,1,0:T(4,128)S(1)} %get-tuple-element.196, f32[6,4,384]{2,1,0:T(4,128)S(1)} %bitcast.356), kind=kLoop, calls=%fused_computation | loop fusion | flops 188743680 | bytes 377561088 | tf_op jit(solution)/shard_map/convert_element_type | solution.py:95
  2971.2 34.0 fusion.104
  3068.5 34.4 multiply_convert_fusion.2
  3103.0 56.4 %fusion.34 = bf16[6,4,64,4096]{3,2,1,0:T(8,128)(2,1)} fusion(bf16[6,384,4,64]{1,3,2,0:T(8,128)(2,1)} %copy.437, f32[6,4,384,4096]{3,2,1,0:T(8,128)} %get-tuple-element.190, f32[6,4,384]{2,1,0:T(4,128)S(1)} %bitcast.357), kind=kOutput, calls=%fused_computation.82 | convolution fusion | flops 4951375872 | bytes 164794368 | tf_op jit(solution)/shard_map/ihqp,iqhe->iphe/dot_general | solution.py:87
  3215.0 39.8 %psum.70 = f32[80]{0:T(128)} all-reduce(f32[80]{0:T(128)S(1)} %reduce_sum.259), channel_id=1, replica_groups=mesh['seq'=8,'tp'=4] {'seq','tp'}, use_global_device_ids=true, to_apply=%region_39.40 | all-reduce | flops 80 | bytes 640 | tf_op jit(solution)/shard_map/psum | solution.py:363
  3261.4 103.9 %all-reduce.24.cloned.1.call-done = (f32[12,6,32,1024]{3,2,0,1:T(8,128)}, f32[12,6,32,1024]{3,2,0,1:T(8,128)}) async-done(((f32[12,6,32,1024]{3,2,0,1:T(8,128)}, f32[12,6,32,1024]{3,2,0,1:T(8,128)}), (f32[12,6,32,1024]{3,2,0,1:T(8,128)}, f32[12,6,32,1024]{3,2,0,1:T(8,128)})) %all-reduce.24.cloned.1.call-update) | async-done | bytes 18874384 | tf_op jit(solution)/shard_map/psum | solution.py:197
  3506.2 33.5 reduce-scatter.27.cloned.1.call-done
  3539.7 33.7 reduce-scatter.29.cloned.1.call-done
  3671.9 33.5 reduce-scatter.21.cloned.1.call-done
  3705.4 33.4 reduce-scatter.23.cloned.1.call-done
  3738.8 158.2 %all-reduce.22.cloned.1.call-done = (f32[1024,1280]{1,0:T(8,128)}, f32[16,9216]{1,0:T(8,128)}) async-done(((f32[1024,1280]{1,0:T(8,128)}, f32[16,9216]{1,0:T(8,128)}), (f32[1024,1280]{1,0:T(8,128)}, f32[16,9216]{1,0:T(8,128)})) %all-reduce.22.cloned.1.call-update) | async-done | bytes 5832720 | tf_op jit(solution)/shard_map/psum | solution.py:363
  (378 shorter events, 949.4 us)
Async XLA Ops:
  7.2 865.6 %copy-start = (bf16[1024,1280]{1,0:T(8,128)(2,1)S(1)}, bf16[1024,1280]{1,0:T(8,128)(2,1)}, u32[]{:S(2)}) copy-start(bf16[1024,1280]{1,0:T(8,128)(2,1)} %param.32) | copy-start | bytes 7864324
  7.2 421.7 %all-reduce.14.cloned.1.call-start = ((), (), s32[]{:S(2)}) async-start(), calls=%async_computation.10 | async-start | bytes 18874368 | tf_op jit(solution)/shard_map/psum | solution.py:165
  230.9 198.0 %copy-start.45 = (f32[6,1024]{1,0:T(8,128)S(1)}, f32[6,1024]{1,0:T(8,128)}, u32[]{:S(2)}) copy-start(f32[6,1024]{1,0:T(8,128)} %get-tuple-element.188) | copy-start | bytes 73732
  237.3 306.9 %all-gather.4.cloned.1.call-start = ((), (), s32[]{:S(2)}) async-start(), calls=%async_computation.11 | async-start | bytes 10616832 | tf_op jit(solution)/shard_map/all_gather | solution.py:110
  453.4 181.8 %all-gather.6.cloned.1.call-start = ((), (), s32[]{:S(2)}) async-start(), calls=%async_computation.12 | async-start | bytes 10616832 | tf_op jit(solution)/shard_map/all_gather | solution.py:109
  458.3 563.4 %all-reduce.16.cloned.1.call-start = ((), (), s32[]{:S(2)}) async-start(), calls=%async_computation.13 | async-start | bytes 18874368 | tf_op jit(solution)/shard_map/psum | solution.py:189
  832.5 287.3 %all-gather.8.cloned.1.call-start = ((), (), s32[]{:S(2)}) async-start(), calls=%async_computation.14 | async-start | bytes 11796480 | tf_op jit(solution)/shard_map/all_gather | solution.py:247
  833.4 8.6 collective-permute-start.3
  835.4 7.3 collective-permute-start.2
  843.6 7.5 collective-permute-start.5
  844.9 7.6 collective-permute-start.4
  877.6 456.1 %all-reduce.18.cloned.1.call-start = ((), (), s32[]{:S(2)}) async-start(), calls=%async_computation.15 | async-start | bytes 18874368 | tf_op jit(solution)/shard_map/psum | solution.py:257
  1033.8 309.9 %copy-start.25 = (f32[12,6,32]{2,0,1:T(8,128)}, f32[12,6,32]{2,0,1:T(8,128)S(1)}, u32[]{:S(2)}) copy-start(f32[12,6,32]{2,0,1:T(8,128)S(1)} %broadcast_multiply_fusion.6) | copy-start | bytes 27652
  1039.4 304.4 %copy-start.39 = (f32[12,6,32]{2,0,1:T(8,128)}, f32[12,6,32]{2,0,1:T(8,128)S(1)}, u32[]{:S(2)}) copy-start(f32[12,6,32]{2,0,1:T(8,128)S(1)} %add_rsqrt_fusion) | copy-start | bytes 27652
  1144.9 1572.6 %all-reduce.20.cloned.1.call-start = ((), (), s32[]{:S(2)}) async-start(), calls=%async_computation.16 | async-start | bytes 18874368 | tf_op jit(solution)/shard_map/psum | solution.py:303
  1786.6 731.6 %copy-start.32 = (bf16[1024,256]{1,0:T(8,128)(2,1)S(1)}, bf16[1024,256]{1,0:T(8,128)(2,1)}, u32[]{:S(2)}) copy-start(bf16[1024,256]{1,0:T(8,128)(2,1)} %param.27) | copy-start | bytes 1572868
  2530.4 834.9 %all-reduce.24.cloned.1.call-start = ((), (), s32[]{:S(2)}) async-start(), calls=%async_computation.28 | async-start | bytes 37748736 | tf_op jit(solution)/shard_map/psum | solution.py:197
  2531.2 324.5 %copy-start.10 = (f32[3,8,384]{2,1,0:T(8,128)}, f32[3,8,384]{2,1,0:T(8,128)S(1)}, u32[]{:S(2)}) copy-start(f32[3,8,384]{2,1,0:T(8,128)S(1)} %log_add_fusion) | copy-start | bytes 110596
  2531.2 186.3 %copy-start.20 = (f32[12,6,32]{2,0,1:T(8,128)S(1)}, f32[12,6,32]{2,0,1:T(8,128)}, u32[]{:S(2)}) copy-start(f32[12,6,32]{2,0,1:T(8,128)} %copy-done.19) | copy-start | bytes 27652
  3021.3 420.6 %reduce-scatter.33.cloned.1.call-start = ((), (), s32[]{:S(2)}) async-start(), calls=%async_computation.23 | async-start | bytes 4718592 | tf_op jit(solution)/shard_map/reduce_scatter | solution.py:386
  3035.1 437.8 %reduce-scatter.35.cloned.1.call-start = ((), (), s32[]{:S(2)}) async-start(), calls=%async_computation.24 | async-start | bytes 4718592 | tf_op jit(solution)/shard_map/reduce_scatter | solution.py:387
  3046.2 460.1 %reduce-scatter.25.cloned.1.call-start = ((), (), s32[]{:S(2)}) async-start(), calls=%async_computation.19 | async-start | bytes 1179648 | tf_op jit(solution)/shard_map/reduce_scatter | solution.py:382
  3051.4 488.3 %reduce-scatter.27.cloned.1.call-start = ((), (), s32[]{:S(2)}) async-start(), calls=%async_computation.20 | async-start | bytes 1179648 | tf_op jit(solution)/shard_map/reduce_scatter | solution.py:383
  3056.7 516.7 %reduce-scatter.29.cloned.1.call-start = ((), (), s32[]{:S(2)}) async-start(), calls=%async_computation.21 | async-start | bytes 1179648 | tf_op jit(solution)/shard_map/reduce_scatter | solution.py:384
  3061.9 544.9 %reduce-scatter.31.cloned.1.call-start = ((), (), s32[]{:S(2)}) async-start(), calls=%async_computation.22 | async-start | bytes 1179648 | tf_op jit(solution)/shard_map/reduce_scatter | solution.py:385
  3068.5 570.9 %reduce-scatter.37.cloned.1.call-start = ((), (), s32[]{:S(2)}) async-start(), calls=%async_computation.25 | async-start | bytes 884736
  3181.1 490.8 %reduce-scatter.39.cloned.1.call-start = ((), (), s32[]{:S(2)}) async-start(), calls=%async_computation.26 | async-start | bytes 884736
  3208.2 497.2 %reduce-scatter.21.cloned.1.call-start = ((), (), s32[]{:S(2)}) async-start(), calls=%async_computation.17 | async-start | bytes 1179648 | tf_op jit(solution)/shard_map/reduce_scatter | solution.py:378
  3214.7 524.2 %reduce-scatter.23.cloned.1.call-start = ((), (), s32[]{:S(2)}) async-start(), calls=%async_computation.18 | async-start | bytes 1179648 | tf_op jit(solution)/shard_map/reduce_scatter | solution.py:381
  3261.3 635.6 %all-reduce.22.cloned.1.call-start = ((), (), s32[]{:S(2)}) async-start(), calls=%async_computation.27 | async-start | bytes 11665408 | tf_op jit(solution)/shard_map/psum | solution.py:363
  3383.7 27.9 collective-permute-start.1
  3385.3 26.3 collective-permute-start
  (76 other events, 1740.8 us)
Sparse Core Ops, SparseCore 0:
  237.5 191.3 all-reduce.13
  453.5 90.7 all-gather.3
  545.9 89.1 all-gather.5
  832.6 189.0 all-reduce.15
  1023.4 96.3 all-gather.7
  1145.0 188.6 all-reduce.17
  2530.5 186.8 all-reduce.19
  3021.4 343.8 all-reduce.23
  3368.3 53.4 reduce-scatter.32
  3424.7 48.1 reduce-scatter.34
  3475.8 30.3 reduce-scatter.24
  3509.0 30.6 reduce-scatter.26
  3542.7 30.6 reduce-scatter.28
  3576.2 30.5 reduce-scatter.30
  3609.6 29.8 reduce-scatter.36
  3642.1 29.7 reduce-scatter.38
  3674.7 30.6 reduce-scatter.20
  3708.2 30.5 reduce-scatter.22
  3746.2 150.7 all-reduce.21
where the time goes:
time: 3920 us; the launch traced here: 3910 us
  waiting for transfers between devices  1410 us (36%)
  matrix products  874 us (22%)
  blocking collectives  771 us (20%)
  local copies, waits for them, and re-layouts  417 us (11%)
  other arithmetic  406 us (10%)
    unnamed x1, blocking collectives  732 us
    convert_element_type x2, other arithmetic, attend_back(): grad_scores = (probs_again * (grad_probs - jnp.sum(probs_again * grad_pro...  204 us
    psum x1, waiting for transfers between devices, body(): branch_a = lax.psum(cross_part, 'tp')  191 us
    psum x1, waiting for transfers between devices, body(): grad_second = lax.psum(second_part, 'tp')  187 us
    dot_general x2, matrix products, attend_back(): jnp.einsum('iqhe,iphe->ihqp', grad_mixed, value_heads, preferred_element_...  177 us
    psum x1, waiting for transfers between devices, body(): grad_third = lax.psum(self_back, 'tp')  176 us
    psum x1, waiting for transfers between devices, body(): lax.psum((grad_deconv, grad_bias, grad_table), ('seq', 'tp'))  158 us
    psum x1, waiting for transfers between devices, body(): branch_s = lax.psum(self_part, 'tp')  144 us
  transfers between devices with their start and end apart: 25, of which 20 were waited for; matrix products, arithmetic and copies ran while one was open for 11% of the time, Pallas kernels for 0%

commit v1 on v0

v1 whole, which is shorter than its diff:
```python
import jax
import jax.numpy as jnp
from jax import lax
from jax.experimental import pallas as pl
from jax.experimental.pallas import tpu as pltpu
from jax.sharding import PartitionSpec as P

HEAD = 64
COUT = 80
PLANE = 32
IMG = 4096
LOG2E = 1.4426950408889634
bf16 = jnp.bfloat16
f32 = jnp.float32
GROUPS = 16


highest = lax.Precision.HIGHEST
epsilon = 1e-06


def with_halo(x, sides, width):
    for axis, dim in sides:
        peers, length = (lax.axis_size(axis), x.shape[dim])
        up = [(i, (i + 1) % peers) for i in range(peers - 1)]
        down = [(j, i) for i, j in up]
        last = lax.slice_in_dim(x, length - width, length, axis=dim)
        initial = lax.slice_in_dim(x, 0, width, axis=dim)
        before = lax.ppermute(last, axis, up)
        after = lax.ppermute(initial, axis, down)
        x = jnp.concatenate([before, x, after], axis=dim)
    return x


def spread_taps(padded, upper, lower):
    even_rows = padded[1:-1, :, :, 1] + upper * padded[:-2, :, :, 3]
    odd_rows = lower * padded[2:, :, :, 0] + padded[1:-1, :, :, 2]
    rows_both = jnp.stack([even_rows, odd_rows], axis=1)
    even_cols = rows_both[:, :, :, 1:-1, 1] + rows_both[:, :, :, :-2, 3]
    odd_cols = rows_both[:, :, :, 2:, 0] + rows_both[:, :, :, 1:-1, 2]
    joined = jnp.stack([even_cols, odd_cols], axis=4)
    shape = joined.shape
    return joined.reshape(shape[0] * 2, shape[2], shape[3] * 2 * shape[5])


def norm_parts(value):
    centred = value - jnp.mean(value, axis=-1, keepdims=True)
    inverse = lax.rsqrt(jnp.mean(centred * centred, axis=-1, keepdims=True) + epsilon)
    return (centred * inverse, inverse)


def norm_back(normed, inverse, incoming):
    return inverse * (
        incoming
        - jnp.mean(incoming, axis=-1, keepdims=True)
        - normed * jnp.mean(incoming * normed, axis=-1, keepdims=True)
    )


NT = (((1,), (1,)), ((), ()))


def dot_nt(a, b):
    return lax.dot_general(a, b, NT, preferred_element_type=f32)


def dot_nn(a, b):
    return jnp.dot(a, b, preferred_element_type=f32)


def flip(x):
    return x.astype(f32).T.astype(bf16)


def chunk_of(keys):
    return 512 if keys % 512 == 0 else keys


def softmax_sweep(scores, values, chunks, columns):
    top = jnp.full((1, columns), -1e30, f32)
    total = jnp.zeros((1, columns), f32)
    mixed = None
    ahead = scores(0)
    for c in range(chunks):
        now = ahead
        ahead = scores(c + 1) if c + 1 < chunks else None
        new_top = jnp.maximum(top, jnp.max(now, axis=0, keepdims=True))
        fade = jnp.exp2((top - new_top) * LOG2E)
        expon = jnp.exp2(now * LOG2E - new_top * LOG2E)
        total = total * fade + jnp.sum(expon, axis=0, keepdims=True)
        parts = values(c, expon.astype(bf16))
        width = columns // len(parts)
        if mixed is None:
            mixed = parts
        else:
            mixed = [
                m * fade[:, j * width : (j + 1) * width] + part
                for j, (m, part) in enumerate(zip(mixed, parts))
            ]
        top = new_top
    width = columns // len(mixed)
    inverse = 1.0 / total
    mixed = [m * inverse[:, j * width : (j + 1) * width] for j, m in enumerate(mixed)]
    return mixed, top + jnp.log(total)


def cross_forward(q, k, vt):
    items, queries, width = q.shape
    keys = k.shape[1]
    heads = width // HEAD
    step = chunk_of(keys)

    def kernel(q_ref, k_ref, vt_ref, o_ref, log_ref):
        pair = pl.program_id(1)
        owner = lax.broadcasted_iota(jnp.int32, (queries, width), 1) // HEAD
        both = jnp.concatenate(
            [jnp.where(owner == pair * 2 + j, q_ref[0], 0.0).astype(bf16) for j in range(2)], axis=0
        )

        def scores(c):
            return dot_nt(k_ref[0, pl.ds(c * step, step), :], both)

        def values(c, p):
            out = []
            for j in range(2):
                rows = pl.ds(pl.multiple_of((pair * 2 + j) * HEAD, HEAD), HEAD)
                v = vt_ref[0, rows, pl.ds(c * step, step)]
                out.append(dot_nn(v, p[:, j * queries : (j + 1) * queries]))
            return out

        mixed, log_total = softmax_sweep(scores, values, keys // step, 2 * queries)
        o_ref[0] = jnp.concatenate(mixed, axis=0).T.astype(bf16)
        for j in range(2):
            log_ref[0, j] = jnp.broadcast_to(
                log_total[:, j * queries : (j + 1) * queries], (8, queries)
            )

    return pl.pallas_call(
        kernel,
        grid=(items, heads // 2),
        in_specs=[
            pl.BlockSpec((1, queries, width), lambda i, h: (i, 0, 0)),
            pl.BlockSpec((1, keys, width), lambda i, h: (i, 0, 0)),
            pl.BlockSpec((1, width, keys), lambda i, h: (i, 0, 0)),
        ],
        out_specs=[
            pl.BlockSpec((1, queries, 2 * HEAD), lambda i, h: (i, 0, h)),
            pl.BlockSpec((1, 2, 8, queries), lambda i, h: (i, h, 0, 0)),
        ],
        out_shape=[
            jax.ShapeDtypeStruct((items, queries, width), bf16),
            jax.ShapeDtypeStruct((items, heads, 8, queries), f32),
        ],
        compiler_params=pltpu.CompilerParams(vmem_limit_bytes=48 << 20),
        cost_estimate=pl.CostEstimate(
            flops=16 * items * queries * keys * width,
            bytes_accessed=4 * items * (queries + keys) * width,
            transcendentals=items * queries * keys * heads,
        ),
        name="cross_forward",
    )(q, k, vt)


def cross_backward(q, do, o, logs, k, vt):
    items, queries, width = q.shape
    keys = k.shape[1]
    heads = width // HEAD
    step = chunk_of(keys)

    def kernel(q_ref, do_ref, o_ref, log_ref, k_ref, vt_ref, dq_ref, dk_ref, dv_ref, qt, dot):
        head = pl.program_id(1)

        @pl.when(head == 0)
        def _():
            qt[...] = flip(q_ref[0])
            dot[...] = flip(do_ref[0])

        mine = lax.broadcasted_iota(jnp.int32, (queries, width), 1) // HEAD == head
        q_mine = jnp.where(mine, q_ref[0], 0.0).astype(bf16)
        do_mine = jnp.where(mine, do_ref[0], 0.0).astype(bf16)
        delta = jnp.sum(do_mine.astype(f32) * o_ref[0].astype(f32), axis=1, keepdims=True)
        log_total = log_ref[0, 0].T[:, :1] * LOG2E
        rows = pl.ds(pl.multiple_of(head * HEAD, HEAD), HEAD)
        qt_mine = qt[rows, :]
        dot_mine = dot[rows, :]

        def scores(c):
            s = dot_nt(q_mine, k_ref[0, pl.ds(c * step, step), :])
            return s, dot_nn(do_mine, vt_ref[0, :, pl.ds(c * step, step)])

        dq = jnp.zeros((queries, width), f32)
        ahead = scores(0)
        for c in range(keys // step):
            s, dp = ahead
            ahead = scores(c + 1) if c + 1 < keys // step else None
            p = jnp.exp2(s * LOG2E - log_total)
            ds = (p * (dp - delta)).astype(bf16)
            cols = pl.ds(c * step, step)
            dv_ref[0, :, cols] = dot_nn(dot_mine, p.astype(bf16)).astype(bf16)
            dk_ref[0, :, cols] = dot_nn(qt_mine, ds).astype(bf16)
            dq = dq + dot_nn(ds, k_ref[0, cols, :])
        dq = (dq * 0.125).astype(bf16)
        rest = jnp.where(head == 0, jnp.zeros_like(dq), dq_ref[0])
        dq_ref[0] = jnp.where(mine, dq, rest)

    rows_spec = pl.BlockSpec((1, queries, width), lambda i, h: (i, 0, 0))
    grads_spec = pl.BlockSpec((1, HEAD, keys), lambda i, h: (i, h, 0))
    return pl.pallas_call(
        kernel,
        grid=(items, heads),
        in_specs=[
            rows_spec,
            rows_spec,
            rows_spec,
            pl.BlockSpec((1, 1, 8, queries), lambda i, h: (i, h, 0, 0)),
            pl.BlockSpec((1, keys, width), lambda i, h: (i, 0, 0)),
            pl.BlockSpec((1, width, keys), lambda i, h: (i, 0, 0)),
        ],
        out_specs=[rows_spec, grads_spec, grads_spec],
        out_shape=[
            jax.ShapeDtypeStruct((items, queries, width), bf16),
            jax.ShapeDtypeStruct((items, width, keys), bf16),
            jax.ShapeDtypeStruct((items, width, keys), bf16),
        ],
        scratch_shapes=[pltpu.VMEM((width, queries), bf16), pltpu.VMEM((width, queries), bf16)],
        compiler_params=pltpu.CompilerParams(vmem_limit_bytes=48 << 20),
        cost_estimate=pl.CostEstimate(
            flops=40 * items * queries * keys * width,
            bytes_accessed=8 * items * (queries + keys) * width,
            transcendentals=items * queries * keys * heads,
        ),
        name="cross_backward",
    )(q, do, o, logs, k, vt)


def split_pair(x):
    low = lax.broadcasted_iota(jnp.int32, x.shape, 1) < HEAD
    wide = x.astype(f32)
    first = jnp.where(low, wide, 0.0)
    second = jnp.where(low, pltpu.roll(wide, HEAD, 1), 0.0)
    return jnp.concatenate([first, second], axis=0).astype(bf16)


def self_forward(q, kv):
    rows = q.shape[0]
    keys = kv.shape[0]
    block = 384 if rows % 384 == 0 else rows
    step = chunk_of(keys)

    def kernel(q_ref, kv_ref, o_ref, log_ref, vt):
        @pl.when(pl.program_id(0) == 0)
        def _():
            vt[...] = flip(kv_ref[...])

        both = split_pair(q_ref[...])

        def scores(c):
            return dot_nt(kv_ref[pl.ds(c * step, step), :], both)

        def values(c, p):
            return [dot_nn(vt[HEAD:, pl.ds(c * step, step)], p)]

        mixed, log_total = softmax_sweep(scores, values, keys // step, 2 * block)
        mixed = mixed[0]
        o_ref[...] = (
            jnp.concatenate([mixed[:, :block], mixed[:, block:]], axis=0).T.astype(bf16)
        )
        log_ref[0] = jnp.broadcast_to(log_total, (8, 2 * block))

    return pl.pallas_call(
        kernel,
        grid=(rows // block,),
        in_specs=[
            pl.BlockSpec((block, 2 * HEAD), lambda i: (i, 0)),
            pl.BlockSpec((keys, 2 * HEAD), lambda i: (0, 0)),
        ],
        out_specs=[
            pl.BlockSpec((block, 2 * HEAD), lambda i: (i, 0)),
            pl.BlockSpec((1, 8, 2 * block), lambda i: (i, 0, 0)),
        ],
        out_shape=[
            jax.ShapeDtypeStruct((rows, 2 * HEAD), bf16),
            jax.ShapeDtypeStruct((rows // block, 8, 2 * block), f32),
        ],
        scratch_shapes=[pltpu.VMEM((2 * HEAD, keys), bf16)],
        compiler_params=pltpu.CompilerParams(vmem_limit_bytes=48 << 20),
        cost_estimate=pl.CostEstimate(
            flops=16 * 2 * rows * keys * HEAD,
            bytes_accessed=4 * (rows + keys) * 2 * HEAD,
            transcendentals=2 * rows * keys,
        ),
        name="self_forward",
    )(q, kv)


def self_backward(q, do, o, logs, kv):
    rows = q.shape[0]
    keys = kv.shape[0]
    blocks = logs.shape[0]
    block = rows // blocks
    step = chunk_of(keys)

    def kernel(q_ref, do_ref, o_ref, log_ref, kv_ref, dq_ref, dkv_ref, vt, grads):
        i = pl.program_id(0)

        @pl.when(i == 0)
        def _():
            vt[...] = flip(kv_ref[...])
            grads[...] = jnp.zeros_like(grads)

        q_both = split_pair(q_ref[...])
        do_both = split_pair(do_ref[...])
        product = do_both.astype(f32) * split_pair(o_ref[...]).astype(f32)
        delta = jnp.sum(product, axis=1, keepdims=True)
        log_total = log_ref[0].T[:, :1] * LOG2E
        qt = flip(q_both)[:HEAD]
        dot = flip(do_both)[:HEAD]
        do_low = do_both[:, :HEAD]

        def scores(c):
            s = dot_nt(q_both, kv_ref[pl.ds(c * step, step), :])
            return s, dot_nn(do_low, vt[HEAD:, pl.ds(c * step, step)])

        dq = jnp.zeros((2 * block, 2 * HEAD), f32)
        ahead = scores(0)
        for c in range(keys // step):
            s, dp = ahead
            ahead = scores(c + 1) if c + 1 < keys // step else None
            p = jnp.exp2(s * LOG2E - log_total)
            ds = (p * (dp - delta)).astype(bf16)
            cols = pl.ds(c * step, step)
            grads[:HEAD, cols] += dot_nn(qt, ds)
            grads[HEAD:, cols] += dot_nn(dot, p.astype(bf16))
            dq = dq + dot_nn(ds, kv_ref[cols, :])
        dq = dq * 0.125
        low = lax.broadcasted_iota(jnp.int32, (block, 2 * HEAD), 1) < HEAD
        dq_ref[...] = jnp.where(low, dq[:block], pltpu.roll(dq[block:], HEAD, 1)).astype(bf16)

        @pl.when(i == blocks - 1)
        def _():
            dkv_ref[...] = grads[...].T.astype(bf16)

    rows_spec = pl.BlockSpec((block, 2 * HEAD), lambda i: (i, 0))
    keys_spec = pl.BlockSpec((keys, 2 * HEAD), lambda i: (0, 0))
    return pl.pallas_call(
        kernel,
        grid=(blocks,),
        in_specs=[
            rows_spec,
            rows_spec,
            rows_spec,
            pl.BlockSpec((1, 8, 2 * block), lambda i: (i, 0, 0)),
            keys_spec,
        ],
        out_specs=[rows_spec, keys_spec],
        out_shape=[
            jax.ShapeDtypeStruct((rows, 2 * HEAD), bf16),
            jax.ShapeDtypeStruct((keys, 2 * HEAD), bf16),
        ],
        scratch_shapes=[
            pltpu.VMEM((2 * HEAD, keys), bf16),
            pltpu.VMEM((2 * HEAD, keys), f32),
        ],
        compiler_params=pltpu.CompilerParams(vmem_limit_bytes=48 << 20),
        cost_estimate=pl.CostEstimate(
            flops=40 * 2 * rows * keys * HEAD,
            bytes_accessed=8 * (rows + keys) * 2 * HEAD,
            transcendentals=2 * rows * keys,
        ),
        name="self_backward",
    )(q, do, o, logs, kv)


def exchange(x, axis):
    return lax.all_to_all(x, axis, 0, 0, tiled=True)


def gather(x, axis):
    return exchange(jnp.broadcast_to(x[None], (lax.axis_size(axis),) + x.shape), axis)


def reduce_blocks(x, axis):
    return jnp.sum(exchange(x.astype(bf16), axis).astype(f32), axis=0)


def body(
    tokens,
    context,
    group_ids,
    source_table,
    w_query,
    w_key,
    w_value,
    w_out,
    w_self_query,
    w_self_key,
    w_self_value,
    w_self_out,
    w_up,
    w_down,
    w_deconv,
    deconv_bias,
    out_cotangent,
    plane_cotangent,
):
    rows_here, items, plane_cols, width = tokens.shape
    cols_here = out_cotangent.shape[2]
    tp = lax.axis_size("tp")
    seq = lax.axis_size("seq")
    devices = tp * seq
    local = w_query.shape[1]
    heads_here = local // HEAD
    heads = heads_here * tp
    tile = rows_here * cols_here
    half = tile // 2
    groups = devices // heads
    turns = -(-items // groups)
    spare = groups * turns - items
    me_tp = lax.axis_index("tp")

    picker = (group_ids[:, None] == jnp.arange(GROUPS, dtype=jnp.int32)[None, :]).astype(f32)
    mods = jnp.dot(picker, source_table, precision=highest).reshape(items, 9, 1, width)

    def piece(index):
        return mods[:, index]

    def dot(spec, a, b):
        return jnp.einsum(spec, a, b, preferred_element_type=f32)

    def to_tile(x):
        return x.transpose(1, 0, 2, 3).reshape(items, tile, width)

    def from_tile(x):
        return x.reshape(items, rows_here, cols_here, width).transpose(1, 0, 2, 3)

    out_whole = gather(w_out, "tp")
    self_local = jnp.concatenate(
        [
            jnp.concatenate(
                [
                    w_self_key.reshape(width, heads_here, HEAD),
                    w_self_value.reshape(width, heads_here, HEAD),
                ],
                axis=2,
            ).reshape(width, 2 * local),
            w_self_query,
        ],
        axis=1,
    )
    self_whole = gather(self_local, "tp")
    self_out_whole = gather(w_self_out, "tp")
    up_whole = gather(w_up, "tp")
    down_whole = gather(w_down, "tp")
    query_whole = gather(w_query, "tp")

    ordered = (
        tokens.reshape(rows_here, items, tp, cols_here, width)
        .transpose(1, 2, 0, 3, 4)
        .reshape(items, tp * tile, width)
    )
    first_hat, first_inv = norm_parts(ordered.astype(f32))
    first_in = (first_hat * (1.0 + piece(1)) + piece(0)).astype(bf16)
    queries = dot("iqd,de->iqe", first_in, w_query).astype(bf16) * bf16(0.125)
    keys = dot("pid,de->ipe", context, w_key).astype(bf16)
    values_t = dot("pid,de->iep", context, w_value).astype(bf16)
    mixed, cross_logs = cross_forward(queries, keys, values_t)
    mixed_send = mixed.reshape(items, tp, tile, local).transpose(1, 0, 2, 3)
    mixed_tile = exchange(mixed_send, "tp")
    branch_a = dot("time,tef->imf", mixed_tile, out_whole)
    residual = to_tile(
        lax.dynamic_slice_in_dim(tokens, me_tp * cols_here, cols_here, 2)
    ).astype(f32)
    middle = residual + piece(2) * branch_a

    self_hat, self_inv = norm_parts(middle)
    self_in = (self_hat * (1.0 + piece(4)) + piece(3)).astype(bf16)
    projected = dot("imd,tde->time", self_in, self_whole).astype(bf16)

    def pad_items(x):
        return jnp.pad(x, ((0, 0), (0, spare)) + ((0, 0),) * (x.ndim - 2)) if spare else x

    kv_send = (
        pad_items(projected[..., : 2 * local].reshape(tp, items, tile, heads_here, 2 * HEAD))
        .reshape(tp, groups, turns, tile, heads_here, 2 * HEAD)
        .transpose(2, 1, 0, 4, 3, 5)
        .reshape(turns, devices, tile, 2 * HEAD)
    )

    def pack_rows(x):
        return (
            pad_items(x)
            .reshape(tp, groups, turns, 2, half, heads_here, HEAD)
            .transpose(2, 1, 0, 5, 4, 3, 6)
            .reshape(turns, devices, half, 2 * HEAD)
        )

    def unpack_rows(x):
        return (
            x.reshape(turns, groups, tp, heads_here, half, 2, HEAD)
            .transpose(2, 1, 0, 5, 4, 3, 6)
            .reshape(tp, groups * turns, tile, local)[:, :items]
        )

    q_send = pack_rows(projected[..., 2 * local :] * bf16(0.125))
    both_axes = ("seq", "tp")
    q_mine, kv_mine, so_mine, self_logs, so_back = [], [], [], [], []
    for turn in range(turns):
        kv_mine.append(exchange(kv_send[turn], both_axes).reshape(devices * tile, 2 * HEAD))
        q_mine.append(exchange(q_send[turn], both_axes).reshape(devices * half, 2 * HEAD))
    for turn in range(turns):
        so, logs = self_forward(q_mine[turn], kv_mine[turn])
        so_mine.append(so)
        self_logs.append(logs)
        so_back.append(exchange(so.reshape(devices, half, 2 * HEAD), both_axes))
    self_tile = unpack_rows(jnp.stack(so_back))
    branch_s = dot("time,tef->imf", self_tile, self_out_whole)
    middle_two = middle + piece(5) * branch_s

    incoming = plane_cotangent.reshape(2 * rows_here, items, 2 * cols_here, COUT)
    plane_row = (lax.axis_index("seq") * rows_here + jnp.arange(rows_here, dtype=jnp.int32)) % PLANE
    upper_keep = (plane_row != 0).astype(f32)
    lower_keep = (plane_row != PLANE - 1).astype(f32)
    grad_edges = with_halo(incoming, (("seq", 0), ("tp", 2)), 1)
    upper_mask = upper_keep.astype(bf16)[:, None, None, None]
    lower_mask = lower_keep.astype(bf16)[:, None, None, None]
    first_pair = grad_edges[:-2].reshape(rows_here, 2, items, 2 * cols_here + 2, COUT)
    last_pair = grad_edges[2:].reshape(rows_here, 2, items, 2 * cols_here + 2, COUT)
    row_taps = jnp.stack(
        [
            first_pair[:, 0] * upper_mask,
            first_pair[:, 1],
            last_pair[:, 0],
            last_pair[:, 1] * lower_mask,
        ],
        axis=3,
    )
    left_pair = row_taps[:, :, :-2].reshape(rows_here, items, cols_here, 2, 4, COUT)
    right_pair = row_taps[:, :, 2:].reshape(rows_here, items, cols_here, 2, 4, COUT)
    tap_grads = jnp.stack(
        [
            left_pair[:, :, :, 0],
            left_pair[:, :, :, 1],
            right_pair[:, :, :, 0],
            right_pair[:, :, :, 1],
        ],
        axis=4,
    )
    tap_grads = tap_grads.reshape(rows_here, items, cols_here, 16 * COUT)
    grad_result = to_tile(
        out_cotangent.astype(f32) + dot("rict,dt->ricd", tap_grads, w_deconv)
    )
    grad_bias = jnp.sum(incoming.astype(f32), axis=(0, 1, 2))
    grad_mlp = (piece(8) * grad_result).astype(bf16)

    second_hat, second_inv = norm_parts(middle_two)
    second_in = (second_hat * (1.0 + piece(7)) + piece(6)).astype(bf16)
    hidden = dot("imd,tdf->timf", second_in, up_whole)
    active_f, gelu_back = jax.vjp(lambda value: jax.nn.gelu(value, approximate=False), hidden)
    active = active_f.astype(bf16)
    branch_b = dot("timf,tfd->imd", active, down_whole)
    result = middle_two + piece(8) * branch_b
    out_tile = from_tile(result.astype(bf16))

    grad_active = dot("imd,tfd->timf", grad_mlp, down_whole)
    grad_hidden = gelu_back(grad_active)[0].astype(bf16)
    grad_second = dot("timf,tdf->imd", grad_hidden, up_whole)
    grad_gate_b = jnp.sum(grad_result * branch_b, axis=1)
    grad_shift_b = jnp.sum(grad_second, axis=1)
    grad_scale_b = jnp.sum(grad_second * second_hat, axis=1)
    grad_mid_two = grad_result + norm_back(second_hat, second_inv, grad_second * (1.0 + piece(7)))

    grad_self = (piece(5) * grad_mid_two).astype(bf16)
    grad_gate_s = jnp.sum(grad_mid_two * branch_s, axis=1)
    dso_send = pack_rows(dot("imf,tef->time", grad_self, self_out_whole).astype(bf16))
    dq_back, dkv_back = [], []
    dso_mine = [exchange(dso_send[turn], both_axes) for turn in range(turns)]
    for turn in range(turns):
        dq, dkv = self_backward(
            q_mine[turn],
            dso_mine[turn].reshape(devices * half, 2 * HEAD),
            so_mine[turn],
            self_logs[turn],
            kv_mine[turn],
        )
        dq_back.append(exchange(dq.reshape(devices, half, 2 * HEAD), both_axes))
        dkv_back.append(exchange(dkv.reshape(devices, tile, 2 * HEAD), both_axes))
    dq_tile = unpack_rows(jnp.stack(dq_back))
    dkv_tile = (
        jnp.stack(dkv_back)
        .reshape(turns, groups, tp, heads_here, tile, 2 * HEAD)
        .transpose(2, 1, 0, 4, 3, 5)
        .reshape(tp, groups * turns, tile, 2 * local)[:, :items]
    )
    grad_projected = jnp.concatenate([dkv_tile, dq_tile], axis=3)
    grad_third = dot("time,tde->imd", grad_projected, self_whole)
    grad_shift_s = jnp.sum(grad_third, axis=1)
    grad_scale_s = jnp.sum(grad_third * self_hat, axis=1)
    grad_middle = grad_mid_two + norm_back(self_hat, self_inv, grad_third * (1.0 + piece(4)))

    grad_attn = (piece(2) * grad_middle).astype(bf16)
    grad_gate_a = jnp.sum(grad_middle * branch_a, axis=1)
    do_send = dot("imf,tef->time", grad_attn, out_whole).astype(bf16)
    do_mine = exchange(do_send, "tp").transpose(1, 0, 2, 3).reshape(items, tp * tile, local)
    middle_all = gather(grad_middle.astype(bf16), "tp")
    dq_cross, dk_t, dv_t = cross_backward(queries, do_mine, mixed, cross_logs, keys, values_t)
    dq_all = gather(dq_cross, "tp")
    grad_first = dot("tiqe,tde->iqd", dq_all, query_whole)
    grad_shift_a = jnp.sum(grad_first, axis=1)
    grad_scale_a = jnp.sum(grad_first * first_hat, axis=1)
    grad_tokens = middle_all.astype(f32).transpose(1, 0, 2, 3).reshape(
        items, tp * tile, width
    ) + norm_back(first_hat, first_inv, grad_first * (1.0 + piece(1)))
    grad_tokens = (
        grad_tokens.reshape(items, tp, rows_here, cols_here, width)
        .transpose(2, 0, 1, 3, 4)
        .reshape(rows_here, items, plane_cols, width)
    )

    widened = with_halo(out_tile, (("seq", 0), ("tp", 2)), 1)
    taps = dot("ricd,dt->rict", widened, w_deconv)
    taps = taps.reshape(rows_here + 2, items, cols_here + 2, 4, 4, COUT)
    planes = spread_taps(
        taps, upper_keep[:, None, None, None, None], lower_keep[:, None, None, None, None]
    )
    planes = planes + jnp.tile(deconv_bias, 2 * cols_here)

    def over_seq_rows(x):
        return reduce_blocks(x.reshape((seq, x.shape[0] // seq) + x.shape[1:]), "seq")

    def over_seq_columns(x):
        return reduce_blocks(
            x.reshape(x.shape[0], seq, x.shape[1] // seq).transpose(1, 0, 2), "seq"
        )

    grad_down = over_seq_columns(reduce_blocks(dot("timf,imd->tfd", active, grad_mlp), "tp"))
    grad_up = over_seq_rows(reduce_blocks(dot("imd,timf->tdf", second_in, grad_hidden), "tp"))
    grad_self_out = over_seq_columns(
        reduce_blocks(dot("time,imf->tef", self_tile, grad_self), "tp")
    )
    grad_three = over_seq_rows(
        reduce_blocks(dot("imd,time->tde", self_in, grad_projected), "tp")
    )
    grad_out = over_seq_columns(reduce_blocks(dot("time,imf->tef", mixed_tile, grad_attn), "tp"))
    share = grad_three.shape[0]
    grad_pair = grad_three[:, : 2 * local].reshape(share, heads_here, 2, HEAD)
    grad_self_key = grad_pair[:, :, 0].reshape(share, local)
    grad_self_value = grad_pair[:, :, 1].reshape(share, local)
    grad_self_query = grad_three[:, 2 * local :]
    grad_query = over_seq_rows(dot("iqd,iqe->de", first_in, dq_cross))
    grad_key = over_seq_rows(dot("pid,iep->de", context, dk_t))
    grad_value = over_seq_rows(dot("pid,iep->de", context, dv_t))

    grad_deconv = dot("ricd,rict->dt", out_tile, tap_grads)
    early = jnp.stack(
        [
            grad_gate_a,
            grad_shift_s,
            grad_scale_s,
            grad_gate_s,
            grad_shift_b,
            grad_scale_b,
            grad_gate_b,
        ],
        axis=1,
    )
    grad_deconv, grad_bias = lax.psum((grad_deconv, grad_bias), both_axes)
    early = lax.psum(early, both_axes)
    late = lax.psum(jnp.stack([grad_shift_a, grad_scale_a], axis=1), "seq")
    grad_mods = jnp.concatenate([late, early], axis=1)
    grad_table = jnp.dot(picker.T, grad_mods.reshape(items, 9 * width), precision=highest)
    return (
        out_tile,
        planes,
        grad_tokens,
        grad_query,
        grad_key,
        grad_value,
        grad_out,
        grad_self_query,
        grad_self_key,
        grad_self_value,
        grad_self_out,
        grad_up,
        grad_down,
        grad_deconv,
        grad_bias,
        grad_table,
    )


def solution(mesh):
    in_specs = (
        P("seq", None, None, None),
        P(),
        P(),
        P(),
        P(None, "tp"),
        P(None, "tp"),
        P(None, "tp"),
        P("tp", None),
        P(None, "tp"),
        P(None, "tp"),
        P(None, "tp"),
        P("tp", None),
        P(None, "tp"),
        P("tp", None),
        P(),
        P(),
        P("seq", None, "tp", None),
        P("seq", None, "tp"),
    )
    out_specs = (
        P("seq", None, "tp", None),
        P("seq", None, "tp"),
        P("seq", None, None, None),
        P("seq", "tp"),
        P("seq", "tp"),
        P("seq", "tp"),
        P("tp", "seq"),
        P("seq", "tp"),
        P("seq", "tp"),
        P("seq", "tp"),
        P("tp", "seq"),
        P("seq", "tp"),
        P("tp", "seq"),
        P(),
        P(),
        P(),
    )
    return jax.shard_map(body, mesh=mesh, in_specs=in_specs, out_specs=out_specs, check_vma=False)
```

time: 3920 us -> 2120 us (0.54)
  waiting for transfers between devices: 1410 us -> 635 us
  matrix products: 874 us -> 271 us
  blocking collectives: 771 us -> 318 us
  other arithmetic: 406 us -> 111 us
  Pallas kernels: 0 us -> 277 us
  starting transfers between devices: 17.4 us -> 186 us
  local copies, waits for them, and re-layouts: 417 us -> 292 us
    psum x6 -> x1, waiting for transfers between devices: 960 us -> 72.4 us  [body(): grad_deconv, grad_bias = lax.psum((grad_deconv, grad_bias), both_axes)]
    unnamed x1 -> x0, blocking collectives: 732 us -> none
    dot_general x45 -> x27, matrix products: 874 us -> 271 us  [the longest x25 268 us: dot(): return jnp.einsum(spec, a, b, preferred_element_type=f32)]
    all_to_all x0 -> x35, waiting for transfers between devices: none -> 488 us  [exchange(): return lax.all_to_all(x, axis, 0, 0, tiled=True)]
    pallas_call x0 -> x8, Pallas kernels: none -> 277 us  [the longest x1 97.2 us: cross_backward(): pl.pallas_call(kernel, grid=(items, heads), in_specs=[rows_spec, rows_spe...]
    reduce_scatter x8 -> x0, waiting for transfers between devices: 232 us -> none  [the longest x1 33.7 us: body(): lax.psum_scatter(grad_self_value, 'seq', scatter_dimension=0, tiled=True)]
    reshape x23 -> x13, local copies, waits for them, and re-layouts: 257 us -> 53.4 us  [the longest x1 10.4 us: body(): taps = taps.reshape(rows_here + 2, items, cols_here + 2, 4, 4, COUT)]
    convert_element_type x5, other arithmetic: 207 us -> 15.5 us  [the longest x1 7.54 us: body(): first_hat, first_inv = norm_parts(ordered.astype(f32))]
  transfers between devices with their start and end apart: 25 -> 44, of which waited for: 20 -> 24; matrix products, arithmetic and copies ran while one was open for 11% -> 23% of each run, Pallas kernels for 0% -> 10%
where the time goes in v1:
time: 2120 us; the launch traced here: 2100 us
  waiting for transfers between devices  635 us (30%)
  blocking collectives  318 us (15%)
  local copies, waits for them, and re-layouts  292 us (14%)
  Pallas kernels  277 us (13%)
  matrix products  271 us (13%)
  starting transfers between devices  186 us (9%)
  other arithmetic  111 us (5%)
    all_to_all x35, waiting for transfers between devices, exchange(): return lax.all_to_all(x, axis, 0, 0, tiled=True)  488 us
    dot_general x25, matrix products, dot(): return jnp.einsum(spec, a, b, preferred_element_type=f32)  268 us
    all_to_all x6, blocking collectives, exchange(): return lax.all_to_all(x, axis, 0, 0, tiled=True)  185 us
    all_to_all x35, starting transfers between devices, exchange(): return lax.all_to_all(x, axis, 0, 0, tiled=True)  163 us
    pallas_call x1, Pallas kernels, cross_backward(): pl.pallas_call(kernel, grid=(items, heads), in_specs=[rows_spec, rows_spe...  97.2 us
    psum x1, blocking collectives, body(): grad_deconv, grad_bias = lax.psum((grad_deconv, grad_bias), both_axes)  83.5 us
    pallas_call x3, Pallas kernels, self_backward(): pl.pallas_call(kernel, grid=(blocks,), in_specs=[rows_spec, rows_spec, ro...  77.5 us
    ppermute x4, waiting for transfers between devices, with_halo(): after = lax.ppermute(initial, axis, down)  73.5 us
  transfers between devices with their start and end apart: 44, of which 24 were waited for; matrix products, arithmetic and copies ran while one was open for 23% of the time, Pallas kernels for 10%

profile of v1, /device:TPU:0, one launch (start us, length us, event | category | flops | bytes accessed | tf_op | source)
XLA Modules:
  0.0 2105.0 jit_solution(11897042085976659374)
XLA Ops:
  28.7 19.4 convert_bitcast_fusion.1.k_ref
  48.1 19.5 convert_bitcast_fusion.vt_ref
  76.5 60.9 %cross_forward.1 = (bf16[6,384,256]{2,1,0:T(8,128)(2,1)S(1)}, f32[6,4,8,384]{3,2,1,0:T(8,128)S(1)}) custom-call(bf16[6,384,256]{2,1,0:T(8,128)(2,1)S(1)} %fusion.97.q_ref, bf16[6,4096,256]{2,1,0:T(8,128)(2,1)} %convert_bitcast_fusion.1.k_ref, bf16[6,256,4096]{2,1,0:T(8,128)(2,1)} %convert_bitcast_fusion.vt_ref), custom_call_target="tpu_custom_call" | custom-call | flops 38654705664 | bytes 27525120 | tf_op jit(solution)/shard_map/cross_forward/pallas_call | solution.py:138
  137.5 20.7 all_to_all.205
  204.7 62.4 %all-to-all-done.2 = bf16[4,1024,768]{2,1,0:T(8,128)(2,1)} async-done(((bf16[4,1024,768]{2,1,0:T(8,128)(2,1)}), bf16[4,1024,768]{2,1,0:T(8,128)(2,1)}, u32[]{:S(2)}, u32[]{:S(2)}) %all-to-all-start.2) | async-done | bytes 6291488 | tf_op jit(solution)/shard_map/all_to_all | solution.py:375
  359.3 19.2 all-to-all-done.10
  384.4 19.2 all-to-all-done.7
  409.5 13.8 self_forward.5
  434.2 13.8 self_forward.4
  456.4 13.8 self_forward.3
  471.0 19.5 all_to_all.206
  522.4 73.5 %collective-permute-done.7 = bf16[26,6,1,80]{3,0,2,1:T(8,128)(2,1)S(1)} collective-permute-done((bf16[26,6,1,80]{3,0,2,1:T(8,128)(2,1)S(1)}, bf16[26,6,1,80]{3,0,2,1:T(8,128)(2,1)S(1)}, u32[]{:S(2)}, u32[]{:S(2)}) %collective-permute-start.7) | collective-permute-done | bytes 24992 | tf_op jit(solution)/shard_map/ppermute | solution.py:30
  664.9 30.0 %fusion.11 = (bf16[4,6,96,1024]{3,2,0,1:T(8,128)(2,1)}, f32[4,6,96,1024]{3,2,0,1:T(8,128)}, f32[6,96,4,1024]{3,1,2,0:T(8,128)}) fusion(bf16[4,1024,1024]{2,1,0:T(8,128)(2,1)} %all-to-all-done.13, f32[6,96,1024]{2,1,0:T(8,128)} %copy-done.43, f32[6,1024]{1,0:T(8,128)} %get-tuple-element.254, f32[6,1024]{1,0:T(8,128)} %get-tuple-element.255, ...), kind=kOutput, calls=%fused_computation.29 | convolution fusion | flops 4988141568 | bytes 34394624 | tf_op jit(solution)/shard_map/imd,tdf->timf/dot_general | solution.py:428
  694.9 61.1 %all-to-all-done.14 = bf16[4,1024,1024]{2,1,0:T(8,128)(2,1)} async-done(((bf16[4,1024,1024]{2,1,0:T(8,128)(2,1)}), bf16[4,1024,1024]{2,1,0:T(8,128)(2,1)}, u32[]{:S(2)}, u32[]{:S(2)}) %all-to-all-start.14) | async-done | bytes 8388640 | tf_op jit(solution)/shard_map/all_to_all | solution.py:375
  755.9 15.1 fusion.8
  851.5 25.5 %self_backward.5 = (bf16[1536,128]{1,0:T(8,128)(2,1)S(1)}, bf16[3072,128]{1,0:T(8,128)(2,1)S(1)}) custom-call(bf16[1536,128]{1,0:T(8,128)(2,1)S(1)} %bitcast.599, bf16[1536,128]{1,0:T(8,128)(2,1)} %bitcast.94.do_ref, bf16[1536,128]{1,0:T(8,128)(2,1)S(1)} %copy-done.28, f32[4,8,768]{2,1,0:T(8,128)S(1)} %copy-done.37, bf16[3072,128]{1,0:T(8,128)(2,1)S(1)} %bitcast.591), custom_call_target="tpu_custom_call" | custom-call | flops 24159191040 | bytes 4718592 | tf_op jit(solution)/shard_map/self_backward/pallas_call | solution.py:345
  888.9 25.5 %self_backward.4 = (bf16[1536,128]{1,0:T(8,128)(2,1)S(1)}, bf16[3072,128]{1,0:T(8,128)(2,1)S(1)}) custom-call(bf16[1536,128]{1,0:T(8,128)(2,1)S(1)} %bitcast.597, bf16[1536,128]{1,0:T(8,128)(2,1)} %bitcast.91.do_ref, bf16[1536,128]{1,0:T(8,128)(2,1)S(1)} %copy-done.26, f32[4,8,768]{2,1,0:T(8,128)S(1)} %copy-done.35, bf16[3072,128]{1,0:T(8,128)(2,1)S(1)} %bitcast.589), custom_call_target="tpu_custom_call" | custom-call | flops 24159191040 | bytes 4718592 | tf_op jit(solution)/shard_map/self_backward/pallas_call | solution.py:345
  924.4 26.4 %self_backward.3 = (bf16[1536,128]{1,0:T(8,128)(2,1)S(1)}, bf16[3072,128]{1,0:T(8,128)(2,1)}) custom-call(bf16[1536,128]{1,0:T(8,128)(2,1)S(1)} %bitcast.595, bf16[1536,128]{1,0:T(8,128)(2,1)} %bitcast.88.do_ref, bf16[1536,128]{1,0:T(8,128)(2,1)S(1)} %copy-done.24, f32[4,8,768]{2,1,0:T(8,128)S(1)} %get-tuple-element.37.log_ref, bf16[3072,128]{1,0:T(8,128)(2,1)S(1)} %bitcast.587), custom_call_target="tpu_custom_call" | custom-call | flops 24159191040 | bytes 4718592 | tf_op jit(solution)/shard_map/self_backward/pallas_call | solution.py:345
  951.6 19.7 all_to_all.207
  971.2 24.7 %all_to_all.208 = bf16[32,96,128]{2,1,0:T(8,128)(2,1)} all-to-all(bf16[32,96,128]{2,1,0:T(8,128)(2,1)} %bitcast.592), channel_id=1, replica_groups=mesh['seq'=8,'tp'=4] {'seq','tp'}, dimensions={0} | all-to-all | bytes 1572864 | tf_op jit(solution)/shard_map/all_to_all | solution.py:375
  995.9 24.0 %all_to_all.209 = bf16[32,96,128]{2,1,0:T(8,128)(2,1)} all-to-all(bf16[32,96,128]{2,1,0:T(8,128)(2,1)S(1)} %bitcast.593), channel_id=1, replica_groups=mesh['seq'=8,'tp'=4] {'seq','tp'}, dimensions={0} | all-to-all | bytes 1572864 | tf_op jit(solution)/shard_map/all_to_all | solution.py:375
  1119.3 97.2 %cross_backward.1 = (bf16[6,384,256]{2,1,0:T(8,128)(2,1)S(1)}, bf16[6,256,4096]{2,1,0:T(8,128)(2,1)}, bf16[6,256,4096]{2,1,0:T(8,128)(2,1)}) custom-call(bf16[6,384,256]{2,1,0:T(8,128)(2,1)S(1)} %copy-done.33, bf16[6,384,256]{2,1,0:T(8,128)(2,1)S(1)} %bitcast.585, bf16[6,384,256]{2,1,0:T(8,128)(2,1)S(1)} %copy-done.2, f32[6,4,8,384]{3,2,1,0:T(8,128)S(1)} %copy-done.39, ...), custom_call_target="tpu_custom_call" | custom-call | flops 96636764160 | bytes 55050240 | tf_op jit(solution)/shard_map/cross_backward/pallas_call | solution.py:208
  1222.7 23.4 %fusion.113 = bf16[768,256]{0,1:T(8,128)(2,1)S(1)} fusion(bf16[6,256,4096]{2,1,0:T(8,128)(2,1)} %get-tuple-element.48, bf16[4096,6,768]{2,0,1:T(8,128)(2,1)} %param.19), kind=kOutput, calls=%fused_computation.171 | convolution fusion | flops 9663873024 | bytes 50724864 | tf_op jit(solution)/shard_map/pid,iep->de/dot_general | solution.py:428
  1252.6 24.1 %fusion.112 = bf16[768,256]{0,1:T(8,128)(2,1)} fusion(bf16[6,256,4096]{2,1,0:T(8,128)(2,1)} %get-tuple-element.49, bf16[4096,6,768]{2,0,1:T(8,128)(2,1)} %param.19), kind=kOutput, calls=%fused_computation.170 | convolution fusion | flops 9663873024 | bytes 50724864 | tf_op jit(solution)/shard_map/pid,iep->de/dot_general | solution.py:428
  1305.7 20.4 all-to-all-done.31
  1385.8 41.0 %all-to-all-done.24 = bf16[4,6,96,1024]{3,2,1,0:T(8,128)(2,1)} async-done(((bf16[4,6,96,1024]{3,2,1,0:T(8,128)(2,1)}), bf16[4,6,96,1024]{3,2,1,0:T(8,128)(2,1)}, u32[]{:S(2)}, u32[]{:S(2)}) %all-to-all-start.24) | async-done | bytes 4718624 | tf_op jit(solution)/shard_map/all_to_all | solution.py:375
  1444.3 80.0 %all-to-all-done.37 = bf16[4,1024,1024]{1,2,0:T(8,128)(2,1)} async-done(((bf16[4,1024,1024]{1,2,0:T(8,128)(2,1)}), bf16[4,1024,1024]{1,2,0:T(8,128)(2,1)}, u32[]{:S(2)}, u32[]{:S(2)}) %all-to-all-start.37) | async-done | bytes 8388640 | tf_op jit(solution)/shard_map/all_to_all | solution.py:375
  1539.5 82.2 %all-to-all-done.39 = bf16[4,1024,1024]{2,1,0:T(8,128)(2,1)} async-done(((bf16[4,1024,1024]{2,1,0:T(8,128)(2,1)}), bf16[4,1024,1024]{2,1,0:T(8,128)(2,1)}, u32[]{:S(2)}, u32[]{:S(2)}) %all-to-all-start.39) | async-done | bytes 8388640 | tf_op jit(solution)/shard_map/all_to_all | solution.py:375
  1621.7 76.6 %all_to_all.210 = bf16[4,1024,768]{1,2,0:T(8,128)(2,1)} all-to-all(bf16[4,1024,768]{1,2,0:T(8,128)(2,1)} %fusion.35), channel_id=1, replica_groups=mesh['seq'=8,'tp'=4] {'tp'}, dimensions={0} | all-to-all | bytes 12582912 | tf_op jit(solution)/shard_map/all_to_all | solution.py:375
  1706.5 83.5 %psum.29 = f32[80]{0:T(128)} all-reduce(f32[80]{0:T(128)S(1)} %reduce_sum.364), channel_id=1, replica_groups=mesh['seq'=8,'tp'=4] {'seq','tp'}, use_global_device_ids=true, to_apply=%region_28.29 | all-reduce | flops 80 | bytes 640 | tf_op jit(solution)/shard_map/psum | solution.py:666
  1959.5 48.8 %psum.30 = f32[6,2,1024]{2,0,1:T(8,128)S(1)} all-reduce(f32[6,2,1024]{2,0,1:T(8,128)S(1)} %pad_maximum_fusion.11), channel_id=1, replica_groups=mesh['seq'=8,'tp'=4] {'seq'}, use_global_device_ids=true, to_apply=%region_31.32 | all-reduce | flops 12288 | bytes 98304 | tf_op jit(solution)/shard_map/psum | solution.py:668
  2008.3 72.4 %all-reduce.3.cloned.1.call-done = (f32[1024,1280]{1,0:T(8,128)}, f32[6,7,1024]{2,0,1:T(8,128)}) async-done(((f32[1024,1280]{1,0:T(8,128)}, f32[6,7,1024]{2,0,1:T(8,128)}), (f32[1024,1280]{1,0:T(8,128)}, f32[6,7,1024]{2,0,1:T(8,128)})) %all-reduce.3.cloned.1.call-update) | async-done | bytes 5414928 | tf_op jit(solution)/shard_map/psum | solution.py:666
  (494 shorter events, 831.7 us)
Async XLA Ops:
  159.9 28.1 %all-to-all-start.1 = ((bf16[4,256,1024]{2,1,0:T(8,128)(2,1)}), bf16[4,256,1024]{2,1,0:T(8,128)(2,1)}, u32[]{:S(2)}, u32[]{:S(2)}) async-start(bf16[4,256,1024]{2,1,0:T(8,128)(2,1)} %broadcast_in_dim.16), calls=%async_computation.1 | async-start | bytes 4194304 | tf_op jit(solution)/shard_map/all_to_all | solution.py:375
  192.5 74.6 %all-to-all-start.2 = ((bf16[4,1024,768]{2,1,0:T(8,128)(2,1)}), bf16[4,1024,768]{2,1,0:T(8,128)(2,1)}, u32[]{:S(2)}, u32[]{:S(2)}) async-start(bf16[4,1024,768]{2,1,0:T(8,128)(2,1)} %broadcast_in_dim.17), calls=%async_computation.2 | async-start | bytes 12582912 | tf_op jit(solution)/shard_map/all_to_all | solution.py:375
  268.7 29.3 %all-to-all-start.12 = ((bf16[4,256,1024]{2,1,0:T(8,128)(2,1)}), bf16[4,256,1024]{2,1,0:T(8,128)(2,1)}, u32[]{:S(2)}, u32[]{:S(2)}) async-start(bf16[4,256,1024]{2,1,0:T(8,128)(2,1)} %broadcast_in_dim.18), calls=%async_computation.12 | async-start | bytes 4194304 | tf_op jit(solution)/shard_map/all_to_all | solution.py:375
  351.4 27.1 %all-to-all-start.10 = ((bf16[32,96,128]{2,1,0:T(8,128)(2,1)}), bf16[32,96,128]{2,1,0:T(8,128)(2,1)S(1)}, u32[]{:S(2)}, u32[]{:S(2)}) async-start(bf16[32,96,128]{2,1,0:T(8,128)(2,1)} %bitcast.628), calls=%async_computation.10 | async-start | bytes 1572864 | tf_op jit(solution)/shard_map/all_to_all | solution.py:375
  379.4 24.2 %all-to-all-start.7 = ((bf16[32,96,128]{2,1,0:T(8,128)(2,1)}), bf16[32,96,128]{2,1,0:T(8,128)(2,1)S(1)}, u32[]{:S(2)}, u32[]{:S(2)}) async-start(bf16[32,96,128]{2,1,0:T(8,128)(2,1)} %bitcast.626), calls=%async_computation.7 | async-start | bytes 1572864 | tf_op jit(solution)/shard_map/all_to_all | solution.py:375
  404.6 24.2 %all-to-all-start.4 = ((bf16[32,96,128]{2,1,0:T(8,128)(2,1)}), bf16[32,96,128]{2,1,0:T(8,128)(2,1)S(1)}, u32[]{:S(2)}, u32[]{:S(2)}) async-start(bf16[32,96,128]{2,1,0:T(8,128)(2,1)} %bitcast.627), calls=%async_computation.4 | async-start | bytes 1572864 | tf_op jit(solution)/shard_map/all_to_all | solution.py:375
  428.8 20.7 all-to-all-start.11
  449.5 21.5 %all-to-all-start.8 = ((bf16[32,48,128]{2,1,0:T(8,128)(2,1)}), bf16[32,48,128]{2,1,0:T(8,128)(2,1)}, u32[]{:S(2)}, u32[]{:S(2)}) async-start(bf16[32,48,128]{2,1,0:T(8,128)(2,1)} %bitcast.601), calls=%async_computation.8 | async-start | bytes 786432 | tf_op jit(solution)/shard_map/all_to_all | solution.py:375
  496.7 156.2 %all-to-all-start.13 = ((bf16[4,1024,1024]{2,1,0:T(8,128)(2,1)}), bf16[4,1024,1024]{2,1,0:T(8,128)(2,1)}, u32[]{:S(2)}, u32[]{:S(2)}) async-start(bf16[4,1024,1024]{2,1,0:T(8,128)(2,1)} %broadcast_in_dim.19), calls=%async_computation.13 | async-start | bytes 16777216 | tf_op jit(solution)/shard_map/all_to_all | solution.py:375
  516.1 79.7 %collective-permute-start.7 = (bf16[26,6,1,80]{3,0,2,1:T(8,128)(2,1)S(1)}, bf16[26,6,1,80]{3,0,2,1:T(8,128)(2,1)S(1)}, u32[]{:S(2)}, u32[]{:S(2)}) collective-permute-start(bf16[26,6,1,80]{3,0,2,1:T(8,128)(2,1)S(1)} %get-tuple-element.248), channel_id=1, source_target_pairs={{1,0},{2,1},{3,2},{5,4},{6,5},{7,6},{9,8},{10,9},{11,10},{13,12},{... | collective-permute-start | bytes 74888 | tf_op jit(solution)/shard_map/ppermute | solution.py:30
  517.4 78.4 %collective-permute-start.6 = (bf16[26,6,1,80]{3,0,2,1:T(8,128)(2,1)S(1)}, bf16[26,6,1,80]{3,0,2,1:T(8,128)(2,1)S(1)}, u32[]{:S(2)}, u32[]{:S(2)}) collective-permute-start(bf16[26,6,1,80]{3,0,2,1:T(8,128)(2,1)S(1)} %get-tuple-element.247), channel_id=1, source_target_pairs={{0,1},{1,2},{2,3},{4,5},{5,6},{6,7},{8,9},{9,10},{10,11},{12,13},{... | collective-permute-start | bytes 74888 | tf_op jit(solution)/shard_map/ppermute | solution.py:29
  659.0 96.9 %all-to-all-start.14 = ((bf16[4,1024,1024]{2,1,0:T(8,128)(2,1)}), bf16[4,1024,1024]{2,1,0:T(8,128)(2,1)}, u32[]{:S(2)}, u32[]{:S(2)}) async-start(bf16[4,1024,1024]{2,1,0:T(8,128)(2,1)} %broadcast_in_dim.20), calls=%async_computation.14 | async-start | bytes 16777216 | tf_op jit(solution)/shard_map/all_to_all | solution.py:375
  844.2 34.6 %all-to-all-start.15 = ((bf16[32,48,128]{2,1,0:T(8,128)(2,1)}), bf16[32,48,128]{2,1,0:T(8,128)(2,1)}, u32[]{:S(2)}, u32[]{:S(2)}) async-start(bf16[32,48,128]{2,1,0:T(8,128)(2,1)} %squeeze.76), calls=%async_computation.15 | async-start | bytes 786432 | tf_op jit(solution)/shard_map/all_to_all | solution.py:375
  878.8 37.3 %all-to-all-start.23 = ((bf16[32,48,128]{2,1,0:T(8,128)(2,1)}), bf16[32,48,128]{2,1,0:T(8,128)(2,1)}, u32[]{:S(2)}, u32[]{:S(2)}) async-start(bf16[32,48,128]{2,1,0:T(8,128)(2,1)} %bitcast.603), calls=%async_computation.23 | async-start | bytes 786432 | tf_op jit(solution)/shard_map/all_to_all | solution.py:375
  916.1 35.5 %all-to-all-start.22 = ((bf16[32,48,128]{2,1,0:T(8,128)(2,1)}), bf16[32,48,128]{2,1,0:T(8,128)(2,1)}, u32[]{:S(2)}, u32[]{:S(2)}) async-start(bf16[32,48,128]{2,1,0:T(8,128)(2,1)} %bitcast.604), calls=%async_computation.22 | async-start | bytes 786432 | tf_op jit(solution)/shard_map/all_to_all | solution.py:375
  1020.0 35.8 %all-to-all-start.16 = ((bf16[32,96,128]{2,1,0:T(8,128)(2,1)}), bf16[32,96,128]{2,1,0:T(8,128)(2,1)}, u32[]{:S(2)}, u32[]{:S(2)}) async-start(bf16[32,96,128]{2,1,0:T(8,128)(2,1)} %bitcast.89), calls=%async_computation.16 | async-start | bytes 1572864 | tf_op jit(solution)/shard_map/all_to_all | solution.py:375
  1055.8 34.4 %all-to-all-start.35 = ((bf16[4,256,1024]{2,1,0:T(8,128)(2,1)}), bf16[4,256,1024]{2,1,0:T(8,128)(2,1)}, u32[]{:S(2)}, u32[]{:S(2)}) async-start(bf16[4,256,1024]{2,1,0:T(8,128)(2,1)} %bitcast_convert_fusion.4), calls=%async_computation.35 | async-start | bytes 4194304 | tf_op jit(solution)/shard_map/all_to_all | solution.py:375
  1090.1 20.0 all-to-all-start.25
  1112.7 104.8 %all-to-all-start.27 = ((bf16[4,1024,256]{2,1,0:T(8,128)(2,1)}), bf16[4,1024,256]{2,1,0:T(8,128)(2,1)}, u32[]{:S(2)}, u32[]{:S(2)}) async-start(bf16[4,1024,256]{2,1,0:T(8,128)(2,1)} %broadcast_in_dim.23), calls=%async_computation.27 | async-start | bytes 4194304 | tf_op jit(solution)/shard_map/all_to_all | solution.py:375
  1217.6 29.5 %all-to-all-start.36 = ((bf16[8,256,128]{2,1,0:T(8,128)(2,1)}), bf16[8,256,128]{2,1,0:T(8,128)(2,1)S(1)}, u32[]{:S(2)}, u32[]{:S(2)}) async-start(bf16[8,256,128]{2,1,0:T(8,128)(2,1)} %copy.537), calls=%async_computation.36 | async-start | bytes 1048576 | tf_op jit(solution)/shard_map/all_to_all | solution.py:375
  1247.1 31.6 %all-to-all-start.29 = ((bf16[8,96,256]{2,1,0:T(8,128)(2,1)}), bf16[8,96,256]{2,1,0:T(8,128)(2,1)S(1)}, u32[]{:S(2)}, u32[]{:S(2)}) async-start(bf16[8,96,256]{2,1,0:T(8,128)(2,1)} %bitcast.123), calls=%async_computation.29 | async-start | bytes 786432 | tf_op jit(solution)/shard_map/all_to_all | solution.py:375
  1296.3 29.7 %all-to-all-start.31 = ((bf16[4,256,1024]{2,1,0:T(8,128)(2,1)}), bf16[4,256,1024]{2,1,0:T(8,128)(2,1)}, u32[]{:S(2)}, u32[]{:S(2)}) async-start(bf16[4,256,1024]{2,1,0:T(8,128)(2,1)} %bitcast_convert_fusion.5), calls=%async_computation.31 | async-start | bytes 4194304 | tf_op jit(solution)/shard_map/all_to_all | solution.py:375
  1368.5 58.4 %all-to-all-start.24 = ((bf16[4,6,96,1024]{3,2,1,0:T(8,128)(2,1)}), bf16[4,6,96,1024]{3,2,1,0:T(8,128)(2,1)}, u32[]{:S(2)}, u32[]{:S(2)}) async-start(bf16[4,6,96,1024]{3,2,1,0:T(8,128)(2,1)} %broadcast_in_dim.21), calls=%async_computation.24 | async-start | bytes 9437184 | tf_op jit(solution)/shard_map/all_to_all | solution.py:375
  1426.8 97.4 %all-to-all-start.37 = ((bf16[4,1024,1024]{1,2,0:T(8,128)(2,1)}), bf16[4,1024,1024]{1,2,0:T(8,128)(2,1)}, u32[]{:S(2)}, u32[]{:S(2)}) async-start(bf16[4,1024,1024]{1,2,0:T(8,128)(2,1)} %fusion.42), calls=%async_computation.37 | async-start | bytes 16777216 | tf_op jit(solution)/shard_map/all_to_all | solution.py:375
  1524.3 97.4 %all-to-all-start.39 = ((bf16[4,1024,1024]{2,1,0:T(8,128)(2,1)}), bf16[4,1024,1024]{2,1,0:T(8,128)(2,1)}, u32[]{:S(2)}, u32[]{:S(2)}) async-start(bf16[4,1024,1024]{2,1,0:T(8,128)(2,1)} %bitcast_convert_fusion), calls=%async_computation.39 | async-start | bytes 16777216 | tf_op jit(solution)/shard_map/all_to_all | solution.py:375
  1701.0 112.5 %all-to-all-start.26 = ((bf16[4,6,384,256]{3,2,1,0:T(8,128)(2,1)}), bf16[4,6,384,256]{3,2,1,0:T(8,128)(2,1)}, u32[]{:S(2)}, u32[]{:S(2)}) async-start(bf16[4,6,384,256]{3,2,1,0:T(8,128)(2,1)} %broadcast_in_dim.22), calls=%async_computation.26 | async-start | bytes 9437184 | tf_op jit(solution)/shard_map/all_to_all | solution.py:375
  1797.9 31.3 %collective-permute-start.3 = (bf16[14,6,1,1024]{3,0,2,1:T(8,128)(2,1)S(1)}, bf16[14,6,1,1024]{3,0,2,1:T(8,128)(2,1)}, u32[]{:S(2)}, u32[]{:S(2)}) collective-permute-start(bf16[14,6,1,1024]{3,0,2,1:T(8,128)(2,1)S(1)} %get-tuple-element.236), channel_id=1, source_target_pairs={{1,0},{2,1},{3,2},{5,4},{6,5},{7,6},{9,8},{10,9},{11,10},{13,12},{... | collective-permute-start | bytes 516104 | tf_op jit(solution)/shard_map/ppermute | solution.py:30
  1799.2 30.0 %collective-permute-start.2 = (bf16[14,6,1,1024]{3,0,2,1:T(8,128)(2,1)S(1)}, bf16[14,6,1,1024]{3,0,2,1:T(8,128)(2,1)}, u32[]{:S(2)}, u32[]{:S(2)}) collective-permute-start(bf16[14,6,1,1024]{3,0,2,1:T(8,128)(2,1)S(1)} %get-tuple-element.235), channel_id=1, source_target_pairs={{0,1},{1,2},{2,3},{4,5},{5,6},{6,7},{8,9},{9,10},{10,11},{12,13},{... | collective-permute-start | bytes 516104 | tf_op jit(solution)/shard_map/ppermute | solution.py:29
  1813.5 48.5 %all-to-all-start.34 = ((bf16[8,128,768]{1,2,0:T(8,128)(2,1)}), bf16[8,128,768]{1,2,0:T(8,128)(2,1)}, u32[]{:S(2)}, u32[]{:S(2)}) async-start(bf16[8,128,768]{1,2,0:T(8,128)(2,1)} %copy_bitcast_fusion.2), calls=%async_computation.34 | async-start | bytes 3145728 | tf_op jit(solution)/shard_map/all_to_all | solution.py:375
  1862.1 65.0 %all-to-all-start.38 = ((bf16[8,128,1024]{1,2,0:T(8,128)(2,1)}), bf16[8,128,1024]{1,2,0:T(8,128)(2,1)}, u32[]{:S(2)}, u32[]{:S(2)}) async-start(bf16[8,128,1024]{1,2,0:T(8,128)(2,1)} %copy_bitcast_fusion.1), calls=%async_computation.38 | async-start | bytes 4194304 | tf_op jit(solution)/shard_map/all_to_all | solution.py:375
  1867.4 213.3 %all-reduce.3.cloned.1.call-start = ((), (), s32[]{:S(2)}) async-start(), calls=%async_computation.41 | async-start | bytes 10944512 | tf_op jit(solution)/shard_map/psum | solution.py:666
  1927.1 162.9 %all-to-all-start.40 = ((bf16[8,1024,128]{2,1,0:T(8,128)(2,1)}), bf16[8,1024,128]{2,1,0:T(8,128)(2,1)}, u32[]{:S(2)}, u32[]{:S(2)}) async-start(bf16[8,1024,128]{2,1,0:T(8,128)(2,1)} %copy.541), calls=%async_computation.40 | async-start | bytes 4194304 | tf_op jit(solution)/shard_map/all_to_all | solution.py:375
  (121 other events, 3203.5 us)
Sparse Core Ops, SparseCore 0:
  1885.9 194.7 all-reduce.2

commit v2 on v1

v2 whole, which is shorter than its diff:
```python
import jax
import jax.numpy as jnp
from jax import lax
from jax.experimental import pallas as pl
from jax.experimental.pallas import tpu as pltpu
from jax.sharding import PartitionSpec as P

HEAD = 64
COUT = 80
PLANE = 32
IMG = 4096
LOG2E = 1.4426950408889634
bf16 = jnp.bfloat16
f32 = jnp.float32
GROUPS = 16


highest = lax.Precision.HIGHEST
epsilon = 1e-06


def with_halo(x, sides, width):
    for axis, dim in sides:
        peers, length = (lax.axis_size(axis), x.shape[dim])
        up = [(i, (i + 1) % peers) for i in range(peers - 1)]
        down = [(j, i) for i, j in up]
        last = lax.slice_in_dim(x, length - width, length, axis=dim)
        initial = lax.slice_in_dim(x, 0, width, axis=dim)
        before = lax.ppermute(last, axis, up)
        after = lax.ppermute(initial, axis, down)
        x = jnp.concatenate([before, x, after], axis=dim)
    return x


def spread_taps(padded, upper, lower):
    even_rows = padded[1:-1, :, :, 1] + upper * padded[:-2, :, :, 3]
    odd_rows = lower * padded[2:, :, :, 0] + padded[1:-1, :, :, 2]
    rows_both = jnp.stack([even_rows, odd_rows], axis=1)
    even_cols = rows_both[:, :, :, 1:-1, 1] + rows_both[:, :, :, :-2, 3]
    odd_cols = rows_both[:, :, :, 2:, 0] + rows_both[:, :, :, 1:-1, 2]
    joined = jnp.stack([even_cols, odd_cols], axis=4)
    shape = joined.shape
    return joined.reshape(shape[0] * 2, shape[2], shape[3] * 2 * shape[5])


def norm_parts(value):
    centred = value - jnp.mean(value, axis=-1, keepdims=True)
    inverse = lax.rsqrt(jnp.mean(centred * centred, axis=-1, keepdims=True) + epsilon)
    return (centred * inverse, inverse)


def norm_back(normed, inverse, incoming):
    return inverse * (
        incoming
        - jnp.mean(incoming, axis=-1, keepdims=True)
        - normed * jnp.mean(incoming * normed, axis=-1, keepdims=True)
    )


NT = (((1,), (1,)), ((), ()))
BLOCKS = 4
FORCE_PLAIN = False


def dot_nt(a, b):
    return lax.dot_general(a, b, NT, preferred_element_type=f32)


def dot_nn(a, b):
    return jnp.dot(a, b, preferred_element_type=f32)


def flip(x):
    return x.astype(f32).T.astype(bf16)


def chunk_of(keys):
    return 512 if keys % 512 == 0 else keys


def softmax_sweep(scores, values, chunks, columns):
    top = jnp.full((1, columns), -1e30, f32)
    total = jnp.zeros((1, columns), f32)
    mixed = None
    ahead = scores(0)
    for c in range(chunks):
        now = ahead
        ahead = scores(c + 1) if c + 1 < chunks else None
        new_top = jnp.maximum(top, jnp.max(now, axis=0, keepdims=True))
        fade = jnp.exp2((top - new_top) * LOG2E)
        expon = jnp.exp2(now * LOG2E - new_top * LOG2E)
        total = total * fade + jnp.sum(expon, axis=0, keepdims=True)
        parts = values(c, expon.astype(bf16))
        width = columns // len(parts)
        if mixed is None:
            mixed = parts
        else:
            mixed = [
                m * fade[:, j * width : (j + 1) * width] + part
                for j, (m, part) in enumerate(zip(mixed, parts))
            ]
        top = new_top
    width = columns // len(mixed)
    inverse = 1.0 / total
    mixed = [m * inverse[:, j * width : (j + 1) * width] for j, m in enumerate(mixed)]
    return mixed, top + jnp.log(total)


def cross_forward(q, k, vt, tp):
    items, queries, width = q.shape
    tile = queries // tp
    keys = k.shape[1]
    heads = width // HEAD
    step = chunk_of(keys)

    def kernel(q_ref, k_ref, vt_ref, o_ref, wide_ref, log_ref):
        pair = pl.program_id(1)
        owner = lax.broadcasted_iota(jnp.int32, (queries, width), 1) // HEAD
        both = jnp.concatenate(
            [jnp.where(owner == pair * 2 + j, q_ref[0], 0.0).astype(bf16) for j in range(2)], axis=0
        )

        def scores(c):
            return dot_nt(k_ref[0, pl.ds(c * step, step), :], both)

        def values(c, p):
            out = []
            for j in range(2):
                rows = pl.ds(pl.multiple_of((pair * 2 + j) * HEAD, HEAD), HEAD)
                v = vt_ref[0, rows, pl.ds(c * step, step)]
                out.append(dot_nn(v, p[:, j * queries : (j + 1) * queries]))
            return out

        mixed, log_total = softmax_sweep(scores, values, keys // step, 2 * queries)
        rows = jnp.concatenate(mixed, axis=0).T.reshape(tp, 1, tile, 2 * HEAD)
        o_ref[...] = rows.astype(bf16)
        wide_ref[...] = rows
        for j in range(2):
            log_ref[0, j] = jnp.broadcast_to(
                log_total[:, j * queries : (j + 1) * queries], (8, queries)
            )

    return pl.pallas_call(
        kernel,
        grid=(items, heads // 2),
        in_specs=[
            pl.BlockSpec((1, queries, width), lambda i, h: (i, 0, 0)),
            pl.BlockSpec((1, keys, width), lambda i, h: (i, 0, 0)),
            pl.BlockSpec((1, width, keys), lambda i, h: (i, 0, 0)),
        ],
        out_specs=[
            pl.BlockSpec((tp, 1, tile, 2 * HEAD), lambda i, h: (0, i, 0, h)),
            pl.BlockSpec((tp, 1, tile, 2 * HEAD), lambda i, h: (0, i, 0, h)),
            pl.BlockSpec((1, 2, 8, queries), lambda i, h: (i, h, 0, 0)),
        ],
        out_shape=[
            jax.ShapeDtypeStruct((tp, items, tile, width), bf16),
            jax.ShapeDtypeStruct((tp, items, tile, width), f32),
            jax.ShapeDtypeStruct((items, heads, 8, queries), f32),
        ],
        compiler_params=pltpu.CompilerParams(vmem_limit_bytes=48 << 20),
        cost_estimate=pl.CostEstimate(
            flops=16 * items * queries * keys * width,
            bytes_accessed=4 * items * (queries + keys) * width,
            transcendentals=items * queries * keys * heads,
        ),
        name="cross_forward",
    )(q, k, vt)


def cross_backward(q, do, o, logs, k, vt):
    items, queries, width = q.shape
    tp, _, tile, _ = do.shape
    keys = k.shape[1]
    heads = width // HEAD
    step = chunk_of(keys)

    def kernel(q_ref, do_ref, o_ref, log_ref, k_ref, vt_ref, dq_ref, dk_ref, dv_ref, qt, dot):
        head = pl.program_id(1)

        @pl.when(head == 0)
        def _():
            qt[...] = flip(q_ref[0])
            dot[...] = do_ref[...].astype(f32).reshape(queries, width).T.astype(bf16)

        mine = lax.broadcasted_iota(jnp.int32, (queries, width), 1) // HEAD == head
        q_mine = jnp.where(mine, q_ref[0], 0.0).astype(bf16)
        do_wide = jnp.where(mine, do_ref[...].astype(f32).reshape(queries, width), 0.0)
        do_mine = do_wide.astype(bf16)
        o_wide = o_ref[...].reshape(queries, width)
        delta = jnp.sum(do_wide * o_wide, axis=1, keepdims=True)
        log_total = log_ref[0, 0].T[:, :1] * LOG2E
        rows = pl.ds(pl.multiple_of(head * HEAD, HEAD), HEAD)
        qt_mine = qt[rows, :]
        dot_mine = dot[rows, :]

        def scores(c):
            s = dot_nt(q_mine, k_ref[0, pl.ds(c * step, step), :])
            return s, dot_nn(do_mine, vt_ref[0, :, pl.ds(c * step, step)])

        dq = jnp.zeros((queries, width), f32)
        ahead = scores(0)
        for c in range(keys // step):
            s, dp = ahead
            ahead = scores(c + 1) if c + 1 < keys // step else None
            p = jnp.exp2(s * LOG2E - log_total)
            ds = (p * (dp - delta)).astype(bf16)
            cols = pl.ds(c * step, step)
            dv_ref[0, :, cols] = dot_nn(dot_mine, p.astype(bf16)).astype(bf16)
            dk_ref[0, :, cols] = dot_nn(qt_mine, ds).astype(bf16)
            dq = dq + dot_nn(ds, k_ref[0, cols, :])
        dq = (dq * 0.125).astype(bf16)
        rest = jnp.where(head == 0, jnp.zeros_like(dq), dq_ref[0])
        dq_ref[0] = jnp.where(mine, dq, rest)

    rows_spec = pl.BlockSpec((1, queries, width), lambda i, h: (i, 0, 0))
    tiles_spec = pl.BlockSpec((tp, 1, tile, width), lambda i, h: (0, i, 0, 0))
    grads_spec = pl.BlockSpec((1, HEAD, keys), lambda i, h: (i, h, 0))
    return pl.pallas_call(
        kernel,
        grid=(items, heads),
        in_specs=[
            rows_spec,
            tiles_spec,
            tiles_spec,
            pl.BlockSpec((1, 1, 8, queries), lambda i, h: (i, h, 0, 0)),
            pl.BlockSpec((1, keys, width), lambda i, h: (i, 0, 0)),
            pl.BlockSpec((1, width, keys), lambda i, h: (i, 0, 0)),
        ],
        out_specs=[rows_spec, grads_spec, grads_spec],
        out_shape=[
            jax.ShapeDtypeStruct((items, queries, width), bf16),
            jax.ShapeDtypeStruct((items, width, keys), bf16),
            jax.ShapeDtypeStruct((items, width, keys), bf16),
        ],
        scratch_shapes=[pltpu.VMEM((width, queries), bf16), pltpu.VMEM((width, queries), bf16)],
        compiler_params=pltpu.CompilerParams(vmem_limit_bytes=48 << 20),
        cost_estimate=pl.CostEstimate(
            flops=40 * items * queries * keys * width,
            bytes_accessed=8 * items * (queries + keys) * width,
            transcendentals=items * queries * keys * heads,
        ),
        name="cross_backward",
    )(q, do, o, logs, k, vt)


def split_wide(x):
    low = lax.broadcasted_iota(jnp.int32, x.shape, 1) < HEAD
    wide = x.astype(f32)
    first = jnp.where(low, wide, 0.0)
    second = jnp.where(low, pltpu.roll(wide, HEAD, 1), 0.0)
    return jnp.concatenate([first, second], axis=0)


def split_pair(x):
    return split_wide(x).astype(bf16)


def part_specs(parts, half):
    if len(parts) == 1:
        return [pl.BlockSpec(parts[0].shape, lambda i: (0, 0, 0))]
    rows = parts[1].shape[0] // BLOCKS
    return [
        pl.BlockSpec(parts[0].shape, lambda i: (0, 0)),
        pl.BlockSpec((rows, 2 * HEAD), lambda i: (i, 0)),
    ]


def read_keys(refs, half):
    if len(refs) == 2:
        return refs[0][...]
    devices = refs[0].shape[0]
    return refs[0][:, : 2 * half, :].reshape(devices * 2 * half, 2 * HEAD)


def read_queries(refs, half, i, share):
    if len(refs) == 2:
        return refs[1][...]
    return refs[0][pl.ds(i * share, share), 2 * half :, :].reshape(share * half, 2 * HEAD)


def self_forward(parts, devices, half):
    tile = 2 * half
    keys = devices * tile
    blocks = BLOCKS
    share = devices // blocks
    block = share * half
    step = chunk_of(keys)

    def kernel(*refs):
        ins, (o_ref, wide_ref, log_ref, kv, vt) = refs[: len(parts)], refs[len(parts) :]
        i = pl.program_id(0)

        @pl.when(i == 0)
        def _():
            kv[...] = read_keys(ins, half)
            vt[...] = flip(kv[...])

        both = split_pair(read_queries(ins, half, i, share))

        def scores(c):
            return dot_nt(kv[pl.ds(c * step, step), :], both)

        def values(c, p):
            return [dot_nn(vt[HEAD:, pl.ds(c * step, step)], p)]

        mixed, log_total = softmax_sweep(scores, values, keys // step, 2 * block)
        mixed = mixed[0]
        rows = jnp.concatenate([mixed[:, :block], mixed[:, block:]], axis=0).T
        o_ref[...] = rows.astype(bf16)
        wide_ref[...] = rows
        log_ref[0] = jnp.broadcast_to(log_total, (8, 2 * block))

    return pl.pallas_call(
        kernel,
        grid=(blocks,),
        in_specs=part_specs(parts, half),
        out_specs=[
            pl.BlockSpec((block, 2 * HEAD), lambda i: (i, 0)),
            pl.BlockSpec((block, 2 * HEAD), lambda i: (i, 0)),
            pl.BlockSpec((1, 8, 2 * block), lambda i: (i, 0, 0)),
        ],
        out_shape=[
            jax.ShapeDtypeStruct((devices * half, 2 * HEAD), bf16),
            jax.ShapeDtypeStruct((devices * half, 2 * HEAD), f32),
            jax.ShapeDtypeStruct((blocks, 8, 2 * block), f32),
        ],
        scratch_shapes=[pltpu.VMEM((keys, 2 * HEAD), bf16), pltpu.VMEM((2 * HEAD, keys), bf16)],
        compiler_params=pltpu.CompilerParams(vmem_limit_bytes=48 << 20),
        cost_estimate=pl.CostEstimate(
            flops=16 * keys * keys * HEAD,
            bytes_accessed=8 * keys * 2 * HEAD,
            transcendentals=keys * keys,
        ),
        name="self_forward",
    )(*parts)


def self_backward(parts, do, o, logs, devices, half):
    tile = 2 * half
    keys = devices * tile
    blocks = logs.shape[0]
    share = devices // blocks
    block = share * half
    step = chunk_of(keys)

    def kernel(*refs):
        n = len(parts)
        ins, (do_ref, o_ref, log_ref), outs = refs[:n], refs[n : n + 3], refs[n + 3 : 2 * n + 3]
        kv, vt, grads = refs[2 * n + 3 :]
        i = pl.program_id(0)
        mine = pl.ds(i * share, share)

        @pl.when(i == 0)
        def _():
            kv[...] = read_keys(ins, half)
            vt[...] = flip(kv[...])
            grads[...] = jnp.zeros_like(grads)

        q_both = split_pair(read_queries(ins, half, i, share))
        do_both = split_pair(do_ref[...])
        delta = jnp.sum(do_both.astype(f32) * split_wide(o_ref[...]), axis=1, keepdims=True)
        log_total = log_ref[0].T[:, :1] * LOG2E
        qt = flip(q_both)[:HEAD]
        dot = flip(do_both)[:HEAD]
        do_low = do_both[:, :HEAD]

        def scores(c):
            s = dot_nt(q_both, kv[pl.ds(c * step, step), :])
            return s, dot_nn(do_low, vt[HEAD:, pl.ds(c * step, step)])

        dq = jnp.zeros((2 * block, 2 * HEAD), f32)
        ahead = scores(0)
        for c in range(keys // step):
            s, dp = ahead
            ahead = scores(c + 1) if c + 1 < keys // step else None
            p = jnp.exp2(s * LOG2E - log_total)
            ds = (p * (dp - delta)).astype(bf16)
            cols = pl.ds(c * step, step)
            grads[:HEAD, cols] += dot_nn(qt, ds)
            grads[HEAD:, cols] += dot_nn(dot, p.astype(bf16))
            dq = dq + dot_nn(ds, kv[cols, :])
        dq = dq * 0.125
        low = lax.broadcasted_iota(jnp.int32, (block, 2 * HEAD), 1) < HEAD
        packed = jnp.where(low, dq[:block], pltpu.roll(dq[block:], HEAD, 1)).astype(bf16)
        if n == 1:
            outs[0][mine, tile:, :] = packed.reshape(share, half, 2 * HEAD)
        else:
            outs[1][...] = packed

        @pl.when(i == blocks - 1)
        def _():
            dkv = grads[...].T.astype(bf16)
            if n == 1:
                outs[0][:, :tile, :] = dkv.reshape(devices, tile, 2 * HEAD)
            else:
                outs[0][...] = dkv

    rows_spec = pl.BlockSpec((block, 2 * HEAD), lambda i: (i, 0))
    return pl.pallas_call(
        kernel,
        grid=(blocks,),
        in_specs=part_specs(parts, half)
        + [rows_spec, rows_spec, pl.BlockSpec((1, 8, 2 * block), lambda i: (i, 0, 0))],
        out_specs=part_specs(parts, half),
        out_shape=[jax.ShapeDtypeStruct(p.shape, bf16) for p in parts],
        scratch_shapes=[
            pltpu.VMEM((keys, 2 * HEAD), bf16),
            pltpu.VMEM((2 * HEAD, keys), bf16),
            pltpu.VMEM((2 * HEAD, keys), f32),
        ],
        compiler_params=pltpu.CompilerParams(vmem_limit_bytes=48 << 20),
        cost_estimate=pl.CostEstimate(
            flops=40 * keys * keys * HEAD,
            bytes_accessed=16 * keys * 2 * HEAD,
            transcendentals=keys * keys,
        ),
        name="self_backward",
    )(*parts, do, o, logs)


def swap_pairs(first, second):
    low = lax.broadcasted_iota(jnp.int32, first.shape, 1) < HEAD
    return (
        jnp.where(low, first, pltpu.roll(second, HEAD, 1)),
        jnp.where(low, pltpu.roll(first, HEAD, 1), second),
    )


def tile_places(items, turns, groups, tile):
    return [(i * tile, i % turns, i // turns) for i in range(items)]


def project_pack(x, kv_w, q_w, items, turns, groups):
    rows, width = x.shape
    slots = kv_w.shape[0]
    tile = rows // items
    half = tile // 2

    def kernel(x_ref, kv_ref, q_ref, out_ref):
        kv = dot_nt(x_ref[...], kv_ref[0]).astype(bf16)
        q = dot_nt(x_ref[...], q_ref[0]).astype(bf16).astype(f32) * 0.125
        for start, turn, group in tile_places(items, turns, groups, tile):
            upper, lower = swap_pairs(q[start : start + half], q[start + half : start + tile])
            for h, part in enumerate((upper, lower)):
                out_ref[turn, group, 0, h, :tile, :] = kv[
                    start : start + tile, h * 2 * HEAD : (h + 1) * 2 * HEAD
                ]
                out_ref[turn, group, 0, h, tile:, :] = part.astype(bf16)

    shape = (turns, groups, slots, 2, 3 * half, 2 * HEAD)
    return pl.pallas_call(
        kernel,
        grid=(slots,),
        in_specs=[
            pl.BlockSpec((rows, width), lambda i: (0, 0)),
            pl.BlockSpec((1,) + kv_w.shape[1:], lambda i: (i, 0, 0)),
            pl.BlockSpec((1,) + q_w.shape[1:], lambda i: (i, 0, 0)),
        ],
        out_specs=pl.BlockSpec(
            (turns, groups, 1, 2, 3 * half, 2 * HEAD), lambda i: (0, 0, i, 0, 0, 0)
        ),
        out_shape=jax.ShapeDtypeStruct(shape, bf16),
        compiler_params=pltpu.CompilerParams(vmem_limit_bytes=40 << 20),
        cost_estimate=pl.CostEstimate(
            flops=2 * rows * width * slots * 6 * HEAD,
            bytes_accessed=2 * (rows + slots * 6 * HEAD) * width,
            transcendentals=0,
        ),
        name="project_pack",
    )(x, kv_w, q_w)


def unpack_project(blocks, weights, items, groups):
    turns = len(blocks)
    slots = weights.shape[0]
    half = blocks[0].shape[3]
    tile = 2 * half
    width = weights.shape[2]

    def kernel(*refs):
        ins, w_ref, flat_ref, out_ref = refs[:turns], refs[turns], refs[turns + 1], refs[turns + 2]
        slot = pl.program_id(0)
        for start, turn, group in tile_places(items, turns, groups, tile):
            pair = [ins[turn][group, 0, h].astype(f32) for h in range(2)]
            upper, lower = swap_pairs(*pair)
            flat_ref[start : start + half, :] = upper.astype(bf16)
            flat_ref[start + half : start + tile, :] = lower.astype(bf16)
        part = dot_nn(flat_ref[...], w_ref[0])

        @pl.when(slot == 0)
        def _():
            out_ref[...] = part

        @pl.when(slot > 0)
        def _():
            out_ref[...] += part

    return pl.pallas_call(
        kernel,
        grid=(slots,),
        in_specs=[
            pl.BlockSpec((groups, 1, 2, half, 2 * HEAD), lambda i: (0, i, 0, 0, 0))
            for _ in range(turns)
        ]
        + [pl.BlockSpec((1,) + weights.shape[1:], lambda i: (i, 0, 0))],
        out_specs=[
            pl.BlockSpec((items * tile, 2 * HEAD), lambda i: (0, i)),
            pl.BlockSpec((items * tile, width), lambda i: (0, 0)),
        ],
        out_shape=[
            jax.ShapeDtypeStruct((items * tile, slots * 2 * HEAD), bf16),
            jax.ShapeDtypeStruct((items * tile, width), f32),
        ],
        compiler_params=pltpu.CompilerParams(vmem_limit_bytes=40 << 20),
        cost_estimate=pl.CostEstimate(
            flops=2 * items * tile * width * slots * 2 * HEAD,
            bytes_accessed=4 * items * tile * width,
            transcendentals=0,
        ),
        name="unpack_project",
    )(*blocks, weights)


def back_pack(x, weights, items, turns, groups):
    rows, width = x.shape
    slots = weights.shape[0]
    tile = rows // items
    half = tile // 2

    def kernel(x_ref, w_ref, out_ref):
        grads = dot_nt(x_ref[...], w_ref[0])
        for start, turn, group in tile_places(items, turns, groups, tile):
            pair = swap_pairs(grads[start : start + half], grads[start + half : start + tile])
            for h, part in enumerate(pair):
                out_ref[turn, group, 0, h] = part.astype(bf16)

    return pl.pallas_call(
        kernel,
        grid=(slots,),
        in_specs=[
            pl.BlockSpec((rows, width), lambda i: (0, 0)),
            pl.BlockSpec((1,) + weights.shape[1:], lambda i: (i, 0, 0)),
        ],
        out_specs=pl.BlockSpec(
            (turns, groups, 1, 2, half, 2 * HEAD), lambda i: (0, 0, i, 0, 0, 0)
        ),
        out_shape=jax.ShapeDtypeStruct((turns, groups, slots, 2, half, 2 * HEAD), bf16),
        compiler_params=pltpu.CompilerParams(vmem_limit_bytes=40 << 20),
        cost_estimate=pl.CostEstimate(
            flops=2 * rows * width * slots * 2 * HEAD,
            bytes_accessed=2 * (rows + slots * 2 * HEAD) * width,
            transcendentals=0,
        ),
        name="back_pack",
    )(x, weights)


def unpack_back(blocks, kv_w, q_w, items, groups):
    turns = len(blocks)
    slots, _, width = kv_w.shape
    half = blocks[0].shape[3] // 3
    tile = 2 * half
    rows = items * tile

    def kernel(*refs):
        ins = refs[:turns]
        kv_ref, q_ref, flat_ref, out_ref = refs[turns:]
        slot = pl.program_id(0)
        for start, turn, group in tile_places(items, turns, groups, tile):
            pair = []
            for h in range(2):
                flat_ref[0, start : start + tile, h * 2 * HEAD : (h + 1) * 2 * HEAD] = ins[turn][
                    group, 0, h, :tile, :
                ]
                pair.append(ins[turn][group, 0, h, tile:, :].astype(f32))
            upper, lower = swap_pairs(*pair)
            flat_ref[0, start : start + half, 4 * HEAD :] = upper.astype(bf16)
            flat_ref[0, start + half : start + tile, 4 * HEAD :] = lower.astype(bf16)
        part = dot_nn(flat_ref[0, :, : 4 * HEAD], kv_ref[0])
        part = part + dot_nn(flat_ref[0, :, 4 * HEAD :], q_ref[0])

        @pl.when(slot == 0)
        def _():
            out_ref[...] = part

        @pl.when(slot > 0)
        def _():
            out_ref[...] += part

    return pl.pallas_call(
        kernel,
        grid=(slots,),
        in_specs=[
            pl.BlockSpec((groups, 1, 2, 3 * half, 2 * HEAD), lambda i: (0, i, 0, 0, 0))
            for _ in range(turns)
        ]
        + [
            pl.BlockSpec((1,) + kv_w.shape[1:], lambda i: (i, 0, 0)),
            pl.BlockSpec((1,) + q_w.shape[1:], lambda i: (i, 0, 0)),
        ],
        out_specs=[
            pl.BlockSpec((1, rows, 6 * HEAD), lambda i: (i, 0, 0)),
            pl.BlockSpec((rows, width), lambda i: (0, 0)),
        ],
        out_shape=[
            jax.ShapeDtypeStruct((slots, rows, 6 * HEAD), bf16),
            jax.ShapeDtypeStruct((rows, width), f32),
        ],
        compiler_params=pltpu.CompilerParams(vmem_limit_bytes=40 << 20),
        cost_estimate=pl.CostEstimate(
            flops=2 * rows * width * slots * 6 * HEAD,
            bytes_accessed=4 * rows * width,
            transcendentals=0,
        ),
        name="unpack_back",
    )(*blocks, kv_w, q_w)


def exchange(x, axis):
    return lax.all_to_all(x, axis, 0, 0, tiled=True)


def gather(x, axis):
    return exchange(jnp.broadcast_to(x[None], (lax.axis_size(axis),) + x.shape), axis)


def reduce_blocks(x, axis):
    return jnp.sum(exchange(x.astype(bf16), axis).astype(f32), axis=0)


def body(
    tokens,
    context,
    group_ids,
    source_table,
    w_query,
    w_key,
    w_value,
    w_out,
    w_self_query,
    w_self_key,
    w_self_value,
    w_self_out,
    w_up,
    w_down,
    w_deconv,
    deconv_bias,
    out_cotangent,
    plane_cotangent,
):
    rows_here, items, plane_cols, width = tokens.shape
    cols_here = out_cotangent.shape[2]
    tp = lax.axis_size("tp")
    seq = lax.axis_size("seq")
    both_axes = ("seq", "tp")
    devices = tp * seq
    local = w_query.shape[1]
    hidden_here = w_up.shape[1]
    slots = 2 * tp
    slot_heads = local // HEAD // 2
    slot_width = local // 2
    heads = slots * slot_heads
    tile = rows_here * cols_here
    half = tile // 2
    groups = devices // heads
    turns = -(-items // groups)
    share = width // seq
    fast = slot_heads == 2 and half % 16 == 0 and items == groups * turns and not FORCE_PLAIN
    me_tp = lax.axis_index("tp")
    core = lax.axis_index("seq") % 2

    picker = (group_ids[:, None] == jnp.arange(GROUPS, dtype=jnp.int32)[None, :]).astype(f32)
    mods = jnp.dot(picker, source_table, precision=highest).reshape(items, 9, 1, width)

    def piece(index):
        return mods[:, index]

    def dot(spec, a, b):
        return jnp.einsum(spec, a, b, preferred_element_type=f32)

    def to_tile(x):
        return x.transpose(1, 0, 2, 3).reshape(items, tile, width)

    def from_tile(x):
        return x.reshape(items, rows_here, cols_here, width).transpose(1, 0, 2, 3)

    teams = [
        [(2 * pair + c) * tp + t for c in range(2) for t in range(tp)] for pair in range(seq // 2)
    ]

    def whole(x):
        return lax.all_gather(x, both_axes, axis=0, tiled=False, axis_index_groups=teams)

    def my_rows(x):
        return lax.dynamic_slice_in_dim(x, core * slot_width, slot_width, 0)

    def my_columns(x):
        size = x.shape[1] // 2
        return lax.dynamic_slice_in_dim(x, core * size, size, 1)

    key_value = jnp.stack(
        [
            my_columns(w_self_key).T.reshape(slot_heads, HEAD, width),
            my_columns(w_self_value).T.reshape(slot_heads, HEAD, width),
        ],
        axis=1,
    ).reshape(2 * slot_width, width)
    small = whole(
        jnp.concatenate(
            [
                my_rows(w_out),
                key_value,
                my_columns(w_self_query).T,
                my_rows(w_self_out),
                my_columns(w_query).T,
            ],
            axis=0,
        )
    )
    cuts = [slot_width * k for k in (0, 1, 3, 4, 5, 6)]
    out_slots, kv_slots, q_slots, so_slots, query_slots = [
        small[:, a:b] for a, b in zip(cuts[:-1], cuts[1:])
    ]
    up_slots = whole(my_columns(w_up))
    down_slots = whole(
        lax.dynamic_slice_in_dim(w_down, core * (hidden_here // 2), hidden_here // 2, 0)
    )

    def by_tp(x):
        return x.reshape(2, tp, slot_width, width).transpose(1, 0, 2, 3).reshape(tp, local, width)

    incoming = plane_cotangent.reshape(2 * rows_here, items, 2 * cols_here, COUT)
    plane_row = (lax.axis_index("seq") * rows_here + jnp.arange(rows_here, dtype=jnp.int32)) % PLANE
    upper_keep = (plane_row != 0).astype(f32)
    lower_keep = (plane_row != PLANE - 1).astype(f32)
    grad_edges = with_halo(incoming, (("seq", 0), ("tp", 2)), 1)
    upper_mask = upper_keep.astype(bf16)[:, None, None, None]
    lower_mask = lower_keep.astype(bf16)[:, None, None, None]
    first_pair = grad_edges[:-2].reshape(rows_here, 2, items, 2 * cols_here + 2, COUT)
    last_pair = grad_edges[2:].reshape(rows_here, 2, items, 2 * cols_here + 2, COUT)
    row_taps = jnp.stack(
        [
            first_pair[:, 0] * upper_mask,
            first_pair[:, 1],
            last_pair[:, 0],
            last_pair[:, 1] * lower_mask,
        ],
        axis=3,
    )
    left_pair = row_taps[:, :, :-2].reshape(rows_here, items, cols_here, 2, 4, COUT)
    right_pair = row_taps[:, :, 2:].reshape(rows_here, items, cols_here, 2, 4, COUT)
    tap_grads = jnp.stack(
        [
            left_pair[:, :, :, 0],
            left_pair[:, :, :, 1],
            right_pair[:, :, :, 0],
            right_pair[:, :, :, 1],
        ],
        axis=4,
    )
    tap_grads = tap_grads.reshape(rows_here, items, cols_here, 16 * COUT)
    grad_result = to_tile(out_cotangent.astype(f32) + dot("rict,dt->ricd", tap_grads, w_deconv))
    grad_bias = jnp.sum(incoming.astype(f32), axis=(0, 1, 2))
    grad_mlp = (piece(8) * grad_result).astype(bf16)

    ordered = (
        tokens.reshape(rows_here, items, tp, cols_here, width)
        .transpose(1, 2, 0, 3, 4)
        .reshape(items, tp * tile, width)
    )
    first_hat, first_inv = norm_parts(ordered.astype(f32))
    first_in = (first_hat * (1.0 + piece(1)) + piece(0)).astype(bf16)
    queries = dot("iqd,de->iqe", first_in, w_query).astype(bf16) * bf16(0.125)
    keys = dot("pid,de->ipe", context, w_key).astype(bf16)
    values_t = dot("pid,de->iep", context, w_value).astype(bf16)
    mixed, mixed_wide, cross_logs = cross_forward(queries, keys, values_t, tp)
    mixed_tile = exchange(mixed, "tp")
    out_whole = by_tp(out_slots)
    branch_a = dot("time,tef->imf", mixed_tile, out_whole)
    residual = to_tile(lax.dynamic_slice_in_dim(tokens, me_tp * cols_here, cols_here, 2)).astype(f32)
    middle = residual + piece(2) * branch_a

    self_hat, self_inv = norm_parts(middle)
    self_in = (self_hat * (1.0 + piece(4)) + piece(3)).astype(bf16)
    flat = (items * tile, width)
    spare = groups * turns - items

    def spread_items(x):
        if spare:
            x = jnp.pad(x, ((0, 0), (0, spare)) + ((0, 0),) * (x.ndim - 2))
        return x.reshape((slots, groups, turns) + x.shape[2:])

    def pack_keys(x):
        x = spread_items(x.reshape(slots, items, tile, slot_heads, 2 * HEAD))
        return x.transpose(2, 1, 0, 4, 3, 5).reshape(turns, devices, tile, 2 * HEAD)

    def unpack_keys(x):
        x = x.reshape(turns, groups, slots, slot_heads, tile, 2 * HEAD).transpose(2, 1, 0, 4, 3, 5)
        x = x.reshape(slots, groups * turns, tile, 2 * slot_width)[:, :items]
        return x.reshape(slots, items * tile, 2 * slot_width)

    def pack_rows(x):
        x = spread_items(x.reshape(slots, items, 2, half, slot_heads, HEAD))
        return x.transpose(2, 1, 0, 5, 4, 3, 6).reshape(turns, devices, half, 2 * HEAD)

    def unpack_rows(x):
        x = x.reshape(turns, groups, slots, slot_heads, half, 2, HEAD).transpose(2, 1, 0, 5, 4, 3, 6)
        x = x.reshape(slots, groups * turns, tile, slot_width)[:, :items]
        return x.reshape(slots, items * tile, slot_width)

    if fast:
        sends = project_pack(self_in.reshape(flat), kv_slots, q_slots, items, turns, groups)
        sends = sends.reshape(turns, devices, 3 * half, 2 * HEAD)
        parts = [[exchange(sends[turn], both_axes)] for turn in range(turns)]
    else:
        kv_sends = pack_keys(dot("nd,xed->xne", self_in.reshape(flat), kv_slots).astype(bf16))
        q_sends = dot("nd,xed->xne", self_in.reshape(flat), q_slots).astype(bf16)
        q_sends = pack_rows(q_sends * bf16(0.125))
        parts = [
            [
                exchange(kv_sends[turn], both_axes).reshape(devices * tile, 2 * HEAD),
                exchange(q_sends[turn], both_axes).reshape(devices * half, 2 * HEAD),
            ]
            for turn in range(turns)
        ]
    forward = [self_forward(parts[turn], devices, half) for turn in range(turns)]
    so_back = [exchange(so.reshape(devices, half, 2 * HEAD), both_axes) for so, _, _ in forward]
    if fast:
        blocks = [x.reshape(groups, slots, 2, half, 2 * HEAD) for x in so_back]
        so_tile, branch_s = unpack_project(blocks, so_slots, items, groups)
    else:
        so_tile = unpack_rows(jnp.stack(so_back)).transpose(1, 0, 2)
        branch_s = dot("nxe,xed->nd", so_tile, so_slots)
        so_tile = so_tile.reshape(items * tile, heads * HEAD)
    branch_s = branch_s.reshape(items, tile, width)
    middle_two = middle + piece(5) * branch_s

    second_hat, second_inv = norm_parts(middle_two)
    second_in = (second_hat * (1.0 + piece(7)) + piece(6)).astype(bf16)
    hidden = dot("imd,xdf->ximf", second_in, up_slots)
    active_f, gelu_back = jax.vjp(lambda value: jax.nn.gelu(value, approximate=False), hidden)
    active = active_f.astype(bf16)
    branch_b = dot("ximf,xfd->imd", active, down_slots)
    result = middle_two + piece(8) * branch_b
    out_tile = from_tile(result.astype(bf16))

    grad_active = dot("imd,xfd->ximf", grad_mlp, down_slots)
    grad_hidden = gelu_back(grad_active)[0].astype(bf16)
    grad_second = dot("ximf,xdf->imd", grad_hidden, up_slots)
    grad_gate_b = jnp.sum(grad_result * branch_b, axis=1)
    grad_shift_b = jnp.sum(grad_second, axis=1)
    grad_scale_b = jnp.sum(grad_second * second_hat, axis=1)
    grad_mid_two = grad_result + norm_back(second_hat, second_inv, grad_second * (1.0 + piece(7)))

    widened = with_halo(out_tile, (("seq", 0), ("tp", 2)), 1)
    taps = dot("ricd,dt->rict", widened, w_deconv)
    taps = taps.reshape(rows_here + 2, items, cols_here + 2, 4, 4, COUT)
    planes = spread_taps(
        taps, upper_keep[:, None, None, None, None], lower_keep[:, None, None, None, None]
    )
    planes = planes + jnp.tile(deconv_bias, 2 * cols_here)

    def by_device(x):
        lead = x.shape[0] // tp
        x = x.reshape(lead, tp, x.shape[1], seq, share).transpose(1, 3, 0, 2, 4)
        return x.reshape(devices, -1, share).astype(bf16)

    def total(parts):
        sizes = [p.shape[1] for p in parts]
        summed = lax.psum_scatter(
            jnp.concatenate(parts, axis=1), ("tp", "seq"), scatter_dimension=0, tiled=True
        )[0].astype(f32)
        out, at = [], 0
        for size in sizes:
            out.append(summed[at : at + size])
            at += size
        return out

    terms_b = [
        by_device(dot("ximf,imd->xfd", grad_hidden, second_in)),
        by_device(dot("ximf,imd->xfd", active, grad_mlp)),
        by_device(dot("rict,ricd->td", tap_grads, out_tile).reshape(tp, 16 * COUT // tp, width)),
    ]
    grad_self = (piece(5) * grad_mid_two).astype(bf16)
    grad_gate_s = jnp.sum(grad_mid_two * branch_s, axis=1)
    if fast:
        dso_send = back_pack(grad_self.reshape(flat), so_slots, items, turns, groups)
        dso_send = dso_send.reshape(turns, devices, half, 2 * HEAD)
    else:
        dso_send = pack_rows(dot("nd,xed->xne", grad_self.reshape(flat), so_slots).astype(bf16))
    dso_mine = [
        exchange(dso_send[turn], both_axes).reshape(devices * half, 2 * HEAD)
        for turn in range(turns)
    ]
    dso_mine[0], terms_b = lax.optimization_barrier((dso_mine[0], terms_b))
    grad_up, grad_down, grad_deconv = total(terms_b)
    backward = [
        self_backward(parts[turn], dso_mine[turn], *forward[turn][1:], devices, half)
        for turn in range(turns)
    ]
    if fast:
        blocks = [
            exchange(x[0], both_axes).reshape(groups, slots, 2, 3 * half, 2 * HEAD)
            for x in backward
        ]
        blocks[-1], planes = lax.optimization_barrier((blocks[-1], planes))
        grad_projected, grad_third = unpack_back(blocks, kv_slots, q_slots, items, groups)
    else:
        dkv = [exchange(x[0].reshape(devices, tile, 2 * HEAD), both_axes) for x in backward]
        dq = [exchange(x[1].reshape(devices, half, 2 * HEAD), both_axes) for x in backward]
        grad_projected = jnp.concatenate(
            [unpack_keys(jnp.stack(dkv)), unpack_rows(jnp.stack(dq))], axis=2
        )
        grad_third = dot(
            "xne,xed->nd", grad_projected, jnp.concatenate([kv_slots, q_slots], axis=1)
        )
    grad_third = grad_third.reshape(items, tile, width)
    grad_shift_s = jnp.sum(grad_third, axis=1)
    grad_scale_s = jnp.sum(grad_third * self_hat, axis=1)
    grad_middle = grad_mid_two + norm_back(self_hat, self_inv, grad_third * (1.0 + piece(4)))

    grad_attn = (piece(2) * grad_middle).astype(bf16)
    grad_gate_a = jnp.sum(grad_middle * branch_a, axis=1)
    do_mine = exchange(dot("imf,tef->time", grad_attn, out_whole).astype(bf16), "tp")
    middle_all = gather(grad_middle.astype(bf16), "tp")
    early = jnp.stack(
        [
            grad_gate_a,
            grad_shift_s,
            grad_scale_s,
            grad_gate_s,
            grad_shift_b,
            grad_scale_b,
            grad_gate_b,
        ],
        axis=0,
    ).reshape(7 * items, width)
    early = jnp.concatenate(
        [early, jnp.pad(grad_bias, (0, width - COUT))[None]], axis=0
    )
    spots = -(-early.shape[0] // (16 * tp)) * 16
    early = jnp.pad(early, ((0, spots * tp - early.shape[0]), (0, 0))).reshape(tp, spots, width)
    terms_a = [
            by_device(dot("xne,nd->xed", grad_projected, self_in.reshape(flat))),
            by_device(
                dot("ne,nd->ed", so_tile, grad_self.reshape(flat)).reshape(
                    slots, slot_width, width
                )
            ),
            by_device(dot("time,imf->tef", mixed_tile, grad_attn)),
            by_device(early),
    ]
    do_mine, terms_a = lax.optimization_barrier((do_mine, terms_a))
    terms_a, grad_up = lax.optimization_barrier((terms_a, grad_up))
    grad_three, grad_self_out, grad_out, grad_early = total(terms_a)
    dq_cross, dk_t, dv_t = cross_backward(queries, do_mine, mixed_wide, cross_logs, keys, values_t)
    dq_cross, middle_all = lax.optimization_barrier((dq_cross, middle_all))
    dq_all = gather(dq_cross, "tp")
    grad_three = grad_three.reshape(2, 3 * slot_width, share)
    grad_pair = grad_three[:, : 2 * slot_width].reshape(2, slot_heads, 2, HEAD, share)
    grad_self_key = grad_pair[:, :, 0].reshape(local, share).T
    grad_self_value = grad_pair[:, :, 1].reshape(local, share).T
    grad_self_query = grad_three[:, 2 * slot_width :].reshape(local, share).T

    shared = lax.all_gather(
        jnp.concatenate([grad_deconv, grad_early], axis=0), ("tp", "seq"), axis=0, tiled=False
    )
    shared = shared.reshape(tp, seq, -1, share).transpose(0, 2, 1, 3).reshape(tp, -1, width)
    grad_deconv = shared[:, : 16 * COUT // tp].reshape(16 * COUT, width).T
    early = shared[:, 16 * COUT // tp :].reshape(-1, width)
    grad_bias = early[7 * items, :COUT]
    early = early[: 7 * items].reshape(7, items, width)

    def by_seq(x):
        return x.reshape((seq, x.shape[0] // seq) + x.shape[1:]).astype(bf16)

    last = jnp.concatenate(
        [
            by_seq(dot("iqd,iqe->de", first_in, dq_cross)),
            by_seq(dot("pid,iep->de", context, dk_t)),
            by_seq(dot("pid,iep->de", context, dv_t)),
        ],
        axis=1,
    )
    last, dq_all = lax.optimization_barrier((last, dq_all))
    last = jnp.sum(exchange(last, "seq").astype(f32), axis=0)
    grad_first = dot("tiqe,ted->iqd", dq_all, by_tp(query_slots))
    grad_shift_a = jnp.sum(grad_first, axis=1)
    grad_scale_a = jnp.sum(grad_first * first_hat, axis=1)
    grad_tokens = middle_all.astype(f32).transpose(1, 0, 2, 3).reshape(
        items, tp * tile, width
    ) + norm_back(first_hat, first_inv, grad_first * (1.0 + piece(1)))
    grad_tokens = (
        grad_tokens.reshape(items, tp, rows_here, cols_here, width)
        .transpose(2, 0, 1, 3, 4)
        .reshape(rows_here, items, plane_cols, width)
    )

    depth = (last.shape[0] - share) // 2
    grad_query, grad_key, grad_value = (
        last[:share],
        last[share : share + depth],
        last[share + depth :],
    )
    late = jnp.sum(gather(jnp.stack([grad_shift_a, grad_scale_a], axis=0), "seq"), axis=0)
    grad_mods = jnp.concatenate([late, early], axis=0).transpose(1, 0, 2)
    grad_table = jnp.dot(picker.T, grad_mods.reshape(items, 9 * width), precision=highest)
    return (
        out_tile,
        planes,
        grad_tokens,
        grad_query,
        grad_key,
        grad_value,
        grad_out,
        grad_self_query,
        grad_self_key,
        grad_self_value,
        grad_self_out.reshape(local, share),
        grad_up.T,
        grad_down,
        grad_deconv,
        grad_bias,
        grad_table,
    )


def solution(mesh):
    in_specs = (
        P("seq", None, None, None),
        P(),
        P(),
        P(),
        P(None, "tp"),
        P(None, "tp"),
        P(None, "tp"),
        P("tp", None),
        P(None, "tp"),
        P(None, "tp"),
        P(None, "tp"),
        P("tp", None),
        P(None, "tp"),
        P("tp", None),
        P(),
        P(),
        P("seq", None, "tp", None),
        P("seq", None, "tp"),
    )
    out_specs = (
        P("seq", None, "tp", None),
        P("seq", None, "tp"),
        P("seq", None, None, None),
        P("seq", "tp"),
        P("seq", "tp"),
        P("seq", "tp"),
        P("tp", "seq"),
        P("seq", "tp"),
        P("seq", "tp"),
        P("seq", "tp"),
        P("tp", "seq"),
        P("seq", "tp"),
        P("tp", "seq"),
        P(),
        P(),
        P(),
    )
    return jax.shard_map(body, mesh=mesh, in_specs=in_specs, out_specs=out_specs, check_vma=False)
```

time: 2120 us -> 1230 us (0.58)
  waiting for transfers between devices: 635 us -> 149 us
  blocking collectives: 318 us -> 35.8 us
  starting transfers between devices: 186 us -> 114 us
  local copies, waits for them, and re-layouts: 292 us -> 231 us
  Pallas kernels: 277 us -> 313 us
  matrix products: 271 us -> 236 us
    all_to_all x35 -> x17, waiting for transfers between devices: 488 us -> 72.3 us  [exchange(): return lax.all_to_all(x, axis, 0, 0, tiled=True)]
    all_to_all x6 -> x1, blocking collectives: 185 us -> 35.8 us  [exchange(): return lax.all_to_all(x, axis, 0, 0, tiled=True)]
    psum x2 -> x0, blocking collectives: 132 us -> none  [the longest x1 83.5 us: body(): grad_deconv, grad_bias = lax.psum((grad_deconv, grad_bias), both_axes)]
    psum x1 -> x0, waiting for transfers between devices: 72.4 us -> none  [body(): grad_deconv, grad_bias = lax.psum((grad_deconv, grad_bias), both_axes)]
    reduce_scatter x0 -> x2, waiting for transfers between devices: none -> 71.4 us  [total(): lax.psum_scatter(jnp.concatenate(parts, axis=1), ('tp', 'seq'), scatter_d...]
    ppermute x4, waiting for transfers between devices: 73.5 us -> 4.49 us  [with_halo(): after = lax.ppermute(initial, axis, down)]
    all_to_all x35 -> x17, starting transfers between devices: 163 us -> 96.3 us  [exchange(): return lax.all_to_all(x, axis, 0, 0, tiled=True)]
    another operation x16 -> x4, local copies, waits for them, and re-layouts: 39.5 us -> 4.5 us  [the longest x6 14.8 us: body(): self_tile = unpack_rows(jnp.stack(so_back))]
  transfers between devices with their start and end apart: 44 -> 31, of which waited for: 24 -> 13; matrix products, arithmetic and copies ran while one was open for 23% -> 35% of each run, Pallas kernels for 10% -> 25%
where the time goes in v2:
time: 1230 us; the launch traced here: 1220 us
  Pallas kernels  313 us (25%)
  matrix products  236 us (19%)
  local copies, waits for them, and re-layouts  231 us (19%)
  waiting for transfers between devices  149 us (12%)
  other arithmetic  125 us (10%)
  starting transfers between devices  114 us (9%)
  blocking collectives  35.8 us (3%)
  between operations  16 us (1%)
    dot_general x21, matrix products, dot(): return jnp.einsum(spec, a, b, preferred_element_type=f32)  234 us
    pallas_call x1, Pallas kernels, cross_backward(): pl.pallas_call(kernel, grid=(items, heads), in_specs=[rows_spec, tiles_sp...  98.1 us
    all_to_all x17, starting transfers between devices, exchange(): return lax.all_to_all(x, axis, 0, 0, tiled=True)  96.3 us
    unnamed x230, local copies, waits for them, and re-layouts  84.1 us
    pallas_call x3, Pallas kernels, self_backward(): pl.pallas_call(kernel, grid=(blocks,), in_specs=part_specs(parts, half) +...  77.6 us
    all_to_all x17, waiting for transfers between devices, exchange(): return lax.all_to_all(x, axis, 0, 0, tiled=True)  72.3 us
    reduce_scatter x2, waiting for transfers between devices, total(): lax.psum_scatter(jnp.concatenate(parts, axis=1), ('tp', 'seq'), scatter_d...  71.4 us
    pallas_call x1, Pallas kernels, cross_forward(): pl.pallas_call(kernel, grid=(items, heads // 2), in_specs=[pl.BlockSpec((...  61.9 us
  transfers between devices with their start and end apart: 31, of which 13 were waited for; matrix products, arithmetic and copies ran while one was open for 35% of the time, Pallas kernels for 25%

profile of v2, /device:TPU:0, one launch (start us, length us, event | category | flops | bytes accessed | tf_op | source)
XLA Modules:
  0.0 1220.2 jit_solution(14046853375694759534)
XLA Ops:
  52.3 20.3 %convert_bitcast_fusion.1.k_ref = bf16[6,4096,256]{2,1,0:T(8,128)(2,1)} fusion(bf16[4096,6,768]{2,0,1:T(8,128)(2,1)} %param.19, bf16[768,256]{1,0:T(8,128)(2,1)S(1)} %copy-done.95), kind=kOutput, calls=%fused_computation.6 | convolution fusion | flops 9669967872 | bytes 50724864 | tf_op jit(solution)/shard_map/pid,de->ipe/dot_general | solution.py:680
  72.5 19.6 %convert_bitcast_fusion.vt_ref = bf16[6,256,4096]{2,1,0:T(8,128)(2,1)} fusion(bf16[4096,6,768]{2,0,1:T(8,128)(2,1)} %param.19, bf16[768,256]{1,0:T(8,128)(2,1)S(1)} %copy-done.96), kind=kOutput, calls=%fused_computation.5 | convolution fusion | flops 9669967872 | bytes 50724864 | tf_op jit(solution)/shard_map/pid,de->iep/dot_general | solution.py:680
  92.1 61.9 %cross_forward.1 = (bf16[4,6,96,256]{3,2,1,0:T(8,128)(2,1)S(1)}, f32[4,6,96,256]{3,2,1,0:T(8,128)S(1)}, f32[6,4,8,384]{3,2,1,0:T(8,128)S(1)}) custom-call(bf16[6,384,256]{2,1,0:T(8,128)(2,1)S(1)} %fusion.73.q_ref, bf16[6,4096,256]{2,1,0:T(8,128)(2,1)} %convert_bitcast_fusion.1.k_ref, bf16[6,256,4096]{2,1,0:T(8,128)(2,1)} %convert_bitcast_fusion.vt_ref), custom_call_target="tpu_custom_call" | custom-call | flops 38654705664 | bytes 27525120 | tf_op jit(solution)/shard_map/cross_forward/pallas_call | solution.py:143
  195.8 35.8 %all_to_all.90.refs_0_ = bf16[32,144,128]{2,1,0:T(8,128)(2,1)} all-to-all(bf16[32,144,128]{2,1,0:T(8,128)(2,1)S(1)} %bitcast.636), channel_id=1, replica_groups=mesh['seq'=8,'tp'=4] {'seq','tp'}, dimensions={0} | all-to-all | bytes 2359296 | tf_op jit(solution)/shard_map/all_to_all | solution.py:621
  264.0 16.3 %all-to-all-start.5 = ((bf16[32,144,128]{2,1,0:T(8,128)(2,1)}), bf16[32,144,128]{2,1,0:T(8,128)(2,1)}, u32[]{:S(2)}, u32[]{:S(2)}) async-start(bf16[32,144,128]{2,1,0:T(8,128)(2,1)} %bitcast.633), calls=%async_computation.5 | async-start | bytes 2359296 | tf_op jit(solution)/shard_map/all_to_all | solution.py:621
  304.1 14.8 %self_forward.3 = (bf16[1536,128]{1,0:T(8,128)(2,1)}, f32[1536,128]{1,0:T(8,128)S(1)}, f32[4,8,768]{2,1,0:T(8,128)S(1)}) custom-call(bf16[32,144,128]{2,1,0:T(8,128)(2,1)S(1)} %copy-done.12), custom_call_target="tpu_custom_call" | custom-call | flops 9663676416 | bytes 3145728 | tf_op jit(solution)/shard_map/self_forward/pallas_call | solution.py:314
  325.6 15.3 %self_forward.4 = (bf16[1536,128]{1,0:T(8,128)(2,1)S(1)}, f32[1536,128]{1,0:T(8,128)S(1)}, f32[4,8,768]{2,1,0:T(8,128)S(1)}) custom-call(bf16[32,144,128]{2,1,0:T(8,128)(2,1)} %all-to-all-done.3.refs_0_), custom_call_target="tpu_custom_call" | custom-call | flops 9663676416 | bytes 3145728 | tf_op jit(solution)/shard_map/self_forward/pallas_call | solution.py:314
  349.0 15.3 %self_forward.5 = (bf16[1536,128]{1,0:T(8,128)(2,1)S(1)}, f32[1536,128]{1,0:T(8,128)S(1)}, f32[4,8,768]{2,1,0:T(8,128)S(1)}) custom-call(bf16[32,144,128]{2,1,0:T(8,128)(2,1)} %all-to-all-done.5.refs_0_), custom_call_target="tpu_custom_call" | custom-call | flops 9663676416 | bytes 3145728 | tf_op jit(solution)/shard_map/self_forward/pallas_call | solution.py:314
  397.9 28.3 %fusion = (f32[8,6,96,512]{3,2,1,0:T(8,128)}, f32[8,512,6,96]{1,3,2,0:T(8,128)S(1)}) fusion(bf16[8,1024,512,1]{2,1,3,0:T(8,128)(2,1)} %bitcast.671, f32[6,96,1024]{2,1,0:T(8,128)} %copy-done.47, f32[6,1024]{1,0:T(8,128)S(1)} %copy-done.89, f32[6,1024]{1,0:T(8,128)S(1)} %copy-done.63, f32[6,96]{1,0:T(8,128)S(1)} %add_rsqrt_fusion.1, ...), kind=kOutput, calls=%fused_computation.8 | convolution fusion | flops 4981063680 | bytes 29676032 | tf_op jit(solution)/shard_map/imd,xdf->ximf/dot_general | solution.py:680
  429.9 21.3 %fusion.3 = bf16[8,512,6,96]{1,3,2,0:T(8,128)(2,1)} fusion(f32[8,512,6,96]{1,3,2,0:T(8,128)S(1)} %get-tuple-element.296), kind=kLoop, calls=%fused_computation.11 | loop fusion | flops 153354240 | bytes 14155776 | tf_op jit(solution)/shard_map/convert_element_type | solution.py:843
  451.2 13.3 %fusion.11 = bf16[8,6,96,512]{3,2,1,0:T(8,128)(2,1)S(1)} fusion(f32[8,6,96,512]{3,2,1,0:T(8,128)} %get-tuple-element.295, f32[8,512,6,96]{1,3,2,0:T(8,128)} %copy-done.46, bf16[8,512,1024,1]{2,1,3,0:T(8,128)(2,1)} %bitcast.615, bf16[6,96,1024]{2,1,0:T(8,128)(2,1)} %copy-done.56), kind=kOutput, calls=%fused_computation.26 | convolution fusion | flops 4864868352 | bytes 33161216 | tf_op jit(solution)/shard_map/imd,xfd->ximf/dot_general | solution.py:680
  464.6 9.8 fusion.48
  483.7 15.1 %multiply_reduce_fusion.1 = (bf16[6,1024]{1,0:T(8,128)(2,1)}, f32[6,96,1024]{2,1,0:T(8,128)}, bf16[6,1024]{1,0:T(8,128)(2,1)}, bf16[6,96,1024]{2,1,0:T(8,128)(2,1)}) fusion(f32[6,96,1024]{2,1,0:T(8,128)S(1)} %bitcast.582, f32[6,96]{1,0:T(8,128)S(1)} %broadcast_multiply_fusion.5, f32[6,96,1024]{2,1,0:T(8,128)S(1)} %copy-done.48, ...), kind=kOutput, calls=%fused_computation.105 | convolution fusion | flops 4847751168 | bytes 40322048 | tf_op jit(solution)/shard_map/ximf,xfd->imd/dot_general | solution.py:680
  518.1 11.4 fusion.35
  554.9 18.5 %pad_maximum_fusion = bf16[32,2368,128]{2,1,0:T(8,128)(2,1)} fusion(bf16[32,320,128]{2,1,0:T(8,128)(2,1)} %bitcast.637, bf16[32,1024,128]{2,1,0:T(8,128)(2,1)} %bitcast.599, bf16[32,1024,128]{2,1,0:T(8,128)(2,1)} %bitcast.600), kind=kLoop, calls=%fused_computation | loop fusion | flops 58195968 | bytes 38797312 | tf_op jit(solution)/shard_map/concatenate | solution.py:872
  586.3 9.7 all-to-all-done.11
  605.4 26.2 %self_backward.5 = bf16[32,144,128]{2,1,0:T(8,128)(2,1)S(1)} custom-call(bf16[32,144,128]{2,1,0:T(8,128)(2,1)} %all-to-all-done.3.refs_0_, bf16[1536,128]{1,0:T(8,128)(2,1)S(1)} %bitcast.591, f32[1536,128]{1,0:T(8,128)S(1)} %copy-done.33, f32[4,8,768]{2,1,0:T(8,128)S(1)} %copy-done.39), custom_call_target="tpu_custom_call" | custom-call | flops 24159191040 | bytes 6291456 | tf_op jit(solution)/shard_map/self_backward/pallas_call | solution.py:400
  653.5 26.2 %self_backward.3 = bf16[32,144,128]{2,1,0:T(8,128)(2,1)S(1)} custom-call(bf16[32,144,128]{2,1,0:T(8,128)(2,1)} %all-to-all-done.5.refs_0_, bf16[1536,128]{1,0:T(8,128)(2,1)S(1)} %bitcast.590, f32[1536,128]{1,0:T(8,128)S(1)} %copy-done.31, f32[4,8,768]{2,1,0:T(8,128)S(1)} %copy-done.37), custom_call_target="tpu_custom_call" | custom-call | flops 24159191040 | bytes 6291456 | tf_op jit(solution)/shard_map/self_backward/pallas_call | solution.py:400
  700.6 25.2 %self_backward.4 = bf16[32,144,128]{2,1,0:T(8,128)(2,1)S(1)} custom-call(bf16[32,144,128]{2,1,0:T(8,128)(2,1)S(1)} %copy-done.13, bf16[1536,128]{1,0:T(8,128)(2,1)S(1)} %bitcast.588, f32[1536,128]{1,0:T(8,128)S(1)} %copy-done.29, f32[4,8,768]{2,1,0:T(8,128)S(1)} %get-tuple-element.65.refs_3_), custom_call_target="tpu_custom_call" | custom-call | flops 24159191040 | bytes 6291456 | tf_op jit(solution)/shard_map/self_backward/pallas_call | solution.py:400
  750.8 10.4 reshape.502
  774.5 11.0 all-to-all-done.10
  787.1 10.8 unpack_back.1
  834.6 12.5 %all-to-all-done.13.do_ref = bf16[4,6,96,256]{3,2,1,0:T(8,128)(2,1)} async-done(((bf16[4,6,96,256]{3,2,1,0:T(8,128)(2,1)}), bf16[4,6,96,256]{3,2,1,0:T(8,128)(2,1)}, u32[]{:S(2)}, u32[]{:S(2)}) %all-to-all-start.13) | async-done | bytes 1179680 | tf_op jit(solution)/shard_map/all_to_all | solution.py:621
  847.1 28.4 %reduce-scatter.3.cloned.1.call-done = bf16[1,2368,128]{2,1,0:T(8,128)(2,1)} async-done(((bf16[32,2368,128]{2,1,0:T(8,128)(2,1)}), bf16[1,2368,128]{2,1,0:T(8,128)(2,1)}) %reduce-scatter.3.cloned.1.call-update) | async-done | bytes 606224 | tf_op jit(solution)/shard_map/reduce_scatter | solution.py:871
  878.9 12.6 %pad_maximum_fusion.1 = bf16[32,1296,128]{2,1,0:T(8,128)(2,1)} fusion(bf16[32,16,128]{2,1,0:T(8,128)(2,1)S(1)} %bitcast.669, bf16[32,256,128]{2,1,0:T(8,128)(2,1)} %bitcast.623, bf16[32,256,128]{2,1,0:T(8,128)(2,1)S(1)} %bitcast.622, bf16[32,768,128]{2,1,0:T(8,128)(2,1)} %bitcast.602), kind=kLoop, calls=%fused_computation.7 | loop fusion | flops 42467328 | bytes 21233664 | tf_op jit(solution)/shard_map/concatenate | solution.py:872
  905.9 98.1 %cross_backward.1 = (bf16[6,384,256]{2,1,0:T(8,128)(2,1)S(1)}, bf16[6,256,4096]{2,1,0:T(8,128)(2,1)}, bf16[6,256,4096]{2,1,0:T(8,128)(2,1)}) custom-call(bf16[6,384,256]{2,1,0:T(8,128)(2,1)S(1)} %copy-done.27, bf16[4,6,96,256]{3,2,1,0:T(8,128)(2,1)} %all-to-all-done.13.do_ref, f32[4,6,96,256]{3,2,1,0:T(8,128)S(1)} %copy-done.35, ...), custom_call_target="tpu_custom_call" | custom-call | flops 96636764160 | bytes 55050240 | tf_op jit(solution)/shard_map/cross_backward/pallas_call | solution.py:219
  1014.9 43.1 %reduce-scatter.5.cloned.1.call-done = bf16[1,1296,128]{2,1,0:T(8,128)(2,1)} async-done(((bf16[32,1296,128]{2,1,0:T(8,128)(2,1)}), bf16[1,1296,128]{2,1,0:T(8,128)(2,1)}) %reduce-scatter.5.cloned.1.call-update) | async-done | bytes 331792 | tf_op jit(solution)/shard_map/reduce_scatter | solution.py:871
  1060.6 23.8 %fusion.84 = bf16[768,256]{0,1:T(8,128)(2,1)S(1)} fusion(bf16[6,256,4096]{2,1,0:T(8,128)(2,1)} %get-tuple-element.78, bf16[4096,6,768]{2,0,1:T(8,128)(2,1)} %param.19), kind=kOutput, calls=%fused_computation.156 | convolution fusion | flops 9663873024 | bytes 50724864 | tf_op jit(solution)/shard_map/pid,iep->de/dot_general | solution.py:680
  1084.6 24.4 %fusion.83 = bf16[768,256]{0,1:T(8,128)(2,1)} fusion(bf16[6,256,4096]{2,1,0:T(8,128)(2,1)} %get-tuple-element.79, bf16[4096,6,768]{2,0,1:T(8,128)(2,1)} %param.19), kind=kOutput, calls=%fused_computation.155 | convolution fusion | flops 9663873024 | bytes 50724864 | tf_op jit(solution)/shard_map/pid,iep->de/dot_general | solution.py:680
  1115.5 12.8 %fusion.5 = (f32[6,1024]{1,0:T(8,128)S(1)}, f32[6,384]{1,0:T(8,128)S(1)}, f32[6,384]{1,0:T(8,128)S(1)}, f32[6,1024]{1,0:T(8,128)S(1)}, f32[6,384,1024,1]{2,1,0,3:T(8,128)}) fusion(f32[12,6,4,8,1024]{4,3,0,2,1:T(8,128)} %copy-done.42, f32[6,384]{1,0:T(8,128)S(1)} %copy-done.82, f32[6,384]{1,0:T(8,128)S(1)} %copy-done.80, f32[6,1024]{1,0:T(8,128)S(1)} %copy-done.75, ...), kind=kOutput, calls=%fused_computation.17 | convolution fusion | flops 4853055488 | bytes 25800704 | tf_op jit(solution)/shard_map/tiqe,ted->iqd/dot_general | solution.py:680
  1135.5 10.2 all-to-all-done.17
  1167.2 11.8 bitcast_add_fusion
  (443 shorter events, 490.2 us)
Async XLA Ops:
  7.2 365.7 %copy-start = (bf16[1024,1280]{1,0:T(8,128)(2,1)S(1)}, bf16[1024,1280]{1,0:T(8,128)(2,1)}, u32[]{:S(2)}) copy-start(bf16[1024,1280]{1,0:T(8,128)(2,1)} %param.32) | copy-start | bytes 7864324
  7.2 155.4 %all-gather.9.cloned.1.call-start = ((), (), s32[]{:S(2)}) async-start(), calls=%async_computation.22 | async-start | bytes 14155776 | tf_op jit(solution)/shard_map/all_gather | solution.py:693
  21.7 376.2 %all-gather.11.cloned.1.call-start = ((), (), s32[]{:S(2)}) async-start(), calls=%async_computation.23 | async-start | bytes 9437184 | tf_op jit(solution)/shard_map/all_gather | solution.py:693
  157.2 21.2 %all-to-all-start = ((bf16[4,6,96,256]{3,2,1,0:T(8,128)(2,1)}), bf16[4,6,96,256]{3,2,1,0:T(8,128)(2,1)}, u32[]{:S(2)}, u32[]{:S(2)}) async-start(bf16[4,6,96,256]{3,2,1,0:T(8,128)(2,1)} %copy-done.17), calls=%async_computation | async-start | bytes 2359296 | tf_op jit(solution)/shard_map/all_to_all | solution.py:621
  231.5 32.5 %all-to-all-start.3 = ((bf16[32,144,128]{2,1,0:T(8,128)(2,1)}), bf16[32,144,128]{2,1,0:T(8,128)(2,1)}, u32[]{:S(2)}, u32[]{:S(2)}) async-start(bf16[32,144,128]{2,1,0:T(8,128)(2,1)} %bitcast.634), calls=%async_computation.3 | async-start | bytes 2359296 | tf_op jit(solution)/shard_map/all_to_all | solution.py:621
  234.9 216.3 %all-gather.13.cloned.1.call-start = ((), (), s32[]{:S(2)}) async-start(), calls=%async_computation.24 | async-start | bytes 9437184 | tf_op jit(solution)/shard_map/all_gather | solution.py:693
  235.2 8.6 collective-permute-start
  237.3 6.6 collective-permute-start.1
  244.0 5.3 collective-permute-start.2
  247.6 6.2 collective-permute-start.3
  264.0 55.8 %all-to-all-start.5 = ((bf16[32,144,128]{2,1,0:T(8,128)(2,1)}), bf16[32,144,128]{2,1,0:T(8,128)(2,1)}, u32[]{:S(2)}, u32[]{:S(2)}) async-start(bf16[32,144,128]{2,1,0:T(8,128)(2,1)} %bitcast.633), calls=%async_computation.5 | async-start | bytes 2359296 | tf_op jit(solution)/shard_map/all_to_all | solution.py:621
  319.8 23.3 %all-to-all-start.2 = ((bf16[32,48,128]{2,1,0:T(8,128)(2,1)}), bf16[32,48,128]{2,1,0:T(8,128)(2,1)S(1)}, u32[]{:S(2)}, u32[]{:S(2)}) async-start(bf16[32,48,128]{2,1,0:T(8,128)(2,1)} %bitcast.33), calls=%async_computation.2 | async-start | bytes 786432 | tf_op jit(solution)/shard_map/all_to_all | solution.py:621
  343.1 23.4 %all-to-all-start.4 = ((bf16[32,48,128]{2,1,0:T(8,128)(2,1)}), bf16[32,48,128]{2,1,0:T(8,128)(2,1)S(1)}, u32[]{:S(2)}, u32[]{:S(2)}) async-start(bf16[32,48,128]{2,1,0:T(8,128)(2,1)} %bitcast.593), calls=%async_computation.4 | async-start | bytes 786432 | tf_op jit(solution)/shard_map/all_to_all | solution.py:621
  366.5 20.0 %all-to-all-start.6 = ((bf16[32,48,128]{2,1,0:T(8,128)(2,1)}), bf16[32,48,128]{2,1,0:T(8,128)(2,1)}, u32[]{:S(2)}, u32[]{:S(2)}) async-start(bf16[32,48,128]{2,1,0:T(8,128)(2,1)} %bitcast.594), calls=%async_computation.6 | async-start | bytes 786432 | tf_op jit(solution)/shard_map/all_to_all | solution.py:621
  507.9 47.0 %all-to-all-start.9 = ((bf16[32,48,128]{2,1,0:T(8,128)(2,1)}), bf16[32,48,128]{2,1,0:T(8,128)(2,1)S(1)}, u32[]{:S(2)}, u32[]{:S(2)}) async-start(bf16[32,48,128]{2,1,0:T(8,128)(2,1)} %bitcast.89), calls=%async_computation.9 | async-start | bytes 786432 | tf_op jit(solution)/shard_map/all_to_all | solution.py:621
  510.5 365.1 %reduce-scatter.3.cloned.1.call-start = ((), (), s32[]{:S(2)}) async-start(), calls=%async_computation.20 | async-start | bytes 20004864 | tf_op jit(solution)/shard_map/reduce_scatter | solution.py:871
  573.3 22.7 %all-to-all-start.11 = ((bf16[32,48,128]{2,1,0:T(8,128)(2,1)}), bf16[32,48,128]{2,1,0:T(8,128)(2,1)S(1)}, u32[]{:S(2)}, u32[]{:S(2)}) async-start(bf16[32,48,128]{2,1,0:T(8,128)(2,1)} %bitcast.648), calls=%async_computation.11 | async-start | bytes 786432 | tf_op jit(solution)/shard_map/all_to_all | solution.py:621
  596.8 35.9 %all-to-all-start.7 = ((bf16[32,48,128]{2,1,0:T(8,128)(2,1)}), bf16[32,48,128]{2,1,0:T(8,128)(2,1)S(1)}, u32[]{:S(2)}, u32[]{:S(2)}) async-start(bf16[32,48,128]{2,1,0:T(8,128)(2,1)} %bitcast.647), calls=%async_computation.7 | async-start | bytes 786432 | tf_op jit(solution)/shard_map/all_to_all | solution.py:621
  632.6 53.4 %all-to-all-start.12 = ((bf16[32,144,128]{2,1,0:T(8,128)(2,1)}), bf16[32,144,128]{2,1,0:T(8,128)(2,1)}, u32[]{:S(2)}, u32[]{:S(2)}) async-start(bf16[32,144,128]{2,1,0:T(8,128)(2,1)} %copy-done.18), calls=%async_computation.12 | async-start | bytes 2359296 | tf_op jit(solution)/shard_map/all_to_all | solution.py:621
  641.2 50.2 %collective-permute-start.4 = (bf16[1,6,8,1024]{3,0,2,1:T(2,128)(2,1)}, bf16[1,6,8,1024]{3,0,2,1:T(2,128)(2,1)}, u32[]{:S(2)}, u32[]{:S(2)}) collective-permute-start(bf16[1,6,8,1024]{3,0,2,1:T(2,128)(2,1)} %get-tuple-element.260), channel_id=1, source_target_pairs={{0,4},{4,8},{8,12},{12,16},{16,20},{20,24},{24,28},{1,5},{5,9},{9,... | collective-permute-start | bytes 294920 | tf_op jit(solution)/shard_map/ppermute | solution.py:29
  643.9 47.4 %collective-permute-start.5 = (bf16[1,6,8,1024]{3,0,2,1:T(2,128)(2,1)}, bf16[1,6,8,1024]{3,0,2,1:T(2,128)(2,1)}, u32[]{:S(2)}, u32[]{:S(2)}) collective-permute-start(bf16[1,6,8,1024]{3,0,2,1:T(2,128)(2,1)} %get-tuple-element.261), channel_id=1, source_target_pairs={{4,0},{8,4},{12,8},{16,12},{20,16},{24,20},{28,24},{5,1},{9,5},{13... | collective-permute-start | bytes 294920 | tf_op jit(solution)/shard_map/ppermute | solution.py:30
  686.0 48.3 %all-to-all-start.8 = ((bf16[32,144,128]{2,1,0:T(8,128)(2,1)}), bf16[32,144,128]{2,1,0:T(8,128)(2,1)}, u32[]{:S(2)}, u32[]{:S(2)}) async-start(bf16[32,144,128]{2,1,0:T(8,128)(2,1)} %copy-done.16), calls=%async_computation.8 | async-start | bytes 2359296 | tf_op jit(solution)/shard_map/all_to_all | solution.py:621
  692.6 51.6 %collective-permute-start.6 = (bf16[14,6,1,1024]{3,0,2,1:T(8,128)(2,1)S(1)}, bf16[14,6,1,1024]{3,0,2,1:T(8,128)(2,1)}, u32[]{:S(2)}, u32[]{:S(2)}) collective-permute-start(bf16[14,6,1,1024]{3,0,2,1:T(8,128)(2,1)S(1)} %get-tuple-element.256), channel_id=1, source_target_pairs={{0,1},{1,2},{2,3},{4,5},{5,6},{6,7},{8,9},{9,10},{10,11},{12,13},{... | collective-permute-start | bytes 516104 | tf_op jit(solution)/shard_map/ppermute | solution.py:29
  697.0 47.3 %collective-permute-start.7 = (bf16[14,6,1,1024]{3,0,2,1:T(8,128)(2,1)S(1)}, bf16[14,6,1,1024]{3,0,2,1:T(8,128)(2,1)}, u32[]{:S(2)}, u32[]{:S(2)}) collective-permute-start(bf16[14,6,1,1024]{3,0,2,1:T(8,128)(2,1)S(1)} %get-tuple-element.257), channel_id=1, source_target_pairs={{1,0},{2,1},{3,2},{5,4},{6,5},{7,6},{9,8},{10,9},{11,10},{13,12},{... | collective-permute-start | bytes 516104 | tf_op jit(solution)/shard_map/ppermute | solution.py:30
  734.3 51.1 %all-to-all-start.10 = ((bf16[32,144,128]{2,1,0:T(8,128)(2,1)}), bf16[32,144,128]{2,1,0:T(8,128)(2,1)}, u32[]{:S(2)}, u32[]{:S(2)}) async-start(bf16[32,144,128]{2,1,0:T(8,128)(2,1)} %copy-done.15), calls=%async_computation.10 | async-start | bytes 2359296 | tf_op jit(solution)/shard_map/all_to_all | solution.py:621
  814.5 32.6 %all-to-all-start.13 = ((bf16[4,6,96,256]{3,2,1,0:T(8,128)(2,1)}), bf16[4,6,96,256]{3,2,1,0:T(8,128)(2,1)}, u32[]{:S(2)}, u32[]{:S(2)}) async-start(bf16[4,6,96,256]{3,2,1,0:T(8,128)(2,1)} %fusion.74), calls=%async_computation.13 | async-start | bytes 2359296 | tf_op jit(solution)/shard_map/all_to_all | solution.py:621
  818.8 239.2 %reduce-scatter.5.cloned.1.call-start = ((), (), s32[]{:S(2)}) async-start(), calls=%async_computation.21 | async-start | bytes 10948608 | tf_op jit(solution)/shard_map/reduce_scatter | solution.py:871
  897.5 107.5 %all-to-all-start.14 = ((bf16[4,6,96,1024]{3,2,1,0:T(8,128)(2,1)}), bf16[4,6,96,1024]{3,2,1,0:T(8,128)(2,1)}, u32[]{:S(2)}, u32[]{:S(2)}) async-start(bf16[4,6,96,1024]{3,2,1,0:T(8,128)(2,1)} %broadcast_in_dim.10), calls=%async_computation.14 | async-start | bytes 9437184 | tf_op jit(solution)/shard_map/all_to_all | solution.py:621
  1009.0 106.6 %all-to-all-start.15 = ((bf16[4,6,384,256]{3,2,1,0:T(8,128)(2,1)}), bf16[4,6,384,256]{3,2,1,0:T(8,128)(2,1)}, u32[]{:S(2)}, u32[]{:S(2)}) async-start(bf16[4,6,384,256]{3,2,1,0:T(8,128)(2,1)} %broadcast_in_dim.11), calls=%async_computation.15 | async-start | bytes 9437184 | tf_op jit(solution)/shard_map/all_to_all | solution.py:621
  1013.9 185.0 %all-gather.15.cloned.1.call-start = ((), (), s32[]{:S(2)}) async-start(), calls=%async_computation.25 | async-start | bytes 5677056 | tf_op jit(solution)/shard_map/all_gather | solution.py:966
  1129.3 16.4 %all-to-all-start.17 = ((f32[8,2,6,1024]{3,1,2,0:T(2,128)}), f32[8,2,6,1024]{3,1,2,0:T(2,128)S(1)}, u32[]{:S(2)}, u32[]{:S(2)}) async-start(f32[8,2,6,1024]{3,1,2,0:T(2,128)} %broadcast_in_dim.12), calls=%async_computation.19 | async-start | bytes 786432 | tf_op jit(solution)/shard_map/all_to_all | solution.py:621
  1145.7 45.3 %all-to-all-start.16 = ((bf16[8,320,256]{2,1,0:T(8,128)(2,1)}), bf16[8,320,256]{2,1,0:T(8,128)(2,1)}, u32[]{:S(2)}, u32[]{:S(2)}) async-start(bf16[8,320,256]{2,1,0:T(8,128)(2,1)} %pad_maximum_fusion.4), calls=%async_computation.16 | async-start | bytes 2621440 | tf_op jit(solution)/shard_map/all_to_all | solution.py:621
  (99 other events, 804.3 us)
Sparse Core Ops, SparseCore 0:
  21.8 74.8 all-gather.8
  98.6 54.3 all-gather.10
  241.0 72.7 all-gather.12
  573.5 301.9 reduce-scatter.2
  891.6 166.3 reduce-scatter.4
  1061.3 64.3 all-gather.14

commit v3 on v2

--- a/solution.py
+++ b/solution.py
@@ -59,7 +59,6 @@
 
 NT = (((1,), (1,)), ((), ()))
 BLOCKS = 4
-FORCE_PLAIN = False
 
 
 def dot_nt(a, b):
@@ -615,6 +614,275 @@
         ),
         name="unpack_back",
     )(*blocks, kv_w, q_w)
+
+
+def first_kernel(tokens, shift, scale, w, tp):
+    rows, items, cols, width = tokens.shape
+    cols_here = cols // tp
+    tile = rows * cols_here
+    local = w.shape[1]
+
+    def kernel(x_ref, shift_ref, scale_ref, w_ref, in_ref, q_ref):
+        hat, _ = norm_parts(x_ref[...].astype(f32).reshape(rows, cols, width))
+        value = hat * (1.0 + scale_ref[0]) + shift_ref[0]
+        for t in range(tp):
+            part = value[:, t * cols_here : (t + 1) * cols_here, :].reshape(tile, width)
+            in_ref[0, t * tile : (t + 1) * tile, :] = part.astype(bf16)
+        q = dot_nn(in_ref[0], w_ref[...]).astype(bf16).astype(f32) * 0.125
+        q_ref[0] = q.astype(bf16)
+
+    piece_spec = pl.BlockSpec((1, 1, width), lambda i: (i, 0, 0))
+    return pl.pallas_call(
+        kernel,
+        grid=(items,),
+        in_specs=[
+            pl.BlockSpec((rows, 1, cols, width), lambda i: (0, i, 0, 0)),
+            piece_spec,
+            piece_spec,
+            pl.BlockSpec(w.shape, lambda i: (0, 0)),
+        ],
+        out_specs=[
+            pl.BlockSpec((1, tp * tile, width), lambda i: (i, 0, 0)),
+            pl.BlockSpec((1, tp * tile, local), lambda i: (i, 0, 0)),
+        ],
+        out_shape=[
+            jax.ShapeDtypeStruct((items, tp * tile, width), bf16),
+            jax.ShapeDtypeStruct((items, tp * tile, local), bf16),
+        ],
+        compiler_params=pltpu.CompilerParams(vmem_limit_bytes=48 << 20),
+        cost_estimate=pl.CostEstimate(
+            flops=2 * items * tp * tile * width * local,
+            bytes_accessed=4 * items * tp * tile * width,
+            transcendentals=0,
+        ),
+        name="first_kernel",
+    )(tokens, shift, scale, w)
+
+
+def key_value_kernel(context, w_key, w_value_t):
+    items, keys, depth = context.shape
+    local = w_key.shape[1]
+    step = 1024 if keys % 1024 == 0 else keys
+
+    def kernel(x_ref, wk_ref, wv_ref, k_ref, vt_ref):
+        k_ref[0] = dot_nn(x_ref[0], wk_ref[...]).astype(bf16)
+        vt_ref[0] = dot_nt(wv_ref[...], x_ref[0]).astype(bf16)
+
+    return pl.pallas_call(
+        kernel,
+        grid=(items, keys // step),
+        in_specs=[
+            pl.BlockSpec((1, step, depth), lambda i, j: (i, j, 0)),
+            pl.BlockSpec(w_key.shape, lambda i, j: (0, 0)),
+            pl.BlockSpec(w_value_t.shape, lambda i, j: (0, 0)),
+        ],
+        out_specs=[
+            pl.BlockSpec((1, step, local), lambda i, j: (i, j, 0)),
+            pl.BlockSpec((1, local, step), lambda i, j: (i, 0, j)),
+        ],
+        out_shape=[
+            jax.ShapeDtypeStruct((items, keys, local), bf16),
+            jax.ShapeDtypeStruct((items, local, keys), bf16),
+        ],
+        compiler_params=pltpu.CompilerParams(vmem_limit_bytes=40 << 20),
+        cost_estimate=pl.CostEstimate(
+            flops=4 * items * keys * depth * local,
+            bytes_accessed=2 * items * keys * (depth + 2 * local),
+            transcendentals=0,
+        ),
+        name="key_value_kernel",
+    )(context, w_key, w_value_t)
+
+
+def key_value_grads(dk_t, dv_t, context):
+    items, local, keys = dk_t.shape
+    depth = context.shape[2]
+    step = 1024 if keys % 1024 == 0 else keys
+
+    def kernel(dk_ref, dv_ref, x_ref, out_ref):
+        first = (pl.program_id(0) == 0) & (pl.program_id(1) == 0)
+        both = jnp.concatenate([dk_ref[0], dv_ref[0]], axis=0)
+        part = dot_nn(both, x_ref[0])
+
+        @pl.when(first)
+        def _():
+            out_ref[...] = part
+
+        @pl.when(jnp.logical_not(first))
+        def _():
+            out_ref[...] += part
+
+    grads_spec = pl.BlockSpec((1, local, step), lambda i, j: (i, 0, j))
+    return pl.pallas_call(
+        kernel,
+        grid=(items, keys // step),
+        in_specs=[grads_spec, grads_spec, pl.BlockSpec((1, step, depth), lambda i, j: (i, j, 0))],
+        out_specs=pl.BlockSpec((2 * local, depth), lambda i, j: (0, 0)),
+        out_shape=jax.ShapeDtypeStruct((2 * local, depth), f32),
+        compiler_params=pltpu.CompilerParams(vmem_limit_bytes=40 << 20),
+        cost_estimate=pl.CostEstimate(
+            flops=4 * items * keys * depth * local,
+            bytes_accessed=2 * items * keys * (depth + 2 * local),
+            transcendentals=0,
+        ),
+        name="key_value_grads",
+    )(dk_t, dv_t, context)
+
+
+def feed_forward(x, g, up, down):
+    rows, width = x.shape
+    slots, _, hidden = up.shape
+    parts = 4 if rows % 64 == 0 else 1
+    size = rows // parts
+
+    def kernel(x_ref, g_ref, up_ref, down_ref, active_ref, dh_ref, branch_ref, back_ref):
+        slot = pl.program_id(0)
+
+        @pl.when(slot == 0)
+        def _():
+            branch_ref[...] = jnp.zeros_like(branch_ref)
+            back_ref[...] = jnp.zeros_like(back_ref)
+
+        def products(r):
+            mine = pl.ds(r * size, size)
+            return dot_nn(x_ref[mine, :], up_ref[0]), dot_nt(g_ref[mine, :], down_ref[0])
+
+        ahead = products(0)
+        for r in range(parts):
+            h, da = ahead
+            ahead = products(r + 1) if r + 1 < parts else None
+            mine = pl.ds(r * size, size)
+            below = 0.5 * (1.0 + lax.erf(h * 0.7071067811865476))
+            slope = below + h * (jnp.exp(h * h * -0.5) * 0.3989422804014327)
+            active = (h * below).astype(bf16)
+            dh = (da * slope).astype(bf16)
+            active_ref[0, mine, :] = active
+            dh_ref[0, mine, :] = dh
+            branch_ref[mine, :] += dot_nn(active, down_ref[0])
+            back_ref[mine, :] += dot_nt(dh, up_ref[0])
+
+    rows_spec = pl.BlockSpec((rows, width), lambda i: (0, 0))
+    hidden_spec = pl.BlockSpec((1, rows, hidden), lambda i: (i, 0, 0))
+    return pl.pallas_call(
+        kernel,
+        grid=(slots,),
+        in_specs=[
+            rows_spec,
+            rows_spec,
+            pl.BlockSpec((1, width, hidden), lambda i: (i, 0, 0)),
+            pl.BlockSpec((1, hidden, width), lambda i: (i, 0, 0)),
+        ],
+        out_specs=[hidden_spec, hidden_spec, rows_spec, rows_spec],
+        out_shape=[
+            jax.ShapeDtypeStruct((slots, rows, hidden), bf16),
+            jax.ShapeDtypeStruct((slots, rows, hidden), bf16),
+            jax.ShapeDtypeStruct((rows, width), f32),
+            jax.ShapeDtypeStruct((rows, width), f32),
+        ],
+        compiler_params=pltpu.CompilerParams(vmem_limit_bytes=52 << 20),
+        cost_estimate=pl.CostEstimate(
+            flops=8 * slots * rows * width * hidden,
+            bytes_accessed=4 * slots * width * hidden,
+            transcendentals=2 * slots * rows * hidden,
+        ),
+        name="feed_forward",
+    )(x, g, up, down)
+
+
+def weight_terms(buffer, shape, lhs, lhs_block, lhs_place, rhs, tp, size, first):
+    count, width = rhs.shape
+    devices, _, share = shape
+    seq = devices // tp
+    depth = lhs_block[-1]
+
+    def kernel(*refs):
+        a_ref, b_ref, out_ref = refs[0], refs[1], refs[-1]
+        a = a_ref[...]
+        if len(lhs_block) > 3:
+            a = a.astype(f32)
+        a = a.reshape(count, depth).astype(bf16)
+        terms = lax.dot_general(a, b_ref[...], (((0,), (0,)), ((), ())), preferred_element_type=f32)
+        for s in range(seq):
+            out_ref[s] = terms[:, s * share : (s + 1) * share].astype(bf16)
+
+    return pl.pallas_call(
+        kernel,
+        grid=(tp, 2),
+        in_specs=[
+            pl.BlockSpec(lhs_block, lhs_place),
+            pl.BlockSpec(rhs.shape, lambda t, c: (0, 0)),
+        ]
+        + ([] if buffer is None else [pl.BlockSpec(memory_space=pl.ANY)]),
+        out_specs=pl.BlockSpec((seq, size, share), lambda t, c: (t, first // size + c, 0)),
+        out_shape=jax.ShapeDtypeStruct(shape, bf16),
+        input_output_aliases={} if buffer is None else {2: 0},
+        compiler_params=pltpu.CompilerParams(vmem_limit_bytes=40 << 20),
+        cost_estimate=pl.CostEstimate(
+            flops=4 * tp * count * depth * width,
+            bytes_accessed=4 * tp * (count + width) * depth,
+            transcendentals=0,
+        ),
+        name="weight_terms",
+    )(lhs, rhs, *([] if buffer is None else [buffer]))
+
+
+def last_kernel(tokens, scale, middle, dq, query_slots):
+    rows, items, cols, width = tokens.shape
+    tp, _, queries, local = dq.shape
+    cols_here = cols // tp
+    tile = rows * cols_here
+    slot_width = local // 2
+
+    def kernel(x_ref, scale_ref, middle_ref, dq_ref, w_ref, out_ref, sums_ref):
+        hat, inverse = norm_parts(x_ref[...].astype(f32).reshape(rows, cols, width))
+        weights = w_ref[...].reshape(tp * local, width)
+        shift_sum = jnp.zeros((1, width), f32)
+        scale_sum = jnp.zeros((1, width), f32)
+        for t in range(tp):
+            pieces = [
+                dq_ref[u, 0, t * tile : (t + 1) * tile, c * slot_width : (c + 1) * slot_width]
+                for c in range(2)
+                for u in range(tp)
+            ]
+            g = dot_nn(jnp.concatenate(pieces, axis=1), weights)
+            mine = slice(t * cols_here, (t + 1) * cols_here)
+            hat_t = hat[:, mine, :].reshape(tile, width)
+            inverse_t = inverse[:, mine, :].reshape(tile, 1)
+            shift_sum = shift_sum + jnp.sum(g, axis=0, keepdims=True)
+            scale_sum = scale_sum + jnp.sum(g * hat_t, axis=0, keepdims=True)
+            value = middle_ref[t, 0].astype(f32) + norm_back(
+                hat_t, inverse_t, g * (1.0 + scale_ref[0])
+            )
+            out_ref[:, 0, mine, :] = value.reshape(rows, cols_here, width)
+        sums_ref[0, 0:1, :] = shift_sum
+        sums_ref[0, 1:2, :] = scale_sum
+
+    return pl.pallas_call(
+        kernel,
+        grid=(items,),
+        in_specs=[
+            pl.BlockSpec((rows, 1, cols, width), lambda i: (0, i, 0, 0)),
+            pl.BlockSpec((1, 1, width), lambda i: (i, 0, 0)),
+            pl.BlockSpec((tp, 1, tile, width), lambda i: (0, i, 0, 0)),
+            pl.BlockSpec((tp, 1, queries, local), lambda i: (0, i, 0, 0)),
+            pl.BlockSpec(query_slots.shape, lambda i: (0, 0, 0)),
+        ],
+        out_specs=[
+            pl.BlockSpec((rows, 1, cols, width), lambda i: (0, i, 0, 0)),
+            pl.BlockSpec((1, 2, width), lambda i: (i, 0, 0)),
+        ],
+        out_shape=[
+            jax.ShapeDtypeStruct(tokens.shape, f32),
+            jax.ShapeDtypeStruct((items, 2, width), f32),
+        ],
+        compiler_params=pltpu.CompilerParams(vmem_limit_bytes=52 << 20),
+        cost_estimate=pl.CostEstimate(
+            flops=2 * items * queries * width * tp * local,
+            bytes_accessed=10 * items * queries * width,
+            transcendentals=0,
+        ),
+        name="last_kernel",
+    )(tokens, scale, middle, dq, query_slots)
 
 
 def exchange(x, axis):
@@ -666,7 +934,7 @@
     groups = devices // heads
     turns = -(-items // groups)
     share = width // seq
-    fast = slot_heads == 2 and half % 16 == 0 and items == groups * turns and not FORCE_PLAIN
+    fast = slot_heads == 2 and half % 16 == 0 and items == groups * turns and share % 128 == 0
     me_tp = lax.axis_index("tp")
     core = lax.axis_index("seq") % 2
 
@@ -709,17 +977,17 @@
     small = whole(
         jnp.concatenate(
             [
-                my_rows(w_out),
                 key_value,
                 my_columns(w_self_query).T,
                 my_rows(w_self_out),
+                my_rows(w_out),
                 my_columns(w_query).T,
             ],
             axis=0,
         )
     )
-    cuts = [slot_width * k for k in (0, 1, 3, 4, 5, 6)]
-    out_slots, kv_slots, q_slots, so_slots, query_slots = [
+    cuts = [slot_width * k for k in (0, 2, 3, 4, 5, 6)]
+    kv_slots, q_slots, so_slots, out_slots, query_slots = [
         small[:, a:b] for a, b in zip(cuts[:-1], cuts[1:])
     ]
     up_slots = whole(my_columns(w_up))
@@ -764,16 +1032,19 @@
     grad_bias = jnp.sum(incoming.astype(f32), axis=(0, 1, 2))
     grad_mlp = (piece(8) * grad_result).astype(bf16)
 
-    ordered = (
-        tokens.reshape(rows_here, items, tp, cols_here, width)
-        .transpose(1, 2, 0, 3, 4)
-        .reshape(items, tp * tile, width)
-    )
-    first_hat, first_inv = norm_parts(ordered.astype(f32))
-    first_in = (first_hat * (1.0 + piece(1)) + piece(0)).astype(bf16)
-    queries = dot("iqd,de->iqe", first_in, w_query).astype(bf16) * bf16(0.125)
-    keys = dot("pid,de->ipe", context, w_key).astype(bf16)
-    values_t = dot("pid,de->iep", context, w_value).astype(bf16)
+    if fast:
+        first_in, queries = first_kernel(tokens, piece(0), piece(1), w_query, tp)
+    else:
+        ordered = (
+            tokens.reshape(rows_here, items, tp, cols_here, width)
+            .transpose(1, 2, 0, 3, 4)
+            .reshape(items, tp * tile, width)
+        )
+        first_hat, first_inv = norm_parts(ordered.astype(f32))
+        first_in = (first_hat * (1.0 + piece(1)) + piece(0)).astype(bf16)
+        queries = dot("iqd,de->iqe", first_in, w_query).astype(bf16) * bf16(0.125)
+    image = context.transpose(1, 0, 2)
+    keys, values_t = key_value_kernel(image, w_key, w_value.T)
     mixed, mixed_wide, cross_logs = cross_forward(queries, keys, values_t, tp)
     mixed_tile = exchange(mixed, "tp")
     out_whole = by_tp(out_slots)
@@ -812,7 +1083,7 @@
     if fast:
         sends = project_pack(self_in.reshape(flat), kv_slots, q_slots, items, turns, groups)
         sends = sends.reshape(turns, devices, 3 * half, 2 * HEAD)
-        parts = [[exchange(sends[turn], both_axes)] for turn in range(turns)]
+        sends = [sends[turn] for turn in range(turns)]
     else:
         kv_sends = pack_keys(dot("nd,xed->xne", self_in.reshape(flat), kv_slots).astype(bf16))
         q_sends = dot("nd,xed->xne", self_in.reshape(flat), q_slots).astype(bf16)
@@ -824,7 +1095,22 @@
             ]
             for turn in range(turns)
         ]
-    forward = [self_forward(parts[turn], devices, half) for turn in range(turns)]
+    if fast:
+        parts, forward = [], []
+        for turn in range(turns):
+            if turn >= 2:
+                sends[turn], forward[turn - 2] = lax.optimization_barrier(
+                    (sends[turn], forward[turn - 2])
+                )
+            arrived = exchange(sends[turn], both_axes)
+            if turn == 0:
+                arrived, grad_result, grad_mlp = lax.optimization_barrier(
+                    (arrived, grad_result, grad_mlp)
+                )
+            parts.append([arrived])
+            forward.append(self_forward(parts[turn], devices, half))
+    else:
+        forward = [self_forward(parts[turn], devices, half) for turn in range(turns)]
     so_back = [exchange(so.reshape(devices, half, 2 * HEAD), both_axes) for so, _, _ in forward]
     if fast:
         blocks = [x.reshape(groups, slots, 2, half, 2 * HEAD) for x in so_back]
@@ -838,16 +1124,14 @@
 
     second_hat, second_inv = norm_parts(middle_two)
     second_in = (second_hat * (1.0 + piece(7)) + piece(6)).astype(bf16)
-    hidden = dot("imd,xdf->ximf", second_in, up_slots)
-    active_f, gelu_back = jax.vjp(lambda value: jax.nn.gelu(value, approximate=False), hidden)
-    active = active_f.astype(bf16)
-    branch_b = dot("ximf,xfd->imd", active, down_slots)
+    active, grad_hidden, branch_b, grad_second = feed_forward(
+        second_in.reshape(flat), grad_mlp.reshape(flat), up_slots, down_slots
+    )
+    branch_b = branch_b.reshape(items, tile, width)
+    grad_second = grad_second.reshape(items, tile, width)
     result = middle_two + piece(8) * branch_b
     out_tile = from_tile(result.astype(bf16))
 
-    grad_active = dot("imd,xfd->ximf", grad_mlp, down_slots)
-    grad_hidden = gelu_back(grad_active)[0].astype(bf16)
-    grad_second = dot("ximf,xdf->imd", grad_hidden, up_slots)
     grad_gate_b = jnp.sum(grad_result * branch_b, axis=1)
     grad_shift_b = jnp.sum(grad_second, axis=1)
     grad_scale_b = jnp.sum(grad_second * second_hat, axis=1)
@@ -866,22 +1150,39 @@
         x = x.reshape(lead, tp, x.shape[1], seq, share).transpose(1, 3, 0, 2, 4)
         return x.reshape(devices, -1, share).astype(bf16)
 
-    def total(parts):
-        sizes = [p.shape[1] for p in parts]
-        summed = lax.psum_scatter(
-            jnp.concatenate(parts, axis=1), ("tp", "seq"), scatter_dimension=0, tiled=True
-        )[0].astype(f32)
-        out, at = [], 0
-        for size in sizes:
-            out.append(summed[at : at + size])
-            at += size
-        return out
-
-    terms_b = [
-        by_device(dot("ximf,imd->xfd", grad_hidden, second_in)),
-        by_device(dot("ximf,imd->xfd", active, grad_mlp)),
-        by_device(dot("rict,ricd->td", tap_grads, out_tile).reshape(tp, 16 * COUT // tp, width)),
-    ]
+    def total(terms, *cuts):
+        summed = lax.psum_scatter(terms, ("tp", "seq"), scatter_dimension=0, tiled=True)[0]
+        return jnp.split(summed.astype(f32), cuts, axis=0)
+
+    terms_deconv = dot("rict,ricd->td", tap_grads, out_tile)
+    terms_deconv = by_device(terms_deconv.reshape(tp, 16 * COUT // tp, width))
+    size_b = (hidden_here // 2, hidden_here, 2 * hidden_here)
+    if fast:
+        shape = (devices, size_b[2] + terms_deconv.shape[1], share)
+        hidden_block = (1, items * tile, size_b[0])
+
+        def slot_place(t, c):
+            return (c * tp + t, 0, 0)
+
+        terms_b = None
+        for lhs, rhs, first in (
+            (grad_hidden, second_in, 0),
+            (active, grad_mlp, size_b[1]),
+        ):
+            terms_b = weight_terms(
+                terms_b, shape, lhs, hidden_block, slot_place, rhs.reshape(flat), tp, size_b[0], first
+            )
+        terms_b = lax.dynamic_update_slice_in_dim(terms_b, terms_deconv, size_b[2], 1)
+    else:
+        terms_b = jnp.concatenate(
+            [
+                by_device(dot("xnf,nd->xfd", grad_hidden, second_in.reshape(flat))),
+                by_device(dot("xnf,nd->xfd", active, grad_mlp.reshape(flat))),
+                terms_deconv,
+            ],
+            axis=1,
+        )
+
     grad_self = (piece(5) * grad_mid_two).astype(bf16)
     grad_gate_s = jnp.sum(grad_mid_two * branch_s, axis=1)
     if fast:
@@ -889,16 +1190,21 @@
         dso_send = dso_send.reshape(turns, devices, half, 2 * HEAD)
     else:
         dso_send = pack_rows(dot("nd,xed->xne", grad_self.reshape(flat), so_slots).astype(bf16))
-    dso_mine = [
-        exchange(dso_send[turn], both_axes).reshape(devices * half, 2 * HEAD)
-        for turn in range(turns)
-    ]
-    dso_mine[0], terms_b = lax.optimization_barrier((dso_mine[0], terms_b))
-    grad_up, grad_down, grad_deconv = total(terms_b)
-    backward = [
-        self_backward(parts[turn], dso_mine[turn], *forward[turn][1:], devices, half)
-        for turn in range(turns)
-    ]
+    dso_send = [dso_send[turn] for turn in range(turns)]
+    dso_mine, backward = [], []
+    for turn in range(turns):
+        if turn >= 2:
+            dso_send[turn], backward[turn - 2] = lax.optimization_barrier(
+                (dso_send[turn], backward[turn - 2])
+            )
+        arrived = exchange(dso_send[turn], both_axes).reshape(devices * half, 2 * HEAD)
+        if turn == 0:
+            arrived, terms_b = lax.optimization_barrier((arrived, terms_b))
+        dso_mine.append(arrived)
+        backward.append(
+            self_backward(parts[turn], dso_mine[turn], *forward[turn][1:], devices, half)
+        )
+    grad_up, grad_down, grad_deconv = total(terms_b, *size_b[1:])
     if fast:
         blocks = [
             exchange(x[0], both_axes).reshape(groups, slots, 2, 3 * half, 2 * HEAD)
@@ -941,19 +1247,58 @@
     )
     spots = -(-early.shape[0] // (16 * tp)) * 16
     early = jnp.pad(early, ((0, spots * tp - early.shape[0]), (0, 0))).reshape(tp, spots, width)
-    terms_a = [
-            by_device(dot("xne,nd->xed", grad_projected, self_in.reshape(flat))),
-            by_device(
-                dot("ne,nd->ed", so_tile, grad_self.reshape(flat)).reshape(
-                    slots, slot_width, width
-                )
-            ),
-            by_device(dot("time,imf->tef", mixed_tile, grad_attn)),
-            by_device(early),
-    ]
+    early = by_device(early)
+    size_a = [slot_width * k for k in (6, 8, 10)]
+    if fast:
+        shape = (devices, size_a[2] + early.shape[1], share)
+        terms_a = weight_terms(
+            None,
+            shape,
+            grad_projected,
+            (1, items * tile, 3 * slot_width),
+            lambda t, c: (c * tp + t, 0, 0),
+            self_in.reshape(flat),
+            tp,
+            3 * slot_width,
+            0,
+        )
+        terms_a = weight_terms(
+            terms_a,
+            shape,
+            so_tile,
+            (items * tile, slot_width),
+            lambda t, c: (0, c * tp + t),
+            grad_self.reshape(flat),
+            tp,
+            slot_width,
+            size_a[0],
+        )
+        terms_a = weight_terms(
+            terms_a,
+            shape,
+            mixed_tile,
+            (1, items, tile, slot_width),
+            lambda t, c: (t, 0, 0, c),
+            grad_attn.reshape(flat),
+            tp,
+            slot_width,
+            size_a[1],
+        )
+        terms_a = lax.dynamic_update_slice_in_dim(terms_a, early, size_a[2], 1)
+    else:
+        so_terms = dot("ne,nd->ed", so_tile, grad_self.reshape(flat))
+        terms_a = jnp.concatenate(
+            [
+                by_device(dot("xne,nd->xed", grad_projected, self_in.reshape(flat))),
+                by_device(so_terms.reshape(slots, slot_width, width)),
+                by_device(dot("time,imf->tef", mixed_tile, grad_attn)),
+                early,
+            ],
+            axis=1,
+        )
     do_mine, terms_a = lax.optimization_barrier((do_mine, terms_a))
     terms_a, grad_up = lax.optimization_barrier((terms_a, grad_up))
-    grad_three, grad_self_out, grad_out, grad_early = total(terms_a)
+    grad_three, grad_self_out, grad_out, grad_early = total(terms_a, *size_a)
     dq_cross, dk_t, dv_t = cross_backward(queries, do_mine, mixed_wide, cross_logs, keys, values_t)
     dq_cross, middle_all = lax.optimization_barrier((dq_cross, middle_all))
     dq_all = gather(dq_cross, "tp")
@@ -975,27 +1320,33 @@
     def by_seq(x):
         return x.reshape((seq, x.shape[0] // seq) + x.shape[1:]).astype(bf16)
 
+    grad_image = key_value_grads(dk_t, dv_t, image).T
     last = jnp.concatenate(
         [
             by_seq(dot("iqd,iqe->de", first_in, dq_cross)),
-            by_seq(dot("pid,iep->de", context, dk_t)),
-            by_seq(dot("pid,iep->de", context, dv_t)),
+            by_seq(grad_image[:, :local]),
+            by_seq(grad_image[:, local:]),
         ],
         axis=1,
     )
     last, dq_all = lax.optimization_barrier((last, dq_all))
     last = jnp.sum(exchange(last, "seq").astype(f32), axis=0)
-    grad_first = dot("tiqe,ted->iqd", dq_all, by_tp(query_slots))
-    grad_shift_a = jnp.sum(grad_first, axis=1)
-    grad_scale_a = jnp.sum(grad_first * first_hat, axis=1)
-    grad_tokens = middle_all.astype(f32).transpose(1, 0, 2, 3).reshape(
-        items, tp * tile, width
-    ) + norm_back(first_hat, first_inv, grad_first * (1.0 + piece(1)))
-    grad_tokens = (
-        grad_tokens.reshape(items, tp, rows_here, cols_here, width)
-        .transpose(2, 0, 1, 3, 4)
-        .reshape(rows_here, items, plane_cols, width)
-    )
+    if fast:
+        grad_tokens, late = last_kernel(tokens, piece(1), middle_all, dq_all, query_slots)
+        late = late.transpose(1, 0, 2)
+    else:
+        grad_first = dot("tiqe,ted->iqd", dq_all, by_tp(query_slots))
+        grad_shift_a = jnp.sum(grad_first, axis=1)
+        grad_scale_a = jnp.sum(grad_first * first_hat, axis=1)
+        grad_tokens = middle_all.astype(f32).transpose(1, 0, 2, 3).reshape(
+            items, tp * tile, width
+        ) + norm_back(first_hat, first_inv, grad_first * (1.0 + piece(1)))
+        grad_tokens = (
+            grad_tokens.reshape(items, tp, rows_here, cols_here, width)
+            .transpose(2, 0, 1, 3, 4)
+            .reshape(rows_here, items, plane_cols, width)
+        )
+        late = jnp.stack([grad_shift_a, grad_scale_a], axis=0)
 
     depth = (last.shape[0] - share) // 2
     grad_query, grad_key, grad_value = (
@@ -1003,7 +1354,7 @@
         last[share : share + depth],
         last[share + depth :],
     )
-    late = jnp.sum(gather(jnp.stack([grad_shift_a, grad_scale_a], axis=0), "seq"), axis=0)
+    late = jnp.sum(gather(late, "seq"), axis=0)
     grad_mods = jnp.concatenate([late, early], axis=0).transpose(1, 0, 2)
     grad_table = jnp.dot(picker.T, grad_mods.reshape(items, 9 * width), precision=highest)
     return (

time: 1230 us -> 1230 us (level)
  matrix products: 236 us -> 31.6 us
  Pallas kernels: 313 us -> 483 us
  waiting for transfers between devices: 149 us -> 303 us
  other arithmetic: 125 us -> 47 us
  local copies, waits for them, and re-layouts: 231 us -> 204 us
  starting transfers between devices: 114 us -> 93.5 us
    dot_general x21 -> x6, matrix products: 234 us -> 28.9 us  [dot(): return jnp.einsum(spec, a, b, preferred_element_type=f32)]
    pallas_call x0 -> x10, Pallas kernels: none -> 170 us  [the longest x1 39.1 us: feed_forward(): pl.pallas_call(kernel, grid=(slots,), in_specs=[rows_spec, rows_spec, pl....]
    reduce_scatter x2, waiting for transfers between devices: 71.4 us -> 143 us  [total(): lax.psum_scatter(terms, ('tp', 'seq'), scatter_dimension=0, tiled=True)[0]]
    all_to_all x17 -> x16, waiting for transfers between devices: 72.3 us -> 134 us  [exchange(): return lax.all_to_all(x, axis, 0, 0, tiled=True)]
    convert_element_type x5 -> x3, other arithmetic: 35.8 us -> 3.75 us  [the longest x2 2.17 us: total(): return jnp.split(summed.astype(f32), cuts, axis=0)]
    concatenate x3 -> x1, other arithmetic: 32.2 us -> 1.17 us  [body(): jnp.concatenate([by_seq(dot('iqd,iqe->de', first_in, dq_cross)), by_seq(g...]
    convert_element_type x6 -> x1, local copies, waits for them, and re-layouts: 22.8 us -> 0.02 us  [by_device(): return x.reshape(devices, -1, share).astype(bf16)]
    all_to_all x17 -> x16, starting transfers between devices: 96.3 us -> 75.2 us  [exchange(): return lax.all_to_all(x, axis, 0, 0, tiled=True)]
  transfers between devices with their start and end apart: 31 -> 30, of which waited for: 13 -> 14; matrix products, arithmetic and copies ran while one was open for 35% -> 14% of each run, Pallas kernels for 25% -> 36%
where the time goes in v3:
time: 1230 us; the launch traced here: 1210 us
  Pallas kernels  483 us (39%)
  waiting for transfers between devices  303 us (25%)
  local copies, waits for them, and re-layouts  204 us (17%)
  starting transfers between devices  93.5 us (8%)
  other arithmetic  47 us (4%)
  blocking collectives  35.5 us (3%)
  matrix products  31.6 us (3%)
  between operations  15.9 us (1%)
    reduce_scatter x2, waiting for transfers between devices, total(): lax.psum_scatter(terms, ('tp', 'seq'), scatter_dimension=0, tiled=True)[0]  143 us
    all_to_all x16, waiting for transfers between devices, exchange(): return lax.all_to_all(x, axis, 0, 0, tiled=True)  134 us
    pallas_call x1, Pallas kernels, cross_backward(): pl.pallas_call(kernel, grid=(items, heads), in_specs=[rows_spec, tiles_sp...  97.8 us
    unnamed x238, local copies, waits for them, and re-layouts  87.7 us
    pallas_call x3, Pallas kernels, self_backward(): pl.pallas_call(kernel, grid=(blocks,), in_specs=part_specs(parts, half) +...  78.7 us
    all_to_all x16, starting transfers between devices, exchange(): return lax.all_to_all(x, axis, 0, 0, tiled=True)  75.2 us
    pallas_call x1, Pallas kernels, cross_forward(): pl.pallas_call(kernel, grid=(items, heads // 2), in_specs=[pl.BlockSpec((...  61.6 us
    pallas_call x3, Pallas kernels, self_forward(): pl.pallas_call(kernel, grid=(blocks,), in_specs=part_specs(parts, half),...  45.8 us
  transfers between devices with their start and end apart: 30, of which 14 were waited for; matrix products, arithmetic and copies ran while one was open for 14% of the time, Pallas kernels for 36%

profile of v3, /device:TPU:0, one launch (start us, length us, event | category | flops | bytes accessed | tf_op | source)
XLA Modules:
  0.0 1214.7 jit_solution(15378343272143867823)
XLA Ops:
  35.1 7.7 first_kernel.1
  42.9 34.8 %key_value_kernel.1 = (bf16[6,4096,256]{2,1,0:T(8,128)(2,1)S(1)}, bf16[6,256,4096]{2,1,0:T(8,128)(2,1)}) custom-call(bf16[6,4096,768]{2,1,0:T(8,128)(2,1)} %bitcast.359, bf16[768,256]{1,0:T(8,128)(2,1)S(1)} %copy-done.37, bf16[256,768]{1,0:T(8,128)(2,1)S(1)} %bitcast.298), custom_call_target="tpu_custom_call" | custom-call | flops 19327352832 | bytes 62914560 | tf_op jit(solution)/shard_map/key_value_kernel/pallas_call | solution.py:671
  82.3 61.6 %cross_forward.1 = (bf16[4,6,96,256]{3,2,1,0:T(8,128)(2,1)S(1)}, f32[4,6,96,256]{3,2,1,0:T(8,128)S(1)}, f32[6,4,8,384]{3,2,1,0:T(8,128)S(1)}) custom-call(bf16[6,384,256]{2,1,0:T(8,128)(2,1)S(1)} %get-tuple-element.66.q_ref, bf16[6,4096,256]{2,1,0:T(8,128)(2,1)} %copy-done.39, bf16[6,256,4096]{2,1,0:T(8,128)(2,1)} %get-tuple-element.68.vt_ref), custom_call_target="tpu_custom_call" | custom-call | flops 38654705664 | bytes 27525120 | tf_op jit(solution)/shard_map/cross_forward/pallas_call | solution.py:142
  220.6 19.8 %all-to-all-done.1.refs_0_ = bf16[32,144,128]{2,1,0:T(8,128)(2,1)} async-done(((bf16[32,144,128]{2,1,0:T(8,128)(2,1)}), bf16[32,144,128]{2,1,0:T(8,128)(2,1)}, u32[]{:S(2)}, u32[]{:S(2)}) %all-to-all-start.1) | async-done | bytes 1179680 | tf_op jit(solution)/shard_map/all_to_all | solution.py:889
  265.9 15.3 %self_forward.3 = (bf16[1536,128]{1,0:T(8,128)(2,1)S(1)}, f32[1536,128]{1,0:T(8,128)S(1)}, f32[4,8,768]{2,1,0:T(8,128)S(1)}) custom-call(bf16[32,144,128]{2,1,0:T(8,128)(2,1)} %all-to-all-done.1.refs_0_), custom_call_target="tpu_custom_call" | custom-call | flops 9663676416 | bytes 3145728 | tf_op jit(solution)/shard_map/self_forward/pallas_call | solution.py:313
  282.7 19.4 %all_to_all.90 = bf16[32,48,128]{2,1,0:T(8,128)(2,1)S(1)} all-to-all(bf16[32,48,128]{2,1,0:T(8,128)(2,1)S(1)} %bitcast.297), channel_id=1, replica_groups=mesh['seq'=8,'tp'=4] {'seq','tp'}, dimensions={0} | all-to-all | bytes 786432 | tf_op jit(solution)/shard_map/all_to_all | solution.py:889
  305.9 15.3 %self_forward.4 = (bf16[1536,128]{1,0:T(8,128)(2,1)S(1)}, f32[1536,128]{1,0:T(8,128)S(1)}, f32[4,8,768]{2,1,0:T(8,128)S(1)}) custom-call(bf16[32,144,128]{2,1,0:T(8,128)(2,1)} %all-to-all-done.3.refs_0_), custom_call_target="tpu_custom_call" | custom-call | flops 9663676416 | bytes 3145728 | tf_op jit(solution)/shard_map/self_forward/pallas_call | solution.py:313
  323.4 11.1 all-to-all-done.5.refs_0_
  338.0 15.3 %self_forward.5 = (bf16[1536,128]{1,0:T(8,128)(2,1)S(1)}, f32[1536,128]{1,0:T(8,128)S(1)}, f32[4,8,768]{2,1,0:T(8,128)S(1)}) custom-call(bf16[32,144,128]{2,1,0:T(8,128)(2,1)} %all-to-all-done.5.refs_0_), custom_call_target="tpu_custom_call" | custom-call | flops 9663676416 | bytes 3145728 | tf_op jit(solution)/shard_map/self_forward/pallas_call | solution.py:313
  366.9 8.4 all-to-all-done.6
  376.9 7.2 unpack_project.1
  390.5 39.1 %feed_forward.1 = (bf16[8,576,512]{2,1,0:T(8,128)(2,1)}, bf16[8,576,512]{2,1,0:T(8,128)(2,1)}, f32[576,1024]{1,0:T(8,128)}, f32[576,1024]{1,0:T(8,128)}) custom-call(bf16[576,1024]{1,0:T(8,128)(2,1)S(1)} %bitcast.283, bf16[576,1024]{1,0:T(8,128)(2,1)} %bitcast.281, bf16[8,1024,512]{2,1,0:T(8,128)(2,1)} %bitcast.361, bf16[8,512,1024]{2,1,0:T(8,128)(2,1)} %bitcast.362), custom_call_target="tpu_custom_call" | custom-call | flops 19327352832 | bytes 16777216 | tf_op jit(solution)/shard_map/feed_forward/pallas_call | solution.py:766
  461.4 9.2 weight_terms.5.refs_2_
  470.7 9.3 weight_terms.6
  489.3 26.3 %self_backward.3 = bf16[32,144,128]{2,1,0:T(8,128)(2,1)S(1)} custom-call(bf16[32,144,128]{2,1,0:T(8,128)(2,1)} %all-to-all-done.1.refs_0_, bf16[1536,128]{1,0:T(8,128)(2,1)S(1)} %bitcast.291, f32[1536,128]{1,0:T(8,128)S(1)} %copy-done.43, f32[4,8,768]{2,1,0:T(8,128)S(1)} %copy-done.51), custom_call_target="tpu_custom_call" | custom-call | flops 24159191040 | bytes 6291456 | tf_op jit(solution)/shard_map/self_backward/pallas_call | solution.py:399
  525.0 26.2 %self_backward.5 = bf16[32,144,128]{2,1,0:T(8,128)(2,1)S(1)} custom-call(bf16[32,144,128]{2,1,0:T(8,128)(2,1)} %all-to-all-done.3.refs_0_, bf16[1536,128]{1,0:T(8,128)(2,1)S(1)} %bitcast.293, f32[1536,128]{1,0:T(8,128)S(1)} %copy-done.45, f32[4,8,768]{2,1,0:T(8,128)S(1)} %copy-done.53), custom_call_target="tpu_custom_call" | custom-call | flops 24159191040 | bytes 6291456 | tf_op jit(solution)/shard_map/self_backward/pallas_call | solution.py:399
  559.7 26.2 %self_backward.4 = bf16[32,144,128]{2,1,0:T(8,128)(2,1)S(1)} custom-call(bf16[32,144,128]{2,1,0:T(8,128)(2,1)} %all-to-all-done.5.refs_0_, bf16[1536,128]{1,0:T(8,128)(2,1)S(1)} %bitcast.294, f32[1536,128]{1,0:T(8,128)S(1)} %copy-done.41, f32[4,8,768]{2,1,0:T(8,128)S(1)} %copy-done.49), custom_call_target="tpu_custom_call" | custom-call | flops 24159191040 | bytes 6291456 | tf_op jit(solution)/shard_map/self_backward/pallas_call | solution.py:399
  587.0 21.8 %all-to-all-done.12 = bf16[32,144,128]{2,1,0:T(8,128)(2,1)} async-done(((bf16[32,144,128]{2,1,0:T(8,128)(2,1)}), bf16[32,144,128]{2,1,0:T(8,128)(2,1)}, u32[]{:S(2)}, u32[]{:S(2)}) %all-to-all-start.12) | async-done | bytes 1179680 | tf_op jit(solution)/shard_map/all_to_all | solution.py:889
  619.8 38.3 %all-to-all-done.9 = bf16[32,144,128]{2,1,0:T(8,128)(2,1)} async-done(((bf16[32,144,128]{2,1,0:T(8,128)(2,1)}), bf16[32,144,128]{2,1,0:T(8,128)(2,1)}, u32[]{:S(2)}, u32[]{:S(2)}) %all-to-all-start.9) | async-done | bytes 1179680 | tf_op jit(solution)/shard_map/all_to_all | solution.py:889
  670.1 8.0 collective-permute-done.6
  678.1 10.6 collective-permute-done.7
  695.7 10.4 reshape.437
  720.9 10.8 unpack_back.1
  755.1 7.7 weight_terms.7.refs_2_
  767.9 6.9 weight_terms.9
  799.1 137.7 %reduce-scatter.5.cloned.1.call-done = bf16[1,1296,128]{2,1,0:T(8,128)(2,1)} async-done(((bf16[32,1296,128]{2,1,0:T(8,128)(2,1)}), bf16[1,1296,128]{2,1,0:T(8,128)(2,1)}) %reduce-scatter.5.cloned.1.call-update) | async-done | bytes 331792 | tf_op jit(solution)/shard_map/reduce_scatter | solution.py:1154
  943.3 97.8 %cross_backward.1 = (bf16[6,384,256]{2,1,0:T(8,128)(2,1)S(1)}, bf16[6,256,4096]{2,1,0:T(8,128)(2,1)}, bf16[6,256,4096]{2,1,0:T(8,128)(2,1)}) custom-call(bf16[6,384,256]{2,1,0:T(8,128)(2,1)S(1)} %copy-done.36, bf16[4,6,96,256]{3,2,1,0:T(8,128)(2,1)} %all-to-all-done.13.do_ref, f32[4,6,96,256]{3,2,1,0:T(8,128)S(1)} %copy-done.47, ...), custom_call_target="tpu_custom_call" | custom-call | flops 96636764160 | bytes 55050240 | tf_op jit(solution)/shard_map/cross_backward/pallas_call | solution.py:218
  1055.8 34.8 %key_value_grads.1 = f32[512,768]{1,0:T(8,128)S(1)} custom-call(bf16[6,256,4096]{2,1,0:T(8,128)(2,1)S(1)} %copy-done.38, bf16[6,256,4096]{2,1,0:T(8,128)(2,1)} %get-tuple-element.107.dv_ref, bf16[6,4096,768]{2,1,0:T(8,128)(2,1)} %bitcast.360), custom_call_target="tpu_custom_call" | custom-call | flops 19327352832 | bytes 62914560 | tf_op jit(solution)/shard_map/key_value_grads/pallas_call | solution.py:716
  1102.5 15.4 %last_kernel.1 = (f32[12,6,32,1024]{3,2,1,0:T(8,128)}, f32[6,2,1024]{2,1,0:T(2,128)S(1)}) custom-call(bf16[12,6,32,1024]{3,2,1,0:T(8,128)(2,1)} %x_ref.3, f32[6,1,1024]{2,1,0:T(1,128)S(1)} %copy-done.33, bf16[4,6,96,1024]{3,2,1,0:T(8,128)(2,1)} %all-to-all-done.14.middle_ref, bf16[4,6,384,256]{3,2,1,0:T(8,128)(2,1)} %all-to-all-done.15.dq_ref, ...), custom_call_target="tpu_custom_call" | custom-call | flops 4831838208 | bytes 23592960 | tf_op jit(solution)/shard_map/last_kernel/pallas_call | solution.py:860
  1118.1 16.2 %all_to_all.91 = f32[8,2,6,1024]{3,1,2,0:T(2,128)} all-to-all(f32[8,2,6,1024]{3,1,2,0:T(2,128)S(1)} %broadcast_in_dim.12), channel_id=1, replica_groups=mesh['seq'=8,'tp'=4] {'seq'}, dimensions={0} | all-to-all | bytes 786432 | tf_op jit(solution)/shard_map/all_to_all | solution.py:889
  1142.1 28.7 %all-to-all-done.16 = bf16[8,320,256]{2,1,0:T(8,128)(2,1)} async-done(((bf16[8,320,256]{2,1,0:T(8,128)(2,1)}), bf16[8,320,256]{2,1,0:T(8,128)(2,1)}, u32[]{:S(2)}, u32[]{:S(2)}) %all-to-all-start.16) | async-done | bytes 1310752 | tf_op jit(solution)/shard_map/all_to_all | solution.py:889
  1186.2 6.9 reshape.449
  (429 shorter events, 394.5 us)
Async XLA Ops:
  7.2 252.1 %copy-start = (bf16[1024,1280]{1,0:T(8,128)(2,1)S(1)}, bf16[1024,1280]{1,0:T(8,128)(2,1)}, u32[]{:S(2)}) copy-start(bf16[1024,1280]{1,0:T(8,128)(2,1)} %param.32) | copy-start | bytes 7864324
  7.2 168.8 %all-gather.9.cloned.1.call-start = ((), (), s32[]{:S(2)}) async-start(), calls=%async_computation.22 | async-start | bytes 14155776 | tf_op jit(solution)/shard_map/all_gather | solution.py:961
  22.6 366.6 %all-gather.11.cloned.1.call-start = ((), (), s32[]{:S(2)}) async-start(), calls=%async_computation.23 | async-start | bytes 9437184 | tf_op jit(solution)/shard_map/all_gather | solution.py:961
  25.0 364.2 %all-gather.13.cloned.1.call-start = ((), (), s32[]{:S(2)}) async-start(), calls=%async_computation.24 | async-start | bytes 9437184 | tf_op jit(solution)/shard_map/all_gather | solution.py:961
  147.1 40.8 %all-to-all-start = ((bf16[4,6,96,256]{3,2,1,0:T(8,128)(2,1)}), bf16[4,6,96,256]{3,2,1,0:T(8,128)(2,1)}, u32[]{:S(2)}, u32[]{:S(2)}) async-start(bf16[4,6,96,256]{3,2,1,0:T(8,128)(2,1)} %copy-done.26), calls=%async_computation | async-start | bytes 2359296 | tf_op jit(solution)/shard_map/all_to_all | solution.py:889
  152.3 7.4 collective-permute-start
  154.2 5.6 collective-permute-start.1
  159.9 9.0 collective-permute-start.2
  164.1 10.3 collective-permute-start.3
  205.9 34.5 %all-to-all-start.1 = ((bf16[32,144,128]{2,1,0:T(8,128)(2,1)}), bf16[32,144,128]{2,1,0:T(8,128)(2,1)}, u32[]{:S(2)}, u32[]{:S(2)}) async-start(bf16[32,144,128]{2,1,0:T(8,128)(2,1)} %bitcast.326), calls=%async_computation.1 | async-start | bytes 2359296 | tf_op jit(solution)/shard_map/all_to_all | solution.py:889
  240.4 42.3 %all-to-all-start.3 = ((bf16[32,144,128]{2,1,0:T(8,128)(2,1)}), bf16[32,144,128]{2,1,0:T(8,128)(2,1)}, u32[]{:S(2)}, u32[]{:S(2)}) async-start(bf16[32,144,128]{2,1,0:T(8,128)(2,1)} %bitcast.325), calls=%async_computation.3 | async-start | bytes 2359296 | tf_op jit(solution)/shard_map/all_to_all | solution.py:889
  302.1 32.5 %all-to-all-start.5 = ((bf16[32,144,128]{2,1,0:T(8,128)(2,1)}), bf16[32,144,128]{2,1,0:T(8,128)(2,1)}, u32[]{:S(2)}, u32[]{:S(2)}) async-start(bf16[32,144,128]{2,1,0:T(8,128)(2,1)} %bitcast.324), calls=%async_computation.5 | async-start | bytes 2359296 | tf_op jit(solution)/shard_map/all_to_all | solution.py:889
  334.5 21.1 %all-to-all-start.4 = ((bf16[32,48,128]{2,1,0:T(8,128)(2,1)}), bf16[32,48,128]{2,1,0:T(8,128)(2,1)S(1)}, u32[]{:S(2)}, u32[]{:S(2)}) async-start(bf16[32,48,128]{2,1,0:T(8,128)(2,1)} %bitcast.296), calls=%async_computation.4 | async-start | bytes 786432 | tf_op jit(solution)/shard_map/all_to_all | solution.py:889
  355.6 19.7 %all-to-all-start.6 = ((bf16[32,48,128]{2,1,0:T(8,128)(2,1)}), bf16[32,48,128]{2,1,0:T(8,128)(2,1)}, u32[]{:S(2)}, u32[]{:S(2)}) async-start(bf16[32,48,128]{2,1,0:T(8,128)(2,1)} %bitcast.295), calls=%async_computation.6 | async-start | bytes 786432 | tf_op jit(solution)/shard_map/all_to_all | solution.py:889
  450.1 31.9 %all-to-all-start.7 = ((bf16[32,48,128]{2,1,0:T(8,128)(2,1)}), bf16[32,48,128]{2,1,0:T(8,128)(2,1)S(1)}, u32[]{:S(2)}, u32[]{:S(2)}) async-start(bf16[32,48,128]{2,1,0:T(8,128)(2,1)} %bitcast.338), calls=%async_computation.7 | async-start | bytes 786432 | tf_op jit(solution)/shard_map/all_to_all | solution.py:889
  452.7 332.6 %reduce-scatter.3.cloned.1.call-start = ((), (), s32[]{:S(2)}) async-start(), calls=%async_computation.20 | async-start | bytes 20004864 | tf_op jit(solution)/shard_map/reduce_scatter | solution.py:1154
  482.0 34.6 %all-to-all-start.11 = ((bf16[32,48,128]{2,1,0:T(8,128)(2,1)}), bf16[32,48,128]{2,1,0:T(8,128)(2,1)S(1)}, u32[]{:S(2)}, u32[]{:S(2)}) async-start(bf16[32,48,128]{2,1,0:T(8,128)(2,1)} %bitcast.337), calls=%async_computation.11 | async-start | bytes 786432 | tf_op jit(solution)/shard_map/all_to_all | solution.py:889
  516.6 35.7 %all-to-all-start.8 = ((bf16[32,48,128]{2,1,0:T(8,128)(2,1)}), bf16[32,48,128]{2,1,0:T(8,128)(2,1)S(1)}, u32[]{:S(2)}, u32[]{:S(2)}) async-start(bf16[32,48,128]{2,1,0:T(8,128)(2,1)} %bitcast.336), calls=%async_computation.8 | async-start | bytes 786432 | tf_op jit(solution)/shard_map/all_to_all | solution.py:889
  552.3 56.5 %all-to-all-start.12 = ((bf16[32,144,128]{2,1,0:T(8,128)(2,1)}), bf16[32,144,128]{2,1,0:T(8,128)(2,1)}, u32[]{:S(2)}, u32[]{:S(2)}) async-start(bf16[32,144,128]{2,1,0:T(8,128)(2,1)} %copy-done.28), calls=%async_computation.12 | async-start | bytes 2359296 | tf_op jit(solution)/shard_map/all_to_all | solution.py:889
  608.7 49.4 %all-to-all-start.9 = ((bf16[32,144,128]{2,1,0:T(8,128)(2,1)}), bf16[32,144,128]{2,1,0:T(8,128)(2,1)}, u32[]{:S(2)}, u32[]{:S(2)}) async-start(bf16[32,144,128]{2,1,0:T(8,128)(2,1)} %copy-done.27), calls=%async_computation.9 | async-start | bytes 2359296 | tf_op jit(solution)/shard_map/all_to_all | solution.py:889
  616.4 45.7 %collective-permute-start.4 = (bf16[1,6,8,1024]{3,0,2,1:T(2,128)(2,1)}, bf16[1,6,8,1024]{3,0,2,1:T(2,128)(2,1)S(1)}, u32[]{:S(2)}, u32[]{:S(2)}) collective-permute-start(bf16[1,6,8,1024]{3,0,2,1:T(2,128)(2,1)} %get-tuple-element.281), channel_id=1, source_target_pairs={{0,4},{4,8},{8,12},{12,16},{16,20},{20,24},{24,28},{1,5},{5,9},{9,... | collective-permute-start | bytes 294920 | tf_op jit(solution)/shard_map/ppermute | solution.py:29
  618.3 43.7 %collective-permute-start.5 = (bf16[1,6,8,1024]{3,0,2,1:T(2,128)(2,1)}, bf16[1,6,8,1024]{3,0,2,1:T(2,128)(2,1)S(1)}, u32[]{:S(2)}, u32[]{:S(2)}) collective-permute-start(bf16[1,6,8,1024]{3,0,2,1:T(2,128)(2,1)} %get-tuple-element.282), channel_id=1, source_target_pairs={{4,0},{8,4},{12,8},{16,12},{20,16},{24,20},{28,24},{5,1},{9,5},{13... | collective-permute-start | bytes 294920 | tf_op jit(solution)/shard_map/ppermute | solution.py:30
  658.1 61.1 %all-to-all-start.10 = ((bf16[32,144,128]{2,1,0:T(8,128)(2,1)}), bf16[32,144,128]{2,1,0:T(8,128)(2,1)}, u32[]{:S(2)}, u32[]{:S(2)}) async-start(bf16[32,144,128]{2,1,0:T(8,128)(2,1)} %copy-done.25), calls=%async_computation.10 | async-start | bytes 2359296 | tf_op jit(solution)/shard_map/all_to_all | solution.py:889
  664.0 14.1 %collective-permute-start.6 = (bf16[14,6,1,1024]{3,0,2,1:T(8,128)(2,1)}, bf16[14,6,1,1024]{3,0,2,1:T(8,128)(2,1)}, u32[]{:S(2)}, u32[]{:S(2)}) collective-permute-start(bf16[14,6,1,1024]{3,0,2,1:T(8,128)(2,1)} %get-tuple-element.277), channel_id=1, source_target_pairs={{0,1},{1,2},{2,3},{4,5},{5,6},{6,7},{8,9},{9,10},{10,11},{12,13},{... | collective-permute-start | bytes 516104 | tf_op jit(solution)/shard_map/ppermute | solution.py:29
  668.3 20.4 %collective-permute-start.7 = (bf16[14,6,1,1024]{3,0,2,1:T(8,128)(2,1)}, bf16[14,6,1,1024]{3,0,2,1:T(8,128)(2,1)}, u32[]{:S(2)}, u32[]{:S(2)}) collective-permute-start(bf16[14,6,1,1024]{3,0,2,1:T(8,128)(2,1)} %get-tuple-element.278), channel_id=1, source_target_pairs={{1,0},{2,1},{3,2},{5,4},{6,5},{7,6},{9,8},{10,9},{11,10},{13,12},{... | collective-permute-start | bytes 516104 | tf_op jit(solution)/shard_map/ppermute | solution.py:30
  747.0 32.6 %all-to-all-start.13 = ((bf16[4,6,96,256]{3,2,1,0:T(8,128)(2,1)}), bf16[4,6,96,256]{3,2,1,0:T(8,128)(2,1)}, u32[]{:S(2)}, u32[]{:S(2)}) async-start(bf16[4,6,96,256]{3,2,1,0:T(8,128)(2,1)} %fusion.24), calls=%async_computation.13 | async-start | bytes 2359296 | tf_op jit(solution)/shard_map/all_to_all | solution.py:889
  751.5 185.4 %reduce-scatter.5.cloned.1.call-start = ((), (), s32[]{:S(2)}) async-start(), calls=%async_computation.21 | async-start | bytes 10948608 | tf_op jit(solution)/shard_map/reduce_scatter | solution.py:1154
  792.4 148.0 %copy-start.55 = (f32[6,4,8,384]{3,2,1,0:T(8,128)S(1)}, f32[6,4,8,384]{3,2,1,0:T(8,128)}, u32[]{:S(2)}) copy-start(f32[6,4,8,384]{3,2,1,0:T(8,128)} %copy-done.54) | copy-start | bytes 884740
  792.4 249.8 %all-to-all-start.14 = ((bf16[4,6,96,1024]{3,2,1,0:T(8,128)(2,1)}), bf16[4,6,96,1024]{3,2,1,0:T(8,128)(2,1)}, u32[]{:S(2)}, u32[]{:S(2)}) async-start(bf16[4,6,96,1024]{3,2,1,0:T(8,128)(2,1)} %broadcast_in_dim.10), calls=%async_computation.14 | async-start | bytes 9437184 | tf_op jit(solution)/shard_map/all_to_all | solution.py:889
  797.5 382.1 %all-gather.15.cloned.1.call-start = ((), (), s32[]{:S(2)}) async-start(), calls=%async_computation.25 | async-start | bytes 5677056 | tf_op jit(solution)/shard_map/all_gather | solution.py:1311
  1046.1 56.4 %all-to-all-start.15 = ((bf16[4,6,384,256]{3,2,1,0:T(8,128)(2,1)}), bf16[4,6,384,256]{3,2,1,0:T(8,128)(2,1)}, u32[]{:S(2)}, u32[]{:S(2)}) async-start(bf16[4,6,384,256]{3,2,1,0:T(8,128)(2,1)} %broadcast_in_dim.11), calls=%async_computation.15 | async-start | bytes 9437184 | tf_op jit(solution)/shard_map/all_to_all | solution.py:889
  1134.3 36.5 %all-to-all-start.16 = ((bf16[8,320,256]{2,1,0:T(8,128)(2,1)}), bf16[8,320,256]{2,1,0:T(8,128)(2,1)}, u32[]{:S(2)}, u32[]{:S(2)}) async-start(bf16[8,320,256]{2,1,0:T(8,128)(2,1)} %pad_maximum_fusion.2), calls=%async_computation.16 | async-start | bytes 2621440 | tf_op jit(solution)/shard_map/all_to_all | solution.py:889
  (102 other events, 603.4 us)
Sparse Core Ops, SparseCore 0:
  22.7 74.8 all-gather.8
  99.5 54.3 all-gather.10
  155.8 57.9 all-gather.12
  482.1 303.1 reduce-scatter.2
  792.2 144.5 reduce-scatter.4
  940.5 65.2 all-gather.14

commit v4 on v3

--- a/solution.py
+++ b/solution.py
@@ -59,6 +59,7 @@
 
 NT = (((1,), (1,)), ((), ()))
 BLOCKS = 4
+KV_ROWS, Q_ROWS, SO_ROWS, OUT_ROWS, QUERY_ROWS = 0, 256, 384, 512, 640
 
 
 def dot_nt(a, b):
@@ -167,8 +168,8 @@
     )(q, k, vt)
 
 
-def cross_backward(q, do, o, logs, k, vt):
-    items, queries, width = q.shape
+def cross_backward(q, do, o, logs, k, vt, start, items):
+    _, queries, width = q.shape
     tp, _, tile, _ = do.shape
     keys = k.shape[1]
     heads = width // HEAD
@@ -212,8 +213,8 @@
         rest = jnp.where(head == 0, jnp.zeros_like(dq), dq_ref[0])
         dq_ref[0] = jnp.where(mine, dq, rest)
 
-    rows_spec = pl.BlockSpec((1, queries, width), lambda i, h: (i, 0, 0))
-    tiles_spec = pl.BlockSpec((tp, 1, tile, width), lambda i, h: (0, i, 0, 0))
+    rows_spec = pl.BlockSpec((1, queries, width), lambda i, h: (i + start, 0, 0))
+    tiles_spec = pl.BlockSpec((tp, 1, tile, width), lambda i, h: (0, i + start, 0, 0))
     grads_spec = pl.BlockSpec((1, HEAD, keys), lambda i, h: (i, h, 0))
     return pl.pallas_call(
         kernel,
@@ -222,11 +223,15 @@
             rows_spec,
             tiles_spec,
             tiles_spec,
-            pl.BlockSpec((1, 1, 8, queries), lambda i, h: (i, h, 0, 0)),
-            pl.BlockSpec((1, keys, width), lambda i, h: (i, 0, 0)),
-            pl.BlockSpec((1, width, keys), lambda i, h: (i, 0, 0)),
-        ],
-        out_specs=[rows_spec, grads_spec, grads_spec],
+            pl.BlockSpec((1, 1, 8, queries), lambda i, h: (i + start, h, 0, 0)),
+            pl.BlockSpec((1, keys, width), lambda i, h: (i + start, 0, 0)),
+            pl.BlockSpec((1, width, keys), lambda i, h: (i + start, 0, 0)),
+        ],
+        out_specs=[
+            pl.BlockSpec((1, queries, width), lambda i, h: (i, 0, 0)),
+            grads_spec,
+            grads_spec,
+        ],
         out_shape=[
             jax.ShapeDtypeStruct((items, queries, width), bf16),
             jax.ShapeDtypeStruct((items, width, keys), bf16),
@@ -430,9 +435,13 @@
     return [(i * tile, i % turns, i // turns) for i in range(items)]
 
 
-def project_pack(x, kv_w, q_w, items, turns, groups):
+def slot_rows(weights, first, size):
+    return pl.BlockSpec((1, size, weights.shape[2]), lambda i: (i, first // size, 0))
+
+
+def project_pack(x, weights, items, turns, groups):
     rows, width = x.shape
-    slots = kv_w.shape[0]
+    slots = weights.shape[0]
     tile = rows // items
     half = tile // 2
 
@@ -453,8 +462,8 @@
         grid=(slots,),
         in_specs=[
             pl.BlockSpec((rows, width), lambda i: (0, 0)),
-            pl.BlockSpec((1,) + kv_w.shape[1:], lambda i: (i, 0, 0)),
-            pl.BlockSpec((1,) + q_w.shape[1:], lambda i: (i, 0, 0)),
+            slot_rows(weights, KV_ROWS, 4 * HEAD),
+            slot_rows(weights, Q_ROWS, 2 * HEAD),
         ],
         out_specs=pl.BlockSpec(
             (turns, groups, 1, 2, 3 * half, 2 * HEAD), lambda i: (0, 0, i, 0, 0, 0)
@@ -467,7 +476,7 @@
             transcendentals=0,
         ),
         name="project_pack",
-    )(x, kv_w, q_w)
+    )(x, weights, weights)
 
 
 def unpack_project(blocks, weights, items, groups):
@@ -502,7 +511,7 @@
             pl.BlockSpec((groups, 1, 2, half, 2 * HEAD), lambda i: (0, i, 0, 0, 0))
             for _ in range(turns)
         ]
-        + [pl.BlockSpec((1,) + weights.shape[1:], lambda i: (i, 0, 0))],
+        + [slot_rows(weights, SO_ROWS, 2 * HEAD)],
         out_specs=[
             pl.BlockSpec((items * tile, 2 * HEAD), lambda i: (0, i)),
             pl.BlockSpec((items * tile, width), lambda i: (0, 0)),
@@ -539,7 +548,7 @@
         grid=(slots,),
         in_specs=[
             pl.BlockSpec((rows, width), lambda i: (0, 0)),
-            pl.BlockSpec((1,) + weights.shape[1:], lambda i: (i, 0, 0)),
+            slot_rows(weights, SO_ROWS, 2 * HEAD),
         ],
         out_specs=pl.BlockSpec(
             (turns, groups, 1, 2, half, 2 * HEAD), lambda i: (0, 0, i, 0, 0, 0)
@@ -555,9 +564,9 @@
     )(x, weights)
 
 
-def unpack_back(blocks, kv_w, q_w, items, groups):
+def unpack_back(blocks, weights, items, groups):
     turns = len(blocks)
-    slots, _, width = kv_w.shape
+    slots, _, width = weights.shape
     half = blocks[0].shape[3] // 3
     tile = 2 * half
     rows = items * tile
@@ -594,10 +603,7 @@
             pl.BlockSpec((groups, 1, 2, 3 * half, 2 * HEAD), lambda i: (0, i, 0, 0, 0))
             for _ in range(turns)
         ]
-        + [
-            pl.BlockSpec((1,) + kv_w.shape[1:], lambda i: (i, 0, 0)),
-            pl.BlockSpec((1,) + q_w.shape[1:], lambda i: (i, 0, 0)),
-        ],
+        + [slot_rows(weights, KV_ROWS, 4 * HEAD), slot_rows(weights, Q_ROWS, 2 * HEAD)],
         out_specs=[
             pl.BlockSpec((1, rows, 6 * HEAD), lambda i: (i, 0, 0)),
             pl.BlockSpec((rows, width), lambda i: (0, 0)),
@@ -613,7 +619,70 @@
             transcendentals=0,
         ),
         name="unpack_back",
-    )(*blocks, kv_w, q_w)
+    )(*blocks, weights, weights)
+
+
+def out_project(mixed, weights):
+    tp, items, tile, local = mixed.shape
+    slots, _, width = weights.shape
+    rows = items * tile
+
+    def kernel(x_ref, w_ref, out_ref):
+        slot = pl.program_id(0)
+        part = dot_nn(x_ref[0].reshape(rows, local // 2), w_ref[0])
+
+        @pl.when(slot == 0)
+        def _():
+            out_ref[...] = part
+
+        @pl.when(slot > 0)
+        def _():
+            out_ref[...] += part
+
+    return pl.pallas_call(
+        kernel,
+        grid=(slots,),
+        in_specs=[
+            pl.BlockSpec((1, items, tile, local // 2), lambda i: (i % tp, 0, 0, i // tp)),
+            slot_rows(weights, OUT_ROWS, 2 * HEAD),
+        ],
+        out_specs=pl.BlockSpec((rows, width), lambda i: (0, 0)),
+        out_shape=jax.ShapeDtypeStruct((rows, width), f32),
+        compiler_params=pltpu.CompilerParams(vmem_limit_bytes=40 << 20),
+        cost_estimate=pl.CostEstimate(
+            flops=2 * rows * width * tp * local,
+            bytes_accessed=4 * rows * width,
+            transcendentals=0,
+        ),
+        name="out_project",
+    )(mixed, weights)
+
+
+def out_back(x, weights, shape):
+    tp, items, tile, local = shape
+    rows, width = x.shape
+
+    def kernel(x_ref, w_ref, out_ref):
+        part = dot_nt(x_ref[...], w_ref[0])
+        out_ref[0] = part.astype(bf16).reshape(items, tile, local // 2)
+
+    return pl.pallas_call(
+        kernel,
+        grid=(2 * tp,),
+        in_specs=[
+            pl.BlockSpec((rows, width), lambda i: (0, 0)),
+            slot_rows(weights, OUT_ROWS, 2 * HEAD),
+        ],
+        out_specs=pl.BlockSpec((1, items, tile, local // 2), lambda i: (i % tp, 0, 0, i // tp)),
+        out_shape=jax.ShapeDtypeStruct(shape, bf16),
+        compiler_params=pltpu.CompilerParams(vmem_limit_bytes=40 << 20),
+        cost_estimate=pl.CostEstimate(
+            flops=2 * rows * width * tp * local,
+            bytes_accessed=4 * rows * width,
+            transcendentals=0,
+        ),
+        name="out_back",
+    )(x, weights)
 
 
 def first_kernel(tokens, shift, scale, w, tp):
@@ -694,7 +763,7 @@
     )(context, w_key, w_value_t)
 
 
-def key_value_grads(dk_t, dv_t, context):
+def key_value_grads(dk_t, dv_t, context, start):
     items, local, keys = dk_t.shape
     depth = context.shape[2]
     step = 1024 if keys % 1024 == 0 else keys
@@ -716,7 +785,11 @@
     return pl.pallas_call(
         kernel,
         grid=(items, keys // step),
-        in_specs=[grads_spec, grads_spec, pl.BlockSpec((1, step, depth), lambda i, j: (i, j, 0))],
+        in_specs=[
+            grads_spec,
+            grads_spec,
+            pl.BlockSpec((1, step, depth), lambda i, j: (i + start, j, 0)),
+        ],
         out_specs=pl.BlockSpec((2 * local, depth), lambda i, j: (0, 0)),
         out_shape=jax.ShapeDtypeStruct((2 * local, depth), f32),
         compiler_params=pltpu.CompilerParams(vmem_limit_bytes=40 << 20),
@@ -826,14 +899,16 @@
     )(lhs, rhs, *([] if buffer is None else [buffer]))
 
 
-def last_kernel(tokens, scale, middle, dq, query_slots):
-    rows, items, cols, width = tokens.shape
-    tp, _, queries, local = dq.shape
+def last_kernel(buffer, tokens, scale, middle, dq, small, start):
+    rows, _, cols, width = tokens.shape
+    tp, items, queries, local = dq.shape
+    slots = small.shape[0]
     cols_here = cols // tp
     tile = rows * cols_here
     slot_width = local // 2
 
-    def kernel(x_ref, scale_ref, middle_ref, dq_ref, w_ref, out_ref, sums_ref):
+    def kernel(x_ref, scale_ref, middle_ref, dq_ref, w_ref, *refs):
+        out_ref, sums_ref = refs[-2:]
         hat, inverse = norm_parts(x_ref[...].astype(f32).reshape(rows, cols, width))
         weights = w_ref[...].reshape(tp * local, width)
         shift_sum = jnp.zeros((1, width), f32)
@@ -861,20 +936,22 @@
         kernel,
         grid=(items,),
         in_specs=[
-            pl.BlockSpec((rows, 1, cols, width), lambda i: (0, i, 0, 0)),
-            pl.BlockSpec((1, 1, width), lambda i: (i, 0, 0)),
-            pl.BlockSpec((tp, 1, tile, width), lambda i: (0, i, 0, 0)),
+            pl.BlockSpec((rows, 1, cols, width), lambda i: (0, i + start, 0, 0)),
+            pl.BlockSpec((1, 1, width), lambda i: (i + start, 0, 0)),
+            pl.BlockSpec((tp, 1, tile, width), lambda i: (0, i + start, 0, 0)),
             pl.BlockSpec((tp, 1, queries, local), lambda i: (0, i, 0, 0)),
-            pl.BlockSpec(query_slots.shape, lambda i: (0, 0, 0)),
-        ],
+            pl.BlockSpec((slots, slot_width, width), lambda i: (0, QUERY_ROWS // slot_width, 0)),
+        ]
+        + ([] if buffer is None else [pl.BlockSpec(memory_space=pl.ANY)]),
         out_specs=[
-            pl.BlockSpec((rows, 1, cols, width), lambda i: (0, i, 0, 0)),
+            pl.BlockSpec((rows, 1, cols, width), lambda i: (0, i + start, 0, 0)),
             pl.BlockSpec((1, 2, width), lambda i: (i, 0, 0)),
         ],
         out_shape=[
             jax.ShapeDtypeStruct(tokens.shape, f32),
             jax.ShapeDtypeStruct((items, 2, width), f32),
         ],
+        input_output_aliases={} if buffer is None else {5: 0},
         compiler_params=pltpu.CompilerParams(vmem_limit_bytes=52 << 20),
         cost_estimate=pl.CostEstimate(
             flops=2 * items * queries * width * tp * local,
@@ -882,7 +959,7 @@
             transcendentals=0,
         ),
         name="last_kernel",
-    )(tokens, scale, middle, dq, query_slots)
+    )(tokens, scale, middle, dq, small, *([] if buffer is None else [buffer]))
 
 
 def exchange(x, axis):
@@ -890,7 +967,11 @@
 
 
 def gather(x, axis):
-    return exchange(jnp.broadcast_to(x[None], (lax.axis_size(axis),) + x.shape), axis)
+    names = axis if isinstance(axis, tuple) else (axis,)
+    count = 1
+    for name in names:
+        count *= lax.axis_size(name)
+    return exchange(jnp.broadcast_to(x[None], (count,) + x.shape), axis)
 
 
 def reduce_blocks(x, axis):
@@ -1047,8 +1128,10 @@
     keys, values_t = key_value_kernel(image, w_key, w_value.T)
     mixed, mixed_wide, cross_logs = cross_forward(queries, keys, values_t, tp)
     mixed_tile = exchange(mixed, "tp")
-    out_whole = by_tp(out_slots)
-    branch_a = dot("time,tef->imf", mixed_tile, out_whole)
+    if fast:
+        branch_a = out_project(mixed_tile, small).reshape(items, tile, width)
+    else:
+        branch_a = dot("time,tef->imf", mixed_tile, by_tp(out_slots))
     residual = to_tile(lax.dynamic_slice_in_dim(tokens, me_tp * cols_here, cols_here, 2)).astype(f32)
     middle = residual + piece(2) * branch_a
 
@@ -1081,7 +1164,7 @@
         return x.reshape(slots, items * tile, slot_width)
 
     if fast:
-        sends = project_pack(self_in.reshape(flat), kv_slots, q_slots, items, turns, groups)
+        sends = project_pack(self_in.reshape(flat), small, items, turns, groups)
         sends = sends.reshape(turns, devices, 3 * half, 2 * HEAD)
         sends = [sends[turn] for turn in range(turns)]
     else:
@@ -1114,7 +1197,7 @@
     so_back = [exchange(so.reshape(devices, half, 2 * HEAD), both_axes) for so, _, _ in forward]
     if fast:
         blocks = [x.reshape(groups, slots, 2, half, 2 * HEAD) for x in so_back]
-        so_tile, branch_s = unpack_project(blocks, so_slots, items, groups)
+        so_tile, branch_s = unpack_project(blocks, small, items, groups)
     else:
         so_tile = unpack_rows(jnp.stack(so_back)).transpose(1, 0, 2)
         branch_s = dot("nxe,xed->nd", so_tile, so_slots)
@@ -1154,8 +1237,13 @@
         summed = lax.psum_scatter(terms, ("tp", "seq"), scatter_dimension=0, tiled=True)[0]
         return jnp.split(summed.astype(f32), cuts, axis=0)
 
-    terms_deconv = dot("rict,ricd->td", tap_grads, out_tile)
-    terms_deconv = by_device(terms_deconv.reshape(tp, 16 * COUT // tp, width))
+    terms_deconv = dot("ricd,rict->dt", out_tile, tap_grads).astype(bf16)
+    piece_rows = width // devices
+    terms_deconv = (
+        terms_deconv.reshape(devices, piece_rows, -1, share)
+        .transpose(0, 2, 1, 3)
+        .reshape(devices, -1, share)
+    )
     size_b = (hidden_here // 2, hidden_here, 2 * hidden_here)
     if fast:
         shape = (devices, size_b[2] + terms_deconv.shape[1], share)
@@ -1186,7 +1274,7 @@
     grad_self = (piece(5) * grad_mid_two).astype(bf16)
     grad_gate_s = jnp.sum(grad_mid_two * branch_s, axis=1)
     if fast:
-        dso_send = back_pack(grad_self.reshape(flat), so_slots, items, turns, groups)
+        dso_send = back_pack(grad_self.reshape(flat), small, items, turns, groups)
         dso_send = dso_send.reshape(turns, devices, half, 2 * HEAD)
     else:
         dso_send = pack_rows(dot("nd,xed->xne", grad_self.reshape(flat), so_slots).astype(bf16))
@@ -1211,7 +1299,7 @@
             for x in backward
         ]
         blocks[-1], planes = lax.optimization_barrier((blocks[-1], planes))
-        grad_projected, grad_third = unpack_back(blocks, kv_slots, q_slots, items, groups)
+        grad_projected, grad_third = unpack_back(blocks, small, items, groups)
     else:
         dkv = [exchange(x[0].reshape(devices, tile, 2 * HEAD), both_axes) for x in backward]
         dq = [exchange(x[1].reshape(devices, half, 2 * HEAD), both_axes) for x in backward]
@@ -1228,7 +1316,11 @@
 
     grad_attn = (piece(2) * grad_middle).astype(bf16)
     grad_gate_a = jnp.sum(grad_middle * branch_a, axis=1)
-    do_mine = exchange(dot("imf,tef->time", grad_attn, out_whole).astype(bf16), "tp")
+    if fast:
+        do_send = out_back(grad_attn.reshape(flat), small, mixed.shape)
+    else:
+        do_send = dot("imf,tef->time", grad_attn, by_tp(out_slots)).astype(bf16)
+    do_mine = exchange(do_send, "tp")
     middle_all = gather(grad_middle.astype(bf16), "tp")
     early = jnp.stack(
         [
@@ -1299,28 +1391,29 @@
     do_mine, terms_a = lax.optimization_barrier((do_mine, terms_a))
     terms_a, grad_up = lax.optimization_barrier((terms_a, grad_up))
     grad_three, grad_self_out, grad_out, grad_early = total(terms_a, *size_a)
-    dq_cross, dk_t, dv_t = cross_backward(queries, do_mine, mixed_wide, cross_logs, keys, values_t)
-    dq_cross, middle_all = lax.optimization_barrier((dq_cross, middle_all))
-    dq_all = gather(dq_cross, "tp")
+    first_part = items // 2
+    cross = (queries, do_mine, mixed_wide, cross_logs, keys, values_t)
+    one = cross_backward(*cross, 0, first_part)
+    one, middle_all = lax.optimization_barrier((one, middle_all))
+    dq_one = gather(one[0], "tp")
+    do_late, _ = lax.optimization_barrier((do_mine, one[0]))
+    two = cross_backward(queries, do_late, *cross[2:], first_part, items - first_part)
+    one, two, dq_one = lax.optimization_barrier((one, two, dq_one))
+    dq_two = gather(two[0], "tp")
+    two, dq_two = lax.optimization_barrier((two, dq_two))
+    dq_cross = jnp.concatenate([one[0], two[0]], axis=0)
     grad_three = grad_three.reshape(2, 3 * slot_width, share)
     grad_pair = grad_three[:, : 2 * slot_width].reshape(2, slot_heads, 2, HEAD, share)
     grad_self_key = grad_pair[:, :, 0].reshape(local, share).T
     grad_self_value = grad_pair[:, :, 1].reshape(local, share).T
     grad_self_query = grad_three[:, 2 * slot_width :].reshape(local, share).T
 
-    shared = lax.all_gather(
-        jnp.concatenate([grad_deconv, grad_early], axis=0), ("tp", "seq"), axis=0, tiled=False
-    )
-    shared = shared.reshape(tp, seq, -1, share).transpose(0, 2, 1, 3).reshape(tp, -1, width)
-    grad_deconv = shared[:, : 16 * COUT // tp].reshape(16 * COUT, width).T
-    early = shared[:, 16 * COUT // tp :].reshape(-1, width)
-    grad_bias = early[7 * items, :COUT]
-    early = early[: 7 * items].reshape(7, items, width)
-
     def by_seq(x):
         return x.reshape((seq, x.shape[0] // seq) + x.shape[1:]).astype(bf16)
 
-    grad_image = key_value_grads(dk_t, dv_t, image).T
+    grad_image = (
+        key_value_grads(one[1], one[2], image, 0) + key_value_grads(two[1], two[2], image, first_part)
+    ).T
     last = jnp.concatenate(
         [
             by_seq(dot("iqd,iqe->de", first_in, dq_cross)),
@@ -1329,12 +1422,21 @@
         ],
         axis=1,
     )
-    last, dq_all = lax.optimization_barrier((last, dq_all))
+    grad_deconv, grad_image = lax.optimization_barrier((grad_deconv, grad_image))
+    grad_deconv = grad_deconv.reshape(-1, piece_rows, share).transpose(1, 0, 2)
+    grad_deconv = lax.all_gather(
+        grad_deconv.reshape(piece_rows, 16 * COUT), ("tp", "seq"), axis=0, tiled=True
+    )
+    last, dq_one, dq_two = lax.optimization_barrier((last, dq_one, dq_two))
     last = jnp.sum(exchange(last, "seq").astype(f32), axis=0)
     if fast:
-        grad_tokens, late = last_kernel(tokens, piece(1), middle_all, dq_all, query_slots)
-        late = late.transpose(1, 0, 2)
+        grad_tokens, late_one = last_kernel(None, tokens, piece(1), middle_all, dq_one, small, 0)
+        grad_tokens, late_two = last_kernel(
+            grad_tokens, tokens, piece(1), middle_all, dq_two, small, first_part
+        )
+        late = jnp.concatenate([late_one, late_two], axis=0).transpose(1, 0, 2)
     else:
+        dq_all = jnp.concatenate([dq_one, dq_two], axis=1)
         grad_first = dot("tiqe,ted->iqd", dq_all, by_tp(query_slots))
         grad_shift_a = jnp.sum(grad_first, axis=1)
         grad_scale_a = jnp.sum(grad_first * first_hat, axis=1)
@@ -1348,13 +1450,18 @@
         )
         late = jnp.stack([grad_shift_a, grad_scale_a], axis=0)
 
+    late, last = lax.optimization_barrier((late, last))
+    late = jnp.sum(gather(late, "seq"), axis=0)
+    early = gather(grad_early, ("tp", "seq")).reshape(tp, seq, spots, share)
+    early = early.transpose(0, 2, 1, 3).reshape(tp * spots, width)
+    grad_bias = early[7 * items, :COUT]
+    early = early[: 7 * items].reshape(7, items, width)
     depth = (last.shape[0] - share) // 2
     grad_query, grad_key, grad_value = (
         last[:share],
         last[share : share + depth],
         last[share + depth :],
     )
-    late = jnp.sum(gather(late, "seq"), axis=0)
     grad_mods = jnp.concatenate([late, early], axis=0).transpose(1, 0, 2)
     grad_table = jnp.dot(picker.T, grad_mods.reshape(items, 9 * width), precision=highest)
     return (

time: 1230 us -> 1150 us (0.935)
  waiting for transfers between devices: 303 us -> 174 us
  other arithmetic: 47 us -> 81.3 us
  Pallas kernels: 483 us -> 511 us
  blocking collectives: 35.5 us -> 19.4 us
  starting transfers between devices: 93.5 us -> 109 us
    reduce_scatter x2, waiting for transfers between devices: 143 us -> 0.82 us  [total(): lax.psum_scatter(terms, ('tp', 'seq'), scatter_dimension=0, tiled=True)[0]]
    all_to_all x16 -> x19, waiting for transfers between devices: 134 us -> 153 us  [exchange(): return lax.all_to_all(x, axis, 0, 0, tiled=True)]
    slice x4 -> x0, local copies, waits for them, and re-layouts: 16.9 us -> none  [the longest x2 10.3 us: body(): small[:, a:b]]
    all_to_all x2 -> x1, blocking collectives: 35.5 us -> 19.4 us  [exchange(): return lax.all_to_all(x, axis, 0, 0, tiled=True)]
    all_to_all x16 -> x19, starting transfers between devices: 75.2 us -> 91 us  [exchange(): return lax.all_to_all(x, axis, 0, 0, tiled=True)]
    pallas_call x0 -> x2, Pallas kernels: none -> 14.1 us  [the longest x1 7.66 us: out_project(): pl.pallas_call(kernel, grid=(slots,), in_specs=[pl.BlockSpec((1, items, t...]
    dot_general x6 -> x4, matrix products: 28.9 us -> 18.4 us  [dot(): return jnp.einsum(spec, a, b, preferred_element_type=f32)]
    unnamed x238 -> x243, local copies, waits for them, and re-layouts: 87.7 us -> 92.7 us
  transfers between devices with their start and end apart: 30 -> 33, of which waited for: 14 -> 14; matrix products, arithmetic and copies ran while one was open for 14% -> 17% of each run, Pallas kernels for 36% -> 41%
where the time goes in v4:
time: 1150 us; the launch traced here: 1130 us
  Pallas kernels  511 us (44%)
  local copies, waits for them, and re-layouts  199 us (17%)
  waiting for transfers between devices  174 us (15%)
  starting transfers between devices  109 us (9%)
  other arithmetic  81.3 us (7%)
  matrix products  21.1 us (2%)
  blocking collectives  19.4 us (2%)
  between operations  16.1 us (1%)
    all_to_all x19, waiting for transfers between devices, exchange(): return lax.all_to_all(x, axis, 0, 0, tiled=True)  153 us
    pallas_call x2, Pallas kernels, cross_backward(): pl.pallas_call(kernel, grid=(items, heads), in_specs=[rows_spec, tiles_sp...  101 us
    unnamed x243, local copies, waits for them, and re-layouts  92.7 us
    all_to_all x19, starting transfers between devices, exchange(): return lax.all_to_all(x, axis, 0, 0, tiled=True)  91 us
    pallas_call x3, Pallas kernels, self_backward(): pl.pallas_call(kernel, grid=(blocks,), in_specs=part_specs(parts, half) +...  78.7 us
    pallas_call x1, Pallas kernels, cross_forward(): pl.pallas_call(kernel, grid=(items, heads // 2), in_specs=[pl.BlockSpec((...  61.5 us
    pallas_call x3, Pallas kernels, self_forward(): pl.pallas_call(kernel, grid=(blocks,), in_specs=part_specs(parts, half),...  45.8 us
    pallas_call x1, Pallas kernels, feed_forward(): pl.pallas_call(kernel, grid=(slots,), in_specs=[rows_spec, rows_spec, pl....  39.4 us
  transfers between devices with their start and end apart: 33, of which 14 were waited for; matrix products, arithmetic and copies ran while one was open for 17% of the time, Pallas kernels for 41%

profile of v4, /device:TPU:0, one launch (start us, length us, event | category | flops | bytes accessed | tf_op | source)
XLA Modules:
  0.0 1130.2 jit_solution(1142484328628077516)
XLA Ops:
  42.0 34.8 %key_value_kernel.1 = (bf16[6,4096,256]{2,1,0:T(8,128)(2,1)S(1)}, bf16[6,256,4096]{2,1,0:T(8,128)(2,1)}) custom-call(bf16[6,4096,768]{2,1,0:T(8,128)(2,1)} %bitcast.310, bf16[768,256]{1,0:T(8,128)(2,1)S(1)} %copy-done.44, bf16[256,768]{1,0:T(8,128)(2,1)S(1)} %bitcast.299), custom_call_target="tpu_custom_call" | custom-call | flops 19327352832 | bytes 62914560 | tf_op jit(solution)/shard_map/key_value_kernel/pallas_call | solution.py:740
  81.3 61.5 %cross_forward.1 = (bf16[4,6,96,256]{3,2,1,0:T(8,128)(2,1)S(1)}, f32[4,6,96,256]{3,2,1,0:T(8,128)S(1)}, f32[6,4,8,384]{3,2,1,0:T(8,128)S(1)}) custom-call(bf16[6,384,256]{2,1,0:T(8,128)(2,1)S(1)} %get-tuple-element.89.q_ref, bf16[6,4096,256]{2,1,0:T(8,128)(2,1)} %copy-done.45, bf16[6,256,4096]{2,1,0:T(8,128)(2,1)} %get-tuple-element.91.vt_ref), custom_call_target="tpu_custom_call" | custom-call | flops 38654705664 | bytes 27525120 | tf_op jit(solution)/shard_map/cross_forward/pallas_call | solution.py:143
  202.3 9.3 project_pack.1
  213.5 9.6 all-to-all-start.1
  232.4 19.8 %all-to-all-done.1.refs_0_ = bf16[32,144,128]{2,1,0:T(8,128)(2,1)} async-done(((bf16[32,144,128]{2,1,0:T(8,128)(2,1)}), bf16[32,144,128]{2,1,0:T(8,128)(2,1)}, u32[]{:S(2)}, u32[]{:S(2)}) %all-to-all-start.1) | async-done | bytes 1179680 | tf_op jit(solution)/shard_map/all_to_all | solution.py:966
  277.6 15.3 %self_forward.3 = (bf16[1536,128]{1,0:T(8,128)(2,1)S(1)}, f32[1536,128]{1,0:T(8,128)S(1)}, f32[4,8,768]{2,1,0:T(8,128)S(1)}) custom-call(bf16[32,144,128]{2,1,0:T(8,128)(2,1)} %all-to-all-done.1.refs_0_), custom_call_target="tpu_custom_call" | custom-call | flops 9663676416 | bytes 3145728 | tf_op jit(solution)/shard_map/self_forward/pallas_call | solution.py:318
  294.4 19.4 %all_to_all.100 = bf16[32,48,128]{2,1,0:T(8,128)(2,1)S(1)} all-to-all(bf16[32,48,128]{2,1,0:T(8,128)(2,1)S(1)} %bitcast.298), channel_id=1, replica_groups=mesh['seq'=8,'tp'=4] {'seq','tp'}, dimensions={0} | all-to-all | bytes 786432 | tf_op jit(solution)/shard_map/all_to_all | solution.py:966
  317.6 15.3 %self_forward.4 = (bf16[1536,128]{1,0:T(8,128)(2,1)S(1)}, f32[1536,128]{1,0:T(8,128)S(1)}, f32[4,8,768]{2,1,0:T(8,128)S(1)}) custom-call(bf16[32,144,128]{2,1,0:T(8,128)(2,1)} %all-to-all-done.3.refs_0_), custom_call_target="tpu_custom_call" | custom-call | flops 9663676416 | bytes 3145728 | tf_op jit(solution)/shard_map/self_forward/pallas_call | solution.py:318
  335.1 11.1 all-to-all-done.5.refs_0_
  349.7 15.3 %self_forward.5 = (bf16[1536,128]{1,0:T(8,128)(2,1)S(1)}, f32[1536,128]{1,0:T(8,128)S(1)}, f32[4,8,768]{2,1,0:T(8,128)S(1)}) custom-call(bf16[32,144,128]{2,1,0:T(8,128)(2,1)} %all-to-all-done.5.refs_0_), custom_call_target="tpu_custom_call" | custom-call | flops 9663676416 | bytes 3145728 | tf_op jit(solution)/shard_map/self_forward/pallas_call | solution.py:318
  374.2 12.2 %all-to-all-done.6 = bf16[32,48,128]{2,1,0:T(8,128)(2,1)} async-done(((bf16[32,48,128]{2,1,0:T(8,128)(2,1)}), bf16[32,48,128]{2,1,0:T(8,128)(2,1)}, u32[]{:S(2)}, u32[]{:S(2)}) %all-to-all-start.6) | async-done | bytes 393248 | tf_op jit(solution)/shard_map/all_to_all | solution.py:966
  386.4 8.0 unpack_project.1
  411.9 39.4 %feed_forward.1 = (bf16[8,576,512]{2,1,0:T(8,128)(2,1)}, bf16[8,576,512]{2,1,0:T(8,128)(2,1)}, f32[576,1024]{1,0:T(8,128)}, f32[576,1024]{1,0:T(8,128)}) custom-call(bf16[576,1024]{1,0:T(8,128)(2,1)S(1)} %copy-done.20, bf16[576,1024]{1,0:T(8,128)(2,1)} %bitcast.289, bf16[8,1024,512]{2,1,0:T(8,128)(2,1)} %bitcast.360, bf16[8,512,1024]{2,1,0:T(8,128)(2,1)} %bitcast.361), custom_call_target="tpu_custom_call" | custom-call | flops 19327352832 | bytes 16777216 | tf_op jit(solution)/shard_map/feed_forward/pallas_call | solution.py:839
  453.7 8.6 multiply_convert_fusion.1
  489.0 9.7 weight_terms.5.refs_2_
  510.4 9.3 weight_terms.6
  529.5 26.2 %self_backward.3 = bf16[32,144,128]{2,1,0:T(8,128)(2,1)S(1)} custom-call(bf16[32,144,128]{2,1,0:T(8,128)(2,1)} %all-to-all-done.1.refs_0_, bf16[1536,128]{1,0:T(8,128)(2,1)S(1)} %bitcast.293, f32[1536,128]{1,0:T(8,128)S(1)} %copy-done.49, f32[4,8,768]{2,1,0:T(8,128)S(1)} %copy-done.56), custom_call_target="tpu_custom_call" | custom-call | flops 24159191040 | bytes 6291456 | tf_op jit(solution)/shard_map/self_backward/pallas_call | solution.py:404
  564.9 26.2 %self_backward.5 = bf16[32,144,128]{2,1,0:T(8,128)(2,1)S(1)} custom-call(bf16[32,144,128]{2,1,0:T(8,128)(2,1)} %all-to-all-done.3.refs_0_, bf16[1536,128]{1,0:T(8,128)(2,1)S(1)} %bitcast.294, f32[1536,128]{1,0:T(8,128)S(1)} %copy-done.51, f32[4,8,768]{2,1,0:T(8,128)S(1)} %copy-done.58), custom_call_target="tpu_custom_call" | custom-call | flops 24159191040 | bytes 6291456 | tf_op jit(solution)/shard_map/self_backward/pallas_call | solution.py:404
  599.5 26.2 %self_backward.4 = bf16[32,144,128]{2,1,0:T(8,128)(2,1)S(1)} custom-call(bf16[32,144,128]{2,1,0:T(8,128)(2,1)} %all-to-all-done.5.refs_0_, bf16[1536,128]{1,0:T(8,128)(2,1)S(1)} %bitcast.295, f32[1536,128]{1,0:T(8,128)S(1)} %copy-done.47, f32[4,8,768]{2,1,0:T(8,128)S(1)} %get-tuple-element.113.refs_3_), custom_call_target="tpu_custom_call" | custom-call | flops 24159191040 | bytes 6291456 | tf_op jit(solution)/shard_map/self_backward/pallas_call | solution.py:404
  626.8 22.4 %all-to-all-done.12 = bf16[32,144,128]{2,1,0:T(8,128)(2,1)} async-done(((bf16[32,144,128]{2,1,0:T(8,128)(2,1)}), bf16[32,144,128]{2,1,0:T(8,128)(2,1)}, u32[]{:S(2)}, u32[]{:S(2)}) %all-to-all-start.12) | async-done | bytes 1179680 | tf_op jit(solution)/shard_map/all_to_all | solution.py:966
  658.5 40.3 %all-to-all-done.9 = bf16[32,144,128]{2,1,0:T(8,128)(2,1)} async-done(((bf16[32,144,128]{2,1,0:T(8,128)(2,1)}), bf16[32,144,128]{2,1,0:T(8,128)(2,1)}, u32[]{:S(2)}, u32[]{:S(2)}) %all-to-all-start.9) | async-done | bytes 1179680 | tf_op jit(solution)/shard_map/all_to_all | solution.py:966
  718.6 11.3 %collective-permute-done.7 = bf16[14,6,1,1024]{3,0,2,1:T(8,128)(2,1)} collective-permute-done((bf16[14,6,1,1024]{3,0,2,1:T(8,128)(2,1)}, bf16[14,6,1,1024]{3,0,2,1:T(8,128)(2,1)}, u32[]{:S(2)}, u32[]{:S(2)}) %collective-permute-start.7) | collective-permute-done | bytes 172064 | tf_op jit(solution)/shard_map/ppermute | solution.py:30
  736.8 10.8 reshape.539
  760.8 10.6 unpack_back.1
  840.3 50.8 %cross_backward.2 = (bf16[3,384,256]{2,1,0:T(8,128)(2,1)S(1)}, bf16[3,256,4096]{2,1,0:T(8,128)(2,1)}, bf16[3,256,4096]{2,1,0:T(8,128)(2,1)}) custom-call(bf16[6,384,256]{2,1,0:T(8,128)(2,1)S(1)} %copy-done.42, bf16[4,6,96,256]{3,2,1,0:T(8,128)(2,1)} %all-to-all-done.13.do_ref, f32[4,6,96,256]{3,2,1,0:T(8,128)S(1)} %copy-done.53, ...), custom_call_target="tpu_custom_call" | custom-call | flops 48318382080 | bytes 27525120 | tf_op jit(solution)/shard_map/cross_backward/pallas_call | solution.py:219
  902.9 50.5 %cross_backward.3 = (bf16[3,384,256]{2,1,0:T(8,128)(2,1)S(1)}, bf16[3,256,4096]{2,1,0:T(8,128)(2,1)}, bf16[3,256,4096]{2,1,0:T(8,128)(2,1)}) custom-call(bf16[6,384,256]{2,1,0:T(8,128)(2,1)S(1)} %copy-done.43, bf16[4,6,96,256]{3,2,1,0:T(8,128)(2,1)} %all-to-all-done.13.do_ref, f32[4,6,96,256]{3,2,1,0:T(8,128)S(1)} %copy-done.54, ...), custom_call_target="tpu_custom_call" | custom-call | flops 48318382080 | bytes 27525120 | tf_op jit(solution)/shard_map/cross_backward/pallas_call | solution.py:219
  967.5 17.1 %key_value_grads.2 = f32[512,768]{1,0:T(8,128)S(1)} custom-call(bf16[3,256,4096]{2,1,0:T(8,128)(2,1)S(1)} %copy-done.16, bf16[3,256,4096]{2,1,0:T(8,128)(2,1)S(1)} %copy-done.17, bf16[6,4096,768]{2,1,0:T(8,128)(2,1)} %bitcast.311), custom_call_target="tpu_custom_call" | custom-call | flops 9663676416 | bytes 31457280 | tf_op jit(solution)/shard_map/key_value_grads/pallas_call | solution.py:785
  998.0 17.2 %key_value_grads.3 = f32[512,768]{1,0:T(8,128)S(1)} custom-call(bf16[3,256,4096]{2,1,0:T(8,128)(2,1)S(1)} %copy-done.18, bf16[3,256,4096]{2,1,0:T(8,128)(2,1)S(1)} %copy-done.19, bf16[6,4096,768]{2,1,0:T(8,128)(2,1)} %bitcast.312), custom_call_target="tpu_custom_call" | custom-call | flops 9663676416 | bytes 31457280 | tf_op jit(solution)/shard_map/key_value_grads/pallas_call | solution.py:785
  1033.5 9.4 last_kernel.2
  1042.9 9.4 last_kernel.3
  1052.3 20.5 %all-to-all-done.17 = bf16[8,320,256]{2,1,0:T(8,128)(2,1)} async-done(((bf16[8,320,256]{2,1,0:T(8,128)(2,1)}), bf16[8,320,256]{2,1,0:T(8,128)(2,1)}, u32[]{:S(2)}, u32[]{:S(2)}) %all-to-all-start.17) | async-done | bytes 1310752 | tf_op jit(solution)/shard_map/all_to_all | solution.py:966
  1085.3 14.6 %all-to-all-done.19 = f32[8,2,6,1024]{3,1,2,0:T(2,128)} async-done(((f32[8,2,6,1024]{3,1,2,0:T(2,128)}), f32[8,2,6,1024]{3,1,2,0:T(2,128)}, u32[]{:S(2)}, u32[]{:S(2)}) %all-to-all-start.19) | async-done | bytes 393248 | tf_op jit(solution)/shard_map/all_to_all | solution.py:966
  (454 shorter events, 452.0 us)
Async XLA Ops:
  7.2 169.2 %all-gather.10.cloned.1.call-start = ((), (), s32[]{:S(2)}) async-start(), calls=%async_computation.25 | async-start | bytes 14155776 | tf_op jit(solution)/shard_map/all_gather | solution.py:1042
  22.6 388.1 %all-gather.12.cloned.1.call-start = ((), (), s32[]{:S(2)}) async-start(), calls=%async_computation.26 | async-start | bytes 9437184 | tf_op jit(solution)/shard_map/all_gather | solution.py:1042
  25.0 385.7 %all-gather.14.cloned.1.call-start = ((), (), s32[]{:S(2)}) async-start(), calls=%async_computation.27 | async-start | bytes 9437184 | tf_op jit(solution)/shard_map/all_gather | solution.py:1042
  146.0 30.4 %all-to-all-start = ((bf16[4,6,96,256]{3,2,1,0:T(8,128)(2,1)}), bf16[4,6,96,256]{3,2,1,0:T(8,128)(2,1)}, u32[]{:S(2)}, u32[]{:S(2)}) async-start(bf16[4,6,96,256]{3,2,1,0:T(8,128)(2,1)} %copy-done.32), calls=%async_computation | async-start | bytes 2359296 | tf_op jit(solution)/shard_map/all_to_all | solution.py:966
  151.7 11.4 %collective-permute-start = (bf16[1,6,16,80]{3,2,1,0:T(8,128)(2,1)S(1)}, bf16[1,6,16,80]{3,2,1,0:T(8,128)(2,1)S(1)}, u32[]{:S(2)}, u32[]{:S(2)}) collective-permute-start(bf16[1,6,16,80]{3,2,1,0:T(8,128)(2,1)S(1)} %slice.199), channel_id=1, source_target_pairs={{0,4},{4,8},{8,12},{12,16},{16,20},{20,24},{24,28},{1,5},{5,9},{9,... | collective-permute-start | bytes 46088 | tf_op jit(solution)/shard_map/ppermute | solution.py:29
  153.4 9.8 collective-permute-start.1
  163.3 11.0 collective-permute-start.2
  213.5 38.7 %all-to-all-start.1 = ((bf16[32,144,128]{2,1,0:T(8,128)(2,1)}), bf16[32,144,128]{2,1,0:T(8,128)(2,1)}, u32[]{:S(2)}, u32[]{:S(2)}) async-start(bf16[32,144,128]{2,1,0:T(8,128)(2,1)} %bitcast.328), calls=%async_computation.1 | async-start | bytes 2359296 | tf_op jit(solution)/shard_map/all_to_all | solution.py:966
  252.2 42.3 %all-to-all-start.3 = ((bf16[32,144,128]{2,1,0:T(8,128)(2,1)}), bf16[32,144,128]{2,1,0:T(8,128)(2,1)}, u32[]{:S(2)}, u32[]{:S(2)}) async-start(bf16[32,144,128]{2,1,0:T(8,128)(2,1)} %bitcast.327), calls=%async_computation.3 | async-start | bytes 2359296 | tf_op jit(solution)/shard_map/all_to_all | solution.py:966
  313.8 32.4 %all-to-all-start.5 = ((bf16[32,144,128]{2,1,0:T(8,128)(2,1)}), bf16[32,144,128]{2,1,0:T(8,128)(2,1)}, u32[]{:S(2)}, u32[]{:S(2)}) async-start(bf16[32,144,128]{2,1,0:T(8,128)(2,1)} %bitcast.326), calls=%async_computation.5 | async-start | bytes 2359296 | tf_op jit(solution)/shard_map/all_to_all | solution.py:966
  346.2 20.4 %all-to-all-start.4 = ((bf16[32,48,128]{2,1,0:T(8,128)(2,1)}), bf16[32,48,128]{2,1,0:T(8,128)(2,1)S(1)}, u32[]{:S(2)}, u32[]{:S(2)}) async-start(bf16[32,48,128]{2,1,0:T(8,128)(2,1)} %bitcast.297), calls=%async_computation.4 | async-start | bytes 786432 | tf_op jit(solution)/shard_map/all_to_all | solution.py:966
  366.7 19.7 %all-to-all-start.6 = ((bf16[32,48,128]{2,1,0:T(8,128)(2,1)}), bf16[32,48,128]{2,1,0:T(8,128)(2,1)}, u32[]{:S(2)}, u32[]{:S(2)}) async-start(bf16[32,48,128]{2,1,0:T(8,128)(2,1)} %bitcast.296), calls=%async_computation.6 | async-start | bytes 786432 | tf_op jit(solution)/shard_map/all_to_all | solution.py:966
  482.8 38.8 %all-to-all-start.7 = ((bf16[32,48,128]{2,1,0:T(8,128)(2,1)}), bf16[32,48,128]{2,1,0:T(8,128)(2,1)S(1)}, u32[]{:S(2)}, u32[]{:S(2)}) async-start(bf16[32,48,128]{2,1,0:T(8,128)(2,1)} %bitcast.55), calls=%async_computation.7 | async-start | bytes 786432 | tf_op jit(solution)/shard_map/all_to_all | solution.py:966
  485.4 339.3 %reduce-scatter.3.cloned.1.call-start = ((), (), s32[]{:S(2)}) async-start(), calls=%async_computation.22 | async-start | bytes 20004864 | tf_op jit(solution)/shard_map/reduce_scatter | solution.py:1237
  521.6 35.2 %all-to-all-start.11 = ((bf16[32,48,128]{2,1,0:T(8,128)(2,1)}), bf16[32,48,128]{2,1,0:T(8,128)(2,1)S(1)}, u32[]{:S(2)}, u32[]{:S(2)}) async-start(bf16[32,48,128]{2,1,0:T(8,128)(2,1)} %bitcast.336), calls=%async_computation.11 | async-start | bytes 786432 | tf_op jit(solution)/shard_map/all_to_all | solution.py:966
  556.8 35.3 %all-to-all-start.8 = ((bf16[32,48,128]{2,1,0:T(8,128)(2,1)}), bf16[32,48,128]{2,1,0:T(8,128)(2,1)S(1)}, u32[]{:S(2)}, u32[]{:S(2)}) async-start(bf16[32,48,128]{2,1,0:T(8,128)(2,1)} %bitcast.335), calls=%async_computation.8 | async-start | bytes 786432 | tf_op jit(solution)/shard_map/all_to_all | solution.py:966
  592.1 57.1 %all-to-all-start.12 = ((bf16[32,144,128]{2,1,0:T(8,128)(2,1)}), bf16[32,144,128]{2,1,0:T(8,128)(2,1)}, u32[]{:S(2)}, u32[]{:S(2)}) async-start(bf16[32,144,128]{2,1,0:T(8,128)(2,1)} %copy-done.34), calls=%async_computation.12 | async-start | bytes 2359296 | tf_op jit(solution)/shard_map/all_to_all | solution.py:966
  649.2 49.6 %all-to-all-start.9 = ((bf16[32,144,128]{2,1,0:T(8,128)(2,1)}), bf16[32,144,128]{2,1,0:T(8,128)(2,1)}, u32[]{:S(2)}, u32[]{:S(2)}) async-start(bf16[32,144,128]{2,1,0:T(8,128)(2,1)} %copy-done.33), calls=%async_computation.9 | async-start | bytes 2359296 | tf_op jit(solution)/shard_map/all_to_all | solution.py:966
  655.0 48.1 %collective-permute-start.4 = (bf16[1,6,8,1024]{3,0,2,1:T(2,128)(2,1)}, bf16[1,6,8,1024]{3,0,2,1:T(2,128)(2,1)S(1)}, u32[]{:S(2)}, u32[]{:S(2)}) collective-permute-start(bf16[1,6,8,1024]{3,0,2,1:T(2,128)(2,1)} %get-tuple-element.326), channel_id=1, source_target_pairs={{0,4},{4,8},{8,12},{12,16},{16,20},{20,24},{24,28},{1,5},{5,9},{9,... | collective-permute-start | bytes 294920 | tf_op jit(solution)/shard_map/ppermute | solution.py:29
  657.1 46.0 %collective-permute-start.5 = (bf16[1,6,8,1024]{3,0,2,1:T(2,128)(2,1)}, bf16[1,6,8,1024]{3,0,2,1:T(2,128)(2,1)S(1)}, u32[]{:S(2)}, u32[]{:S(2)}) collective-permute-start(bf16[1,6,8,1024]{3,0,2,1:T(2,128)(2,1)} %get-tuple-element.327), channel_id=1, source_target_pairs={{4,0},{8,4},{12,8},{16,12},{20,16},{24,20},{28,24},{5,1},{9,5},{13... | collective-permute-start | bytes 294920 | tf_op jit(solution)/shard_map/ppermute | solution.py:30
  698.7 62.1 %all-to-all-start.10 = ((bf16[32,144,128]{2,1,0:T(8,128)(2,1)}), bf16[32,144,128]{2,1,0:T(8,128)(2,1)}, u32[]{:S(2)}, u32[]{:S(2)}) async-start(bf16[32,144,128]{2,1,0:T(8,128)(2,1)} %copy-done.31), calls=%async_computation.10 | async-start | bytes 2359296 | tf_op jit(solution)/shard_map/all_to_all | solution.py:966
  705.1 13.5 %collective-permute-start.6 = (bf16[14,6,1,1024]{3,0,2,1:T(8,128)(2,1)}, bf16[14,6,1,1024]{3,0,2,1:T(8,128)(2,1)}, u32[]{:S(2)}, u32[]{:S(2)}) collective-permute-start(bf16[14,6,1,1024]{3,0,2,1:T(8,128)(2,1)} %get-tuple-element.322), channel_id=1, source_target_pairs={{0,1},{1,2},{2,3},{4,5},{5,6},{6,7},{8,9},{9,10},{10,11},{12,13},{... | collective-permute-start | bytes 516104 | tf_op jit(solution)/shard_map/ppermute | solution.py:29
  709.4 20.6 %collective-permute-start.7 = (bf16[14,6,1,1024]{3,0,2,1:T(8,128)(2,1)}, bf16[14,6,1,1024]{3,0,2,1:T(8,128)(2,1)}, u32[]{:S(2)}, u32[]{:S(2)}) collective-permute-start(bf16[14,6,1,1024]{3,0,2,1:T(8,128)(2,1)} %get-tuple-element.323), channel_id=1, source_target_pairs={{1,0},{2,1},{3,2},{5,4},{6,5},{7,6},{9,8},{10,9},{11,10},{13,12},{... | collective-permute-start | bytes 516104 | tf_op jit(solution)/shard_map/ppermute | solution.py:30
  792.0 31.8 %all-to-all-start.13 = ((bf16[4,6,96,256]{3,2,1,0:T(8,128)(2,1)}), bf16[4,6,96,256]{3,2,1,0:T(8,128)(2,1)}, u32[]{:S(2)}, u32[]{:S(2)}) async-start(bf16[4,6,96,256]{3,2,1,0:T(8,128)(2,1)} %copy-done.23), calls=%async_computation.13 | async-start | bytes 2359296 | tf_op jit(solution)/shard_map/all_to_all | solution.py:966
  796.4 287.0 %reduce-scatter.5.cloned.1.call-start = ((), (), s32[]{:S(2)}) async-start(), calls=%async_computation.23 | async-start | bytes 10948608 | tf_op jit(solution)/shard_map/reduce_scatter | solution.py:1237
  832.0 61.8 %all-to-all-start.14 = ((bf16[4,6,96,1024]{3,2,1,0:T(8,128)(2,1)}), bf16[4,6,96,1024]{3,2,1,0:T(8,128)(2,1)}, u32[]{:S(2)}, u32[]{:S(2)}) async-start(bf16[4,6,96,1024]{3,2,1,0:T(8,128)(2,1)} %broadcast_in_dim.14), calls=%async_computation.14 | async-start | bytes 9437184 | tf_op jit(solution)/shard_map/all_to_all | solution.py:966
  895.4 58.8 %all-to-all-start.15 = ((bf16[4,3,384,256]{3,2,1,0:T(8,128)(2,1)}), bf16[4,3,384,256]{3,2,1,0:T(8,128)(2,1)}, u32[]{:S(2)}, u32[]{:S(2)}) async-start(bf16[4,3,384,256]{3,2,1,0:T(8,128)(2,1)} %broadcast_in_dim.15), calls=%async_computation.15 | async-start | bytes 4718592 | tf_op jit(solution)/shard_map/all_to_all | solution.py:966
  956.9 35.4 %all-to-all-start.16 = ((bf16[4,3,384,256]{3,2,1,0:T(8,128)(2,1)}), bf16[4,3,384,256]{3,2,1,0:T(8,128)(2,1)}, u32[]{:S(2)}, u32[]{:S(2)}) async-start(bf16[4,3,384,256]{3,2,1,0:T(8,128)(2,1)} %broadcast_in_dim.16), calls=%async_computation.16 | async-start | bytes 4718592 | tf_op jit(solution)/shard_map/all_to_all | solution.py:966
  961.4 149.3 %all-gather.8.cloned.1.call-start = ((), (), s32[]{:S(2)}) async-start(), calls=%async_computation.24 | async-start | bytes 5406720 | tf_op jit(solution)/shard_map/all_gather | solution.py:1427
  1029.2 43.6 %all-to-all-start.17 = ((bf16[8,320,256]{2,1,0:T(8,128)(2,1)}), bf16[8,320,256]{2,1,0:T(8,128)(2,1)}, u32[]{:S(2)}, u32[]{:S(2)}) async-start(bf16[8,320,256]{2,1,0:T(8,128)(2,1)} %pad_maximum_fusion.2), calls=%async_computation.17 | async-start | bytes 2621440 | tf_op jit(solution)/shard_map/all_to_all | solution.py:966
  1076.1 23.8 %all-to-all-start.19 = ((f32[8,2,6,1024]{3,1,2,0:T(2,128)}), f32[8,2,6,1024]{3,1,2,0:T(2,128)}, u32[]{:S(2)}, u32[]{:S(2)}) async-start(f32[8,2,6,1024]{3,1,2,0:T(2,128)} %broadcast_in_dim.18), calls=%async_computation.21 | async-start | bytes 786432 | tf_op jit(solution)/shard_map/all_to_all | solution.py:966
  1100.7 14.2 %all-to-all-start.18 = ((f32[32,16,128]{2,1,0:T(8,128)}), f32[32,16,128]{2,1,0:T(8,128)}, u32[]{:S(2)}, u32[]{:S(2)}) async-start(f32[32,16,128]{2,1,0:T(8,128)} %broadcast_in_dim.17), calls=%async_computation.20 | async-start | bytes 524288 | tf_op jit(solution)/shard_map/all_to_all | solution.py:966
  (107 other events, 1396.3 us)
Sparse Core Ops, SparseCore 0:
  22.7 74.8 all-gather.9
  99.5 54.3 all-gather.11
  155.8 57.1 all-gather.13
  521.8 302.8 reduce-scatter.2
  831.6 169.4 reduce-scatter.4
  1018.2 82.9 all-gather.7

commit v5 on v4

--- a/solution.py
+++ b/solution.py
@@ -864,9 +864,10 @@
 
 def weight_terms(buffer, shape, lhs, lhs_block, lhs_place, rhs, tp, size, first):
     count, width = rhs.shape
-    devices, _, share = shape
-    seq = devices // tp
+    share = shape[-1]
+    seq = width // share
     depth = lhs_block[-1]
+    by_core = len(shape) == 5
 
     def kernel(*refs):
         a_ref, b_ref, out_ref = refs[0], refs[1], refs[-1]
@@ -876,7 +877,11 @@
         a = a.reshape(count, depth).astype(bf16)
         terms = lax.dot_general(a, b_ref[...], (((0,), (0,)), ((), ())), preferred_element_type=f32)
         for s in range(seq):
-            out_ref[s] = terms[:, s * share : (s + 1) * share].astype(bf16)
+            block = terms[:, s * share : (s + 1) * share].astype(bf16)
+            if by_core:
+                out_ref[s % 2, 0, s // 2] = block
+            else:
+                out_ref[s] = block
 
     return pl.pallas_call(
         kernel,
@@ -886,7 +891,9 @@
             pl.BlockSpec(rhs.shape, lambda t, c: (0, 0)),
         ]
         + ([] if buffer is None else [pl.BlockSpec(memory_space=pl.ANY)]),
-        out_specs=pl.BlockSpec((seq, size, share), lambda t, c: (t, first // size + c, 0)),
+        out_specs=pl.BlockSpec((2, 1, seq // 2, size, share), lambda t, c: (0, t, 0, first // size + c, 0))
+        if by_core
+        else pl.BlockSpec((seq, size, share), lambda t, c: (t, first // size + c, 0)),
         out_shape=jax.ShapeDtypeStruct(shape, bf16),
         input_output_aliases={} if buffer is None else {2: 0},
         compiler_params=pltpu.CompilerParams(vmem_limit_bytes=40 << 20),
@@ -1194,7 +1201,10 @@
             forward.append(self_forward(parts[turn], devices, half))
     else:
         forward = [self_forward(parts[turn], devices, half) for turn in range(turns)]
-    so_back = [exchange(so.reshape(devices, half, 2 * HEAD), both_axes) for so, _, _ in forward]
+    outs = [x[0] for x in forward]
+    if fast:
+        outs[0], parts[-1][0] = lax.optimization_barrier((outs[0], parts[-1][0]))
+    so_back = [exchange(so.reshape(devices, half, 2 * HEAD), both_axes) for so in outs]
     if fast:
         blocks = [x.reshape(groups, slots, 2, half, 2 * HEAD) for x in so_back]
         so_tile, branch_s = unpack_project(blocks, small, items, groups)
@@ -1233,6 +1243,20 @@
         x = x.reshape(lead, tp, x.shape[1], seq, share).transpose(1, 3, 0, 2, 4)
         return x.reshape(devices, -1, share).astype(bf16)
 
+    def of_cores(x):
+        return x.reshape((tp, seq // 2, 2) + x.shape[1:]).transpose(2, 0, 1, 3, 4)
+
+    def total_near(terms, after, *cuts):
+        keep = lax.dynamic_index_in_dim(terms, core, 0, False)
+        give = lax.dynamic_index_in_dim(terms, 1 - core, 0, False)
+        got = lax.ppermute(give, "seq", [(i, i ^ 1) for i in range(seq)])
+        got, _ = lax.optimization_barrier((got, after))
+        x = (keep.astype(f32) + got.astype(f32)).astype(bf16)
+        x = lax.psum_scatter(x, "tp", scatter_dimension=0, tiled=True)[0]
+        lines = [list(range(c, seq, 2)) for c in range(2)]
+        x = lax.psum_scatter(x, "seq", scatter_dimension=0, axis_index_groups=lines, tiled=True)[0]
+        return jnp.split(x.astype(f32), cuts, axis=0)
+
     def total(terms, *cuts):
         summed = lax.psum_scatter(terms, ("tp", "seq"), scatter_dimension=0, tiled=True)[0]
         return jnp.split(summed.astype(f32), cuts, axis=0)
@@ -1246,7 +1270,7 @@
     )
     size_b = (hidden_here // 2, hidden_here, 2 * hidden_here)
     if fast:
-        shape = (devices, size_b[2] + terms_deconv.shape[1], share)
+        shape = (2, tp, seq // 2, size_b[2] + terms_deconv.shape[1], share)
         hidden_block = (1, items * tile, size_b[0])
 
         def slot_place(t, c):
@@ -1260,7 +1284,7 @@
             terms_b = weight_terms(
                 terms_b, shape, lhs, hidden_block, slot_place, rhs.reshape(flat), tp, size_b[0], first
             )
-        terms_b = lax.dynamic_update_slice_in_dim(terms_b, terms_deconv, size_b[2], 1)
+        terms_b = lax.dynamic_update_slice_in_dim(terms_b, of_cores(terms_deconv), size_b[2], 3)
     else:
         terms_b = jnp.concatenate(
             [
@@ -1270,6 +1294,7 @@
             ],
             axis=1,
         )
+        terms_b = of_cores(terms_b)
 
     grad_self = (piece(5) * grad_mid_two).astype(bf16)
     grad_gate_s = jnp.sum(grad_mid_two * branch_s, axis=1)
@@ -1292,7 +1317,9 @@
         backward.append(
             self_backward(parts[turn], dso_mine[turn], *forward[turn][1:], devices, half)
         )
-    grad_up, grad_down, grad_deconv = total(terms_b, *size_b[1:])
+    grad_up, grad_down, grad_deconv = total_near(
+        terms_b, (backward[0][0], dso_mine[min(1, turns - 1)]), *size_b[1:]
+    )
     if fast:
         blocks = [
             exchange(x[0], both_axes).reshape(groups, slots, 2, 3 * half, 2 * HEAD)
@@ -1427,7 +1454,9 @@
     grad_deconv = lax.all_gather(
         grad_deconv.reshape(piece_rows, 16 * COUT), ("tp", "seq"), axis=0, tiled=True
     )
-    last, dq_one, dq_two = lax.optimization_barrier((last, dq_one, dq_two))
+    early = gather(grad_early, ("tp", "seq")).reshape(tp, seq, spots, share)
+    early = early.transpose(0, 2, 1, 3).reshape(tp * spots, width)
+    last, dq_one, dq_two, early = lax.optimization_barrier((last, dq_one, dq_two, early))
     last = jnp.sum(exchange(last, "seq").astype(f32), axis=0)
     if fast:
         grad_tokens, late_one = last_kernel(None, tokens, piece(1), middle_all, dq_one, small, 0)
@@ -1452,8 +1481,6 @@
 
     late, last = lax.optimization_barrier((late, last))
     late = jnp.sum(gather(late, "seq"), axis=0)
-    early = gather(grad_early, ("tp", "seq")).reshape(tp, seq, spots, share)
-    early = early.transpose(0, 2, 1, 3).reshape(tp * spots, width)
     grad_bias = early[7 * items, :COUT]
     early = early[: 7 * items].reshape(7, items, width)
     depth = (last.shape[0] - share) // 2
@@ -1462,6 +1489,7 @@
         last[share : share + depth],
         last[share + depth :],
     )
+    late, grad_deconv = lax.optimization_barrier((late, grad_deconv))
     grad_mods = jnp.concatenate([late, early], axis=0).transpose(1, 0, 2)
     grad_table = jnp.dot(picker.T, grad_mods.reshape(items, 9 * width), precision=highest)
     return (

time: 1150 us -> 1130 us (0.983)
  waiting for transfers between devices: 174 us -> 128 us
  other arithmetic: 81.3 us -> 93 us
    all_to_all x19, waiting for transfers between devices: 153 us -> 109 us  [exchange(): return lax.all_to_all(x, axis, 0, 0, tiled=True)]
    convert_element_type x0 -> x2, other arithmetic: none -> 13.4 us  [the longest x1 12.3 us: total_near(): x = (keep.astype(f32) + got.astype(f32)).astype(bf16)]
    unnamed x243 -> x241, local copies, waits for them, and re-layouts: 92.7 us -> 92.2 us
  transfers between devices with their start and end apart: 33 -> 35, of which waited for: 14 -> 10; matrix products, arithmetic and copies ran while one was open for 17% -> 17% of each run, Pallas kernels for 41% -> 42%
where the time goes in v5:
time: 1130 us; the launch traced here: 1110 us
  Pallas kernels  511 us (45%)
  local copies, waits for them, and re-layouts  205 us (18%)
  waiting for transfers between devices  128 us (11%)
  starting transfers between devices  120 us (11%)
  other arithmetic  93 us (8%)
  matrix products  21 us (2%)
  blocking collectives  19.5 us (2%)
  between operations  16 us (1%)
    all_to_all x19, waiting for transfers between devices, exchange(): return lax.all_to_all(x, axis, 0, 0, tiled=True)  109 us
    pallas_call x2, Pallas kernels, cross_backward(): pl.pallas_call(kernel, grid=(items, heads), in_specs=[rows_spec, tiles_sp...  101 us
    all_to_all x19, starting transfers between devices, exchange(): return lax.all_to_all(x, axis, 0, 0, tiled=True)  97.2 us
    unnamed x241, local copies, waits for them, and re-layouts  92.2 us
    pallas_call x3, Pallas kernels, self_backward(): pl.pallas_call(kernel, grid=(blocks,), in_specs=part_specs(parts, half) +...  79.3 us
    pallas_call x1, Pallas kernels, cross_forward(): pl.pallas_call(kernel, grid=(items, heads // 2), in_specs=[pl.BlockSpec((...  61.5 us
    pallas_call x3, Pallas kernels, self_forward(): pl.pallas_call(kernel, grid=(blocks,), in_specs=part_specs(parts, half),...  46.5 us
    pallas_call x1, Pallas kernels, feed_forward(): pl.pallas_call(kernel, grid=(slots,), in_specs=[rows_spec, rows_spec, pl....  39.5 us
  transfers between devices with their start and end apart: 35, of which 10 were waited for; matrix products, arithmetic and copies ran while one was open for 17% of the time, Pallas kernels for 42%

profile of v5, /device:TPU:0, one launch (start us, length us, event | category | flops | bytes accessed | tf_op | source)
XLA Modules:
  0.0 1113.0 jit_solution(1417464238814280946)
XLA Ops:
  42.0 34.8 %key_value_kernel.1 = (bf16[6,4096,256]{2,1,0:T(8,128)(2,1)S(1)}, bf16[6,256,4096]{2,1,0:T(8,128)(2,1)}) custom-call(bf16[6,4096,768]{2,1,0:T(8,128)(2,1)} %bitcast.318, bf16[768,256]{1,0:T(8,128)(2,1)S(1)} %copy-done.44, bf16[256,768]{1,0:T(8,128)(2,1)S(1)} %bitcast.307), custom_call_target="tpu_custom_call" | custom-call | flops 19327352832 | bytes 62914560 | tf_op jit(solution)/shard_map/key_value_kernel/pallas_call | solution.py:740
  81.4 61.5 %cross_forward.1 = (bf16[4,6,96,256]{3,2,1,0:T(8,128)(2,1)S(1)}, f32[4,6,96,256]{3,2,1,0:T(8,128)S(1)}, f32[6,4,8,384]{3,2,1,0:T(8,128)S(1)}) custom-call(bf16[6,384,256]{2,1,0:T(8,128)(2,1)S(1)} %get-tuple-element.95.q_ref, bf16[6,4096,256]{2,1,0:T(8,128)(2,1)} %copy-done.45, bf16[6,256,4096]{2,1,0:T(8,128)(2,1)} %get-tuple-element.97.vt_ref), custom_call_target="tpu_custom_call" | custom-call | flops 38654705664 | bytes 27525120 | tf_op jit(solution)/shard_map/cross_forward/pallas_call | solution.py:143
  203.7 9.3 project_pack.1
  230.9 19.8 %all-to-all-done.1.refs_0_ = bf16[32,144,128]{2,1,0:T(8,128)(2,1)} async-done(((bf16[32,144,128]{2,1,0:T(8,128)(2,1)}), bf16[32,144,128]{2,1,0:T(8,128)(2,1)}, u32[]{:S(2)}, u32[]{:S(2)}) %all-to-all-start.1) | async-done | bytes 1179680 | tf_op jit(solution)/shard_map/all_to_all | solution.py:973
  276.1 15.3 %self_forward.3 = (bf16[1536,128]{1,0:T(8,128)(2,1)S(1)}, f32[1536,128]{1,0:T(8,128)S(1)}, f32[4,8,768]{2,1,0:T(8,128)S(1)}) custom-call(bf16[32,144,128]{2,1,0:T(8,128)(2,1)} %all-to-all-done.1.refs_0_), custom_call_target="tpu_custom_call" | custom-call | flops 9663676416 | bytes 3145728 | tf_op jit(solution)/shard_map/self_forward/pallas_call | solution.py:318
  300.1 15.9 %self_forward.4 = (bf16[1536,128]{1,0:T(8,128)(2,1)}, f32[1536,128]{1,0:T(8,128)S(1)}, f32[4,8,768]{2,1,0:T(8,128)S(1)}) custom-call(bf16[32,144,128]{2,1,0:T(8,128)(2,1)} %all-to-all-done.4.refs_0_), custom_call_target="tpu_custom_call" | custom-call | flops 9663676416 | bytes 3145728 | tf_op jit(solution)/shard_map/self_forward/pallas_call | solution.py:318
  316.9 12.3 %all-to-all-done.2.refs_0_ = bf16[32,144,128]{2,1,0:T(8,128)(2,1)} async-done(((bf16[32,144,128]{2,1,0:T(8,128)(2,1)}), bf16[32,144,128]{2,1,0:T(8,128)(2,1)}, u32[]{:S(2)}, u32[]{:S(2)}) %all-to-all-start.2) | async-done | bytes 1179680 | tf_op jit(solution)/shard_map/all_to_all | solution.py:973
  332.8 13.6 %all-to-all-done.5 = bf16[32,48,128]{2,1,0:T(8,128)(2,1)S(1)} async-done(((bf16[32,48,128]{2,1,0:T(8,128)(2,1)}), bf16[32,48,128]{2,1,0:T(8,128)(2,1)S(1)}, u32[]{:S(2)}, u32[]{:S(2)}) %all-to-all-start.5) | async-done | bytes 393248 | tf_op jit(solution)/shard_map/all_to_all | solution.py:973
  349.0 15.3 %self_forward.5 = (bf16[1536,128]{1,0:T(8,128)(2,1)S(1)}, f32[1536,128]{1,0:T(8,128)S(1)}, f32[4,8,768]{2,1,0:T(8,128)S(1)}) custom-call(bf16[32,144,128]{2,1,0:T(8,128)(2,1)} %all-to-all-done.2.refs_0_), custom_call_target="tpu_custom_call" | custom-call | flops 9663676416 | bytes 3145728 | tf_op jit(solution)/shard_map/self_forward/pallas_call | solution.py:318
  374.1 12.2 %all-to-all-done.6 = bf16[32,48,128]{2,1,0:T(8,128)(2,1)} async-done(((bf16[32,48,128]{2,1,0:T(8,128)(2,1)}), bf16[32,48,128]{2,1,0:T(8,128)(2,1)}, u32[]{:S(2)}, u32[]{:S(2)}) %all-to-all-start.6) | async-done | bytes 393248 | tf_op jit(solution)/shard_map/all_to_all | solution.py:973
  386.3 8.0 unpack_project.1
  411.9 39.5 %feed_forward.1 = (bf16[8,576,512]{2,1,0:T(8,128)(2,1)}, bf16[8,576,512]{2,1,0:T(8,128)(2,1)}, f32[576,1024]{1,0:T(8,128)}, f32[576,1024]{1,0:T(8,128)}) custom-call(bf16[576,1024]{1,0:T(8,128)(2,1)S(1)} %copy-done.20, bf16[576,1024]{1,0:T(8,128)(2,1)} %bitcast.298, bf16[8,1024,512]{2,1,0:T(8,128)(2,1)} %bitcast.370, bf16[8,512,1024]{2,1,0:T(8,128)(2,1)} %bitcast.371), custom_call_target="tpu_custom_call" | custom-call | flops 19327352832 | bytes 16777216 | tf_op jit(solution)/shard_map/feed_forward/pallas_call | solution.py:839
  461.6 8.6 multiply_convert_fusion.1
  484.5 9.2 weight_terms.5.refs_2_
  509.3 9.3 weight_terms.6
  520.6 8.1 dynamic-slice_bitcast_fusion
  536.9 26.7 %self_backward.3 = bf16[32,144,128]{2,1,0:T(8,128)(2,1)S(1)} custom-call(bf16[32,144,128]{2,1,0:T(8,128)(2,1)} %all-to-all-done.1.refs_0_, bf16[1536,128]{1,0:T(8,128)(2,1)S(1)} %bitcast.303, f32[1536,128]{1,0:T(8,128)S(1)} %copy-done.49, f32[4,8,768]{2,1,0:T(8,128)S(1)} %copy-done.56), custom_call_target="tpu_custom_call" | custom-call | flops 24159191040 | bytes 6291456 | tf_op jit(solution)/shard_map/self_backward/pallas_call | solution.py:404
  564.6 12.3 %fusion = bf16[4,4,2368,128]{3,2,1,0:T(8,128)(2,1)} fusion(bf16[4,4,2368,128]{3,2,1,0:T(8,128)(2,1)} %collective-permute-done.8, bf16[2,4,4,2368,128]{4,3,2,1,0:T(8,128)(2,1)} %bitcast_dynamic-update-slice_fusion, s32[]{:T(128)S(6)} %select_n.54), kind=kLoop, calls=%fused_computation.1 | loop fusion | flops 19398656 | bytes 29097988 | tf_op jit(solution)/shard_map/convert_element_type | solution.py:1254
  576.9 19.5 %all_to_all.100 = bf16[32,48,128]{2,1,0:T(8,128)(2,1)S(1)} all-to-all(bf16[32,48,128]{2,1,0:T(8,128)(2,1)} %bitcast.344), channel_id=1, replica_groups=mesh['seq'=8,'tp'=4] {'seq','tp'}, dimensions={0} | all-to-all | bytes 786432 | tf_op jit(solution)/shard_map/all_to_all | solution.py:973
  602.0 26.2 %self_backward.4 = bf16[32,144,128]{2,1,0:T(8,128)(2,1)S(1)} custom-call(bf16[32,144,128]{2,1,0:T(8,128)(2,1)} %all-to-all-done.2.refs_0_, bf16[1536,128]{1,0:T(8,128)(2,1)S(1)} %bitcast.306, f32[1536,128]{1,0:T(8,128)S(1)} %copy-done.51, f32[4,8,768]{2,1,0:T(8,128)S(1)} %copy-done.58), custom_call_target="tpu_custom_call" | custom-call | flops 24159191040 | bytes 6291456 | tf_op jit(solution)/shard_map/self_backward/pallas_call | solution.py:404
  643.9 26.4 %self_backward.5 = bf16[32,144,128]{2,1,0:T(8,128)(2,1)S(1)} custom-call(bf16[32,144,128]{2,1,0:T(8,128)(2,1)} %all-to-all-done.4.refs_0_, bf16[1536,128]{1,0:T(8,128)(2,1)S(1)} %bitcast.302, f32[1536,128]{1,0:T(8,128)S(1)} %copy-done.47, f32[4,8,768]{2,1,0:T(8,128)S(1)} %get-tuple-element.125.refs_3_), custom_call_target="tpu_custom_call" | custom-call | flops 24159191040 | bytes 6291456 | tf_op jit(solution)/shard_map/self_backward/pallas_call | solution.py:404
  685.7 18.2 %collective-permute-done.7 = bf16[14,6,1,1024]{3,0,2,1:T(8,128)(2,1)} collective-permute-done((bf16[14,6,1,1024]{3,0,2,1:T(8,128)(2,1)}, bf16[14,6,1,1024]{3,0,2,1:T(8,128)(2,1)}, u32[]{:S(2)}, u32[]{:S(2)}) %collective-permute-start.7) | collective-permute-done | bytes 172064 | tf_op jit(solution)/shard_map/ppermute | solution.py:30
  710.8 10.8 reshape.537
  734.7 10.6 unpack_back.1
  765.7 11.9 %all-to-all-start.13 = ((bf16[4,6,96,256]{3,2,1,0:T(8,128)(2,1)}), bf16[4,6,96,256]{3,2,1,0:T(8,128)(2,1)}, u32[]{:S(2)}, u32[]{:S(2)}) async-start(bf16[4,6,96,256]{3,2,1,0:T(8,128)(2,1)} %copy-done.23), calls=%async_computation.13 | async-start | bytes 2359296 | tf_op jit(solution)/shard_map/all_to_all | solution.py:973
  817.7 50.7 %cross_backward.2 = (bf16[3,384,256]{2,1,0:T(8,128)(2,1)S(1)}, bf16[3,256,4096]{2,1,0:T(8,128)(2,1)}, bf16[3,256,4096]{2,1,0:T(8,128)(2,1)}) custom-call(bf16[6,384,256]{2,1,0:T(8,128)(2,1)S(1)} %copy-done.42, bf16[4,6,96,256]{3,2,1,0:T(8,128)(2,1)} %all-to-all-done.13.do_ref, f32[4,6,96,256]{3,2,1,0:T(8,128)S(1)} %copy-done.53, ...), custom_call_target="tpu_custom_call" | custom-call | flops 48318382080 | bytes 27525120 | tf_op jit(solution)/shard_map/cross_backward/pallas_call | solution.py:219
  884.3 50.5 %cross_backward.3 = (bf16[3,384,256]{2,1,0:T(8,128)(2,1)S(1)}, bf16[3,256,4096]{2,1,0:T(8,128)(2,1)}, bf16[3,256,4096]{2,1,0:T(8,128)(2,1)}) custom-call(bf16[6,384,256]{2,1,0:T(8,128)(2,1)S(1)} %copy-done.43, bf16[4,6,96,256]{3,2,1,0:T(8,128)(2,1)} %all-to-all-done.13.do_ref, f32[4,6,96,256]{3,2,1,0:T(8,128)S(1)} %copy-done.54, ...), custom_call_target="tpu_custom_call" | custom-call | flops 48318382080 | bytes 27525120 | tf_op jit(solution)/shard_map/cross_backward/pallas_call | solution.py:219
  948.8 17.2 %key_value_grads.2 = f32[512,768]{1,0:T(8,128)S(1)} custom-call(bf16[3,256,4096]{2,1,0:T(8,128)(2,1)S(1)} %copy-done.16, bf16[3,256,4096]{2,1,0:T(8,128)(2,1)S(1)} %copy-done.17, bf16[6,4096,768]{2,1,0:T(8,128)(2,1)} %bitcast.319), custom_call_target="tpu_custom_call" | custom-call | flops 9663676416 | bytes 31457280 | tf_op jit(solution)/shard_map/key_value_grads/pallas_call | solution.py:785
  978.8 17.2 %key_value_grads.3 = f32[512,768]{1,0:T(8,128)S(1)} custom-call(bf16[3,256,4096]{2,1,0:T(8,128)(2,1)S(1)} %copy-done.18, bf16[3,256,4096]{2,1,0:T(8,128)(2,1)S(1)} %copy-done.19, bf16[6,4096,768]{2,1,0:T(8,128)(2,1)} %bitcast.320), custom_call_target="tpu_custom_call" | custom-call | flops 9663676416 | bytes 31457280 | tf_op jit(solution)/shard_map/key_value_grads/pallas_call | solution.py:785
  1036.5 9.4 last_kernel.2
  1045.9 9.4 last_kernel.3
  1055.3 24.6 %all-to-all-done.18 = bf16[8,320,256]{2,1,0:T(8,128)(2,1)} async-done(((bf16[8,320,256]{2,1,0:T(8,128)(2,1)}), bf16[8,320,256]{2,1,0:T(8,128)(2,1)}, u32[]{:S(2)}, u32[]{:S(2)}) %all-to-all-start.18) | async-done | bytes 1310752 | tf_op jit(solution)/shard_map/all_to_all | solution.py:973
  (459 shorter events, 462.9 us)
Async XLA Ops:
  7.2 170.5 %all-gather.10.cloned.1.call-start = ((), (), s32[]{:S(2)}) async-start(), calls=%async_computation.26 | async-start | bytes 14155776 | tf_op jit(solution)/shard_map/all_gather | solution.py:1049
  22.6 388.0 %all-gather.12.cloned.1.call-start = ((), (), s32[]{:S(2)}) async-start(), calls=%async_computation.27 | async-start | bytes 9437184 | tf_op jit(solution)/shard_map/all_gather | solution.py:1049
  25.0 385.6 %all-gather.14.cloned.1.call-start = ((), (), s32[]{:S(2)}) async-start(), calls=%async_computation.28 | async-start | bytes 9437184 | tf_op jit(solution)/shard_map/all_gather | solution.py:1049
  146.0 31.6 %all-to-all-start = ((bf16[4,6,96,256]{3,2,1,0:T(8,128)(2,1)}), bf16[4,6,96,256]{3,2,1,0:T(8,128)(2,1)}, u32[]{:S(2)}, u32[]{:S(2)}) async-start(bf16[4,6,96,256]{3,2,1,0:T(8,128)(2,1)} %copy-done.32), calls=%async_computation | async-start | bytes 2359296 | tf_op jit(solution)/shard_map/all_to_all | solution.py:973
  151.7 12.9 %collective-permute-start.1 = (bf16[1,6,16,80]{3,2,1,0:T(8,128)(2,1)S(1)}, bf16[1,6,16,80]{3,2,1,0:T(8,128)(2,1)S(1)}, u32[]{:S(2)}, u32[]{:S(2)}) collective-permute-start(bf16[1,6,16,80]{3,2,1,0:T(8,128)(2,1)S(1)} %slice.201), channel_id=1, source_target_pairs={{4,0},{8,4},{12,8},{16,12},{20,16},{24,20},{28,24},{5,1},{9,5},{13... | collective-permute-start | bytes 46088 | tf_op jit(solution)/shard_map/ppermute | solution.py:30
  215.0 35.8 %all-to-all-start.1 = ((bf16[32,144,128]{2,1,0:T(8,128)(2,1)}), bf16[32,144,128]{2,1,0:T(8,128)(2,1)}, u32[]{:S(2)}, u32[]{:S(2)}) async-start(bf16[32,144,128]{2,1,0:T(8,128)(2,1)} %bitcast.336), calls=%async_computation.1 | async-start | bytes 2359296 | tf_op jit(solution)/shard_map/all_to_all | solution.py:973
  250.7 42.9 %all-to-all-start.4 = ((bf16[32,144,128]{2,1,0:T(8,128)(2,1)}), bf16[32,144,128]{2,1,0:T(8,128)(2,1)}, u32[]{:S(2)}, u32[]{:S(2)}) async-start(bf16[32,144,128]{2,1,0:T(8,128)(2,1)} %bitcast.335), calls=%async_computation.4 | async-start | bytes 2359296 | tf_op jit(solution)/shard_map/all_to_all | solution.py:973
  293.7 35.6 %all-to-all-start.2 = ((bf16[32,144,128]{2,1,0:T(8,128)(2,1)}), bf16[32,144,128]{2,1,0:T(8,128)(2,1)}, u32[]{:S(2)}, u32[]{:S(2)}) async-start(bf16[32,144,128]{2,1,0:T(8,128)(2,1)} %bitcast.334), calls=%async_computation.2 | async-start | bytes 2359296 | tf_op jit(solution)/shard_map/all_to_all | solution.py:973
  329.2 17.2 %all-to-all-start.5 = ((bf16[32,48,128]{2,1,0:T(8,128)(2,1)}), bf16[32,48,128]{2,1,0:T(8,128)(2,1)S(1)}, u32[]{:S(2)}, u32[]{:S(2)}) async-start(bf16[32,48,128]{2,1,0:T(8,128)(2,1)} %bitcast.36), calls=%async_computation.5 | async-start | bytes 786432 | tf_op jit(solution)/shard_map/all_to_all | solution.py:973
  346.4 20.2 %all-to-all-start.3 = ((bf16[32,48,128]{2,1,0:T(8,128)(2,1)}), bf16[32,48,128]{2,1,0:T(8,128)(2,1)S(1)}, u32[]{:S(2)}, u32[]{:S(2)}) async-start(bf16[32,48,128]{2,1,0:T(8,128)(2,1)} %bitcast.304), calls=%async_computation.3 | async-start | bytes 786432 | tf_op jit(solution)/shard_map/all_to_all | solution.py:973
  366.6 19.7 %all-to-all-start.6 = ((bf16[32,48,128]{2,1,0:T(8,128)(2,1)}), bf16[32,48,128]{2,1,0:T(8,128)(2,1)}, u32[]{:S(2)}, u32[]{:S(2)}) async-start(bf16[32,48,128]{2,1,0:T(8,128)(2,1)} %bitcast.305), calls=%async_computation.6 | async-start | bytes 786432 | tf_op jit(solution)/shard_map/all_to_all | solution.py:973
  478.1 42.6 %all-to-all-start.7 = ((bf16[32,48,128]{2,1,0:T(8,128)(2,1)}), bf16[32,48,128]{2,1,0:T(8,128)(2,1)S(1)}, u32[]{:S(2)}, u32[]{:S(2)}) async-start(bf16[32,48,128]{2,1,0:T(8,128)(2,1)} %bitcast.55), calls=%async_computation.7 | async-start | bytes 786432 | tf_op jit(solution)/shard_map/all_to_all | solution.py:973
  528.7 35.9 %collective-permute-start.8 = (bf16[4,4,2368,128]{3,2,1,0:T(8,128)(2,1)}, bf16[4,4,2368,128]{3,2,1,0:T(8,128)(2,1)}, u32[]{:S(2)}, u32[]{:S(2)}) collective-permute-start(bf16[4,4,2368,128]{3,2,1,0:T(8,128)(2,1)} %dynamic-slice_bitcast_fusion), channel_id=1, source_target_pairs={{0,4},{4,0},{8,12},{12,8},{16,20},{20,16},{24,28},{28,24},{1,5},{5... | collective-permute-start | bytes 29097992 | tf_op jit(solution)/shard_map/ppermute | solution.py:1252
  529.0 35.7 %all-to-all-start.11 = ((bf16[32,48,128]{2,1,0:T(8,128)(2,1)}), bf16[32,48,128]{2,1,0:T(8,128)(2,1)S(1)}, u32[]{:S(2)}, u32[]{:S(2)}) async-start(bf16[32,48,128]{2,1,0:T(8,128)(2,1)} %bitcast.345), calls=%async_computation.11 | async-start | bytes 786432 | tf_op jit(solution)/shard_map/all_to_all | solution.py:973
  534.8 198.9 %reduce-scatter.10.cloned.1.call-start = ((), (), s32[]{:S(2)}) async-start(), calls=%async_computation.29 | async-start | bytes 12124160
  596.4 32.9 %all-to-all-start.10 = ((bf16[32,144,128]{2,1,0:T(8,128)(2,1)}), bf16[32,144,128]{2,1,0:T(8,128)(2,1)}, u32[]{:S(2)}, u32[]{:S(2)}) async-start(bf16[32,144,128]{2,1,0:T(8,128)(2,1)} %copy-done.33), calls=%async_computation.10 | async-start | bytes 2359296 | tf_op jit(solution)/shard_map/all_to_all | solution.py:973
  629.3 42.1 %all-to-all-start.9 = ((bf16[32,144,128]{2,1,0:T(8,128)(2,1)}), bf16[32,144,128]{2,1,0:T(8,128)(2,1)}, u32[]{:S(2)}, u32[]{:S(2)}) async-start(bf16[32,144,128]{2,1,0:T(8,128)(2,1)} %copy-done.34), calls=%async_computation.9 | async-start | bytes 2359296 | tf_op jit(solution)/shard_map/all_to_all | solution.py:973
  637.8 38.9 %collective-permute-start.5 = (bf16[1,6,8,1024]{3,0,2,1:T(2,128)(2,1)}, bf16[1,6,8,1024]{3,0,2,1:T(2,128)(2,1)S(1)}, u32[]{:S(2)}, u32[]{:S(2)}) collective-permute-start(bf16[1,6,8,1024]{3,0,2,1:T(2,128)(2,1)} %get-tuple-element.339), channel_id=1, source_target_pairs={{4,0},{8,4},{12,8},{16,12},{20,16},{24,20},{28,24},{5,1},{9,5},{13... | collective-permute-start | bytes 294920 | tf_op jit(solution)/shard_map/ppermute | solution.py:30
  639.1 37.7 %collective-permute-start.4 = (bf16[1,6,8,1024]{3,0,2,1:T(2,128)(2,1)}, bf16[1,6,8,1024]{3,0,2,1:T(2,128)(2,1)}, u32[]{:S(2)}, u32[]{:S(2)}) collective-permute-start(bf16[1,6,8,1024]{3,0,2,1:T(2,128)(2,1)} %get-tuple-element.338), channel_id=1, source_target_pairs={{0,4},{4,8},{8,12},{12,16},{16,20},{20,24},{24,28},{1,5},{5,9},{9,... | collective-permute-start | bytes 294920 | tf_op jit(solution)/shard_map/ppermute | solution.py:29
  671.4 63.3 %all-to-all-start.12 = ((bf16[32,144,128]{2,1,0:T(8,128)(2,1)}), bf16[32,144,128]{2,1,0:T(8,128)(2,1)}, u32[]{:S(2)}, u32[]{:S(2)}) async-start(bf16[32,144,128]{2,1,0:T(8,128)(2,1)} %copy-done.31), calls=%async_computation.12 | async-start | bytes 2359296 | tf_op jit(solution)/shard_map/all_to_all | solution.py:973
  676.7 125.2 %reduce-scatter.6.cloned.1.call-start = ((), (), s32[]{:S(2)}) async-start(), calls=%async_computation.23 | async-start | bytes 3031040 | tf_op jit(solution)/shard_map/reduce_scatter | solution.py:1257
  678.7 25.2 %collective-permute-start.7 = (bf16[14,6,1,1024]{3,0,2,1:T(8,128)(2,1)}, bf16[14,6,1,1024]{3,0,2,1:T(8,128)(2,1)}, u32[]{:S(2)}, u32[]{:S(2)}) collective-permute-start(bf16[14,6,1,1024]{3,0,2,1:T(8,128)(2,1)} %get-tuple-element.335), channel_id=1, source_target_pairs={{1,0},{2,1},{3,2},{5,4},{6,5},{7,6},{9,8},{10,9},{11,10},{13,12},{... | collective-permute-start | bytes 516104 | tf_op jit(solution)/shard_map/ppermute | solution.py:30
  680.0 23.9 %collective-permute-start.6 = (bf16[14,6,1,1024]{3,0,2,1:T(8,128)(2,1)S(1)}, bf16[14,6,1,1024]{3,0,2,1:T(8,128)(2,1)}, u32[]{:S(2)}, u32[]{:S(2)}) collective-permute-start(bf16[14,6,1,1024]{3,0,2,1:T(8,128)(2,1)S(1)} %get-tuple-element.334), channel_id=1, source_target_pairs={{0,1},{1,2},{2,3},{4,5},{5,6},{6,7},{8,9},{9,10},{10,11},{12,13},{... | collective-permute-start | bytes 516104 | tf_op jit(solution)/shard_map/ppermute | solution.py:29
  765.7 36.1 %all-to-all-start.13 = ((bf16[4,6,96,256]{3,2,1,0:T(8,128)(2,1)}), bf16[4,6,96,256]{3,2,1,0:T(8,128)(2,1)}, u32[]{:S(2)}, u32[]{:S(2)}) async-start(bf16[4,6,96,256]{3,2,1,0:T(8,128)(2,1)} %copy-done.23), calls=%async_computation.13 | async-start | bytes 2359296 | tf_op jit(solution)/shard_map/all_to_all | solution.py:973
  777.6 227.0 %reduce-scatter.8.cloned.1.call-start = ((), (), s32[]{:S(2)}) async-start(), calls=%async_computation.24 | async-start | bytes 10948608 | tf_op jit(solution)/shard_map/reduce_scatter | solution.py:1261
  809.2 65.9 %all-to-all-start.14 = ((bf16[4,6,96,1024]{3,2,1,0:T(8,128)(2,1)}), bf16[4,6,96,1024]{3,2,1,0:T(8,128)(2,1)}, u32[]{:S(2)}, u32[]{:S(2)}) async-start(bf16[4,6,96,1024]{3,2,1,0:T(8,128)(2,1)} %broadcast_in_dim.14), calls=%async_computation.14 | async-start | bytes 9437184 | tf_op jit(solution)/shard_map/all_to_all | solution.py:973
  876.7 58.8 %all-to-all-start.15 = ((bf16[4,3,384,256]{3,2,1,0:T(8,128)(2,1)}), bf16[4,3,384,256]{3,2,1,0:T(8,128)(2,1)}, u32[]{:S(2)}, u32[]{:S(2)}) async-start(bf16[4,3,384,256]{3,2,1,0:T(8,128)(2,1)} %broadcast_in_dim.15), calls=%async_computation.15 | async-start | bytes 4718592 | tf_op jit(solution)/shard_map/all_to_all | solution.py:973
  938.2 35.0 %all-to-all-start.16 = ((bf16[4,3,384,256]{3,2,1,0:T(8,128)(2,1)}), bf16[4,3,384,256]{3,2,1,0:T(8,128)(2,1)}, u32[]{:S(2)}, u32[]{:S(2)}) async-start(bf16[4,3,384,256]{3,2,1,0:T(8,128)(2,1)} %broadcast_in_dim.16), calls=%async_computation.16 | async-start | bytes 4718592 | tf_op jit(solution)/shard_map/all_to_all | solution.py:973
  942.7 155.6 %all-gather.8.cloned.1.call-start = ((), (), s32[]{:S(2)}) async-start(), calls=%async_computation.25 | async-start | bytes 5406720 | tf_op jit(solution)/shard_map/all_gather | solution.py:1454
  1007.3 17.5 %all-to-all-start.17 = ((f32[32,16,128]{2,1,0:T(8,128)}), f32[32,16,128]{2,1,0:T(8,128)S(1)}, u32[]{:S(2)}, u32[]{:S(2)}) async-start(f32[32,16,128]{2,1,0:T(8,128)} %broadcast_in_dim.17), calls=%async_computation.19 | async-start | bytes 524288 | tf_op jit(solution)/shard_map/all_to_all | solution.py:973
  1025.6 54.3 %all-to-all-start.18 = ((bf16[8,320,256]{2,1,0:T(8,128)(2,1)}), bf16[8,320,256]{2,1,0:T(8,128)(2,1)}, u32[]{:S(2)}, u32[]{:S(2)}) async-start(bf16[8,320,256]{2,1,0:T(8,128)(2,1)} %pad_maximum_fusion.2), calls=%async_computation.20 | async-start | bytes 2621440 | tf_op jit(solution)/shard_map/all_to_all | solution.py:973
  1082.3 15.9 %all-to-all-start.19 = ((f32[8,2,6,1024]{3,1,2,0:T(2,128)}), f32[8,2,6,1024]{3,1,2,0:T(2,128)S(1)}, u32[]{:S(2)}, u32[]{:S(2)}) async-start(f32[8,2,6,1024]{3,1,2,0:T(2,128)} %broadcast_in_dim.18), calls=%async_computation.21 | async-start | bytes 786432 | tf_op jit(solution)/shard_map/all_to_all | solution.py:973
  (108 other events, 1338.2 us)
Sparse Core Ops, SparseCore 0:
  22.7 74.8 all-gather.9
  99.5 54.3 all-gather.11
  155.8 57.1 all-gather.13
  577.0 147.5 reduce-scatter.9
  733.9 57.6 reduce-scatter.5
  805.2 169.2 reduce-scatter.7
  998.9 83.5 all-gather.7

commit v6 on v5

--- a/solution.py
+++ b/solution.py
@@ -78,32 +78,61 @@
     return 512 if keys % 512 == 0 else keys
 
 
-def softmax_sweep(scores, values, chunks, columns):
-    top = jnp.full((1, columns), -1e30, f32)
+SAFE = 40.0
+
+
+def softmax_sweep(scores, values, chunks, columns, write):
+    def spread(mixed, total, top):
+        width = columns // len(mixed)
+        inverse = 1.0 / total
+        mixed = [m * inverse[:, j * width : (j + 1) * width] for j, m in enumerate(mixed)]
+        write(mixed, top + jnp.log(total))
+
+    ahead = scores(0)
+    top = jnp.max(ahead, axis=0, keepdims=True)
+    base = top * LOG2E
+    peak = top
     total = jnp.zeros((1, columns), f32)
     mixed = None
-    ahead = scores(0)
     for c in range(chunks):
         now = ahead
         ahead = scores(c + 1) if c + 1 < chunks else None
-        new_top = jnp.maximum(top, jnp.max(now, axis=0, keepdims=True))
-        fade = jnp.exp2((top - new_top) * LOG2E)
-        expon = jnp.exp2(now * LOG2E - new_top * LOG2E)
-        total = total * fade + jnp.sum(expon, axis=0, keepdims=True)
+        expon = jnp.exp2(now * LOG2E - base)
+        if c > 0:
+            peak = jnp.maximum(peak, jnp.max(now, axis=0, keepdims=True))
+        total = total + jnp.sum(expon, axis=0, keepdims=True)
         parts = values(c, expon.astype(bf16))
-        width = columns // len(parts)
-        if mixed is None:
-            mixed = parts
-        else:
+        mixed = parts if mixed is None else [m + part for m, part in zip(mixed, parts)]
+    spread(mixed, total, top)
+
+    @pl.when(jnp.max(peak - top) > SAFE)
+    def _():
+        def body(c, carry):
+            top, total, mixed = carry
+            now = scores(c)
+            new_top = jnp.maximum(top, jnp.max(now, axis=0, keepdims=True))
+            fade = jnp.exp2((top - new_top) * LOG2E)
+            expon = jnp.exp2((now - new_top) * LOG2E)
+            total = total * fade + jnp.sum(expon, axis=0, keepdims=True)
+            parts = values(c, expon.astype(bf16))
+            width = columns // len(parts)
             mixed = [
                 m * fade[:, j * width : (j + 1) * width] + part
                 for j, (m, part) in enumerate(zip(mixed, parts))
             ]
-        top = new_top
-    width = columns // len(mixed)
-    inverse = 1.0 / total
-    mixed = [m * inverse[:, j * width : (j + 1) * width] for j, m in enumerate(mixed)]
-    return mixed, top + jnp.log(total)
+            return new_top, total, mixed
+
+        start = (
+            jnp.full((1, columns), -3e38, f32),
+            jnp.zeros((1, columns), f32),
+            [jnp.zeros(m.shape, f32) for m in mixed],
+        )
+        top, total, again = lax.fori_loop(0, chunks, body, start)
+        spread(again, total, top)
+
+
+def at_chunk(c, step):
+    return pl.ds(c * step if isinstance(c, int) else pl.multiple_of(c * step, step), step)
 
 
 def cross_forward(q, k, vt, tp):
@@ -121,24 +150,26 @@
         )
 
         def scores(c):
-            return dot_nt(k_ref[0, pl.ds(c * step, step), :], both)
+            return dot_nt(k_ref[0, at_chunk(c, step), :], both)
 
         def values(c, p):
             out = []
             for j in range(2):
                 rows = pl.ds(pl.multiple_of((pair * 2 + j) * HEAD, HEAD), HEAD)
-                v = vt_ref[0, rows, pl.ds(c * step, step)]
+                v = vt_ref[0, rows, at_chunk(c, step)]
                 out.append(dot_nn(v, p[:, j * queries : (j + 1) * queries]))
             return out
 
-        mixed, log_total = softmax_sweep(scores, values, keys // step, 2 * queries)
-        rows = jnp.concatenate(mixed, axis=0).T.reshape(tp, 1, tile, 2 * HEAD)
-        o_ref[...] = rows.astype(bf16)
-        wide_ref[...] = rows
-        for j in range(2):
-            log_ref[0, j] = jnp.broadcast_to(
-                log_total[:, j * queries : (j + 1) * queries], (8, queries)
-            )
+        def write(mixed, log_total):
+            rows = jnp.concatenate(mixed, axis=0).T.reshape(tp, 1, tile, 2 * HEAD)
+            o_ref[...] = rows.astype(bf16)
+            wide_ref[...] = rows
+            for j in range(2):
+                log_ref[0, j] = jnp.broadcast_to(
+                    log_total[:, j * queries : (j + 1) * queries], (8, queries)
+                )
+
+        softmax_sweep(scores, values, keys // step, 2 * queries, write)
 
     return pl.pallas_call(
         kernel,
@@ -303,17 +334,19 @@
         both = split_pair(read_queries(ins, half, i, share))
 
         def scores(c):
-            return dot_nt(kv[pl.ds(c * step, step), :], both)
+            return dot_nt(kv[at_chunk(c, step), :], both)
 
         def values(c, p):
-            return [dot_nn(vt[HEAD:, pl.ds(c * step, step)], p)]
-
-        mixed, log_total = softmax_sweep(scores, values, keys // step, 2 * block)
-        mixed = mixed[0]
-        rows = jnp.concatenate([mixed[:, :block], mixed[:, block:]], axis=0).T
-        o_ref[...] = rows.astype(bf16)
-        wide_ref[...] = rows
-        log_ref[0] = jnp.broadcast_to(log_total, (8, 2 * block))
+            return [dot_nn(vt[HEAD:, at_chunk(c, step)], p)]
+
+        def write(mixed, log_total):
+            mixed = mixed[0]
+            rows = jnp.concatenate([mixed[:, :block], mixed[:, block:]], axis=0).T
+            o_ref[...] = rows.astype(bf16)
+            wide_ref[...] = rows
+            log_ref[0] = jnp.broadcast_to(log_total, (8, 2 * block))
+
+        softmax_sweep(scores, values, keys // step, 2 * block, write)
 
     return pl.pallas_call(
         kernel,
@@ -620,6 +653,77 @@
         ),
         name="unpack_back",
     )(*blocks, weights, weights)
+
+
+def norm_forward(base, branch, gate, shift, scale):
+    items, tile, width = base.shape
+
+    def kernel(base_ref, branch_ref, gate_ref, shift_ref, scale_ref, sum_ref, out_ref):
+        value = base_ref[0] + gate_ref[0] * branch_ref[0]
+        hat, _ = norm_parts(value)
+        sum_ref[0] = value
+        out_ref[0] = (hat * (1.0 + scale_ref[0]) + shift_ref[0]).astype(bf16)
+
+    tile_spec = pl.BlockSpec((1, tile, width), lambda i: (i, 0, 0))
+    piece_spec = pl.BlockSpec((1, 1, width), lambda i: (i, 0, 0))
+    return pl.pallas_call(
+        kernel,
+        grid=(items,),
+        in_specs=[tile_spec, tile_spec, piece_spec, piece_spec, piece_spec],
+        out_specs=[tile_spec, tile_spec],
+        out_shape=[
+            jax.ShapeDtypeStruct(base.shape, f32),
+            jax.ShapeDtypeStruct(base.shape, bf16),
+        ],
+        cost_estimate=pl.CostEstimate(
+            flops=16 * items * tile * width,
+            bytes_accessed=14 * items * tile * width,
+            transcendentals=0,
+        ),
+        name="norm_forward",
+    )(base, branch, gate, shift, scale)
+
+
+def norm_backward(g, value, incoming, branch, scale, gate):
+    items, tile, width = g.shape
+
+    def kernel(g_ref, value_ref, in_ref, branch_ref, scale_ref, gate_ref, *outs):
+        out_ref, gated_ref, low_ref, sums_ref = outs
+        hat, inverse = norm_parts(value_ref[0])
+        incoming = in_ref[0]
+        sums_ref[0, 0:1] = jnp.sum(incoming, axis=0, keepdims=True)
+        sums_ref[0, 1:2] = jnp.sum(incoming * hat, axis=0, keepdims=True)
+        sums_ref[0, 2:3] = jnp.sum(g_ref[0] * branch_ref[0], axis=0, keepdims=True)
+        out = g_ref[0] + norm_back(hat, inverse, incoming * (1.0 + scale_ref[0]))
+        out_ref[0] = out
+        gated_ref[0] = (gate_ref[0] * out).astype(bf16)
+        low_ref[0] = out.astype(bf16)
+
+    tile_spec = pl.BlockSpec((1, tile, width), lambda i: (i, 0, 0))
+    piece_spec = pl.BlockSpec((1, 1, width), lambda i: (i, 0, 0))
+    return pl.pallas_call(
+        kernel,
+        grid=(items,),
+        in_specs=[tile_spec] * 4 + [piece_spec, piece_spec],
+        out_specs=[
+            tile_spec,
+            tile_spec,
+            tile_spec,
+            pl.BlockSpec((1, 3, width), lambda i: (i, 0, 0)),
+        ],
+        out_shape=[
+            jax.ShapeDtypeStruct(g.shape, f32),
+            jax.ShapeDtypeStruct(g.shape, bf16),
+            jax.ShapeDtypeStruct(g.shape, bf16),
+            jax.ShapeDtypeStruct((items, 3, width), f32),
+        ],
+        cost_estimate=pl.CostEstimate(
+            flops=30 * items * tile * width,
+            bytes_accessed=24 * items * tile * width,
+            transcendentals=0,
+        ),
+        name="norm_backward",
+    )(g, value, incoming, branch, scale, gate)
 
 
 def out_project(mixed, weights):
@@ -1091,35 +1195,6 @@
     upper_keep = (plane_row != 0).astype(f32)
     lower_keep = (plane_row != PLANE - 1).astype(f32)
     grad_edges = with_halo(incoming, (("seq", 0), ("tp", 2)), 1)
-    upper_mask = upper_keep.astype(bf16)[:, None, None, None]
-    lower_mask = lower_keep.astype(bf16)[:, None, None, None]
-    first_pair = grad_edges[:-2].reshape(rows_here, 2, items, 2 * cols_here + 2, COUT)
-    last_pair = grad_edges[2:].reshape(rows_here, 2, items, 2 * cols_here + 2, COUT)
-    row_taps = jnp.stack(
-        [
-            first_pair[:, 0] * upper_mask,
-            first_pair[:, 1],
-            last_pair[:, 0],
-            last_pair[:, 1] * lower_mask,
-        ],
-        axis=3,
-    )
-    left_pair = row_taps[:, :, :-2].reshape(rows_here, items, cols_here, 2, 4, COUT)
-    right_pair = row_taps[:, :, 2:].reshape(rows_here, items, cols_here, 2, 4, COUT)
-    tap_grads = jnp.stack(
-        [
-            left_pair[:, :, :, 0],
-            left_pair[:, :, :, 1],
-            right_pair[:, :, :, 0],
-            right_pair[:, :, :, 1],
-        ],
-        axis=4,
-    )
-    tap_grads = tap_grads.reshape(rows_here, items, cols_here, 16 * COUT)
-    grad_result = to_tile(out_cotangent.astype(f32) + dot("rict,dt->ricd", tap_grads, w_deconv))
-    grad_bias = jnp.sum(incoming.astype(f32), axis=(0, 1, 2))
-    grad_mlp = (piece(8) * grad_result).astype(bf16)
-
     if fast:
         first_in, queries = first_kernel(tokens, piece(0), piece(1), w_query, tp)
     else:
@@ -1132,7 +1207,36 @@
         first_in = (first_hat * (1.0 + piece(1)) + piece(0)).astype(bf16)
         queries = dot("iqd,de->iqe", first_in, w_query).astype(bf16) * bf16(0.125)
     image = context.transpose(1, 0, 2)
+    queries, grad_edges = lax.optimization_barrier((queries, grad_edges))
     keys, values_t = key_value_kernel(image, w_key, w_value.T)
+    upper_mask = upper_keep.astype(bf16)[:, None, None, None]
+    lower_mask = lower_keep.astype(bf16)[:, None, None, None]
+    first_pair = grad_edges[:-2].reshape(rows_here, 2, items, 2 * cols_here + 2, COUT)
+    last_pair = grad_edges[2:].reshape(rows_here, 2, items, 2 * cols_here + 2, COUT)
+    row_taps = jnp.stack(
+        [
+            first_pair[:, 0] * upper_mask,
+            first_pair[:, 1],
+            last_pair[:, 0],
+            last_pair[:, 1] * lower_mask,
+        ],
+        axis=3,
+    )
+    left_pair = row_taps[:, :, :-2].reshape(rows_here, items, cols_here, 2, 4, COUT)
+    right_pair = row_taps[:, :, 2:].reshape(rows_here, items, cols_here, 2, 4, COUT)
+    tap_grads = jnp.stack(
+        [
+            left_pair[:, :, :, 0],
+            left_pair[:, :, :, 1],
+            right_pair[:, :, :, 0],
+            right_pair[:, :, :, 1],
+        ],
+        axis=4,
+    )
+    tap_grads = tap_grads.reshape(rows_here, items, cols_here, 16 * COUT)
+    grad_result = to_tile(out_cotangent.astype(f32) + dot("rict,dt->ricd", tap_grads, w_deconv))
+    grad_bias = jnp.sum(incoming.astype(f32), axis=(0, 1, 2))
+    grad_mlp = (piece(8) * grad_result).astype(bf16)
     mixed, mixed_wide, cross_logs = cross_forward(queries, keys, values_t, tp)
     mixed_tile = exchange(mixed, "tp")
     if fast:
@@ -1140,10 +1244,8 @@
     else:
         branch_a = dot("time,tef->imf", mixed_tile, by_tp(out_slots))
     residual = to_tile(lax.dynamic_slice_in_dim(tokens, me_tp * cols_here, cols_here, 2)).astype(f32)
-    middle = residual + piece(2) * branch_a
-
-    self_hat, self_inv = norm_parts(middle)
-    self_in = (self_hat * (1.0 + piece(4)) + piece(3)).astype(bf16)
+    middle, self_in = norm_forward(residual, branch_a, piece(2), piece(3), piece(4))
+
     flat = (items * tile, width)
     spare = groups * turns - items
 
@@ -1213,10 +1315,8 @@
         branch_s = dot("nxe,xed->nd", so_tile, so_slots)
         so_tile = so_tile.reshape(items * tile, heads * HEAD)
     branch_s = branch_s.reshape(items, tile, width)
-    middle_two = middle + piece(5) * branch_s
-
-    second_hat, second_inv = norm_parts(middle_two)
-    second_in = (second_hat * (1.0 + piece(7)) + piece(6)).astype(bf16)
+    middle_two, second_in = norm_forward(middle, branch_s, piece(5), piece(6), piece(7))
+
     active, grad_hidden, branch_b, grad_second = feed_forward(
         second_in.reshape(flat), grad_mlp.reshape(flat), up_slots, down_slots
     )
@@ -1225,10 +1325,9 @@
     result = middle_two + piece(8) * branch_b
     out_tile = from_tile(result.astype(bf16))
 
-    grad_gate_b = jnp.sum(grad_result * branch_b, axis=1)
-    grad_shift_b = jnp.sum(grad_second, axis=1)
-    grad_scale_b = jnp.sum(grad_second * second_hat, axis=1)
-    grad_mid_two = grad_result + norm_back(second_hat, second_inv, grad_second * (1.0 + piece(7)))
+    grad_mid_two, grad_self, _, sums_b = norm_backward(
+        grad_result, middle_two, grad_second, branch_b, piece(7), piece(5)
+    )
 
     widened = with_halo(out_tile, (("seq", 0), ("tp", 2)), 1)
     taps = dot("ricd,dt->rict", widened, w_deconv)
@@ -1246,13 +1345,16 @@
     def of_cores(x):
         return x.reshape((tp, seq // 2, 2) + x.shape[1:]).transpose(2, 0, 1, 3, 4)
 
-    def total_near(terms, after, *cuts):
+    def total_near(terms, after):
         keep = lax.dynamic_index_in_dim(terms, core, 0, False)
         give = lax.dynamic_index_in_dim(terms, 1 - core, 0, False)
         got = lax.ppermute(give, "seq", [(i, i ^ 1) for i in range(seq)])
         got, _ = lax.optimization_barrier((got, after))
         x = (keep.astype(f32) + got.astype(f32)).astype(bf16)
-        x = lax.psum_scatter(x, "tp", scatter_dimension=0, tiled=True)[0]
+        return lax.psum_scatter(x, "tp", scatter_dimension=0, tiled=True)[0]
+
+    def total_far(x, after, *cuts):
+        x, _ = lax.optimization_barrier((x, after))
         lines = [list(range(c, seq, 2)) for c in range(2)]
         x = lax.psum_scatter(x, "seq", scatter_dimension=0, axis_index_groups=lines, tiled=True)[0]
         return jnp.split(x.astype(f32), cuts, axis=0)
@@ -1296,8 +1398,6 @@
         )
         terms_b = of_cores(terms_b)
 
-    grad_self = (piece(5) * grad_mid_two).astype(bf16)
-    grad_gate_s = jnp.sum(grad_mid_two * branch_s, axis=1)
     if fast:
         dso_send = back_pack(grad_self.reshape(flat), small, items, turns, groups)
         dso_send = dso_send.reshape(turns, devices, half, 2 * HEAD)
@@ -1317,9 +1417,7 @@
         backward.append(
             self_backward(parts[turn], dso_mine[turn], *forward[turn][1:], devices, half)
         )
-    grad_up, grad_down, grad_deconv = total_near(
-        terms_b, (backward[0][0], dso_mine[min(1, turns - 1)]), *size_b[1:]
-    )
+    near_b = total_near(terms_b, (backward[0][0], dso_mine[min(1, turns - 1)]))
     if fast:
         blocks = [
             exchange(x[0], both_axes).reshape(groups, slots, 2, 3 * half, 2 * HEAD)
@@ -1336,31 +1434,21 @@
         grad_third = dot(
             "xne,xed->nd", grad_projected, jnp.concatenate([kv_slots, q_slots], axis=1)
         )
+    grad_up, grad_down, grad_deconv = total_far(near_b, grad_third, *size_b[1:])
     grad_third = grad_third.reshape(items, tile, width)
-    grad_shift_s = jnp.sum(grad_third, axis=1)
-    grad_scale_s = jnp.sum(grad_third * self_hat, axis=1)
-    grad_middle = grad_mid_two + norm_back(self_hat, self_inv, grad_third * (1.0 + piece(4)))
-
-    grad_attn = (piece(2) * grad_middle).astype(bf16)
+    grad_middle, grad_attn, middle_low, sums_s = norm_backward(
+        grad_mid_two, middle, grad_third, branch_s, piece(4), piece(2)
+    )
+
     grad_gate_a = jnp.sum(grad_middle * branch_a, axis=1)
     if fast:
         do_send = out_back(grad_attn.reshape(flat), small, mixed.shape)
     else:
         do_send = dot("imf,tef->time", grad_attn, by_tp(out_slots)).astype(bf16)
     do_mine = exchange(do_send, "tp")
-    middle_all = gather(grad_middle.astype(bf16), "tp")
-    early = jnp.stack(
-        [
-            grad_gate_a,
-            grad_shift_s,
-            grad_scale_s,
-            grad_gate_s,
-            grad_shift_b,
-            grad_scale_b,
-            grad_gate_b,
-        ],
-        axis=0,
-    ).reshape(7 * items, width)
+    middle_all = gather(middle_low, "tp")
+    early = jnp.concatenate([grad_gate_a[:, None], sums_s, sums_b], axis=1)
+    early = early.transpose(1, 0, 2).reshape(7 * items, width)
     early = jnp.concatenate(
         [early, jnp.pad(grad_bias, (0, width - COUT))[None]], axis=0
     )
@@ -1452,11 +1540,9 @@
     grad_deconv, grad_image = lax.optimization_barrier((grad_deconv, grad_image))
     grad_deconv = grad_deconv.reshape(-1, piece_rows, share).transpose(1, 0, 2)
     grad_deconv = lax.all_gather(
-        grad_deconv.reshape(piece_rows, 16 * COUT), ("tp", "seq"), axis=0, tiled=True
-    )
-    early = gather(grad_early, ("tp", "seq")).reshape(tp, seq, spots, share)
-    early = early.transpose(0, 2, 1, 3).reshape(tp * spots, width)
-    last, dq_one, dq_two, early = lax.optimization_barrier((last, dq_one, dq_two, early))
+        grad_deconv.reshape(piece_rows, 16 * COUT).astype(bf16), ("tp", "seq"), axis=0, tiled=True
+    )
+    last, dq_one, dq_two = lax.optimization_barrier((last, dq_one, dq_two))
     last = jnp.sum(exchange(last, "seq").astype(f32), axis=0)
     if fast:
         grad_tokens, late_one = last_kernel(None, tokens, piece(1), middle_all, dq_one, small, 0)
@@ -1480,7 +1566,12 @@
         late = jnp.stack([grad_shift_a, grad_scale_a], axis=0)
 
     late, last = lax.optimization_barrier((late, last))
-    late = jnp.sum(gather(late, "seq"), axis=0)
+    part = 2 * items * width // tp
+    mine = lax.dynamic_slice_in_dim(late.reshape(-1, share), me_tp * (part // share), part // share, 0)
+    sums = gather(jnp.concatenate([mine, grad_early], axis=0), ("tp", "seq"))
+    sums = sums.reshape(tp, seq, part // share + spots, share)
+    late = jnp.sum(sums[:, :, : part // share], axis=1).reshape(2, items, width)
+    early = sums[:, :, part // share :].transpose(0, 2, 1, 3).reshape(tp * spots, width)
     grad_bias = early[7 * items, :COUT]
     early = early[: 7 * items].reshape(7, items, width)
     depth = (last.shape[0] - share) // 2
@@ -1506,7 +1597,7 @@
         grad_self_out.reshape(local, share),
         grad_up.T,
         grad_down,
-        grad_deconv,
+        grad_deconv.astype(f32),
         grad_bias,
         grad_table,
     )

time: 1130 us -> 1080 us (0.956)
  other arithmetic: 93 us -> 50.6 us
  waiting for transfers between devices: 128 us -> 159 us
  local copies, waits for them, and re-layouts: 205 us -> 182 us
  blocking collectives: 19.5 us -> 0 us
  Pallas kernels: 511 us -> 524 us
    pallas_call x0 -> x4, Pallas kernels: none -> 27.8 us  [the longest x2 15.9 us: norm_backward(): pl.pallas_call(kernel, grid=(items,), in_specs=[tile_spec] * 4 + [piece_s...]
    all_to_all x19, waiting for transfers between devices: 109 us -> 135 us  [exchange(): return lax.all_to_all(x, axis, 0, 0, tiled=True)]
    reduce_sum x8 -> x1, other arithmetic: 25 us -> 0.64 us  [body(): late = jnp.sum(sums[:, :, :part // share], axis=1).reshape(2, items, width)]
    all_to_all x1 -> x0, blocking collectives: 19.5 us -> none  [exchange(): return lax.all_to_all(x, axis, 0, 0, tiled=True)]
    ppermute x4, waiting for transfers between devices: 0.01 us -> 16.2 us  [with_halo(): before = lax.ppermute(last, axis, up)]
    convert_element_type x4 -> x2, other arithmetic: 19.2 us -> 5.63 us  [the longest x1 4.49 us: body(): grad_deconv.astype(f32)]
    unnamed x241 -> x175, local copies, waits for them, and re-layouts: 92.2 us -> 80.3 us
  transfers between devices with their start and end apart: 35 -> 35, of which waited for: 10 -> 14; matrix products, arithmetic and copies ran while one was open for 17% -> 14% of each run, Pallas kernels for 42% -> 44%
where the time goes in v6:
time: 1080 us; the launch traced here: 1060 us
  Pallas kernels  524 us (49%)
  local copies, waits for them, and re-layouts  182 us (17%)
  waiting for transfers between devices  159 us (15%)
  starting transfers between devices  109 us (10%)
  other arithmetic  50.6 us (5%)
  matrix products  22.6 us (2%)
  between operations  15.7 us (1%)
    all_to_all x19, waiting for transfers between devices, exchange(): return lax.all_to_all(x, axis, 0, 0, tiled=True)  135 us
    pallas_call x2, Pallas kernels, cross_backward(): pl.pallas_call(kernel, grid=(items, heads), in_specs=[rows_spec, tiles_sp...  101 us
    all_to_all x19, starting transfers between devices, exchange(): return lax.all_to_all(x, axis, 0, 0, tiled=True)  89 us
    unnamed x175, local copies, waits for them, and re-layouts  80.3 us
    pallas_call x3, Pallas kernels, self_backward(): pl.pallas_call(kernel, grid=(blocks,), in_specs=part_specs(parts, half) +...  79 us
    pallas_call x1, Pallas kernels, cross_forward(): pl.pallas_call(kernel, grid=(items, heads // 2), in_specs=[pl.BlockSpec((...  53.2 us
    pallas_call x3, Pallas kernels, self_forward(): pl.pallas_call(kernel, grid=(blocks,), in_specs=part_specs(parts, half),...  41.2 us
    pallas_call x1, Pallas kernels, feed_forward(): pl.pallas_call(kernel, grid=(slots,), in_specs=[rows_spec, rows_spec, pl....  39.2 us
  transfers between devices with their start and end apart: 35, of which 14 were waited for; matrix products, arithmetic and copies ran while one was open for 14% of the time, Pallas kernels for 44%

profile of v6, /device:TPU:0, one launch (start us, length us, event | category | flops | bytes accessed | tf_op | source)
XLA Modules:
  0.0 1063.1 jit_solution(6756160318895857234)
XLA Ops:
  32.6 34.4 %key_value_kernel.1 = (bf16[6,4096,256]{2,1,0:T(8,128)(2,1)S(1)}, bf16[6,256,4096]{2,1,0:T(8,128)(2,1)}) custom-call(bf16[6,4096,768]{2,1,0:T(8,128)(2,1)} %bitcast.270, bf16[768,256]{1,0:T(8,128)(2,1)S(1)} %copy-done.39, bf16[256,768]{1,0:T(8,128)(2,1)S(1)} %bitcast.259), custom_call_target="tpu_custom_call" | custom-call | flops 19327352832 | bytes 62914560 | tf_op jit(solution)/shard_map/key_value_kernel/pallas_call | solution.py:844
  90.4 53.2 %cross_forward.1 = (bf16[4,6,96,256]{3,2,1,0:T(8,128)(2,1)S(1)}, f32[4,6,96,256]{3,2,1,0:T(8,128)S(1)}, f32[6,4,8,384]{3,2,1,0:T(8,128)S(1)}) custom-call(bf16[6,384,256]{2,1,0:T(8,128)(2,1)S(1)} %get-tuple-element.109.q_ref, bf16[6,4096,256]{2,1,0:T(8,128)(2,1)} %copy-done.40, bf16[6,256,4096]{2,1,0:T(8,128)(2,1)} %get-tuple-element.111.vt_ref), custom_call_target="tpu_custom_call" | custom-call | flops 38654705664 | bytes 27525120 | tf_op jit(solution)/shard_map/cross_forward/pallas_call | solution.py:174
  155.6 18.6 %all-to-all-done.x_ref.refs_0_ = bf16[4,6,96,256]{3,2,1,0:T(8,128)(2,1)} async-done(((bf16[4,6,96,256]{3,2,1,0:T(8,128)(2,1)}), bf16[4,6,96,256]{3,2,1,0:T(8,128)(2,1)}, u32[]{:S(2)}, u32[]{:S(2)}) %all-to-all-start) | async-done | bytes 1179680 | tf_op jit(solution)/shard_map/all_to_all | solution.py:1077
  190.6 8.9 project_pack.1
  215.2 19.9 %all-to-all-done.1.refs_0_ = bf16[32,144,128]{2,1,0:T(8,128)(2,1)} async-done(((bf16[32,144,128]{2,1,0:T(8,128)(2,1)}), bf16[32,144,128]{2,1,0:T(8,128)(2,1)}, u32[]{:S(2)}, u32[]{:S(2)}) %all-to-all-start.1) | async-done | bytes 1179680 | tf_op jit(solution)/shard_map/all_to_all | solution.py:1077
  260.6 13.5 %self_forward.3 = (bf16[1536,128]{1,0:T(8,128)(2,1)S(1)}, f32[1536,128]{1,0:T(8,128)S(1)}, f32[4,8,768]{2,1,0:T(8,128)S(1)}) custom-call(bf16[32,144,128]{2,1,0:T(8,128)(2,1)} %all-to-all-done.1.refs_0_), custom_call_target="tpu_custom_call" | custom-call | flops 9663676416 | bytes 3145728 | tf_op jit(solution)/shard_map/self_forward/pallas_call | solution.py:351
  282.5 14.2 %self_forward.4 = (bf16[1536,128]{1,0:T(8,128)(2,1)}, f32[1536,128]{1,0:T(8,128)S(1)}, f32[4,8,768]{2,1,0:T(8,128)S(1)}) custom-call(bf16[32,144,128]{2,1,0:T(8,128)(2,1)} %all-to-all-done.4.refs_0_), custom_call_target="tpu_custom_call" | custom-call | flops 9663676416 | bytes 3145728 | tf_op jit(solution)/shard_map/self_forward/pallas_call | solution.py:351
  297.6 14.0 %all-to-all-done.2.refs_0_ = bf16[32,144,128]{2,1,0:T(8,128)(2,1)} async-done(((bf16[32,144,128]{2,1,0:T(8,128)(2,1)}), bf16[32,144,128]{2,1,0:T(8,128)(2,1)}, u32[]{:S(2)}, u32[]{:S(2)}) %all-to-all-start.2) | async-done | bytes 1179680 | tf_op jit(solution)/shard_map/all_to_all | solution.py:1077
  315.1 13.6 %all-to-all-done.5 = bf16[32,48,128]{2,1,0:T(8,128)(2,1)S(1)} async-done(((bf16[32,48,128]{2,1,0:T(8,128)(2,1)}), bf16[32,48,128]{2,1,0:T(8,128)(2,1)S(1)}, u32[]{:S(2)}, u32[]{:S(2)}) %all-to-all-start.5) | async-done | bytes 393248 | tf_op jit(solution)/shard_map/all_to_all | solution.py:1077
  331.4 13.5 %self_forward.5 = (bf16[1536,128]{1,0:T(8,128)(2,1)S(1)}, f32[1536,128]{1,0:T(8,128)S(1)}, f32[4,8,768]{2,1,0:T(8,128)S(1)}) custom-call(bf16[32,144,128]{2,1,0:T(8,128)(2,1)} %all-to-all-done.2.refs_0_), custom_call_target="tpu_custom_call" | custom-call | flops 9663676416 | bytes 3145728 | tf_op jit(solution)/shard_map/self_forward/pallas_call | solution.py:351
  353.4 13.6 %all-to-all-done.6 = bf16[32,48,128]{2,1,0:T(8,128)(2,1)} async-done(((bf16[32,48,128]{2,1,0:T(8,128)(2,1)}), bf16[32,48,128]{2,1,0:T(8,128)(2,1)}, u32[]{:S(2)}, u32[]{:S(2)}) %all-to-all-start.6) | async-done | bytes 393248 | tf_op jit(solution)/shard_map/all_to_all | solution.py:1077
  384.5 39.2 %feed_forward.1 = (bf16[8,576,512]{2,1,0:T(8,128)(2,1)}, bf16[8,576,512]{2,1,0:T(8,128)(2,1)}, f32[576,1024]{1,0:T(8,128)}, f32[576,1024]{1,0:T(8,128)}) custom-call(bf16[576,1024]{1,0:T(8,128)(2,1)S(1)} %bitcast.252, bf16[576,1024]{1,0:T(8,128)(2,1)} %bitcast.243, bf16[8,1024,512]{2,1,0:T(8,128)(2,1)} %bitcast.326, bf16[8,512,1024]{2,1,0:T(8,128)(2,1)} %bitcast.327), custom_call_target="tpu_custom_call" | custom-call | flops 19327352832 | bytes 16777216 | tf_op jit(solution)/shard_map/feed_forward/pallas_call | solution.py:943
  462.4 9.2 weight_terms.5.refs_2_
  471.7 9.3 weight_terms.6
  483.0 8.1 dynamic-slice_bitcast_fusion
  499.3 26.2 %self_backward.3 = bf16[32,144,128]{2,1,0:T(8,128)(2,1)S(1)} custom-call(bf16[32,144,128]{2,1,0:T(8,128)(2,1)} %all-to-all-done.1.refs_0_, bf16[1536,128]{1,0:T(8,128)(2,1)S(1)} %bitcast.254, f32[1536,128]{1,0:T(8,128)S(1)} %copy-done.46, f32[4,8,768]{2,1,0:T(8,128)S(1)} %copy-done.53), custom_call_target="tpu_custom_call" | custom-call | flops 24159191040 | bytes 6291456 | tf_op jit(solution)/shard_map/self_backward/pallas_call | solution.py:437
  526.5 12.2 %fusion = bf16[4,4,2368,128]{3,2,1,0:T(8,128)(2,1)} fusion(bf16[4,4,2368,128]{3,2,1,0:T(8,128)(2,1)} %collective-permute-done.8, bf16[2,4,4,2368,128]{4,3,2,1,0:T(8,128)(2,1)} %bitcast_dynamic-update-slice_fusion, s32[]{:T(128)S(6)} %select_n.57), kind=kLoop, calls=%fused_computation.1 | loop fusion | flops 19398656 | bytes 29097988 | tf_op jit(solution)/shard_map/convert_element_type | solution.py:1353
  546.2 26.6 %self_backward.5 = bf16[32,144,128]{2,1,0:T(8,128)(2,1)S(1)} custom-call(bf16[32,144,128]{2,1,0:T(8,128)(2,1)} %all-to-all-done.4.refs_0_, bf16[1536,128]{1,0:T(8,128)(2,1)S(1)} %bitcast.255, f32[1536,128]{1,0:T(8,128)S(1)} %copy-done.42, f32[4,8,768]{2,1,0:T(8,128)S(1)} %get-tuple-element.146.refs_3_), custom_call_target="tpu_custom_call" | custom-call | flops 24159191040 | bytes 6291456 | tf_op jit(solution)/shard_map/self_backward/pallas_call | solution.py:437
  581.2 26.2 %self_backward.4 = bf16[32,144,128]{2,1,0:T(8,128)(2,1)S(1)} custom-call(bf16[32,144,128]{2,1,0:T(8,128)(2,1)} %all-to-all-done.2.refs_0_, bf16[1536,128]{1,0:T(8,128)(2,1)S(1)} %bitcast.257, f32[1536,128]{1,0:T(8,128)S(1)} %copy-done.44, f32[4,8,768]{2,1,0:T(8,128)S(1)} %copy-done.51), custom_call_target="tpu_custom_call" | custom-call | flops 24159191040 | bytes 6291456 | tf_op jit(solution)/shard_map/self_backward/pallas_call | solution.py:437
  623.3 20.4 %all-to-all-done.9 = bf16[32,144,128]{2,1,0:T(8,128)(2,1)} async-done(((bf16[32,144,128]{2,1,0:T(8,128)(2,1)}), bf16[32,144,128]{2,1,0:T(8,128)(2,1)}, u32[]{:S(2)}, u32[]{:S(2)}) %all-to-all-start.9) | async-done | bytes 1179680 | tf_op jit(solution)/shard_map/all_to_all | solution.py:1077
  654.5 16.2 %collective-permute-done.6 = bf16[14,6,1,1024]{3,0,2,1:T(8,128)(2,1)} collective-permute-done((bf16[14,6,1,1024]{3,0,2,1:T(8,128)(2,1)S(1)}, bf16[14,6,1,1024]{3,0,2,1:T(8,128)(2,1)}, u32[]{:S(2)}, u32[]{:S(2)}) %collective-permute-start.6) | collective-permute-done | bytes 172064 | tf_op jit(solution)/shard_map/ppermute | solution.py:29
  685.2 10.6 reshape.358
  708.9 10.6 unpack_back.1
  750.5 8.1 weight_terms.7.refs_2_
  787.4 50.7 %cross_backward.2 = (bf16[3,384,256]{2,1,0:T(8,128)(2,1)S(1)}, bf16[3,256,4096]{2,1,0:T(8,128)(2,1)}, bf16[3,256,4096]{2,1,0:T(8,128)(2,1)}) custom-call(bf16[6,384,256]{2,1,0:T(8,128)(2,1)S(1)} %copy-done.37, bf16[4,6,96,256]{3,2,1,0:T(8,128)(2,1)} %all-to-all-done.13.do_ref, f32[4,6,96,256]{3,2,1,0:T(8,128)S(1)} %copy-done.48, ...), custom_call_target="tpu_custom_call" | custom-call | flops 48318382080 | bytes 27525120 | tf_op jit(solution)/shard_map/cross_backward/pallas_call | solution.py:250
  851.9 50.6 %cross_backward.3 = (bf16[3,384,256]{2,1,0:T(8,128)(2,1)S(1)}, bf16[3,256,4096]{2,1,0:T(8,128)(2,1)}, bf16[3,256,4096]{2,1,0:T(8,128)(2,1)}) custom-call(bf16[6,384,256]{2,1,0:T(8,128)(2,1)S(1)} %copy-done.38, bf16[4,6,96,256]{3,2,1,0:T(8,128)(2,1)} %all-to-all-done.13.do_ref, f32[4,6,96,256]{3,2,1,0:T(8,128)S(1)} %copy-done.49, ...), custom_call_target="tpu_custom_call" | custom-call | flops 48318382080 | bytes 27525120 | tf_op jit(solution)/shard_map/cross_backward/pallas_call | solution.py:250
  916.3 17.4 %key_value_grads.2 = f32[512,768]{1,0:T(8,128)S(1)} custom-call(bf16[3,256,4096]{2,1,0:T(8,128)(2,1)S(1)} %copy-done.5, bf16[3,256,4096]{2,1,0:T(8,128)(2,1)S(1)} %copy-done.6, bf16[6,4096,768]{2,1,0:T(8,128)(2,1)} %bitcast.271), custom_call_target="tpu_custom_call" | custom-call | flops 9663676416 | bytes 31457280 | tf_op jit(solution)/shard_map/key_value_grads/pallas_call | solution.py:889
  943.3 17.2 %key_value_grads.3 = f32[512,768]{1,0:T(8,128)S(1)} custom-call(bf16[3,256,4096]{2,1,0:T(8,128)(2,1)S(1)} %copy-done.7, bf16[3,256,4096]{2,1,0:T(8,128)(2,1)S(1)} %copy-done.8, bf16[6,4096,768]{2,1,0:T(8,128)(2,1)} %bitcast.272), custom_call_target="tpu_custom_call" | custom-call | flops 9663676416 | bytes 31457280 | tf_op jit(solution)/shard_map/key_value_grads/pallas_call | solution.py:889
  978.5 9.4 last_kernel.2
  987.9 9.4 last_kernel.3
  997.3 18.3 %all-to-all-done.17 = bf16[8,320,256]{2,1,0:T(8,128)(2,1)} async-done(((bf16[8,320,256]{2,1,0:T(8,128)(2,1)}), bf16[8,320,256]{2,1,0:T(8,128)(2,1)}, u32[]{:S(2)}, u32[]{:S(2)}) %all-to-all-start.17) | async-done | bytes 1310752 | tf_op jit(solution)/shard_map/all_to_all | solution.py:1077
  1038.2 8.3 all-to-all-done.18
  (370 shorter events, 426.1 us)
Async XLA Ops:
  7.2 167.0 %all-gather.10.cloned.1.call-start = ((), (), s32[]{:S(2)}) async-start(), calls=%async_computation.25 | async-start | bytes 14155776 | tf_op jit(solution)/shard_map/all_gather | solution.py:1153
  18.4 364.8 %all-gather.12.cloned.1.call-start = ((), (), s32[]{:S(2)}) async-start(), calls=%async_computation.26 | async-start | bytes 9437184 | tf_op jit(solution)/shard_map/all_gather | solution.py:1153
  20.8 362.4 %all-gather.14.cloned.1.call-start = ((), (), s32[]{:S(2)}) async-start(), calls=%async_computation.27 | async-start | bytes 9437184 | tf_op jit(solution)/shard_map/all_gather | solution.py:1153
  22.0 54.2 %collective-permute-start.1 = (bf16[1,6,16,80]{3,2,1,0:T(8,128)(2,1)S(1)}, bf16[1,6,16,80]{3,2,1,0:T(8,128)(2,1)S(1)}, u32[]{:S(2)}, u32[]{:S(2)}) collective-permute-start(bf16[1,6,16,80]{3,2,1,0:T(8,128)(2,1)S(1)} %slice.201), channel_id=1, source_target_pairs={{4,0},{8,4},{12,8},{16,12},{20,16},{24,20},{28,24},{5,1},{9,5},{13... | collective-permute-start | bytes 46088 | tf_op jit(solution)/shard_map/ppermute | solution.py:30
  23.4 52.9 %collective-permute-start = (bf16[1,6,16,80]{3,2,1,0:T(8,128)(2,1)S(1)}, bf16[1,6,16,80]{3,2,1,0:T(8,128)(2,1)S(1)}, u32[]{:S(2)}, u32[]{:S(2)}) collective-permute-start(bf16[1,6,16,80]{3,2,1,0:T(8,128)(2,1)S(1)} %slice.199), channel_id=1, source_target_pairs={{0,4},{4,8},{8,12},{12,16},{16,20},{20,24},{24,28},{1,5},{5,9},{9,... | collective-permute-start | bytes 46088 | tf_op jit(solution)/shard_map/ppermute | solution.py:29
  146.7 27.5 %all-to-all-start = ((bf16[4,6,96,256]{3,2,1,0:T(8,128)(2,1)}), bf16[4,6,96,256]{3,2,1,0:T(8,128)(2,1)}, u32[]{:S(2)}, u32[]{:S(2)}) async-start(bf16[4,6,96,256]{3,2,1,0:T(8,128)(2,1)} %copy-done.27), calls=%async_computation | async-start | bytes 2359296 | tf_op jit(solution)/shard_map/all_to_all | solution.py:1077
  201.3 33.7 %all-to-all-start.1 = ((bf16[32,144,128]{2,1,0:T(8,128)(2,1)}), bf16[32,144,128]{2,1,0:T(8,128)(2,1)}, u32[]{:S(2)}, u32[]{:S(2)}) async-start(bf16[32,144,128]{2,1,0:T(8,128)(2,1)} %bitcast.288), calls=%async_computation.1 | async-start | bytes 2359296 | tf_op jit(solution)/shard_map/all_to_all | solution.py:1077
  235.0 41.4 %all-to-all-start.4 = ((bf16[32,144,128]{2,1,0:T(8,128)(2,1)}), bf16[32,144,128]{2,1,0:T(8,128)(2,1)}, u32[]{:S(2)}, u32[]{:S(2)}) async-start(bf16[32,144,128]{2,1,0:T(8,128)(2,1)} %bitcast.287), calls=%async_computation.4 | async-start | bytes 2359296 | tf_op jit(solution)/shard_map/all_to_all | solution.py:1077
  276.4 35.1 %all-to-all-start.2 = ((bf16[32,144,128]{2,1,0:T(8,128)(2,1)}), bf16[32,144,128]{2,1,0:T(8,128)(2,1)}, u32[]{:S(2)}, u32[]{:S(2)}) async-start(bf16[32,144,128]{2,1,0:T(8,128)(2,1)} %bitcast.286), calls=%async_computation.2 | async-start | bytes 2359296 | tf_op jit(solution)/shard_map/all_to_all | solution.py:1077
  328.8 18.5 %all-to-all-start.3 = ((bf16[32,48,128]{2,1,0:T(8,128)(2,1)}), bf16[32,48,128]{2,1,0:T(8,128)(2,1)S(1)}, u32[]{:S(2)}, u32[]{:S(2)}) async-start(bf16[32,48,128]{2,1,0:T(8,128)(2,1)} %bitcast.256), calls=%async_computation.3 | async-start | bytes 786432 | tf_op jit(solution)/shard_map/all_to_all | solution.py:1077
  347.2 19.8 %all-to-all-start.6 = ((bf16[32,48,128]{2,1,0:T(8,128)(2,1)}), bf16[32,48,128]{2,1,0:T(8,128)(2,1)}, u32[]{:S(2)}, u32[]{:S(2)}) async-start(bf16[32,48,128]{2,1,0:T(8,128)(2,1)} %bitcast.258), calls=%async_computation.6 | async-start | bytes 786432 | tf_op jit(solution)/shard_map/all_to_all | solution.py:1077
  447.9 35.1 %all-to-all-start.7 = ((bf16[32,48,128]{2,1,0:T(8,128)(2,1)}), bf16[32,48,128]{2,1,0:T(8,128)(2,1)S(1)}, u32[]{:S(2)}, u32[]{:S(2)}) async-start(bf16[32,48,128]{2,1,0:T(8,128)(2,1)} %bitcast.56), calls=%async_computation.7 | async-start | bytes 786432 | tf_op jit(solution)/shard_map/all_to_all | solution.py:1077
  491.1 35.5 %collective-permute-start.8 = (bf16[4,4,2368,128]{3,2,1,0:T(8,128)(2,1)}, bf16[4,4,2368,128]{3,2,1,0:T(8,128)(2,1)}, u32[]{:S(2)}, u32[]{:S(2)}) collective-permute-start(bf16[4,4,2368,128]{3,2,1,0:T(8,128)(2,1)} %dynamic-slice_bitcast_fusion), channel_id=1, source_target_pairs={{0,4},{4,0},{8,12},{12,8},{16,20},{20,16},{24,28},{28,24},{1,5},{5... | collective-permute-start | bytes 29097992 | tf_op jit(solution)/shard_map/ppermute | solution.py:1351
  491.3 35.2 %all-to-all-start.11 = ((bf16[32,48,128]{2,1,0:T(8,128)(2,1)}), bf16[32,48,128]{2,1,0:T(8,128)(2,1)S(1)}, u32[]{:S(2)}, u32[]{:S(2)}) async-start(bf16[32,48,128]{2,1,0:T(8,128)(2,1)} %bitcast.300), calls=%async_computation.11 | async-start | bytes 786432 | tf_op jit(solution)/shard_map/all_to_all | solution.py:1077
  497.2 225.6 %reduce-scatter.10.cloned.1.call-start = ((), (), s32[]{:S(2)}) async-start(), calls=%async_computation.28 | async-start | bytes 12124160
  538.8 35.0 %all-to-all-start.8 = ((bf16[32,48,128]{2,1,0:T(8,128)(2,1)}), bf16[32,48,128]{2,1,0:T(8,128)(2,1)S(1)}, u32[]{:S(2)}, u32[]{:S(2)}) async-start(bf16[32,48,128]{2,1,0:T(8,128)(2,1)} %bitcast.299), calls=%async_computation.8 | async-start | bytes 786432 | tf_op jit(solution)/shard_map/all_to_all | solution.py:1077
  573.8 35.3 %all-to-all-start.12 = ((bf16[32,144,128]{2,1,0:T(8,128)(2,1)}), bf16[32,144,128]{2,1,0:T(8,128)(2,1)}, u32[]{:S(2)}, u32[]{:S(2)}) async-start(bf16[32,144,128]{2,1,0:T(8,128)(2,1)} %copy-done.29), calls=%async_computation.12 | async-start | bytes 2359296 | tf_op jit(solution)/shard_map/all_to_all | solution.py:1077
  609.2 34.6 %all-to-all-start.9 = ((bf16[32,144,128]{2,1,0:T(8,128)(2,1)}), bf16[32,144,128]{2,1,0:T(8,128)(2,1)}, u32[]{:S(2)}, u32[]{:S(2)}) async-start(bf16[32,144,128]{2,1,0:T(8,128)(2,1)} %copy-done.28), calls=%async_computation.9 | async-start | bytes 2359296 | tf_op jit(solution)/shard_map/all_to_all | solution.py:1077
  619.9 27.6 %collective-permute-start.4 = (bf16[1,6,8,1024]{3,0,2,1:T(2,128)(2,1)S(1)}, bf16[1,6,8,1024]{3,0,2,1:T(2,128)(2,1)S(1)}, u32[]{:S(2)}, u32[]{:S(2)}) collective-permute-start(bf16[1,6,8,1024]{3,0,2,1:T(2,128)(2,1)S(1)} %get-tuple-element.325), channel_id=1, source_target_pairs={{0,4},{4,8},{8,12},{12,16},{16,20},{20,24},{24,28},{1,5},{5,9},{9,... | collective-permute-start | bytes 294920 | tf_op jit(solution)/shard_map/ppermute | solution.py:29
  622.0 25.5 %collective-permute-start.5 = (bf16[1,6,8,1024]{3,0,2,1:T(2,128)(2,1)S(1)}, bf16[1,6,8,1024]{3,0,2,1:T(2,128)(2,1)S(1)}, u32[]{:S(2)}, u32[]{:S(2)}) collective-permute-start(bf16[1,6,8,1024]{3,0,2,1:T(2,128)(2,1)S(1)} %get-tuple-element.326), channel_id=1, source_target_pairs={{4,0},{8,4},{12,8},{16,12},{20,16},{24,20},{28,24},{5,1},{9,5},{13... | collective-permute-start | bytes 294920 | tf_op jit(solution)/shard_map/ppermute | solution.py:30
  643.7 65.2 %all-to-all-start.10 = ((bf16[32,144,128]{2,1,0:T(8,128)(2,1)}), bf16[32,144,128]{2,1,0:T(8,128)(2,1)}, u32[]{:S(2)}, u32[]{:S(2)}) async-start(bf16[32,144,128]{2,1,0:T(8,128)(2,1)} %copy-done.26), calls=%async_computation.10 | async-start | bytes 2359296 | tf_op jit(solution)/shard_map/all_to_all | solution.py:1077
  647.5 124.4 %reduce-scatter.6.cloned.1.call-start = ((), (), s32[]{:S(2)}) async-start(), calls=%async_computation.22 | async-start | bytes 3031040 | tf_op jit(solution)/shard_map/reduce_scatter | solution.py:1359
  648.8 21.9 %collective-permute-start.6 = (bf16[14,6,1,1024]{3,0,2,1:T(8,128)(2,1)S(1)}, bf16[14,6,1,1024]{3,0,2,1:T(8,128)(2,1)}, u32[]{:S(2)}, u32[]{:S(2)}) collective-permute-start(bf16[14,6,1,1024]{3,0,2,1:T(8,128)(2,1)S(1)} %get-tuple-element.321), channel_id=1, source_target_pairs={{0,1},{1,2},{2,3},{4,5},{5,6},{6,7},{8,9},{9,10},{10,11},{12,13},{... | collective-permute-start | bytes 516104 | tf_op jit(solution)/shard_map/ppermute | solution.py:29
  653.1 25.2 %collective-permute-start.7 = (bf16[14,6,1,1024]{3,0,2,1:T(8,128)(2,1)S(1)}, bf16[14,6,1,1024]{3,0,2,1:T(8,128)(2,1)}, u32[]{:S(2)}, u32[]{:S(2)}) collective-permute-start(bf16[14,6,1,1024]{3,0,2,1:T(8,128)(2,1)S(1)} %get-tuple-element.322), channel_id=1, source_target_pairs={{1,0},{2,1},{3,2},{5,4},{6,5},{7,6},{9,8},{10,9},{11,10},{13,12},{... | collective-permute-start | bytes 516104 | tf_op jit(solution)/shard_map/ppermute | solution.py:30
  742.5 28.8 %all-to-all-start.13 = ((bf16[4,6,96,256]{3,2,1,0:T(8,128)(2,1)}), bf16[4,6,96,256]{3,2,1,0:T(8,128)(2,1)}, u32[]{:S(2)}, u32[]{:S(2)}) async-start(bf16[4,6,96,256]{3,2,1,0:T(8,128)(2,1)} %copy-done.14), calls=%async_computation.13 | async-start | bytes 2359296 | tf_op jit(solution)/shard_map/all_to_all | solution.py:1077
  746.8 271.1 %reduce-scatter.8.cloned.1.call-start = ((), (), s32[]{:S(2)}) async-start(), calls=%async_computation.23 | async-start | bytes 10948608 | tf_op jit(solution)/shard_map/reduce_scatter | solution.py:1363
  779.2 63.6 %all-to-all-start.14 = ((bf16[4,6,96,1024]{3,2,1,0:T(8,128)(2,1)}), bf16[4,6,96,1024]{3,2,1,0:T(8,128)(2,1)}, u32[]{:S(2)}, u32[]{:S(2)}) async-start(bf16[4,6,96,1024]{3,2,1,0:T(8,128)(2,1)} %broadcast_in_dim.16), calls=%async_computation.14 | async-start | bytes 9437184 | tf_op jit(solution)/shard_map/all_to_all | solution.py:1077
  844.4 58.9 %all-to-all-start.15 = ((bf16[4,3,384,256]{3,2,1,0:T(8,128)(2,1)}), bf16[4,3,384,256]{3,2,1,0:T(8,128)(2,1)}, u32[]{:S(2)}, u32[]{:S(2)}) async-start(bf16[4,3,384,256]{3,2,1,0:T(8,128)(2,1)} %broadcast_in_dim.17), calls=%async_computation.15 | async-start | bytes 4718592 | tf_op jit(solution)/shard_map/all_to_all | solution.py:1077
  906.0 31.8 %all-to-all-start.16 = ((bf16[4,3,384,256]{3,2,1,0:T(8,128)(2,1)}), bf16[4,3,384,256]{3,2,1,0:T(8,128)(2,1)}, u32[]{:S(2)}, u32[]{:S(2)}) async-start(bf16[4,3,384,256]{3,2,1,0:T(8,128)(2,1)} %broadcast_in_dim.18), calls=%async_computation.16 | async-start | bytes 4718592 | tf_op jit(solution)/shard_map/all_to_all | solution.py:1077
  910.5 138.8 %all-gather.8.cloned.1.call-start = ((), (), s32[]{:S(2)}) async-start(), calls=%async_computation.24 | async-start | bytes 2703360 | tf_op jit(solution)/shard_map/all_gather | solution.py:1542
  973.3 42.2 %all-to-all-start.17 = ((bf16[8,320,256]{2,1,0:T(8,128)(2,1)}), bf16[8,320,256]{2,1,0:T(8,128)(2,1)}, u32[]{:S(2)}, u32[]{:S(2)}) async-start(bf16[8,320,256]{2,1,0:T(8,128)(2,1)} %pad_maximum_fusion.2), calls=%async_computation.17 | async-start | bytes 2621440 | tf_op jit(solution)/shard_map/all_to_all | solution.py:1077
  1020.6 25.8 %all-to-all-start.18 = ((f32[32,40,128]{2,1,0:T(8,128)}), f32[32,40,128]{2,1,0:T(8,128)S(1)}, u32[]{:S(2)}, u32[]{:S(2)}) async-start(f32[32,40,128]{2,1,0:T(8,128)} %broadcast_in_dim.19), calls=%async_computation.20 | async-start | bytes 1310720 | tf_op jit(solution)/shard_map/all_to_all | solution.py:1077
  (80 other events, 960.1 us)
Sparse Core Ops, SparseCore 0:
  18.5 76.3 all-gather.9
  96.8 54.3 all-gather.11
  153.1 62.1 all-gather.13
  538.9 134.9 reduce-scatter.9
  722.9 48.9 reduce-scatter.5
  778.8 161.1 reduce-scatter.7
  968.0 70.1 all-gather.7

commit v7 on v6

--- a/solution.py
+++ b/solution.py
@@ -189,7 +189,7 @@
             jax.ShapeDtypeStruct((tp, items, tile, width), f32),
             jax.ShapeDtypeStruct((items, heads, 8, queries), f32),
         ],
-        compiler_params=pltpu.CompilerParams(vmem_limit_bytes=48 << 20),
+        compiler_params=pltpu.CompilerParams(vmem_limit_bytes=60 << 20),
         cost_estimate=pl.CostEstimate(
             flops=16 * items * queries * keys * width,
             bytes_accessed=4 * items * (queries + keys) * width,
@@ -269,7 +269,7 @@
             jax.ShapeDtypeStruct((items, width, keys), bf16),
         ],
         scratch_shapes=[pltpu.VMEM((width, queries), bf16), pltpu.VMEM((width, queries), bf16)],
-        compiler_params=pltpu.CompilerParams(vmem_limit_bytes=48 << 20),
+        compiler_params=pltpu.CompilerParams(vmem_limit_bytes=60 << 20),
         cost_estimate=pl.CostEstimate(
             flops=40 * items * queries * keys * width,
             bytes_accessed=8 * items * (queries + keys) * width,
@@ -363,7 +363,7 @@
             jax.ShapeDtypeStruct((blocks, 8, 2 * block), f32),
         ],
         scratch_shapes=[pltpu.VMEM((keys, 2 * HEAD), bf16), pltpu.VMEM((2 * HEAD, keys), bf16)],
-        compiler_params=pltpu.CompilerParams(vmem_limit_bytes=48 << 20),
+        compiler_params=pltpu.CompilerParams(vmem_limit_bytes=60 << 20),
         cost_estimate=pl.CostEstimate(
             flops=16 * keys * keys * HEAD,
             bytes_accessed=8 * keys * 2 * HEAD,
@@ -446,7 +446,7 @@
             pltpu.VMEM((2 * HEAD, keys), bf16),
             pltpu.VMEM((2 * HEAD, keys), f32),
         ],
-        compiler_params=pltpu.CompilerParams(vmem_limit_bytes=48 << 20),
+        compiler_params=pltpu.CompilerParams(vmem_limit_bytes=60 << 20),
         cost_estimate=pl.CostEstimate(
             flops=40 * keys * keys * HEAD,
             bytes_accessed=16 * keys * 2 * HEAD,
@@ -502,7 +502,7 @@
             (turns, groups, 1, 2, 3 * half, 2 * HEAD), lambda i: (0, 0, i, 0, 0, 0)
         ),
         out_shape=jax.ShapeDtypeStruct(shape, bf16),
-        compiler_params=pltpu.CompilerParams(vmem_limit_bytes=40 << 20),
+        compiler_params=pltpu.CompilerParams(vmem_limit_bytes=60 << 20),
         cost_estimate=pl.CostEstimate(
             flops=2 * rows * width * slots * 6 * HEAD,
             bytes_accessed=2 * (rows + slots * 6 * HEAD) * width,
@@ -553,7 +553,7 @@
             jax.ShapeDtypeStruct((items * tile, slots * 2 * HEAD), bf16),
             jax.ShapeDtypeStruct((items * tile, width), f32),
         ],
-        compiler_params=pltpu.CompilerParams(vmem_limit_bytes=40 << 20),
+        compiler_params=pltpu.CompilerParams(vmem_limit_bytes=60 << 20),
         cost_estimate=pl.CostEstimate(
             flops=2 * items * tile * width * slots * 2 * HEAD,
             bytes_accessed=4 * items * tile * width,
@@ -587,7 +587,7 @@
             (turns, groups, 1, 2, half, 2 * HEAD), lambda i: (0, 0, i, 0, 0, 0)
         ),
         out_shape=jax.ShapeDtypeStruct((turns, groups, slots, 2, half, 2 * HEAD), bf16),
-        compiler_params=pltpu.CompilerParams(vmem_limit_bytes=40 << 20),
+        compiler_params=pltpu.CompilerParams(vmem_limit_bytes=60 << 20),
         cost_estimate=pl.CostEstimate(
             flops=2 * rows * width * slots * 2 * HEAD,
             bytes_accessed=2 * (rows + slots * 2 * HEAD) * width,
@@ -645,7 +645,7 @@
             jax.ShapeDtypeStruct((slots, rows, 6 * HEAD), bf16),
             jax.ShapeDtypeStruct((rows, width), f32),
         ],
-        compiler_params=pltpu.CompilerParams(vmem_limit_bytes=40 << 20),
+        compiler_params=pltpu.CompilerParams(vmem_limit_bytes=60 << 20),
         cost_estimate=pl.CostEstimate(
             flops=2 * rows * width * slots * 6 * HEAD,
             bytes_accessed=4 * rows * width,
@@ -675,6 +675,7 @@
             jax.ShapeDtypeStruct(base.shape, f32),
             jax.ShapeDtypeStruct(base.shape, bf16),
         ],
+        compiler_params=pltpu.CompilerParams(vmem_limit_bytes=60 << 20),
         cost_estimate=pl.CostEstimate(
             flops=16 * items * tile * width,
             bytes_accessed=14 * items * tile * width,
@@ -717,6 +718,7 @@
             jax.ShapeDtypeStruct(g.shape, bf16),
             jax.ShapeDtypeStruct((items, 3, width), f32),
         ],
+        compiler_params=pltpu.CompilerParams(vmem_limit_bytes=60 << 20),
         cost_estimate=pl.CostEstimate(
             flops=30 * items * tile * width,
             bytes_accessed=24 * items * tile * width,
@@ -752,7 +754,7 @@
         ],
         out_specs=pl.BlockSpec((rows, width), lambda i: (0, 0)),
         out_shape=jax.ShapeDtypeStruct((rows, width), f32),
-        compiler_params=pltpu.CompilerParams(vmem_limit_bytes=40 << 20),
+        compiler_params=pltpu.CompilerParams(vmem_limit_bytes=60 << 20),
         cost_estimate=pl.CostEstimate(
             flops=2 * rows * width * tp * local,
             bytes_accessed=4 * rows * width,
@@ -779,7 +781,7 @@
         ],
         out_specs=pl.BlockSpec((1, items, tile, local // 2), lambda i: (i % tp, 0, 0, i // tp)),
         out_shape=jax.ShapeDtypeStruct(shape, bf16),
-        compiler_params=pltpu.CompilerParams(vmem_limit_bytes=40 << 20),
+        compiler_params=pltpu.CompilerParams(vmem_limit_bytes=60 << 20),
         cost_estimate=pl.CostEstimate(
             flops=2 * rows * width * tp * local,
             bytes_accessed=4 * rows * width,
@@ -822,7 +824,7 @@
             jax.ShapeDtypeStruct((items, tp * tile, width), bf16),
             jax.ShapeDtypeStruct((items, tp * tile, local), bf16),
         ],
-        compiler_params=pltpu.CompilerParams(vmem_limit_bytes=48 << 20),
+        compiler_params=pltpu.CompilerParams(vmem_limit_bytes=60 << 20),
         cost_estimate=pl.CostEstimate(
             flops=2 * items * tp * tile * width * local,
             bytes_accessed=4 * items * tp * tile * width,
@@ -835,7 +837,7 @@
 def key_value_kernel(context, w_key, w_value_t):
     items, keys, depth = context.shape
     local = w_key.shape[1]
-    step = 1024 if keys % 1024 == 0 else keys
+    step = 4096 if keys % 4096 == 0 else keys
 
     def kernel(x_ref, wk_ref, wv_ref, k_ref, vt_ref):
         k_ref[0] = dot_nn(x_ref[0], wk_ref[...]).astype(bf16)
@@ -857,7 +859,7 @@
             jax.ShapeDtypeStruct((items, keys, local), bf16),
             jax.ShapeDtypeStruct((items, local, keys), bf16),
         ],
-        compiler_params=pltpu.CompilerParams(vmem_limit_bytes=40 << 20),
+        compiler_params=pltpu.CompilerParams(vmem_limit_bytes=60 << 20),
         cost_estimate=pl.CostEstimate(
             flops=4 * items * keys * depth * local,
             bytes_accessed=2 * items * keys * (depth + 2 * local),
@@ -870,7 +872,7 @@
 def key_value_grads(dk_t, dv_t, context, start):
     items, local, keys = dk_t.shape
     depth = context.shape[2]
-    step = 1024 if keys % 1024 == 0 else keys
+    step = 4096 if keys % 4096 == 0 else keys
 
     def kernel(dk_ref, dv_ref, x_ref, out_ref):
         first = (pl.program_id(0) == 0) & (pl.program_id(1) == 0)
@@ -896,7 +898,7 @@
         ],
         out_specs=pl.BlockSpec((2 * local, depth), lambda i, j: (0, 0)),
         out_shape=jax.ShapeDtypeStruct((2 * local, depth), f32),
-        compiler_params=pltpu.CompilerParams(vmem_limit_bytes=40 << 20),
+        compiler_params=pltpu.CompilerParams(vmem_limit_bytes=60 << 20),
         cost_estimate=pl.CostEstimate(
             flops=4 * items * keys * depth * local,
             bytes_accessed=2 * items * keys * (depth + 2 * local),
@@ -956,7 +958,7 @@
             jax.ShapeDtypeStruct((rows, width), f32),
             jax.ShapeDtypeStruct((rows, width), f32),
         ],
-        compiler_params=pltpu.CompilerParams(vmem_limit_bytes=52 << 20),
+        compiler_params=pltpu.CompilerParams(vmem_limit_bytes=60 << 20),
         cost_estimate=pl.CostEstimate(
             flops=8 * slots * rows * width * hidden,
             bytes_accessed=4 * slots * width * hidden,
@@ -1000,7 +1002,7 @@
         else pl.BlockSpec((seq, size, share), lambda t, c: (t, first // size + c, 0)),
         out_shape=jax.ShapeDtypeStruct(shape, bf16),
         input_output_aliases={} if buffer is None else {2: 0},
-        compiler_params=pltpu.CompilerParams(vmem_limit_bytes=40 << 20),
+        compiler_params=pltpu.CompilerParams(vmem_limit_bytes=60 << 20),
         cost_estimate=pl.CostEstimate(
             flops=4 * tp * count * depth * width,
             bytes_accessed=4 * tp * (count + width) * depth,
@@ -1063,7 +1065,7 @@
             jax.ShapeDtypeStruct((items, 2, width), f32),
         ],
         input_output_aliases={} if buffer is None else {5: 0},
-        compiler_params=pltpu.CompilerParams(vmem_limit_bytes=52 << 20),
+        compiler_params=pltpu.CompilerParams(vmem_limit_bytes=60 << 20),
         cost_estimate=pl.CostEstimate(
             flops=2 * items * queries * width * tp * local,
             bytes_accessed=10 * items * queries * width,

time: 1080 us -> 1070 us (level)
  local copies, waits for them, and re-layouts: 182 us -> 133 us
  Pallas kernels: 524 us -> 544 us
  waiting for transfers between devices: 159 us -> 176 us
    unnamed x175 -> x77, local copies, waits for them, and re-layouts: 80.3 us -> 24.3 us
    all_to_all x19, waiting for transfers between devices: 135 us -> 147 us  [exchange(): return lax.all_to_all(x, axis, 0, 0, tiled=True)]
    pallas_call x5, Pallas kernels: 38.7 us -> 49.9 us  [weight_terms(): pl.pallas_call(kernel, grid=(tp, 2), in_specs=[pl.BlockSpec(lhs_block, lh...]
  transfers between devices with their start and end apart: 35 -> 35, of which waited for: 14 -> 13; matrix products, arithmetic and copies ran while one was open for 14% -> 14% of each run, Pallas kernels for 44% -> 46%
where the time goes in v7:
time: 1070 us; the launch traced here: 1050 us
  Pallas kernels  544 us (51%)
  waiting for transfers between devices  176 us (16%)
  local copies, waits for them, and re-layouts  133 us (12%)
  starting transfers between devices  110 us (10%)
  other arithmetic  54.3 us (5%)
  matrix products  22.4 us (2%)
  between operations  15.3 us (1%)
    all_to_all x19, waiting for transfers between devices, exchange(): return lax.all_to_all(x, axis, 0, 0, tiled=True)  147 us
    pallas_call x2, Pallas kernels, cross_backward(): pl.pallas_call(kernel, grid=(items, heads), in_specs=[rows_spec, tiles_sp...  102 us
    all_to_all x19, starting transfers between devices, exchange(): return lax.all_to_all(x, axis, 0, 0, tiled=True)  87.7 us
    pallas_call x3, Pallas kernels, self_backward(): pl.pallas_call(kernel, grid=(blocks,), in_specs=part_specs(parts, half) +...  83.2 us
    pallas_call x1, Pallas kernels, cross_forward(): pl.pallas_call(kernel, grid=(items, heads // 2), in_specs=[pl.BlockSpec((...  53.7 us
    pallas_call x5, Pallas kernels, weight_terms(): pl.pallas_call(kernel, grid=(tp, 2), in_specs=[pl.BlockSpec(lhs_block, lh...  49.9 us
    pallas_call x3, Pallas kernels, self_forward(): pl.pallas_call(kernel, grid=(blocks,), in_specs=part_specs(parts, half),...  42.9 us
    pallas_call x1, Pallas kernels, feed_forward(): pl.pallas_call(kernel, grid=(slots,), in_specs=[rows_spec, rows_spec, pl....  39.2 us
  transfers between devices with their start and end apart: 35, of which 13 were waited for; matrix products, arithmetic and copies ran while one was open for 14% of the time, Pallas kernels for 46%

profile of v7, /device:TPU:0, one launch (start us, length us, event | category | flops | bytes accessed | tf_op | source)
XLA Modules:
  0.0 1054.0 jit_solution(14649559138396194206)
XLA Ops:
  33.3 27.7 %key_value_kernel.1 = (bf16[6,4096,256]{2,1,0:T(8,128)(2,1)}, bf16[6,256,4096]{2,1,0:T(8,128)(2,1)}) custom-call(bf16[6,4096,768]{2,1,0:T(8,128)(2,1)} %bitcast.245, bf16[768,256]{1,0:T(8,128)(2,1)} %wk_ref.1, bf16[256,768]{1,0:T(8,128)(2,1)} %bitcast.319), custom_call_target="tpu_custom_call" | custom-call | flops 19327352832 | bytes 62914560 | tf_op jit(solution)/shard_map/key_value_kernel/pallas_call | solution.py:846
  81.6 53.7 %cross_forward.1 = (bf16[4,6,96,256]{3,2,1,0:T(8,128)(2,1)}, f32[4,6,96,256]{3,2,1,0:T(8,128)}, f32[6,4,8,384]{3,2,1,0:T(8,128)}) custom-call(bf16[6,384,256]{2,1,0:T(8,128)(2,1)} %get-tuple-element.109.q_ref, bf16[6,4096,256]{2,1,0:T(8,128)(2,1)} %get-tuple-element.110.k_ref, bf16[6,256,4096]{2,1,0:T(8,128)(2,1)} %get-tuple-element.111.vt_ref), custom_call_target="tpu_custom_call" | custom-call | flops 38654705664 | bytes 27525120 | tf_op jit(solution)/shard_map/cross_forward/pallas_call | solution.py:174
  143.9 18.1 %all-to-all-done.x_ref.refs_0_ = bf16[4,6,96,256]{3,2,1,0:T(8,128)(2,1)} async-done(((bf16[4,6,96,256]{3,2,1,0:T(8,128)(2,1)}), bf16[4,6,96,256]{3,2,1,0:T(8,128)(2,1)}, u32[]{:S(2)}, u32[]{:S(2)}) %all-to-all-start) | async-done | bytes 1179680 | tf_op jit(solution)/shard_map/all_to_all | solution.py:1079
  177.0 10.6 %project_pack.1 = bf16[3,2,8,2,144,128]{5,4,3,2,1,0:T(8,128)(2,1)} custom-call(bf16[576,1024]{1,0:T(8,128)(2,1)} %bitcast.274, bf16[8,768,1024]{2,1,0:T(8,128)(2,1)} %bitcast.236, bf16[8,768,1024]{2,1,0:T(8,128)(2,1)} %bitcast.237), custom_call_target="tpu_custom_call" | custom-call | flops 3623878656 | bytes 7471104 | tf_op jit(solution)/shard_map/project_pack/pallas_call | solution.py:493
  205.6 19.8 %all-to-all-done.1.refs_0_ = bf16[32,144,128]{2,1,0:T(8,128)(2,1)} async-done(((bf16[32,144,128]{2,1,0:T(8,128)(2,1)}), bf16[32,144,128]{2,1,0:T(8,128)(2,1)}, u32[]{:S(2)}, u32[]{:S(2)}) %all-to-all-start.1) | async-done | bytes 1179680 | tf_op jit(solution)/shard_map/all_to_all | solution.py:1079
  251.1 14.3 %self_forward.3 = (bf16[1536,128]{1,0:T(8,128)(2,1)}, f32[1536,128]{1,0:T(8,128)}, f32[4,8,768]{2,1,0:T(8,128)}) custom-call(bf16[32,144,128]{2,1,0:T(8,128)(2,1)} %all-to-all-done.1.refs_0_), custom_call_target="tpu_custom_call" | custom-call | flops 9663676416 | bytes 3145728 | tf_op jit(solution)/shard_map/self_forward/pallas_call | solution.py:351
  271.4 14.3 %self_forward.4 = (bf16[1536,128]{1,0:T(8,128)(2,1)}, f32[1536,128]{1,0:T(8,128)}, f32[4,8,768]{2,1,0:T(8,128)}) custom-call(bf16[32,144,128]{2,1,0:T(8,128)(2,1)} %all-to-all-done.4.refs_0_), custom_call_target="tpu_custom_call" | custom-call | flops 9663676416 | bytes 3145728 | tf_op jit(solution)/shard_map/self_forward/pallas_call | solution.py:351
  285.7 14.8 %all-to-all-done.2.refs_0_ = bf16[32,144,128]{2,1,0:T(8,128)(2,1)} async-done(((bf16[32,144,128]{2,1,0:T(8,128)(2,1)}), bf16[32,144,128]{2,1,0:T(8,128)(2,1)}, u32[]{:S(2)}, u32[]{:S(2)}) %all-to-all-start.2) | async-done | bytes 1179680 | tf_op jit(solution)/shard_map/all_to_all | solution.py:1079
  304.1 13.6 %all-to-all-done.5 = bf16[32,48,128]{2,1,0:T(8,128)(2,1)S(1)} async-done(((bf16[32,48,128]{2,1,0:T(8,128)(2,1)}), bf16[32,48,128]{2,1,0:T(8,128)(2,1)S(1)}, u32[]{:S(2)}, u32[]{:S(2)}) %all-to-all-start.5) | async-done | bytes 393248 | tf_op jit(solution)/shard_map/all_to_all | solution.py:1079
  320.3 14.3 %self_forward.5 = (bf16[1536,128]{1,0:T(8,128)(2,1)}, f32[1536,128]{1,0:T(8,128)}, f32[4,8,768]{2,1,0:T(8,128)}) custom-call(bf16[32,144,128]{2,1,0:T(8,128)(2,1)} %all-to-all-done.2.refs_0_), custom_call_target="tpu_custom_call" | custom-call | flops 9663676416 | bytes 3145728 | tf_op jit(solution)/shard_map/self_forward/pallas_call | solution.py:351
  340.7 13.6 %all-to-all-done.6 = bf16[32,48,128]{2,1,0:T(8,128)(2,1)S(1)} async-done(((bf16[32,48,128]{2,1,0:T(8,128)(2,1)}), bf16[32,48,128]{2,1,0:T(8,128)(2,1)S(1)}, u32[]{:S(2)}, u32[]{:S(2)}) %all-to-all-start.6) | async-done | bytes 393248 | tf_op jit(solution)/shard_map/all_to_all | solution.py:1079
  355.1 9.5 unpack_project.1
  370.4 39.2 %feed_forward.1 = (bf16[8,576,512]{2,1,0:T(8,128)(2,1)}, bf16[8,576,512]{2,1,0:T(8,128)(2,1)}, f32[576,1024]{1,0:T(8,128)}, f32[576,1024]{1,0:T(8,128)}) custom-call(bf16[576,1024]{1,0:T(8,128)(2,1)} %bitcast.294, bf16[576,1024]{1,0:T(8,128)(2,1)} %bitcast.269, bf16[8,1024,512]{2,1,0:T(8,128)(2,1)} %bitcast.324, bf16[8,512,1024]{2,1,0:T(8,128)(2,1)} %bitcast.325), custom_call_target="tpu_custom_call" | custom-call | flops 19327352832 | bytes 16777216 | tf_op jit(solution)/shard_map/feed_forward/pallas_call | solution.py:945
  449.6 12.1 %weight_terms.5.refs_2_ = bf16[2,4,4,2368,128]{4,3,2,1,0:T(8,128)(2,1)} custom-call(bf16[8,576,512]{2,1,0:T(8,128)(2,1)} %get-tuple-element.135.refs_0_, bf16[576,1024]{1,0:T(8,128)(2,1)} %bitcast.295), custom_call_target="tpu_custom_call" | custom-call | flops 4831838208 | bytes 13107200 | tf_op jit(solution)/shard_map/weight_terms/pallas_call | solution.py:992
  461.7 12.1 %weight_terms.6 = bf16[2,4,4,2368,128]{4,3,2,1,0:T(8,128)(2,1)} custom-call(bf16[8,576,512]{2,1,0:T(8,128)(2,1)} %get-tuple-element.134.refs_0_, bf16[576,1024]{1,0:T(8,128)(2,1)} %bitcast.270, bf16[2,4,4,2368,128]{4,3,2,1,0:T(8,128)(2,1)} %weight_terms.5.refs_2_), custom_call_target="tpu_custom_call", output_to_operand_aliasing={{}: (2, {})} | custom-call | flops 4831838208 | bytes 13107200 | tf_op jit(solution)/shard_map/weight_terms/pallas_call | solution.py:992
  492.0 27.6 %self_backward.3 = bf16[32,144,128]{2,1,0:T(8,128)(2,1)} custom-call(bf16[32,144,128]{2,1,0:T(8,128)(2,1)} %all-to-all-done.1.refs_0_, bf16[1536,128]{1,0:T(8,128)(2,1)} %bitcast.313, f32[1536,128]{1,0:T(8,128)} %get-tuple-element.137.refs_2_, f32[4,8,768]{2,1,0:T(8,128)} %get-tuple-element.138.refs_3_), custom_call_target="tpu_custom_call" | custom-call | flops 24159191040 | bytes 6291456 | tf_op jit(solution)/shard_map/self_backward/pallas_call | solution.py:437
  519.6 12.4 %fusion = bf16[4,4,2368,128]{3,2,1,0:T(8,128)(2,1)} fusion(bf16[4,4,2368,128]{3,2,1,0:T(8,128)(2,1)} %collective-permute-done.8, bf16[2,4,4,2368,128]{4,3,2,1,0:T(8,128)(2,1)} %bitcast_dynamic-update-slice_fusion, s32[]{:T(128)S(6)} %select_n.57), kind=kLoop, calls=%fused_computation.1 | loop fusion | flops 19398656 | bytes 29097988 | tf_op jit(solution)/shard_map/convert_element_type | solution.py:1355
  538.3 27.6 %self_backward.5 = bf16[32,144,128]{2,1,0:T(8,128)(2,1)} custom-call(bf16[32,144,128]{2,1,0:T(8,128)(2,1)} %all-to-all-done.4.refs_0_, bf16[1536,128]{1,0:T(8,128)(2,1)} %bitcast.314, f32[1536,128]{1,0:T(8,128)} %get-tuple-element.145.refs_2_, f32[4,8,768]{2,1,0:T(8,128)} %get-tuple-element.146.refs_3_), custom_call_target="tpu_custom_call" | custom-call | flops 24159191040 | bytes 6291456 | tf_op jit(solution)/shard_map/self_backward/pallas_call | solution.py:437
  572.3 27.9 %self_backward.4 = bf16[32,144,128]{2,1,0:T(8,128)(2,1)} custom-call(bf16[32,144,128]{2,1,0:T(8,128)(2,1)} %all-to-all-done.2.refs_0_, bf16[1536,128]{1,0:T(8,128)(2,1)} %bitcast.316, f32[1536,128]{1,0:T(8,128)} %get-tuple-element.140.refs_2_, f32[4,8,768]{2,1,0:T(8,128)} %get-tuple-element.141.refs_3_), custom_call_target="tpu_custom_call" | custom-call | flops 24159191040 | bytes 6291456 | tf_op jit(solution)/shard_map/self_backward/pallas_call | solution.py:437
  614.6 20.5 %all-to-all-done.9 = bf16[32,144,128]{2,1,0:T(8,128)(2,1)} async-done(((bf16[32,144,128]{2,1,0:T(8,128)(2,1)}), bf16[32,144,128]{2,1,0:T(8,128)(2,1)}, u32[]{:S(2)}, u32[]{:S(2)}) %all-to-all-start.9) | async-done | bytes 1179680 | tf_op jit(solution)/shard_map/all_to_all | solution.py:1079
  645.8 16.9 %collective-permute-done.6 = bf16[14,6,1,1024]{3,0,2,1:T(8,128)(2,1)} collective-permute-done((bf16[14,6,1,1024]{3,0,2,1:T(8,128)(2,1)S(1)}, bf16[14,6,1,1024]{3,0,2,1:T(8,128)(2,1)}, u32[]{:S(2)}, u32[]{:S(2)}) %collective-permute-start.6) | collective-permute-done | bytes 172064 | tf_op jit(solution)/shard_map/ppermute | solution.py:29
  662.7 11.9 %collective-permute-done.7 = bf16[14,6,1,1024]{3,0,2,1:T(8,128)(2,1)} collective-permute-done((bf16[14,6,1,1024]{3,0,2,1:T(8,128)(2,1)S(1)}, bf16[14,6,1,1024]{3,0,2,1:T(8,128)(2,1)}, u32[]{:S(2)}, u32[]{:S(2)}) %collective-permute-start.7) | collective-permute-done | bytes 172064 | tf_op jit(solution)/shard_map/ppermute | solution.py:30
  681.5 10.6 %reshape.358 = f32[14,6,10,4,4,80]{5,4,3,0,2,1:T(4,128)} reshape(f32[14,6,10,1280]{3,0,2,1:T(8,128)} %fusion.1) | data formatting | bytes 8601600 | tf_op jit(solution)/shard_map/reshape | solution.py:1336
  705.2 12.6 %unpack_back.1 = (bf16[8,576,384]{2,1,0:T(8,128)(2,1)}, f32[576,1024]{1,0:T(8,128)}) custom-call(bf16[2,8,2,144,128]{4,3,2,1,0:T(8,128)(2,1)} %bitcast.71.refs_0_, bf16[2,8,2,144,128]{4,3,2,1,0:T(8,128)(2,1)} %bitcast.74.refs_1_, bf16[2,8,2,144,128]{4,3,2,1,0:T(8,128)(2,1)} %bitcast.65.refs_2_, bf16[8,768,1024]{2,1,0:T(8,128)(2,1)} %bitcast.240, ...), custom_call_target="tpu_custom_call" | custom-call | flops 3623878656 | bytes 2359296 | tf_op jit(solution)/shard_map/unpack_back/pallas_call | solution.py:632
  742.3 10.9 %weight_terms.7.refs_2_ = bf16[32,1296,128]{2,1,0:T(8,128)(2,1)} custom-call(bf16[8,576,384]{2,1,0:T(8,128)(2,1)} %get-tuple-element.151.refs_0_, bf16[576,1024]{1,0:T(8,128)(2,1)} %bitcast.275), custom_call_target="tpu_custom_call" | custom-call | flops 3623878656 | bytes 9830400 | tf_op jit(solution)/shard_map/weight_terms/pallas_call | solution.py:992
  781.3 51.1 %cross_backward.2 = (bf16[3,384,256]{2,1,0:T(8,128)(2,1)}, bf16[3,256,4096]{2,1,0:T(8,128)(2,1)}, bf16[3,256,4096]{2,1,0:T(8,128)(2,1)}) custom-call(bf16[6,384,256]{2,1,0:T(8,128)(2,1)} %get-tuple-element.109.q_ref, bf16[4,6,96,256]{3,2,1,0:T(8,128)(2,1)} %all-to-all-done.13.do_ref, f32[4,6,96,256]{3,2,1,0:T(8,128)} %get-tuple-element.156.o_ref, ...), custom_call_target="tpu_custom_call" | custom-call | flops 48318382080 | bytes 27525120 | tf_op jit(solution)/shard_map/cross_backward/pallas_call | solution.py:250
  848.7 51.0 %cross_backward.3 = (bf16[3,384,256]{2,1,0:T(8,128)(2,1)}, bf16[3,256,4096]{2,1,0:T(8,128)(2,1)}, bf16[3,256,4096]{2,1,0:T(8,128)(2,1)}) custom-call(bf16[6,384,256]{2,1,0:T(8,128)(2,1)} %get-tuple-element.109.q_ref, bf16[4,6,96,256]{3,2,1,0:T(8,128)(2,1)} %all-to-all-done.13.do_ref, f32[4,6,96,256]{3,2,1,0:T(8,128)} %get-tuple-element.156.o_ref, ...), custom_call_target="tpu_custom_call" | custom-call | flops 48318382080 | bytes 27525120 | tf_op jit(solution)/shard_map/cross_backward/pallas_call | solution.py:250
  906.9 16.8 %key_value_grads.2 = f32[512,768]{1,0:T(8,128)} custom-call(bf16[3,256,4096]{2,1,0:T(8,128)(2,1)} %get-tuple-element.176.dk_ref, bf16[3,256,4096]{2,1,0:T(8,128)(2,1)} %get-tuple-element.177.dv_ref, bf16[6,4096,768]{2,1,0:T(8,128)(2,1)} %bitcast.246), custom_call_target="tpu_custom_call" | custom-call | flops 9663676416 | bytes 31457280 | tf_op jit(solution)/shard_map/key_value_grads/pallas_call | solution.py:891
  923.8 10.7 %all-to-all-done.16.dq_ref = bf16[4,3,384,256]{3,2,1,0:T(8,128)(2,1)} async-done(((bf16[4,3,384,256]{3,2,1,0:T(8,128)(2,1)}), bf16[4,3,384,256]{3,2,1,0:T(8,128)(2,1)}, u32[]{:S(2)}, u32[]{:S(2)}) %all-to-all-start.16) | async-done | bytes 2359328 | tf_op jit(solution)/shard_map/all_to_all | solution.py:1079
  934.4 16.3 %key_value_grads.3 = f32[512,768]{1,0:T(8,128)} custom-call(bf16[3,256,4096]{2,1,0:T(8,128)(2,1)} %get-tuple-element.178.dk_ref, bf16[3,256,4096]{2,1,0:T(8,128)(2,1)} %get-tuple-element.179.dv_ref, bf16[6,4096,768]{2,1,0:T(8,128)(2,1)} %bitcast.247), custom_call_target="tpu_custom_call" | custom-call | flops 9663676416 | bytes 31457280 | tf_op jit(solution)/shard_map/key_value_grads/pallas_call | solution.py:891
  978.7 9.4 last_kernel.3
  988.9 17.5 %all-to-all-done.17 = bf16[8,320,256]{2,1,0:T(8,128)(2,1)} async-done(((bf16[8,320,256]{2,1,0:T(8,128)(2,1)}), bf16[8,320,256]{2,1,0:T(8,128)(2,1)}, u32[]{:S(2)}, u32[]{:S(2)}) %all-to-all-start.17) | async-done | bytes 1310752 | tf_op jit(solution)/shard_map/all_to_all | solution.py:1079
  (271 shorter events, 399.4 us)
Async XLA Ops:
  7.2 154.8 %all-gather.10.cloned.1.call-start = ((), (), s32[]{:S(2)}) async-start(), calls=%async_computation.25 | async-start | bytes 14155776 | tf_op jit(solution)/shard_map/all_gather | solution.py:1155
  18.4 352.0 %all-gather.12.cloned.1.call-start = ((), (), s32[]{:S(2)}) async-start(), calls=%async_computation.26 | async-start | bytes 9437184 | tf_op jit(solution)/shard_map/all_gather | solution.py:1155
  20.8 349.7 %all-gather.14.cloned.1.call-start = ((), (), s32[]{:S(2)}) async-start(), calls=%async_computation.27 | async-start | bytes 9437184 | tf_op jit(solution)/shard_map/all_gather | solution.py:1155
  22.1 41.7 %collective-permute-start.1 = (bf16[1,6,16,80]{3,2,1,0:T(8,128)(2,1)S(1)}, bf16[1,6,16,80]{3,2,1,0:T(8,128)(2,1)S(1)}, u32[]{:S(2)}, u32[]{:S(2)}) collective-permute-start(bf16[1,6,16,80]{3,2,1,0:T(8,128)(2,1)S(1)} %slice.201), channel_id=1, source_target_pairs={{4,0},{8,4},{12,8},{16,12},{20,16},{24,20},{28,24},{5,1},{9,5},{13... | collective-permute-start | bytes 46088 | tf_op jit(solution)/shard_map/ppermute | solution.py:30
  24.1 39.7 %collective-permute-start = (bf16[1,6,16,80]{3,2,1,0:T(8,128)(2,1)}, bf16[1,6,16,80]{3,2,1,0:T(8,128)(2,1)}, u32[]{:S(2)}, u32[]{:S(2)}) collective-permute-start(bf16[1,6,16,80]{3,2,1,0:T(8,128)(2,1)} %slice.199), channel_id=1, source_target_pairs={{0,4},{4,8},{8,12},{12,16},{16,20},{20,24},{24,28},{1,5},{5,9},{9,... | collective-permute-start | bytes 46088 | tf_op jit(solution)/shard_map/ppermute | solution.py:29
  135.3 26.7 %all-to-all-start = ((bf16[4,6,96,256]{3,2,1,0:T(8,128)(2,1)}), bf16[4,6,96,256]{3,2,1,0:T(8,128)(2,1)}, u32[]{:S(2)}, u32[]{:S(2)}) async-start(bf16[4,6,96,256]{3,2,1,0:T(8,128)(2,1)} %get-tuple-element.112), calls=%async_computation | async-start | bytes 2359296 | tf_op jit(solution)/shard_map/all_to_all | solution.py:1079
  191.4 34.1 %all-to-all-start.1 = ((bf16[32,144,128]{2,1,0:T(8,128)(2,1)}), bf16[32,144,128]{2,1,0:T(8,128)(2,1)}, u32[]{:S(2)}, u32[]{:S(2)}) async-start(bf16[32,144,128]{2,1,0:T(8,128)(2,1)} %bitcast.273), calls=%async_computation.1 | async-start | bytes 2359296 | tf_op jit(solution)/shard_map/all_to_all | solution.py:1079
  225.5 39.9 %all-to-all-start.4 = ((bf16[32,144,128]{2,1,0:T(8,128)(2,1)}), bf16[32,144,128]{2,1,0:T(8,128)(2,1)}, u32[]{:S(2)}, u32[]{:S(2)}) async-start(bf16[32,144,128]{2,1,0:T(8,128)(2,1)} %bitcast.272), calls=%async_computation.4 | async-start | bytes 2359296 | tf_op jit(solution)/shard_map/all_to_all | solution.py:1079
  265.3 35.2 %all-to-all-start.2 = ((bf16[32,144,128]{2,1,0:T(8,128)(2,1)}), bf16[32,144,128]{2,1,0:T(8,128)(2,1)}, u32[]{:S(2)}, u32[]{:S(2)}) async-start(bf16[32,144,128]{2,1,0:T(8,128)(2,1)} %bitcast.271), calls=%async_computation.2 | async-start | bytes 2359296 | tf_op jit(solution)/shard_map/all_to_all | solution.py:1079
  300.5 17.2 %all-to-all-start.5 = ((bf16[32,48,128]{2,1,0:T(8,128)(2,1)}), bf16[32,48,128]{2,1,0:T(8,128)(2,1)S(1)}, u32[]{:S(2)}, u32[]{:S(2)}) async-start(bf16[32,48,128]{2,1,0:T(8,128)(2,1)} %bitcast.318), calls=%async_computation.5 | async-start | bytes 786432 | tf_op jit(solution)/shard_map/all_to_all | solution.py:1079
  334.6 19.7 %all-to-all-start.6 = ((bf16[32,48,128]{2,1,0:T(8,128)(2,1)}), bf16[32,48,128]{2,1,0:T(8,128)(2,1)S(1)}, u32[]{:S(2)}, u32[]{:S(2)}) async-start(bf16[32,48,128]{2,1,0:T(8,128)(2,1)} %bitcast.317), calls=%async_computation.6 | async-start | bytes 786432 | tf_op jit(solution)/shard_map/all_to_all | solution.py:1079
  436.0 41.6 %all-to-all-start.7 = ((bf16[32,48,128]{2,1,0:T(8,128)(2,1)}), bf16[32,48,128]{2,1,0:T(8,128)(2,1)S(1)}, u32[]{:S(2)}, u32[]{:S(2)}) async-start(bf16[32,48,128]{2,1,0:T(8,128)(2,1)} %bitcast.56), calls=%async_computation.7 | async-start | bytes 786432 | tf_op jit(solution)/shard_map/all_to_all | solution.py:1079
  485.8 33.8 %collective-permute-start.8 = (bf16[4,4,2368,128]{3,2,1,0:T(8,128)(2,1)}, bf16[4,4,2368,128]{3,2,1,0:T(8,128)(2,1)}, u32[]{:S(2)}, u32[]{:S(2)}) collective-permute-start(bf16[4,4,2368,128]{3,2,1,0:T(8,128)(2,1)} %dynamic-slice_bitcast_fusion), channel_id=1, source_target_pairs={{0,4},{4,0},{8,12},{12,8},{16,20},{20,16},{24,28},{28,24},{1,5},{5... | collective-permute-start | bytes 29097992 | tf_op jit(solution)/shard_map/ppermute | solution.py:1353
  486.0 33.6 %all-to-all-start.11 = ((bf16[32,48,128]{2,1,0:T(8,128)(2,1)}), bf16[32,48,128]{2,1,0:T(8,128)(2,1)S(1)}, u32[]{:S(2)}, u32[]{:S(2)}) async-start(bf16[32,48,128]{2,1,0:T(8,128)(2,1)} %bitcast.72), calls=%async_computation.11 | async-start | bytes 786432 | tf_op jit(solution)/shard_map/all_to_all | solution.py:1079
  491.9 225.9 %reduce-scatter.10.cloned.1.call-start = ((), (), s32[]{:S(2)}) async-start(), calls=%async_computation.28 | async-start | bytes 12124160
  532.0 33.9 %all-to-all-start.8 = ((bf16[32,48,128]{2,1,0:T(8,128)(2,1)}), bf16[32,48,128]{2,1,0:T(8,128)(2,1)S(1)}, u32[]{:S(2)}, u32[]{:S(2)}) async-start(bf16[32,48,128]{2,1,0:T(8,128)(2,1)} %bitcast.55), calls=%async_computation.8 | async-start | bytes 786432 | tf_op jit(solution)/shard_map/all_to_all | solution.py:1079
  566.0 35.4 %all-to-all-start.12 = ((bf16[32,144,128]{2,1,0:T(8,128)(2,1)}), bf16[32,144,128]{2,1,0:T(8,128)(2,1)}, u32[]{:S(2)}, u32[]{:S(2)}) async-start(bf16[32,144,128]{2,1,0:T(8,128)(2,1)} %self_backward.5), calls=%async_computation.12 | async-start | bytes 2359296 | tf_op jit(solution)/shard_map/all_to_all | solution.py:1079
  601.3 33.7 %all-to-all-start.9 = ((bf16[32,144,128]{2,1,0:T(8,128)(2,1)}), bf16[32,144,128]{2,1,0:T(8,128)(2,1)}, u32[]{:S(2)}, u32[]{:S(2)}) async-start(bf16[32,144,128]{2,1,0:T(8,128)(2,1)} %self_backward.4), calls=%async_computation.9 | async-start | bytes 2359296 | tf_op jit(solution)/shard_map/all_to_all | solution.py:1079
  611.2 27.7 %collective-permute-start.4 = (bf16[1,6,8,1024]{3,0,2,1:T(2,128)(2,1)S(1)}, bf16[1,6,8,1024]{3,0,2,1:T(2,128)(2,1)S(1)}, u32[]{:S(2)}, u32[]{:S(2)}) collective-permute-start(bf16[1,6,8,1024]{3,0,2,1:T(2,128)(2,1)S(1)} %get-tuple-element.325), channel_id=1, source_target_pairs={{0,4},{4,8},{8,12},{12,16},{16,20},{20,24},{24,28},{1,5},{5,9},{9,... | collective-permute-start | bytes 294920 | tf_op jit(solution)/shard_map/ppermute | solution.py:29
  613.3 25.6 %collective-permute-start.5 = (bf16[1,6,8,1024]{3,0,2,1:T(2,128)(2,1)S(1)}, bf16[1,6,8,1024]{3,0,2,1:T(2,128)(2,1)S(1)}, u32[]{:S(2)}, u32[]{:S(2)}) collective-permute-start(bf16[1,6,8,1024]{3,0,2,1:T(2,128)(2,1)S(1)} %get-tuple-element.326), channel_id=1, source_target_pairs={{4,0},{8,4},{12,8},{16,12},{20,16},{24,20},{28,24},{5,1},{9,5},{13... | collective-permute-start | bytes 294920 | tf_op jit(solution)/shard_map/ppermute | solution.py:30
  635.1 70.1 %all-to-all-start.10 = ((bf16[32,144,128]{2,1,0:T(8,128)(2,1)}), bf16[32,144,128]{2,1,0:T(8,128)(2,1)}, u32[]{:S(2)}, u32[]{:S(2)}) async-start(bf16[32,144,128]{2,1,0:T(8,128)(2,1)} %self_backward.3), calls=%async_computation.10 | async-start | bytes 2359296 | tf_op jit(solution)/shard_map/all_to_all | solution.py:1079
  638.8 130.0 %reduce-scatter.6.cloned.1.call-start = ((), (), s32[]{:S(2)}) async-start(), calls=%async_computation.22 | async-start | bytes 3031040 | tf_op jit(solution)/shard_map/reduce_scatter | solution.py:1361
  640.1 22.6 %collective-permute-start.6 = (bf16[14,6,1,1024]{3,0,2,1:T(8,128)(2,1)S(1)}, bf16[14,6,1,1024]{3,0,2,1:T(8,128)(2,1)}, u32[]{:S(2)}, u32[]{:S(2)}) collective-permute-start(bf16[14,6,1,1024]{3,0,2,1:T(8,128)(2,1)S(1)} %get-tuple-element.321), channel_id=1, source_target_pairs={{0,1},{1,2},{2,3},{4,5},{5,6},{6,7},{8,9},{9,10},{10,11},{12,13},{... | collective-permute-start | bytes 516104 | tf_op jit(solution)/shard_map/ppermute | solution.py:29
  644.4 30.2 %collective-permute-start.7 = (bf16[14,6,1,1024]{3,0,2,1:T(8,128)(2,1)S(1)}, bf16[14,6,1,1024]{3,0,2,1:T(8,128)(2,1)}, u32[]{:S(2)}, u32[]{:S(2)}) collective-permute-start(bf16[14,6,1,1024]{3,0,2,1:T(8,128)(2,1)S(1)} %get-tuple-element.322), channel_id=1, source_target_pairs={{1,0},{2,1},{3,2},{5,4},{6,5},{7,6},{9,8},{10,9},{11,10},{13,12},{... | collective-permute-start | bytes 516104 | tf_op jit(solution)/shard_map/ppermute | solution.py:30
  737.7 31.1 %all-to-all-start.13 = ((bf16[4,6,96,256]{3,2,1,0:T(8,128)(2,1)}), bf16[4,6,96,256]{3,2,1,0:T(8,128)(2,1)}, u32[]{:S(2)}, u32[]{:S(2)}) async-start(bf16[4,6,96,256]{3,2,1,0:T(8,128)(2,1)} %out_back.1), calls=%async_computation.13 | async-start | bytes 2359296 | tf_op jit(solution)/shard_map/all_to_all | solution.py:1079
  742.0 266.7 %reduce-scatter.8.cloned.1.call-start = ((), (), s32[]{:S(2)}) async-start(), calls=%async_computation.23 | async-start | bytes 10948608 | tf_op jit(solution)/shard_map/reduce_scatter | solution.py:1365
  776.1 65.4 %all-to-all-start.14 = ((bf16[4,6,96,1024]{3,2,1,0:T(8,128)(2,1)}), bf16[4,6,96,1024]{3,2,1,0:T(8,128)(2,1)}, u32[]{:S(2)}, u32[]{:S(2)}) async-start(bf16[4,6,96,1024]{3,2,1,0:T(8,128)(2,1)} %broadcast_in_dim.16), calls=%async_computation.14 | async-start | bytes 9437184 | tf_op jit(solution)/shard_map/all_to_all | solution.py:1079
  844.2 55.5 %all-to-all-start.15 = ((bf16[4,3,384,256]{3,2,1,0:T(8,128)(2,1)}), bf16[4,3,384,256]{3,2,1,0:T(8,128)(2,1)}, u32[]{:S(2)}, u32[]{:S(2)}) async-start(bf16[4,3,384,256]{3,2,1,0:T(8,128)(2,1)} %broadcast_in_dim.17), calls=%async_computation.15 | async-start | bytes 4718592 | tf_op jit(solution)/shard_map/all_to_all | solution.py:1079
  902.4 32.0 %all-to-all-start.16 = ((bf16[4,3,384,256]{3,2,1,0:T(8,128)(2,1)}), bf16[4,3,384,256]{3,2,1,0:T(8,128)(2,1)}, u32[]{:S(2)}, u32[]{:S(2)}) async-start(bf16[4,3,384,256]{3,2,1,0:T(8,128)(2,1)} %broadcast_in_dim.18), calls=%async_computation.16 | async-start | bytes 4718592 | tf_op jit(solution)/shard_map/all_to_all | solution.py:1079
  906.9 133.2 %all-gather.8.cloned.1.call-start = ((), (), s32[]{:S(2)}) async-start(), calls=%async_computation.24 | async-start | bytes 2703360 | tf_op jit(solution)/shard_map/all_gather | solution.py:1544
  964.6 41.7 %all-to-all-start.17 = ((bf16[8,320,256]{2,1,0:T(8,128)(2,1)}), bf16[8,320,256]{2,1,0:T(8,128)(2,1)}, u32[]{:S(2)}, u32[]{:S(2)}) async-start(bf16[8,320,256]{2,1,0:T(8,128)(2,1)} %pad_maximum_fusion.2), calls=%async_computation.17 | async-start | bytes 2621440 | tf_op jit(solution)/shard_map/all_to_all | solution.py:1079
  1011.5 25.8 %all-to-all-start.18 = ((f32[32,40,128]{2,1,0:T(8,128)}), f32[32,40,128]{2,1,0:T(8,128)S(1)}, u32[]{:S(2)}, u32[]{:S(2)}) async-start(f32[32,40,128]{2,1,0:T(8,128)} %broadcast_in_dim.19), calls=%async_computation.20 | async-start | bytes 1310720 | tf_op jit(solution)/shard_map/all_to_all | solution.py:1079
  (31 other events, 714.3 us)
Sparse Core Ops, SparseCore 0:
  18.5 76.3 all-gather.9
  96.8 65.4 all-gather.11
  164.2 67.6 all-gather.13
  532.1 145.8 reduce-scatter.9
  718.0 49.0 reduce-scatter.5
  774.1 164.1 reduce-scatter.7
  959.3 69.6 all-gather.7

commit v8 on v7

--- a/solution.py
+++ b/solution.py
@@ -1332,12 +1332,6 @@
     )
 
     widened = with_halo(out_tile, (("seq", 0), ("tp", 2)), 1)
-    taps = dot("ricd,dt->rict", widened, w_deconv)
-    taps = taps.reshape(rows_here + 2, items, cols_here + 2, 4, 4, COUT)
-    planes = spread_taps(
-        taps, upper_keep[:, None, None, None, None], lower_keep[:, None, None, None, None]
-    )
-    planes = planes + jnp.tile(deconv_bias, 2 * cols_here)
 
     def by_device(x):
         lead = x.shape[0] // tp
@@ -1414,11 +1408,18 @@
             )
         arrived = exchange(dso_send[turn], both_axes).reshape(devices * half, 2 * HEAD)
         if turn == 0:
-            arrived, terms_b = lax.optimization_barrier((arrived, terms_b))
+            arrived, terms_b, widened = lax.optimization_barrier((arrived, terms_b, widened))
         dso_mine.append(arrived)
         backward.append(
             self_backward(parts[turn], dso_mine[turn], *forward[turn][1:], devices, half)
         )
+    taps = dot("ricd,dt->rict", widened, w_deconv)
+    taps = taps.reshape(rows_here + 2, items, cols_here + 2, 4, 4, COUT)
+    planes = spread_taps(
+        taps, upper_keep[:, None, None, None, None], lower_keep[:, None, None, None, None]
+    )
+    planes = planes + jnp.tile(deconv_bias, 2 * cols_here)
+
     near_b = total_near(terms_b, (backward[0][0], dso_mine[min(1, turns - 1)]))
     if fast:
         blocks = [
@@ -1508,7 +1509,7 @@
     do_mine, terms_a = lax.optimization_barrier((do_mine, terms_a))
     terms_a, grad_up = lax.optimization_barrier((terms_a, grad_up))
     grad_three, grad_self_out, grad_out, grad_early = total(terms_a, *size_a)
-    first_part = items // 2
+    first_part = items - items // 3
     cross = (queries, do_mine, mixed_wide, cross_logs, keys, values_t)
     one = cross_backward(*cross, 0, first_part)
     one, middle_all = lax.optimization_barrier((one, middle_all))
@@ -1517,8 +1518,8 @@
     two = cross_backward(queries, do_late, *cross[2:], first_part, items - first_part)
     one, two, dq_one = lax.optimization_barrier((one, two, dq_one))
     dq_two = gather(two[0], "tp")
-    two, dq_two = lax.optimization_barrier((two, dq_two))
-    dq_cross = jnp.concatenate([one[0], two[0]], axis=0)
+    grad_query = dot("iqd,iqe->de", first_in, jnp.concatenate([one[0], two[0]], axis=0))
+    two, dq_two, grad_query = lax.optimization_barrier((two, dq_two, grad_query))
     grad_three = grad_three.reshape(2, 3 * slot_width, share)
     grad_pair = grad_three[:, : 2 * slot_width].reshape(2, slot_heads, 2, HEAD, share)
     grad_self_key = grad_pair[:, :, 0].reshape(local, share).T
@@ -1533,7 +1534,7 @@
     ).T
     last = jnp.concatenate(
         [
-            by_seq(dot("iqd,iqe->de", first_in, dq_cross)),
+            by_seq(grad_query),
             by_seq(grad_image[:, :local]),
             by_seq(grad_image[:, local:]),
         ],

time: 1070 us -> 1020 us (0.953)
  waiting for transfers between devices: 176 us -> 121 us
  blocking collectives: 0 us -> 19.4 us
    all_to_all x19 -> x18, waiting for transfers between devices: 147 us -> 118 us  [exchange(): return lax.all_to_all(x, axis, 0, 0, tiled=True)]
    all_to_all x0 -> x1, blocking collectives: none -> 19.4 us  [exchange(): return lax.all_to_all(x, axis, 0, 0, tiled=True)]
    ppermute x4, waiting for transfers between devices: 16.9 us -> 1.59 us  [with_halo(): before = lax.ppermute(last, axis, up)]
    all_to_all x19 -> x18, starting transfers between devices: 87.7 us -> 82.1 us  [exchange(): return lax.all_to_all(x, axis, 0, 0, tiled=True)]
    unnamed x77 -> x62, local copies, waits for them, and re-layouts: 24.3 us -> 23.3 us
  transfers between devices with their start and end apart: 35 -> 34, of which waited for: 13 -> 12; matrix products, arithmetic and copies ran while one was open for 14% -> 15% of each run, Pallas kernels for 46% -> 48%
where the time goes in v8:
time: 1020 us; the launch traced here: 1010 us
  Pallas kernels  542 us (53%)
  local copies, waits for them, and re-layouts  129 us (13%)
  waiting for transfers between devices  121 us (12%)
  starting transfers between devices  107 us (10%)
  other arithmetic  52.7 us (5%)
  matrix products  21.6 us (2%)
  blocking collectives  19.4 us (2%)
  between operations  15.3 us (2%)
    all_to_all x18, waiting for transfers between devices, exchange(): return lax.all_to_all(x, axis, 0, 0, tiled=True)  118 us
    pallas_call x2, Pallas kernels, cross_backward(): pl.pallas_call(kernel, grid=(items, heads), in_specs=[rows_spec, tiles_sp...  102 us
    pallas_call x3, Pallas kernels, self_backward(): pl.pallas_call(kernel, grid=(blocks,), in_specs=part_specs(parts, half) +...  82.9 us
    all_to_all x18, starting transfers between devices, exchange(): return lax.all_to_all(x, axis, 0, 0, tiled=True)  82.1 us
    pallas_call x1, Pallas kernels, cross_forward(): pl.pallas_call(kernel, grid=(items, heads // 2), in_specs=[pl.BlockSpec((...  53.9 us
    pallas_call x5, Pallas kernels, weight_terms(): pl.pallas_call(kernel, grid=(tp, 2), in_specs=[pl.BlockSpec(lhs_block, lh...  49.6 us
    pallas_call x3, Pallas kernels, self_forward(): pl.pallas_call(kernel, grid=(blocks,), in_specs=part_specs(parts, half),...  42.9 us
    pallas_call x1, Pallas kernels, feed_forward(): pl.pallas_call(kernel, grid=(slots,), in_specs=[rows_spec, rows_spec, pl....  39.1 us
  transfers between devices with their start and end apart: 34, of which 12 were waited for; matrix products, arithmetic and copies ran while one was open for 15% of the time, Pallas kernels for 48%

profile of v8, /device:TPU:0, one launch (start us, length us, event | category | flops | bytes accessed | tf_op | source)
XLA Modules:
  0.0 1008.5 jit_solution(8214530178001670506)
XLA Ops:
  34.8 27.7 %key_value_kernel.1 = (bf16[6,4096,256]{2,1,0:T(8,128)(2,1)}, bf16[6,256,4096]{2,1,0:T(8,128)(2,1)}) custom-call(bf16[6,4096,768]{2,1,0:T(8,128)(2,1)} %bitcast.243, bf16[768,256]{1,0:T(8,128)(2,1)} %wk_ref.1, bf16[256,768]{1,0:T(8,128)(2,1)} %bitcast.310), custom_call_target="tpu_custom_call" | custom-call | flops 19327352832 | bytes 62914560 | tf_op jit(solution)/shard_map/key_value_kernel/pallas_call | solution.py:846
  83.8 53.9 %cross_forward.1 = (bf16[4,6,96,256]{3,2,1,0:T(8,128)(2,1)}, f32[4,6,96,256]{3,2,1,0:T(8,128)}, f32[6,4,8,384]{3,2,1,0:T(8,128)}) custom-call(bf16[6,384,256]{2,1,0:T(8,128)(2,1)} %get-tuple-element.110.q_ref, bf16[6,4096,256]{2,1,0:T(8,128)(2,1)} %get-tuple-element.111.k_ref, bf16[6,256,4096]{2,1,0:T(8,128)(2,1)} %get-tuple-element.112.vt_ref), custom_call_target="tpu_custom_call" | custom-call | flops 38654705664 | bytes 27525120 | tf_op jit(solution)/shard_map/cross_forward/pallas_call | solution.py:174
  145.7 17.9 %all-to-all-done.x_ref.refs_0_ = bf16[4,6,96,256]{3,2,1,0:T(8,128)(2,1)} async-done(((bf16[4,6,96,256]{3,2,1,0:T(8,128)(2,1)}), bf16[4,6,96,256]{3,2,1,0:T(8,128)(2,1)}, u32[]{:S(2)}, u32[]{:S(2)}) %all-to-all-start) | async-done | bytes 1179680 | tf_op jit(solution)/shard_map/all_to_all | solution.py:1079
  163.5 8.9 out_project.1
  178.5 10.5 %project_pack.1 = bf16[3,2,8,2,144,128]{5,4,3,2,1,0:T(8,128)(2,1)} custom-call(bf16[576,1024]{1,0:T(8,128)(2,1)} %bitcast.268, bf16[8,768,1024]{2,1,0:T(8,128)(2,1)} %bitcast.234, bf16[8,768,1024]{2,1,0:T(8,128)(2,1)} %bitcast.235), custom_call_target="tpu_custom_call" | custom-call | flops 3623878656 | bytes 7471104 | tf_op jit(solution)/shard_map/project_pack/pallas_call | solution.py:493
  207.4 19.8 %all-to-all-done.1.refs_0_ = bf16[32,144,128]{2,1,0:T(8,128)(2,1)} async-done(((bf16[32,144,128]{2,1,0:T(8,128)(2,1)}), bf16[32,144,128]{2,1,0:T(8,128)(2,1)}, u32[]{:S(2)}, u32[]{:S(2)}) %all-to-all-start.1) | async-done | bytes 1179680 | tf_op jit(solution)/shard_map/all_to_all | solution.py:1079
  252.6 14.3 %self_forward.3 = (bf16[1536,128]{1,0:T(8,128)(2,1)}, f32[1536,128]{1,0:T(8,128)}, f32[4,8,768]{2,1,0:T(8,128)}) custom-call(bf16[32,144,128]{2,1,0:T(8,128)(2,1)} %all-to-all-done.1.refs_0_), custom_call_target="tpu_custom_call" | custom-call | flops 9663676416 | bytes 3145728 | tf_op jit(solution)/shard_map/self_forward/pallas_call | solution.py:351
  273.0 14.3 %self_forward.4 = (bf16[1536,128]{1,0:T(8,128)(2,1)}, f32[1536,128]{1,0:T(8,128)}, f32[4,8,768]{2,1,0:T(8,128)}) custom-call(bf16[32,144,128]{2,1,0:T(8,128)(2,1)} %all-to-all-done.4.refs_0_), custom_call_target="tpu_custom_call" | custom-call | flops 9663676416 | bytes 3145728 | tf_op jit(solution)/shard_map/self_forward/pallas_call | solution.py:351
  287.3 14.8 %all-to-all-done.2.refs_0_ = bf16[32,144,128]{2,1,0:T(8,128)(2,1)} async-done(((bf16[32,144,128]{2,1,0:T(8,128)(2,1)}), bf16[32,144,128]{2,1,0:T(8,128)(2,1)}, u32[]{:S(2)}, u32[]{:S(2)}) %all-to-all-start.2) | async-done | bytes 1179680 | tf_op jit(solution)/shard_map/all_to_all | solution.py:1079
  305.6 13.6 %all-to-all-done.5 = bf16[32,48,128]{2,1,0:T(8,128)(2,1)S(1)} async-done(((bf16[32,48,128]{2,1,0:T(8,128)(2,1)}), bf16[32,48,128]{2,1,0:T(8,128)(2,1)S(1)}, u32[]{:S(2)}, u32[]{:S(2)}) %all-to-all-start.5) | async-done | bytes 393248 | tf_op jit(solution)/shard_map/all_to_all | solution.py:1079
  321.9 14.3 %self_forward.5 = (bf16[1536,128]{1,0:T(8,128)(2,1)}, f32[1536,128]{1,0:T(8,128)}, f32[4,8,768]{2,1,0:T(8,128)}) custom-call(bf16[32,144,128]{2,1,0:T(8,128)(2,1)} %all-to-all-done.2.refs_0_), custom_call_target="tpu_custom_call" | custom-call | flops 9663676416 | bytes 3145728 | tf_op jit(solution)/shard_map/self_forward/pallas_call | solution.py:351
  342.3 13.6 %all-to-all-done.6 = bf16[32,48,128]{2,1,0:T(8,128)(2,1)S(1)} async-done(((bf16[32,48,128]{2,1,0:T(8,128)(2,1)}), bf16[32,48,128]{2,1,0:T(8,128)(2,1)S(1)}, u32[]{:S(2)}, u32[]{:S(2)}) %all-to-all-start.6) | async-done | bytes 393248 | tf_op jit(solution)/shard_map/all_to_all | solution.py:1079
  356.6 9.5 unpack_project.1
  372.0 39.1 %feed_forward.1 = (bf16[8,576,512]{2,1,0:T(8,128)(2,1)}, bf16[8,576,512]{2,1,0:T(8,128)(2,1)}, f32[576,1024]{1,0:T(8,128)}, f32[576,1024]{1,0:T(8,128)}) custom-call(bf16[576,1024]{1,0:T(8,128)(2,1)} %bitcast.289, bf16[576,1024]{1,0:T(8,128)(2,1)} %bitcast.263, bf16[8,1024,512]{2,1,0:T(8,128)(2,1)} %bitcast.317, bf16[8,512,1024]{2,1,0:T(8,128)(2,1)} %bitcast.318), custom_call_target="tpu_custom_call" | custom-call | flops 19327352832 | bytes 16777216 | tf_op jit(solution)/shard_map/feed_forward/pallas_call | solution.py:945
  441.1 12.1 %weight_terms.5.refs_2_ = bf16[2,4,4,2368,128]{4,3,2,1,0:T(8,128)(2,1)} custom-call(bf16[8,576,512]{2,1,0:T(8,128)(2,1)} %get-tuple-element.136.refs_0_, bf16[576,1024]{1,0:T(8,128)(2,1)} %bitcast.290), custom_call_target="tpu_custom_call" | custom-call | flops 4831838208 | bytes 13107200 | tf_op jit(solution)/shard_map/weight_terms/pallas_call | solution.py:992
  458.9 12.1 %weight_terms.6 = bf16[2,4,4,2368,128]{4,3,2,1,0:T(8,128)(2,1)} custom-call(bf16[8,576,512]{2,1,0:T(8,128)(2,1)} %get-tuple-element.135.refs_0_, bf16[576,1024]{1,0:T(8,128)(2,1)} %bitcast.264, bf16[2,4,4,2368,128]{4,3,2,1,0:T(8,128)(2,1)} %weight_terms.5.refs_2_), custom_call_target="tpu_custom_call", output_to_operand_aliasing={{}: (2, {})} | custom-call | flops 4831838208 | bytes 13107200 | tf_op jit(solution)/shard_map/weight_terms/pallas_call | solution.py:992
  511.0 27.6 %self_backward.3 = bf16[32,144,128]{2,1,0:T(8,128)(2,1)} custom-call(bf16[32,144,128]{2,1,0:T(8,128)(2,1)} %all-to-all-done.1.refs_0_, bf16[1536,128]{1,0:T(8,128)(2,1)} %bitcast.56.refs_1_, f32[1536,128]{1,0:T(8,128)} %get-tuple-element.138.refs_2_, f32[4,8,768]{2,1,0:T(8,128)} %get-tuple-element.139.refs_3_), custom_call_target="tpu_custom_call" | custom-call | flops 24159191040 | bytes 6291456 | tf_op jit(solution)/shard_map/self_backward/pallas_call | solution.py:437
  538.6 12.4 %fusion = bf16[4,4,2368,128]{3,2,1,0:T(8,128)(2,1)} fusion(bf16[4,4,2368,128]{3,2,1,0:T(8,128)(2,1)} %collective-permute-done.8, bf16[2,4,4,2368,128]{4,3,2,1,0:T(8,128)(2,1)} %bitcast_dynamic-update-slice_fusion, s32[]{:T(128)S(6)} %select_n.57), kind=kLoop, calls=%fused_computation.1 | loop fusion | flops 19398656 | bytes 29097988 | tf_op jit(solution)/shard_map/convert_element_type | solution.py:1349
  551.1 19.4 %all_to_all.95 = bf16[32,48,128]{2,1,0:T(8,128)(2,1)} all-to-all(bf16[32,48,128]{2,1,0:T(8,128)(2,1)S(1)} %bitcast.281), channel_id=1, replica_groups=mesh['seq'=8,'tp'=4] {'seq','tp'}, dimensions={0} | all-to-all | bytes 786432 | tf_op jit(solution)/shard_map/all_to_all | solution.py:1079
  574.1 27.6 %self_backward.4 = bf16[32,144,128]{2,1,0:T(8,128)(2,1)} custom-call(bf16[32,144,128]{2,1,0:T(8,128)(2,1)} %all-to-all-done.2.refs_0_, bf16[1536,128]{1,0:T(8,128)(2,1)} %bitcast.309, f32[1536,128]{1,0:T(8,128)} %get-tuple-element.141.refs_2_, f32[4,8,768]{2,1,0:T(8,128)} %get-tuple-element.142.refs_3_), custom_call_target="tpu_custom_call" | custom-call | flops 24159191040 | bytes 6291456 | tf_op jit(solution)/shard_map/self_backward/pallas_call | solution.py:437
  608.0 27.6 %self_backward.5 = bf16[32,144,128]{2,1,0:T(8,128)(2,1)} custom-call(bf16[32,144,128]{2,1,0:T(8,128)(2,1)} %all-to-all-done.4.refs_0_, bf16[1536,128]{1,0:T(8,128)(2,1)} %bitcast.305, f32[1536,128]{1,0:T(8,128)} %get-tuple-element.147.refs_2_, f32[4,8,768]{2,1,0:T(8,128)} %get-tuple-element.148.refs_3_), custom_call_target="tpu_custom_call" | custom-call | flops 24159191040 | bytes 6291456 | tf_op jit(solution)/shard_map/self_backward/pallas_call | solution.py:437
  649.8 10.4 %reshape.358 = f32[14,6,10,4,4,80]{5,4,3,0,2,1:T(4,128)} reshape(f32[14,6,10,1280]{3,0,2,1:T(8,128)} %fusion.1) | data formatting | bytes 8601600 | tf_op jit(solution)/shard_map/reshape | solution.py:1417
  673.3 12.7 %unpack_back.1 = (bf16[8,576,384]{2,1,0:T(8,128)(2,1)}, f32[576,1024]{1,0:T(8,128)}) custom-call(bf16[2,8,2,144,128]{4,3,2,1,0:T(8,128)(2,1)} %bitcast.70.refs_0_, bf16[2,8,2,144,128]{4,3,2,1,0:T(8,128)(2,1)} %bitcast.73.refs_1_, bf16[2,8,2,144,128]{4,3,2,1,0:T(8,128)(2,1)} %bitcast.64.refs_2_, bf16[8,768,1024]{2,1,0:T(8,128)(2,1)} %bitcast.238, ...), custom_call_target="tpu_custom_call" | custom-call | flops 3623878656 | bytes 2359296 | tf_op jit(solution)/shard_map/unpack_back/pallas_call | solution.py:632
  710.9 10.5 %weight_terms.7.refs_2_ = bf16[32,1296,128]{2,1,0:T(8,128)(2,1)} custom-call(bf16[8,576,384]{2,1,0:T(8,128)(2,1)} %get-tuple-element.153.refs_0_, bf16[576,1024]{1,0:T(8,128)(2,1)} %bitcast.269), custom_call_target="tpu_custom_call" | custom-call | flops 3623878656 | bytes 9830400 | tf_op jit(solution)/shard_map/weight_terms/pallas_call | solution.py:992
  749.2 66.8 %cross_backward.2 = (bf16[4,384,256]{2,1,0:T(8,128)(2,1)}, bf16[4,256,4096]{2,1,0:T(8,128)(2,1)}, bf16[4,256,4096]{2,1,0:T(8,128)(2,1)}) custom-call(bf16[6,384,256]{2,1,0:T(8,128)(2,1)} %get-tuple-element.110.q_ref, bf16[4,6,96,256]{3,2,1,0:T(8,128)(2,1)} %all-to-all-done.13.do_ref, f32[4,6,96,256]{3,2,1,0:T(8,128)} %get-tuple-element.158.o_ref, ...), custom_call_target="tpu_custom_call" | custom-call | flops 64424509440 | bytes 36700160 | tf_op jit(solution)/shard_map/cross_backward/pallas_call | solution.py:250
  823.8 35.2 %cross_backward.3 = (bf16[2,384,256]{2,1,0:T(8,128)(2,1)}, bf16[2,256,4096]{2,1,0:T(8,128)(2,1)}, bf16[2,256,4096]{2,1,0:T(8,128)(2,1)}) custom-call(bf16[6,384,256]{2,1,0:T(8,128)(2,1)} %get-tuple-element.110.q_ref, bf16[4,6,96,256]{3,2,1,0:T(8,128)(2,1)} %all-to-all-done.13.do_ref, f32[4,6,96,256]{3,2,1,0:T(8,128)} %get-tuple-element.158.o_ref, ...), custom_call_target="tpu_custom_call" | custom-call | flops 32212254720 | bytes 18350080 | tf_op jit(solution)/shard_map/cross_backward/pallas_call | solution.py:250
  859.0 9.1 all-to-all-done.15.dq_ref
  879.8 19.9 %key_value_grads.2 = f32[512,768]{1,0:T(8,128)} custom-call(bf16[4,256,4096]{2,1,0:T(8,128)(2,1)} %get-tuple-element.178.dk_ref, bf16[4,256,4096]{2,1,0:T(8,128)(2,1)} %get-tuple-element.179.dv_ref, bf16[6,4096,768]{2,1,0:T(8,128)(2,1)} %bitcast.244), custom_call_target="tpu_custom_call" | custom-call | flops 12884901888 | bytes 41943040 | tf_op jit(solution)/shard_map/key_value_grads/pallas_call | solution.py:891
  899.8 12.4 %key_value_grads.3 = f32[512,768]{1,0:T(8,128)} custom-call(bf16[2,256,4096]{2,1,0:T(8,128)(2,1)} %get-tuple-element.180.dk_ref, bf16[2,256,4096]{2,1,0:T(8,128)(2,1)} %get-tuple-element.181.dv_ref, bf16[6,4096,768]{2,1,0:T(8,128)(2,1)} %bitcast.245), custom_call_target="tpu_custom_call" | custom-call | flops 6442450944 | bytes 20971520 | tf_op jit(solution)/shard_map/key_value_grads/pallas_call | solution.py:891
  925.6 11.4 %last_kernel.2 = (f32[12,6,32,1024]{3,2,1,0:T(8,128)}, f32[4,2,1024]{2,1,0:T(2,128)}) custom-call(bf16[12,6,32,1024]{3,2,1,0:T(8,128)(2,1)} %x_ref.5, f32[6,1,1024]{2,1,0:T(1,128)} %get-tuple-element.373.scale_ref, bf16[4,6,96,1024]{3,2,1,0:T(8,128)(2,1)} %all-to-all-done.14.middle_ref, bf16[4,4,384,256]{3,2,1,0:T(8,128)(2,1)} %all-to-all-done.15.dq_ref, ...), custom_call_target="tpu_custom_call" | custom-call | flops 3221225472 | bytes 15728640 | tf_op jit(solution)/shard_map/last_kernel/pallas_call | solution.py:1048
  945.1 14.4 %all-to-all-done.17 = bf16[8,320,256]{2,1,0:T(8,128)(2,1)} async-done(((bf16[8,320,256]{2,1,0:T(8,128)(2,1)}), bf16[8,320,256]{2,1,0:T(8,128)(2,1)}, u32[]{:S(2)}, u32[]{:S(2)}) %all-to-all-start.17) | async-done | bytes 1310752 | tf_op jit(solution)/shard_map/all_to_all | solution.py:1079
  982.7 12.0 %all-to-all-done.18 = f32[32,40,128]{2,1,0:T(8,128)S(1)} async-done(((f32[32,40,128]{2,1,0:T(8,128)}), f32[32,40,128]{2,1,0:T(8,128)S(1)}, u32[]{:S(2)}, u32[]{:S(2)}) %all-to-all-start.18) | async-done | bytes 655392 | tf_op jit(solution)/shard_map/all_to_all | solution.py:1079
  (259 shorter events, 367.1 us)
Async XLA Ops:
  7.2 156.4 %all-gather.10.cloned.1.call-start = ((), (), s32[]{:S(2)}) async-start(), calls=%async_computation.25 | async-start | bytes 14155776 | tf_op jit(solution)/shard_map/all_gather | solution.py:1155
  20.0 352.0 %all-gather.12.cloned.1.call-start = ((), (), s32[]{:S(2)}) async-start(), calls=%async_computation.26 | async-start | bytes 9437184 | tf_op jit(solution)/shard_map/all_gather | solution.py:1155
  22.3 349.7 %all-gather.14.cloned.1.call-start = ((), (), s32[]{:S(2)}) async-start(), calls=%async_computation.27 | async-start | bytes 9437184 | tf_op jit(solution)/shard_map/all_gather | solution.py:1155
  23.7 41.6 %collective-permute-start.1 = (bf16[1,6,16,80]{3,2,1,0:T(8,128)(2,1)S(1)}, bf16[1,6,16,80]{3,2,1,0:T(8,128)(2,1)S(1)}, u32[]{:S(2)}, u32[]{:S(2)}) collective-permute-start(bf16[1,6,16,80]{3,2,1,0:T(8,128)(2,1)S(1)} %slice.201), channel_id=1, source_target_pairs={{4,0},{8,4},{12,8},{16,12},{20,16},{24,20},{28,24},{5,1},{9,5},{13... | collective-permute-start | bytes 46088 | tf_op jit(solution)/shard_map/ppermute | solution.py:30
  25.7 39.6 %collective-permute-start = (bf16[1,6,16,80]{3,2,1,0:T(8,128)(2,1)}, bf16[1,6,16,80]{3,2,1,0:T(8,128)(2,1)}, u32[]{:S(2)}, u32[]{:S(2)}) collective-permute-start(bf16[1,6,16,80]{3,2,1,0:T(8,128)(2,1)} %slice.199), channel_id=1, source_target_pairs={{0,4},{4,8},{8,12},{12,16},{16,20},{20,24},{24,28},{1,5},{5,9},{9,... | collective-permute-start | bytes 46088 | tf_op jit(solution)/shard_map/ppermute | solution.py:29
  66.2 16.0 %collective-permute-start.3 = (bf16[26,6,1,80]{3,0,2,1:T(8,128)(2,1)S(1)}, bf16[26,6,1,80]{3,0,2,1:T(8,128)(2,1)S(1)}, u32[]{:S(2)}, u32[]{:S(2)}) collective-permute-start(bf16[26,6,1,80]{3,0,2,1:T(8,128)(2,1)S(1)} %get-tuple-element.359), channel_id=1, source_target_pairs={{1,0},{2,1},{3,2},{5,4},{6,5},{7,6},{9,8},{10,9},{11,10},{13,12},{... | collective-permute-start | bytes 74888 | tf_op jit(solution)/shard_map/ppermute | solution.py:30
  67.5 14.7 %collective-permute-start.2 = (bf16[26,6,1,80]{3,0,2,1:T(8,128)(2,1)S(1)}, bf16[26,6,1,80]{3,0,2,1:T(8,128)(2,1)S(1)}, u32[]{:S(2)}, u32[]{:S(2)}) collective-permute-start(bf16[26,6,1,80]{3,0,2,1:T(8,128)(2,1)S(1)} %get-tuple-element.358), channel_id=1, source_target_pairs={{0,1},{1,2},{2,3},{4,5},{5,6},{6,7},{8,9},{9,10},{10,11},{12,13},{... | collective-permute-start | bytes 74888 | tf_op jit(solution)/shard_map/ppermute | solution.py:29
  137.6 25.9 %all-to-all-start = ((bf16[4,6,96,256]{3,2,1,0:T(8,128)(2,1)}), bf16[4,6,96,256]{3,2,1,0:T(8,128)(2,1)}, u32[]{:S(2)}, u32[]{:S(2)}) async-start(bf16[4,6,96,256]{3,2,1,0:T(8,128)(2,1)} %get-tuple-element.113), calls=%async_computation | async-start | bytes 2359296 | tf_op jit(solution)/shard_map/all_to_all | solution.py:1079
  192.9 34.4 %all-to-all-start.1 = ((bf16[32,144,128]{2,1,0:T(8,128)(2,1)}), bf16[32,144,128]{2,1,0:T(8,128)(2,1)}, u32[]{:S(2)}, u32[]{:S(2)}) async-start(bf16[32,144,128]{2,1,0:T(8,128)(2,1)} %bitcast.267), calls=%async_computation.1 | async-start | bytes 2359296 | tf_op jit(solution)/shard_map/all_to_all | solution.py:1079
  227.3 39.6 %all-to-all-start.4 = ((bf16[32,144,128]{2,1,0:T(8,128)(2,1)}), bf16[32,144,128]{2,1,0:T(8,128)(2,1)}, u32[]{:S(2)}, u32[]{:S(2)}) async-start(bf16[32,144,128]{2,1,0:T(8,128)(2,1)} %bitcast.266), calls=%async_computation.4 | async-start | bytes 2359296 | tf_op jit(solution)/shard_map/all_to_all | solution.py:1079
  266.9 35.1 %all-to-all-start.2 = ((bf16[32,144,128]{2,1,0:T(8,128)(2,1)}), bf16[32,144,128]{2,1,0:T(8,128)(2,1)}, u32[]{:S(2)}, u32[]{:S(2)}) async-start(bf16[32,144,128]{2,1,0:T(8,128)(2,1)} %bitcast.265), calls=%async_computation.2 | async-start | bytes 2359296 | tf_op jit(solution)/shard_map/all_to_all | solution.py:1079
  302.0 17.2 %all-to-all-start.5 = ((bf16[32,48,128]{2,1,0:T(8,128)(2,1)}), bf16[32,48,128]{2,1,0:T(8,128)(2,1)S(1)}, u32[]{:S(2)}, u32[]{:S(2)}) async-start(bf16[32,48,128]{2,1,0:T(8,128)(2,1)} %bitcast.308), calls=%async_computation.5 | async-start | bytes 786432 | tf_op jit(solution)/shard_map/all_to_all | solution.py:1079
  319.3 16.9 %all-to-all-start.3 = ((bf16[32,48,128]{2,1,0:T(8,128)(2,1)}), bf16[32,48,128]{2,1,0:T(8,128)(2,1)S(1)}, u32[]{:S(2)}, u32[]{:S(2)}) async-start(bf16[32,48,128]{2,1,0:T(8,128)(2,1)} %bitcast.306), calls=%async_computation.3 | async-start | bytes 786432 | tf_op jit(solution)/shard_map/all_to_all | solution.py:1079
  336.2 19.7 %all-to-all-start.6 = ((bf16[32,48,128]{2,1,0:T(8,128)(2,1)}), bf16[32,48,128]{2,1,0:T(8,128)(2,1)S(1)}, u32[]{:S(2)}, u32[]{:S(2)}) async-start(bf16[32,48,128]{2,1,0:T(8,128)(2,1)} %bitcast.307), calls=%async_computation.6 | async-start | bytes 786432 | tf_op jit(solution)/shard_map/all_to_all | solution.py:1079
  437.7 57.7 %all-to-all-start.7 = ((bf16[32,48,128]{2,1,0:T(8,128)(2,1)}), bf16[32,48,128]{2,1,0:T(8,128)(2,1)}, u32[]{:S(2)}, u32[]{:S(2)}) async-start(bf16[32,48,128]{2,1,0:T(8,128)(2,1)} %bitcast.55), calls=%async_computation.7 | async-start | bytes 786432 | tf_op jit(solution)/shard_map/all_to_all | solution.py:1079
  454.1 26.3 %collective-permute-start.5 = (bf16[1,6,8,1024]{3,2,1,0:T(8,128)(2,1)S(1)}, bf16[1,6,8,1024]{3,2,1,0:T(8,128)(2,1)S(1)}, u32[]{:S(2)}, u32[]{:S(2)}) collective-permute-start(bf16[1,6,8,1024]{3,2,1,0:T(8,128)(2,1)S(1)} %get-tuple-element.349), channel_id=1, source_target_pairs={{4,0},{8,4},{12,8},{16,12},{20,16},{24,20},{28,24},{5,1},{9,5},{13... | collective-permute-start | bytes 294920 | tf_op jit(solution)/shard_map/ppermute | solution.py:30
  455.4 25.0 %collective-permute-start.4 = (bf16[1,6,8,1024]{3,2,1,0:T(8,128)(2,1)S(1)}, bf16[1,6,8,1024]{3,2,1,0:T(8,128)(2,1)S(1)}, u32[]{:S(2)}, u32[]{:S(2)}) collective-permute-start(bf16[1,6,8,1024]{3,2,1,0:T(8,128)(2,1)S(1)} %get-tuple-element.348), channel_id=1, source_target_pairs={{0,4},{4,8},{8,12},{12,16},{16,20},{20,24},{24,28},{1,5},{5,9},{9,... | collective-permute-start | bytes 294920 | tf_op jit(solution)/shard_map/ppermute | solution.py:29
  503.5 35.1 %collective-permute-start.8 = (bf16[4,4,2368,128]{3,2,1,0:T(8,128)(2,1)}, bf16[4,4,2368,128]{3,2,1,0:T(8,128)(2,1)}, u32[]{:S(2)}, u32[]{:S(2)}) collective-permute-start(bf16[4,4,2368,128]{3,2,1,0:T(8,128)(2,1)} %dynamic-slice_bitcast_fusion), channel_id=1, source_target_pairs={{0,4},{4,0},{8,12},{12,8},{16,20},{20,16},{24,28},{28,24},{1,5},{5... | collective-permute-start | bytes 29097992 | tf_op jit(solution)/shard_map/ppermute | solution.py:1347
  503.7 34.9 %all-to-all-start.11 = ((bf16[32,48,128]{2,1,0:T(8,128)(2,1)}), bf16[32,48,128]{2,1,0:T(8,128)(2,1)S(1)}, u32[]{:S(2)}, u32[]{:S(2)}) async-start(bf16[32,48,128]{2,1,0:T(8,128)(2,1)} %bitcast.71), calls=%async_computation.11 | async-start | bytes 786432 | tf_op jit(solution)/shard_map/all_to_all | solution.py:1079
  510.8 175.3 %reduce-scatter.10.cloned.1.call-start = ((), (), s32[]{:S(2)}) async-start(), calls=%async_computation.28 | async-start | bytes 12124160
  570.5 32.7 %all-to-all-start.10 = ((bf16[32,144,128]{2,1,0:T(8,128)(2,1)}), bf16[32,144,128]{2,1,0:T(8,128)(2,1)}, u32[]{:S(2)}, u32[]{:S(2)}) async-start(bf16[32,144,128]{2,1,0:T(8,128)(2,1)} %self_backward.3), calls=%async_computation.10 | async-start | bytes 2359296 | tf_op jit(solution)/shard_map/all_to_all | solution.py:1079
  603.2 34.0 %all-to-all-start.9 = ((bf16[32,144,128]{2,1,0:T(8,128)(2,1)}), bf16[32,144,128]{2,1,0:T(8,128)(2,1)}, u32[]{:S(2)}, u32[]{:S(2)}) async-start(bf16[32,144,128]{2,1,0:T(8,128)(2,1)} %self_backward.4), calls=%async_computation.9 | async-start | bytes 2359296 | tf_op jit(solution)/shard_map/all_to_all | solution.py:1079
  637.1 36.2 %all-to-all-start.12 = ((bf16[32,144,128]{2,1,0:T(8,128)(2,1)}), bf16[32,144,128]{2,1,0:T(8,128)(2,1)}, u32[]{:S(2)}, u32[]{:S(2)}) async-start(bf16[32,144,128]{2,1,0:T(8,128)(2,1)} %self_backward.5), calls=%async_computation.12 | async-start | bytes 2359296 | tf_op jit(solution)/shard_map/all_to_all | solution.py:1079
  641.9 95.0 %reduce-scatter.6.cloned.1.call-start = ((), (), s32[]{:S(2)}) async-start(), calls=%async_computation.22 | async-start | bytes 3031040 | tf_op jit(solution)/shard_map/reduce_scatter | solution.py:1355
  703.1 33.8 %all-to-all-start.13 = ((bf16[4,6,96,256]{3,2,1,0:T(8,128)(2,1)}), bf16[4,6,96,256]{3,2,1,0:T(8,128)(2,1)}, u32[]{:S(2)}, u32[]{:S(2)}) async-start(bf16[4,6,96,256]{3,2,1,0:T(8,128)(2,1)} %out_back.1), calls=%async_computation.13 | async-start | bytes 2359296 | tf_op jit(solution)/shard_map/all_to_all | solution.py:1079
  707.7 254.2 %reduce-scatter.8.cloned.1.call-start = ((), (), s32[]{:S(2)}) async-start(), calls=%async_computation.23 | async-start | bytes 10948608 | tf_op jit(solution)/shard_map/reduce_scatter | solution.py:1359
  744.3 71.8 %all-to-all-start.14 = ((bf16[4,6,96,1024]{3,2,1,0:T(8,128)(2,1)}), bf16[4,6,96,1024]{3,2,1,0:T(8,128)(2,1)}, u32[]{:S(2)}, u32[]{:S(2)}) async-start(bf16[4,6,96,1024]{3,2,1,0:T(8,128)(2,1)} %broadcast_in_dim.16), calls=%async_computation.14 | async-start | bytes 9437184 | tf_op jit(solution)/shard_map/all_to_all | solution.py:1079
  819.2 49.0 %all-to-all-start.15 = ((bf16[4,4,384,256]{3,2,1,0:T(8,128)(2,1)}), bf16[4,4,384,256]{3,2,1,0:T(8,128)(2,1)}, u32[]{:S(2)}, u32[]{:S(2)}) async-start(bf16[4,4,384,256]{3,2,1,0:T(8,128)(2,1)} %broadcast_in_dim.17), calls=%async_computation.15 | async-start | bytes 6291456 | tf_op jit(solution)/shard_map/all_to_all | solution.py:1079
  870.4 29.4 %all-to-all-start.16 = ((bf16[4,2,384,256]{3,2,1,0:T(8,128)(2,1)}), bf16[4,2,384,256]{3,2,1,0:T(8,128)(2,1)}, u32[]{:S(2)}, u32[]{:S(2)}) async-start(bf16[4,2,384,256]{3,2,1,0:T(8,128)(2,1)} %broadcast_in_dim.18), calls=%async_computation.16 | async-start | bytes 3145728 | tf_op jit(solution)/shard_map/all_to_all | solution.py:1079
  874.9 120.6 %all-gather.8.cloned.1.call-start = ((), (), s32[]{:S(2)}) async-start(), calls=%async_computation.24 | async-start | bytes 2703360 | tf_op jit(solution)/shard_map/all_gather | solution.py:1545
  921.3 38.2 %all-to-all-start.17 = ((bf16[8,320,256]{2,1,0:T(8,128)(2,1)}), bf16[8,320,256]{2,1,0:T(8,128)(2,1)}, u32[]{:S(2)}, u32[]{:S(2)}) async-start(bf16[8,320,256]{2,1,0:T(8,128)(2,1)} %pad_maximum_fusion.3), calls=%async_computation.17 | async-start | bytes 2621440 | tf_op jit(solution)/shard_map/all_to_all | solution.py:1079
  964.6 30.1 %all-to-all-start.18 = ((f32[32,40,128]{2,1,0:T(8,128)}), f32[32,40,128]{2,1,0:T(8,128)S(1)}, u32[]{:S(2)}, u32[]{:S(2)}) async-start(f32[32,40,128]{2,1,0:T(8,128)} %broadcast_in_dim.19), calls=%async_computation.20 | async-start | bytes 1310720 | tf_op jit(solution)/shard_map/all_to_all | solution.py:1079
  (23 other events, 361.9 us)
Sparse Core Ops, SparseCore 0:
  20.1 76.3 all-gather.9
  98.4 66.0 all-gather.11
  166.4 67.0 all-gather.13
  551.2 134.4 reduce-scatter.9
  687.9 48.7 reduce-scatter.5
  743.6 180.1 reduce-scatter.7
  927.1 67.4 all-gather.7

commit v9 on v8

--- a/solution.py
+++ b/solution.py
@@ -1305,10 +1305,14 @@
             forward.append(self_forward(parts[turn], devices, half))
     else:
         forward = [self_forward(parts[turn], devices, half) for turn in range(turns)]
-    outs = [x[0] for x in forward]
-    if fast:
-        outs[0], parts[-1][0] = lax.optimization_barrier((outs[0], parts[-1][0]))
-    so_back = [exchange(so.reshape(devices, half, 2 * HEAD), both_axes) for so in outs]
+    outs = [x[0].reshape(devices, half, 2 * HEAD) for x in forward]
+    if fast and turns > 2:
+        joined, _ = lax.optimization_barrier((jnp.stack(outs[:-1], axis=1), parts[-1][0]))
+        joined = exchange(joined, both_axes)
+        so_back = [joined[:, turn] for turn in range(turns - 1)]
+        so_back.append(exchange(outs[-1], both_axes))
+    else:
+        so_back = [exchange(so, both_axes) for so in outs]
     if fast:
         blocks = [x.reshape(groups, slots, 2, half, 2 * HEAD) for x in so_back]
         so_tile, branch_s = unpack_project(blocks, small, items, groups)

time: 1020 us -> 1010 us (level)
    all_to_all x18 -> x17, waiting for transfers between devices: 118 us -> 109 us  [exchange(): return lax.all_to_all(x, axis, 0, 0, tiled=True)]
    all_to_all x18 -> x17, starting transfers between devices: 82.1 us -> 77 us  [exchange(): return lax.all_to_all(x, axis, 0, 0, tiled=True)]
    unnamed x62 -> x58, local copies, waits for them, and re-layouts: 23.3 us -> 22.6 us
  transfers between devices with their start and end apart: 34 -> 33, of which waited for: 12 -> 12; matrix products, arithmetic and copies ran while one was open for 15% -> 15% of each run, Pallas kernels for 48% -> 49%
where the time goes in v9:
time: 1010 us; the launch traced here: 996 us
  Pallas kernels  542 us (54%)
  local copies, waits for them, and re-layouts  129 us (13%)
  waiting for transfers between devices  112 us (11%)
  starting transfers between devices  102 us (10%)
  other arithmetic  54.6 us (5%)
  matrix products  21.6 us (2%)
  blocking collectives  19.4 us (2%)
  between operations  15.3 us (2%)
    all_to_all x17, waiting for transfers between devices, exchange(): return lax.all_to_all(x, axis, 0, 0, tiled=True)  109 us
    pallas_call x2, Pallas kernels, cross_backward(): pl.pallas_call(kernel, grid=(items, heads), in_specs=[rows_spec, tiles_sp...  102 us
    pallas_call x3, Pallas kernels, self_backward(): pl.pallas_call(kernel, grid=(blocks,), in_specs=part_specs(parts, half) +...  82.9 us
    all_to_all x17, starting transfers between devices, exchange(): return lax.all_to_all(x, axis, 0, 0, tiled=True)  77 us
    pallas_call x1, Pallas kernels, cross_forward(): pl.pallas_call(kernel, grid=(items, heads // 2), in_specs=[pl.BlockSpec((...  53.8 us
    pallas_call x5, Pallas kernels, weight_terms(): pl.pallas_call(kernel, grid=(tp, 2), in_specs=[pl.BlockSpec(lhs_block, lh...  49.6 us
    pallas_call x3, Pallas kernels, self_forward(): pl.pallas_call(kernel, grid=(blocks,), in_specs=part_specs(parts, half),...  42.9 us
    pallas_call x1, Pallas kernels, feed_forward(): pl.pallas_call(kernel, grid=(slots,), in_specs=[rows_spec, rows_spec, pl....  39.1 us
  transfers between devices with their start and end apart: 33, of which 12 were waited for; matrix products, arithmetic and copies ran while one was open for 15% of the time, Pallas kernels for 49%

profile of v9, /device:TPU:0, one launch (start us, length us, event | category | flops | bytes accessed | tf_op | source)
XLA Modules:
  0.0 996.2 jit_solution(10073515130123463022)
XLA Ops:
  34.9 27.7 %key_value_kernel.1 = (bf16[6,4096,256]{2,1,0:T(8,128)(2,1)}, bf16[6,256,4096]{2,1,0:T(8,128)(2,1)}) custom-call(bf16[6,4096,768]{2,1,0:T(8,128)(2,1)} %bitcast.247, bf16[768,256]{1,0:T(8,128)(2,1)} %wk_ref.1, bf16[256,768]{1,0:T(8,128)(2,1)} %bitcast.311), custom_call_target="tpu_custom_call" | custom-call | flops 19327352832 | bytes 62914560 | tf_op jit(solution)/shard_map/key_value_kernel/pallas_call | solution.py:846
  83.9 53.8 %cross_forward.1 = (bf16[4,6,96,256]{3,2,1,0:T(8,128)(2,1)}, f32[4,6,96,256]{3,2,1,0:T(8,128)}, f32[6,4,8,384]{3,2,1,0:T(8,128)}) custom-call(bf16[6,384,256]{2,1,0:T(8,128)(2,1)} %get-tuple-element.109.q_ref, bf16[6,4096,256]{2,1,0:T(8,128)(2,1)} %get-tuple-element.110.k_ref, bf16[6,256,4096]{2,1,0:T(8,128)(2,1)} %get-tuple-element.111.vt_ref), custom_call_target="tpu_custom_call" | custom-call | flops 38654705664 | bytes 27525120 | tf_op jit(solution)/shard_map/cross_forward/pallas_call | solution.py:174
  145.8 17.7 %all-to-all-done.x_ref.refs_0_ = bf16[4,6,96,256]{3,2,1,0:T(8,128)(2,1)} async-done(((bf16[4,6,96,256]{3,2,1,0:T(8,128)(2,1)}), bf16[4,6,96,256]{3,2,1,0:T(8,128)(2,1)}, u32[]{:S(2)}, u32[]{:S(2)}) %all-to-all-start) | async-done | bytes 1179680 | tf_op jit(solution)/shard_map/all_to_all | solution.py:1079
  163.6 8.9 out_project.1
  178.5 10.6 %project_pack.1 = bf16[3,2,8,2,144,128]{5,4,3,2,1,0:T(8,128)(2,1)} custom-call(bf16[576,1024]{1,0:T(8,128)(2,1)} %bitcast.272, bf16[8,768,1024]{2,1,0:T(8,128)(2,1)} %bitcast.238, bf16[8,768,1024]{2,1,0:T(8,128)(2,1)} %bitcast.239), custom_call_target="tpu_custom_call" | custom-call | flops 3623878656 | bytes 7471104 | tf_op jit(solution)/shard_map/project_pack/pallas_call | solution.py:493
  207.5 19.8 %all-to-all-done.1.refs_0_ = bf16[32,144,128]{2,1,0:T(8,128)(2,1)} async-done(((bf16[32,144,128]{2,1,0:T(8,128)(2,1)}), bf16[32,144,128]{2,1,0:T(8,128)(2,1)}, u32[]{:S(2)}, u32[]{:S(2)}) %all-to-all-start.1) | async-done | bytes 1179680 | tf_op jit(solution)/shard_map/all_to_all | solution.py:1079
  252.6 14.3 %self_forward.3 = (bf16[1536,128]{1,0:T(8,128)(2,1)}, f32[1536,128]{1,0:T(8,128)}, f32[4,8,768]{2,1,0:T(8,128)}) custom-call(bf16[32,144,128]{2,1,0:T(8,128)(2,1)} %all-to-all-done.1.refs_0_), custom_call_target="tpu_custom_call" | custom-call | flops 9663676416 | bytes 3145728 | tf_op jit(solution)/shard_map/self_forward/pallas_call | solution.py:351
  273.0 14.3 %self_forward.4 = (bf16[1536,128]{1,0:T(8,128)(2,1)}, f32[1536,128]{1,0:T(8,128)}, f32[4,8,768]{2,1,0:T(8,128)}) custom-call(bf16[32,144,128]{2,1,0:T(8,128)(2,1)} %all-to-all-done.2.refs_0_), custom_call_target="tpu_custom_call" | custom-call | flops 9663676416 | bytes 3145728 | tf_op jit(solution)/shard_map/self_forward/pallas_call | solution.py:351
  289.3 12.8 %all-to-all-done.3.refs_0_ = bf16[32,144,128]{2,1,0:T(8,128)(2,1)} async-done(((bf16[32,144,128]{2,1,0:T(8,128)(2,1)}), bf16[32,144,128]{2,1,0:T(8,128)(2,1)}, u32[]{:S(2)}, u32[]{:S(2)}) %all-to-all-start.3) | async-done | bytes 1179680 | tf_op jit(solution)/shard_map/all_to_all | solution.py:1079
  305.7 14.3 %self_forward.5 = (bf16[1536,128]{1,0:T(8,128)(2,1)}, f32[1536,128]{1,0:T(8,128)}, f32[4,8,768]{2,1,0:T(8,128)}) custom-call(bf16[32,144,128]{2,1,0:T(8,128)(2,1)} %all-to-all-done.3.refs_0_), custom_call_target="tpu_custom_call" | custom-call | flops 9663676416 | bytes 3145728 | tf_op jit(solution)/shard_map/self_forward/pallas_call | solution.py:351
  331.5 12.7 %all-to-all-done.5 = bf16[32,48,128]{2,1,0:T(8,128)(2,1)} async-done(((bf16[32,48,128]{2,1,0:T(8,128)(2,1)}), bf16[32,48,128]{2,1,0:T(8,128)(2,1)}, u32[]{:S(2)}, u32[]{:S(2)}) %all-to-all-start.5) | async-done | bytes 393248 | tf_op jit(solution)/shard_map/all_to_all | solution.py:1079
  344.2 9.5 unpack_project.1
  359.6 39.1 %feed_forward.1 = (bf16[8,576,512]{2,1,0:T(8,128)(2,1)}, bf16[8,576,512]{2,1,0:T(8,128)(2,1)}, f32[576,1024]{1,0:T(8,128)}, f32[576,1024]{1,0:T(8,128)}) custom-call(bf16[576,1024]{1,0:T(8,128)(2,1)} %bitcast.292, bf16[576,1024]{1,0:T(8,128)(2,1)} %bitcast.267, bf16[8,1024,512]{2,1,0:T(8,128)(2,1)} %bitcast.320, bf16[8,512,1024]{2,1,0:T(8,128)(2,1)} %bitcast.321), custom_call_target="tpu_custom_call" | custom-call | flops 19327352832 | bytes 16777216 | tf_op jit(solution)/shard_map/feed_forward/pallas_call | solution.py:945
  428.7 12.2 %weight_terms.5.refs_2_ = bf16[2,4,4,2368,128]{4,3,2,1,0:T(8,128)(2,1)} custom-call(bf16[8,576,512]{2,1,0:T(8,128)(2,1)} %get-tuple-element.134.refs_0_, bf16[576,1024]{1,0:T(8,128)(2,1)} %bitcast.293), custom_call_target="tpu_custom_call" | custom-call | flops 4831838208 | bytes 13107200 | tf_op jit(solution)/shard_map/weight_terms/pallas_call | solution.py:992
  446.6 12.1 %weight_terms.6 = bf16[2,4,4,2368,128]{4,3,2,1,0:T(8,128)(2,1)} custom-call(bf16[8,576,512]{2,1,0:T(8,128)(2,1)} %get-tuple-element.133.refs_0_, bf16[576,1024]{1,0:T(8,128)(2,1)} %bitcast.268, bf16[2,4,4,2368,128]{4,3,2,1,0:T(8,128)(2,1)} %weight_terms.5.refs_2_), custom_call_target="tpu_custom_call", output_to_operand_aliasing={{}: (2, {})} | custom-call | flops 4831838208 | bytes 13107200 | tf_op jit(solution)/shard_map/weight_terms/pallas_call | solution.py:992
  498.7 27.6 %self_backward.3 = bf16[32,144,128]{2,1,0:T(8,128)(2,1)} custom-call(bf16[32,144,128]{2,1,0:T(8,128)(2,1)} %all-to-all-done.1.refs_0_, bf16[1536,128]{1,0:T(8,128)(2,1)} %bitcast.58.refs_1_, f32[1536,128]{1,0:T(8,128)} %get-tuple-element.136.refs_2_, f32[4,8,768]{2,1,0:T(8,128)} %get-tuple-element.137.refs_3_), custom_call_target="tpu_custom_call" | custom-call | flops 24159191040 | bytes 6291456 | tf_op jit(solution)/shard_map/self_backward/pallas_call | solution.py:437
  526.3 12.4 %fusion = bf16[4,4,2368,128]{3,2,1,0:T(8,128)(2,1)} fusion(bf16[4,4,2368,128]{3,2,1,0:T(8,128)(2,1)} %collective-permute-done.8, bf16[2,4,4,2368,128]{4,3,2,1,0:T(8,128)(2,1)} %bitcast_dynamic-update-slice_fusion, s32[]{:T(128)S(6)} %select_n.57), kind=kLoop, calls=%fused_computation.1 | loop fusion | flops 19398656 | bytes 29097988 | tf_op jit(solution)/shard_map/convert_element_type | solution.py:1353
  538.7 19.4 %all_to_all.90 = bf16[32,48,128]{2,1,0:T(8,128)(2,1)} all-to-all(bf16[32,48,128]{2,1,0:T(8,128)(2,1)S(1)} %bitcast.285), channel_id=1, replica_groups=mesh['seq'=8,'tp'=4] {'seq','tp'}, dimensions={0} | all-to-all | bytes 786432 | tf_op jit(solution)/shard_map/all_to_all | solution.py:1079
  561.7 27.6 %self_backward.4 = bf16[32,144,128]{2,1,0:T(8,128)(2,1)} custom-call(bf16[32,144,128]{2,1,0:T(8,128)(2,1)} %all-to-all-done.3.refs_0_, bf16[1536,128]{1,0:T(8,128)(2,1)} %bitcast.310, f32[1536,128]{1,0:T(8,128)} %get-tuple-element.139.refs_2_, f32[4,8,768]{2,1,0:T(8,128)} %get-tuple-element.140.refs_3_), custom_call_target="tpu_custom_call" | custom-call | flops 24159191040 | bytes 6291456 | tf_op jit(solution)/shard_map/self_backward/pallas_call | solution.py:437
  595.6 27.6 %self_backward.5 = bf16[32,144,128]{2,1,0:T(8,128)(2,1)} custom-call(bf16[32,144,128]{2,1,0:T(8,128)(2,1)} %all-to-all-done.2.refs_0_, bf16[1536,128]{1,0:T(8,128)(2,1)} %bitcast.308, f32[1536,128]{1,0:T(8,128)} %get-tuple-element.145.refs_2_, f32[4,8,768]{2,1,0:T(8,128)} %get-tuple-element.146.refs_3_), custom_call_target="tpu_custom_call" | custom-call | flops 24159191040 | bytes 6291456 | tf_op jit(solution)/shard_map/self_backward/pallas_call | solution.py:437
  637.4 10.4 %reshape.342 = f32[14,6,10,4,4,80]{5,4,3,0,2,1:T(4,128)} reshape(f32[14,6,10,1280]{3,0,2,1:T(8,128)} %fusion.1) | data formatting | bytes 8601600 | tf_op jit(solution)/shard_map/reshape | solution.py:1421
  660.9 12.7 %unpack_back.1 = (bf16[8,576,384]{2,1,0:T(8,128)(2,1)}, f32[576,1024]{1,0:T(8,128)}) custom-call(bf16[2,8,2,144,128]{4,3,2,1,0:T(8,128)(2,1)} %bitcast.72.refs_0_, bf16[2,8,2,144,128]{4,3,2,1,0:T(8,128)(2,1)} %bitcast.75.refs_1_, bf16[2,8,2,144,128]{4,3,2,1,0:T(8,128)(2,1)} %bitcast.66.refs_2_, bf16[8,768,1024]{2,1,0:T(8,128)(2,1)} %bitcast.242, ...), custom_call_target="tpu_custom_call" | custom-call | flops 3623878656 | bytes 2359296 | tf_op jit(solution)/shard_map/unpack_back/pallas_call | solution.py:632
  674.8 8.2 norm_backward.3
  698.5 10.5 %weight_terms.7.refs_2_ = bf16[32,1296,128]{2,1,0:T(8,128)(2,1)} custom-call(bf16[8,576,384]{2,1,0:T(8,128)(2,1)} %get-tuple-element.151.refs_0_, bf16[576,1024]{1,0:T(8,128)(2,1)} %bitcast.273), custom_call_target="tpu_custom_call" | custom-call | flops 3623878656 | bytes 9830400 | tf_op jit(solution)/shard_map/weight_terms/pallas_call | solution.py:992
  736.9 66.8 %cross_backward.2 = (bf16[4,384,256]{2,1,0:T(8,128)(2,1)}, bf16[4,256,4096]{2,1,0:T(8,128)(2,1)}, bf16[4,256,4096]{2,1,0:T(8,128)(2,1)}) custom-call(bf16[6,384,256]{2,1,0:T(8,128)(2,1)} %get-tuple-element.109.q_ref, bf16[4,6,96,256]{3,2,1,0:T(8,128)(2,1)} %all-to-all-done.12.do_ref, f32[4,6,96,256]{3,2,1,0:T(8,128)} %get-tuple-element.156.o_ref, ...), custom_call_target="tpu_custom_call" | custom-call | flops 64424509440 | bytes 36700160 | tf_op jit(solution)/shard_map/cross_backward/pallas_call | solution.py:250
  811.6 35.2 %cross_backward.3 = (bf16[2,384,256]{2,1,0:T(8,128)(2,1)}, bf16[2,256,4096]{2,1,0:T(8,128)(2,1)}, bf16[2,256,4096]{2,1,0:T(8,128)(2,1)}) custom-call(bf16[6,384,256]{2,1,0:T(8,128)(2,1)} %get-tuple-element.109.q_ref, bf16[4,6,96,256]{3,2,1,0:T(8,128)(2,1)} %all-to-all-done.12.do_ref, f32[4,6,96,256]{3,2,1,0:T(8,128)} %get-tuple-element.156.o_ref, ...), custom_call_target="tpu_custom_call" | custom-call | flops 32212254720 | bytes 18350080 | tf_op jit(solution)/shard_map/cross_backward/pallas_call | solution.py:250
  846.8 9.1 all-to-all-done.14.dq_ref
  867.5 19.9 %key_value_grads.2 = f32[512,768]{1,0:T(8,128)} custom-call(bf16[4,256,4096]{2,1,0:T(8,128)(2,1)} %get-tuple-element.176.dk_ref, bf16[4,256,4096]{2,1,0:T(8,128)(2,1)} %get-tuple-element.177.dv_ref, bf16[6,4096,768]{2,1,0:T(8,128)(2,1)} %bitcast.248), custom_call_target="tpu_custom_call" | custom-call | flops 12884901888 | bytes 41943040 | tf_op jit(solution)/shard_map/key_value_grads/pallas_call | solution.py:891
  887.5 12.4 %key_value_grads.3 = f32[512,768]{1,0:T(8,128)} custom-call(bf16[2,256,4096]{2,1,0:T(8,128)(2,1)} %get-tuple-element.178.dk_ref, bf16[2,256,4096]{2,1,0:T(8,128)(2,1)} %get-tuple-element.179.dv_ref, bf16[6,4096,768]{2,1,0:T(8,128)(2,1)} %bitcast.249), custom_call_target="tpu_custom_call" | custom-call | flops 6442450944 | bytes 20971520 | tf_op jit(solution)/shard_map/key_value_grads/pallas_call | solution.py:891
  913.3 11.4 %last_kernel.2 = (f32[12,6,32,1024]{3,2,1,0:T(8,128)}, f32[4,2,1024]{2,1,0:T(2,128)}) custom-call(bf16[12,6,32,1024]{3,2,1,0:T(8,128)(2,1)} %x_ref.5, f32[6,1,1024]{2,1,0:T(1,128)} %get-tuple-element.373.scale_ref, bf16[4,6,96,1024]{3,2,1,0:T(8,128)(2,1)} %all-to-all-done.13.middle_ref, bf16[4,4,384,256]{3,2,1,0:T(8,128)(2,1)} %all-to-all-done.14.dq_ref, ...), custom_call_target="tpu_custom_call" | custom-call | flops 3221225472 | bytes 15728640 | tf_op jit(solution)/shard_map/last_kernel/pallas_call | solution.py:1048
  932.8 14.4 %all-to-all-done.16 = bf16[8,320,256]{2,1,0:T(8,128)(2,1)} async-done(((bf16[8,320,256]{2,1,0:T(8,128)(2,1)}), bf16[8,320,256]{2,1,0:T(8,128)(2,1)}, u32[]{:S(2)}, u32[]{:S(2)}) %all-to-all-start.16) | async-done | bytes 1310752 | tf_op jit(solution)/shard_map/all_to_all | solution.py:1079
  970.4 12.0 %all-to-all-done.17 = f32[32,40,128]{2,1,0:T(8,128)S(1)} async-done(((f32[32,40,128]{2,1,0:T(8,128)}), f32[32,40,128]{2,1,0:T(8,128)S(1)}, u32[]{:S(2)}, u32[]{:S(2)}) %all-to-all-start.17) | async-done | bytes 655392 | tf_op jit(solution)/shard_map/all_to_all | solution.py:1079
  (255 shorter events, 363.4 us)
Async XLA Ops:
  7.2 156.4 %all-gather.10.cloned.1.call-start = ((), (), s32[]{:S(2)}) async-start(), calls=%async_computation.24 | async-start | bytes 14155776 | tf_op jit(solution)/shard_map/all_gather | solution.py:1155
  20.0 339.6 %all-gather.12.cloned.1.call-start = ((), (), s32[]{:S(2)}) async-start(), calls=%async_computation.25 | async-start | bytes 9437184 | tf_op jit(solution)/shard_map/all_gather | solution.py:1155
  22.4 337.2 %all-gather.14.cloned.1.call-start = ((), (), s32[]{:S(2)}) async-start(), calls=%async_computation.26 | async-start | bytes 9437184 | tf_op jit(solution)/shard_map/all_gather | solution.py:1155
  23.7 41.7 %collective-permute-start.1 = (bf16[1,6,16,80]{3,2,1,0:T(8,128)(2,1)S(1)}, bf16[1,6,16,80]{3,2,1,0:T(8,128)(2,1)S(1)}, u32[]{:S(2)}, u32[]{:S(2)}) collective-permute-start(bf16[1,6,16,80]{3,2,1,0:T(8,128)(2,1)S(1)} %slice.207), channel_id=1, source_target_pairs={{4,0},{8,4},{12,8},{16,12},{20,16},{24,20},{28,24},{5,1},{9,5},{13... | collective-permute-start | bytes 46088 | tf_op jit(solution)/shard_map/ppermute | solution.py:30
  25.7 39.7 %collective-permute-start = (bf16[1,6,16,80]{3,2,1,0:T(8,128)(2,1)}, bf16[1,6,16,80]{3,2,1,0:T(8,128)(2,1)}, u32[]{:S(2)}, u32[]{:S(2)}) collective-permute-start(bf16[1,6,16,80]{3,2,1,0:T(8,128)(2,1)} %slice.205), channel_id=1, source_target_pairs={{0,4},{4,8},{8,12},{12,16},{16,20},{20,24},{24,28},{1,5},{5,9},{9,... | collective-permute-start | bytes 46088 | tf_op jit(solution)/shard_map/ppermute | solution.py:29
  66.3 16.1 %collective-permute-start.3 = (bf16[26,6,1,80]{3,0,2,1:T(8,128)(2,1)S(1)}, bf16[26,6,1,80]{3,0,2,1:T(8,128)(2,1)S(1)}, u32[]{:S(2)}, u32[]{:S(2)}) collective-permute-start(bf16[26,6,1,80]{3,0,2,1:T(8,128)(2,1)S(1)} %get-tuple-element.359), channel_id=1, source_target_pairs={{1,0},{2,1},{3,2},{5,4},{6,5},{7,6},{9,8},{10,9},{11,10},{13,12},{... | collective-permute-start | bytes 74888 | tf_op jit(solution)/shard_map/ppermute | solution.py:30
  67.6 14.8 %collective-permute-start.2 = (bf16[26,6,1,80]{3,0,2,1:T(8,128)(2,1)S(1)}, bf16[26,6,1,80]{3,0,2,1:T(8,128)(2,1)S(1)}, u32[]{:S(2)}, u32[]{:S(2)}) collective-permute-start(bf16[26,6,1,80]{3,0,2,1:T(8,128)(2,1)S(1)} %get-tuple-element.358), channel_id=1, source_target_pairs={{0,1},{1,2},{2,3},{4,5},{5,6},{6,7},{8,9},{9,10},{10,11},{12,13},{... | collective-permute-start | bytes 74888 | tf_op jit(solution)/shard_map/ppermute | solution.py:29
  137.8 25.8 %all-to-all-start = ((bf16[4,6,96,256]{3,2,1,0:T(8,128)(2,1)}), bf16[4,6,96,256]{3,2,1,0:T(8,128)(2,1)}, u32[]{:S(2)}, u32[]{:S(2)}) async-start(bf16[4,6,96,256]{3,2,1,0:T(8,128)(2,1)} %get-tuple-element.112), calls=%async_computation | async-start | bytes 2359296 | tf_op jit(solution)/shard_map/all_to_all | solution.py:1079
  192.9 34.4 %all-to-all-start.1 = ((bf16[32,144,128]{2,1,0:T(8,128)(2,1)}), bf16[32,144,128]{2,1,0:T(8,128)(2,1)}, u32[]{:S(2)}, u32[]{:S(2)}) async-start(bf16[32,144,128]{2,1,0:T(8,128)(2,1)} %bitcast.271), calls=%async_computation.1 | async-start | bytes 2359296 | tf_op jit(solution)/shard_map/all_to_all | solution.py:1079
  227.3 39.6 %all-to-all-start.2 = ((bf16[32,144,128]{2,1,0:T(8,128)(2,1)}), bf16[32,144,128]{2,1,0:T(8,128)(2,1)}, u32[]{:S(2)}, u32[]{:S(2)}) async-start(bf16[32,144,128]{2,1,0:T(8,128)(2,1)} %bitcast.270), calls=%async_computation.2 | async-start | bytes 2359296 | tf_op jit(solution)/shard_map/all_to_all | solution.py:1079
  266.9 35.2 %all-to-all-start.3 = ((bf16[32,144,128]{2,1,0:T(8,128)(2,1)}), bf16[32,144,128]{2,1,0:T(8,128)(2,1)}, u32[]{:S(2)}, u32[]{:S(2)}) async-start(bf16[32,144,128]{2,1,0:T(8,128)(2,1)} %bitcast.269), calls=%async_computation.3 | async-start | bytes 2359296 | tf_op jit(solution)/shard_map/all_to_all | solution.py:1079
  302.1 25.0 %all-to-all-start.4 = ((bf16[32,2,48,128]{3,2,1,0:T(8,128)(2,1)}), bf16[32,2,48,128]{3,2,1,0:T(8,128)(2,1)S(1)}, u32[]{:S(2)}, u32[]{:S(2)}) async-start(bf16[32,2,48,128]{3,2,1,0:T(8,128)(2,1)} %pad_maximum_fusion.6), calls=%async_computation.4 | async-start | bytes 1572864 | tf_op jit(solution)/shard_map/all_to_all | solution.py:1079
  327.0 17.2 %all-to-all-start.5 = ((bf16[32,48,128]{2,1,0:T(8,128)(2,1)}), bf16[32,48,128]{2,1,0:T(8,128)(2,1)}, u32[]{:S(2)}, u32[]{:S(2)}) async-start(bf16[32,48,128]{2,1,0:T(8,128)(2,1)} %bitcast.309), calls=%async_computation.5 | async-start | bytes 786432 | tf_op jit(solution)/shard_map/all_to_all | solution.py:1079
  425.4 57.7 %all-to-all-start.6 = ((bf16[32,48,128]{2,1,0:T(8,128)(2,1)}), bf16[32,48,128]{2,1,0:T(8,128)(2,1)}, u32[]{:S(2)}, u32[]{:S(2)}) async-start(bf16[32,48,128]{2,1,0:T(8,128)(2,1)} %bitcast.57), calls=%async_computation.6 | async-start | bytes 786432 | tf_op jit(solution)/shard_map/all_to_all | solution.py:1079
  441.8 26.2 %collective-permute-start.5 = (bf16[1,6,8,1024]{3,2,1,0:T(8,128)(2,1)S(1)}, bf16[1,6,8,1024]{3,2,1,0:T(8,128)(2,1)S(1)}, u32[]{:S(2)}, u32[]{:S(2)}) collective-permute-start(bf16[1,6,8,1024]{3,2,1,0:T(8,128)(2,1)S(1)} %get-tuple-element.347), channel_id=1, source_target_pairs={{4,0},{8,4},{12,8},{16,12},{20,16},{24,20},{28,24},{5,1},{9,5},{13... | collective-permute-start | bytes 294920 | tf_op jit(solution)/shard_map/ppermute | solution.py:30
  443.1 24.9 %collective-permute-start.4 = (bf16[1,6,8,1024]{3,2,1,0:T(8,128)(2,1)S(1)}, bf16[1,6,8,1024]{3,2,1,0:T(8,128)(2,1)S(1)}, u32[]{:S(2)}, u32[]{:S(2)}) collective-permute-start(bf16[1,6,8,1024]{3,2,1,0:T(8,128)(2,1)S(1)} %get-tuple-element.346), channel_id=1, source_target_pairs={{0,4},{4,8},{8,12},{12,16},{16,20},{20,24},{24,28},{1,5},{5,9},{9,... | collective-permute-start | bytes 294920 | tf_op jit(solution)/shard_map/ppermute | solution.py:29
  470.0 9.8 collective-permute-start.6
  491.2 35.1 %collective-permute-start.8 = (bf16[4,4,2368,128]{3,2,1,0:T(8,128)(2,1)}, bf16[4,4,2368,128]{3,2,1,0:T(8,128)(2,1)}, u32[]{:S(2)}, u32[]{:S(2)}) collective-permute-start(bf16[4,4,2368,128]{3,2,1,0:T(8,128)(2,1)} %dynamic-slice_bitcast_fusion), channel_id=1, source_target_pairs={{0,4},{4,0},{8,12},{12,8},{16,20},{20,16},{24,28},{28,24},{1,5},{5... | collective-permute-start | bytes 29097992 | tf_op jit(solution)/shard_map/ppermute | solution.py:1351
  491.3 34.9 %all-to-all-start.10 = ((bf16[32,48,128]{2,1,0:T(8,128)(2,1)}), bf16[32,48,128]{2,1,0:T(8,128)(2,1)S(1)}, u32[]{:S(2)}, u32[]{:S(2)}) async-start(bf16[32,48,128]{2,1,0:T(8,128)(2,1)} %bitcast.73), calls=%async_computation.10 | async-start | bytes 786432 | tf_op jit(solution)/shard_map/all_to_all | solution.py:1079
  498.4 175.2 %reduce-scatter.10.cloned.1.call-start = ((), (), s32[]{:S(2)}) async-start(), calls=%async_computation.27 | async-start | bytes 12124160
  558.1 32.7 %all-to-all-start.9 = ((bf16[32,144,128]{2,1,0:T(8,128)(2,1)}), bf16[32,144,128]{2,1,0:T(8,128)(2,1)}, u32[]{:S(2)}, u32[]{:S(2)}) async-start(bf16[32,144,128]{2,1,0:T(8,128)(2,1)} %self_backward.3), calls=%async_computation.9 | async-start | bytes 2359296 | tf_op jit(solution)/shard_map/all_to_all | solution.py:1079
  590.8 34.0 %all-to-all-start.8 = ((bf16[32,144,128]{2,1,0:T(8,128)(2,1)}), bf16[32,144,128]{2,1,0:T(8,128)(2,1)}, u32[]{:S(2)}, u32[]{:S(2)}) async-start(bf16[32,144,128]{2,1,0:T(8,128)(2,1)} %self_backward.4), calls=%async_computation.8 | async-start | bytes 2359296 | tf_op jit(solution)/shard_map/all_to_all | solution.py:1079
  624.7 36.2 %all-to-all-start.11 = ((bf16[32,144,128]{2,1,0:T(8,128)(2,1)}), bf16[32,144,128]{2,1,0:T(8,128)(2,1)}, u32[]{:S(2)}, u32[]{:S(2)}) async-start(bf16[32,144,128]{2,1,0:T(8,128)(2,1)} %self_backward.5), calls=%async_computation.11 | async-start | bytes 2359296 | tf_op jit(solution)/shard_map/all_to_all | solution.py:1079
  629.5 95.1 %reduce-scatter.6.cloned.1.call-start = ((), (), s32[]{:S(2)}) async-start(), calls=%async_computation.21 | async-start | bytes 3031040 | tf_op jit(solution)/shard_map/reduce_scatter | solution.py:1359
  690.7 33.9 %all-to-all-start.12 = ((bf16[4,6,96,256]{3,2,1,0:T(8,128)(2,1)}), bf16[4,6,96,256]{3,2,1,0:T(8,128)(2,1)}, u32[]{:S(2)}, u32[]{:S(2)}) async-start(bf16[4,6,96,256]{3,2,1,0:T(8,128)(2,1)} %out_back.1), calls=%async_computation.12 | async-start | bytes 2359296 | tf_op jit(solution)/shard_map/all_to_all | solution.py:1079
  695.3 254.3 %reduce-scatter.8.cloned.1.call-start = ((), (), s32[]{:S(2)}) async-start(), calls=%async_computation.22 | async-start | bytes 10948608 | tf_op jit(solution)/shard_map/reduce_scatter | solution.py:1363
  732.0 71.8 %all-to-all-start.13 = ((bf16[4,6,96,1024]{3,2,1,0:T(8,128)(2,1)}), bf16[4,6,96,1024]{3,2,1,0:T(8,128)(2,1)}, u32[]{:S(2)}, u32[]{:S(2)}) async-start(bf16[4,6,96,1024]{3,2,1,0:T(8,128)(2,1)} %broadcast_in_dim.16), calls=%async_computation.13 | async-start | bytes 9437184 | tf_op jit(solution)/shard_map/all_to_all | solution.py:1079
  806.9 49.0 %all-to-all-start.14 = ((bf16[4,4,384,256]{3,2,1,0:T(8,128)(2,1)}), bf16[4,4,384,256]{3,2,1,0:T(8,128)(2,1)}, u32[]{:S(2)}, u32[]{:S(2)}) async-start(bf16[4,4,384,256]{3,2,1,0:T(8,128)(2,1)} %broadcast_in_dim.17), calls=%async_computation.14 | async-start | bytes 6291456 | tf_op jit(solution)/shard_map/all_to_all | solution.py:1079
  858.1 29.4 %all-to-all-start.15 = ((bf16[4,2,384,256]{3,2,1,0:T(8,128)(2,1)}), bf16[4,2,384,256]{3,2,1,0:T(8,128)(2,1)}, u32[]{:S(2)}, u32[]{:S(2)}) async-start(bf16[4,2,384,256]{3,2,1,0:T(8,128)(2,1)} %broadcast_in_dim.18), calls=%async_computation.15 | async-start | bytes 3145728 | tf_op jit(solution)/shard_map/all_to_all | solution.py:1079
  862.6 120.6 %all-gather.8.cloned.1.call-start = ((), (), s32[]{:S(2)}) async-start(), calls=%async_computation.23 | async-start | bytes 2703360 | tf_op jit(solution)/shard_map/all_gather | solution.py:1549
  909.0 38.2 %all-to-all-start.16 = ((bf16[8,320,256]{2,1,0:T(8,128)(2,1)}), bf16[8,320,256]{2,1,0:T(8,128)(2,1)}, u32[]{:S(2)}, u32[]{:S(2)}) async-start(bf16[8,320,256]{2,1,0:T(8,128)(2,1)} %pad_maximum_fusion.3), calls=%async_computation.16 | async-start | bytes 2621440 | tf_op jit(solution)/shard_map/all_to_all | solution.py:1079
  952.3 30.1 %all-to-all-start.17 = ((f32[32,40,128]{2,1,0:T(8,128)}), f32[32,40,128]{2,1,0:T(8,128)S(1)}, u32[]{:S(2)}, u32[]{:S(2)}) async-start(f32[32,40,128]{2,1,0:T(8,128)} %broadcast_in_dim.19), calls=%async_computation.19 | async-start | bytes 1310720 | tf_op jit(solution)/shard_map/all_to_all | solution.py:1079
  (20 other events, 329.1 us)
Sparse Core Ops, SparseCore 0:
  20.1 76.3 all-gather.9
  98.4 65.9 all-gather.11
  166.3 67.1 all-gather.13
  538.8 134.4 reduce-scatter.9
  675.5 48.6 reduce-scatter.5
  731.2 179.9 reduce-scatter.7
  914.5 67.8 all-gather.7
